TPU v7x, 128 devices: a whole 4x4x4 slice. The times are simulated.
128 devices in a mesh: section: 4 (over x), lat: 32 (over z, y, core).
Axes of the slice: x: 4, y: 4, z: 4, core: 2. Of those that a mesh axis runs over, the one named last changes fastest.
Arguments:
- saved_input: bfloat16 [4, 384, 192, 768], P('section', 'lat'), may hold values from -6 to 6
- incoming: bfloat16 [4, 384, 192, 768], P('section', 'lat'), may hold values from -6 to 6
- spectral_gain: float32 [4, 384, 192], P('section'), may hold values from 0.5 to 2
- mix_weight: bfloat16 [4, 2, 192, 192], P('section'), may hold values from -0.3125 to 0.3125
- proj_weight: bfloat16 [4, 192, 192], P('section'), may hold values from -0.4375 to 0.4375
Outputs:
- received: bfloat16 [4, 384, 192, 768], P('section', 'lat')
- grad_w2: float32 [4, 192, 192], P('section')
- grad_mix: float32 [4, 2, 192, 192], P('section')
- grad_gain: float32 [4, 384, 192], P('section')
All inputs are finite; a program needn't handle non-finite values.
Results may differ from a plain program's by a relative error of at most 0.025.
Values may be sent and summed in bfloat16 or wider, within the bound.
No kernel may reach another device: no remote copies, remote signals or barrier semaphores. Data moves between devices by JAX's collectives and lax.ppermute only.
A program may use at most 192 MiB of HBM per device.

v0:
```python
import math

import jax
import jax.numpy as jnp
from jax import lax
from jax.sharding import PartitionSpec as P

NLAT = 384
NLON = 768
MODES = 384


log_gamma_half = 0.5723649429247001


def from_behind(value, axis, steps):
    count = lax.axis_size(axis)
    pairs = [(source, (source + steps) % count) for source in range(count)]
    return lax.ppermute(value, axis, pairs)


def quadrature(colatitude):
    harmonic = jnp.arange(1, NLAT // 2 + 1, dtype=jnp.float32)
    terms = (
        jnp.cos(2.0 * harmonic[None, :] * colatitude[:, None])
        / (4.0 * harmonic * harmonic - 1.0)[None, :]
    )
    return 2.0 / NLAT * (1.0 - 2.0 * jnp.sum(terms, axis=1))


def legendre_table(orders, cos_lat, sin_lat, degrees):
    order_col = orders[:, None]
    cosine = cos_lat[None, :]
    log_start = (
        0.5 * jnp.log((2.0 * order_col + 1.0) / 2.0)
        + 0.5
        * (
            jax.scipy.special.gammaln(order_col + 0.5)
            - log_gamma_half
            - jax.scipy.special.gammaln(order_col + 1.0)
        )
        + order_col * jnp.log(sin_lat)[None, :]
    )
    zero_state = jnp.zeros(log_start.shape, jnp.float32)

    def block_step(state_in, block_index):
        previous, current, log_scale = state_in
        row_list = []
        for inner_step in range(16):
            degree = (block_index * 16 + inner_step).astype(jnp.float32)
            factor_up = jnp.sqrt(
                jnp.maximum(4.0 * degree * degree - 1.0, 1.0)
                / jnp.maximum(degree * degree - order_col * order_col, 1.0)
            )
            lower_degree = degree - 1.0
            factor_down = jnp.sqrt(
                jnp.maximum(lower_degree * lower_degree - order_col * order_col, 0.0)
                / jnp.maximum(4.0 * lower_degree * lower_degree - 1.0, 1.0)
            )
            general = factor_up * (cosine * current - factor_down * previous)
            second = jnp.sqrt(2.0 * order_col + 3.0) * cosine * current
            new_row = jnp.where(
                degree == order_col,
                1.0,
                jnp.where(
                    degree == order_col + 1.0,
                    second,
                    jnp.where(degree > order_col + 1.0, general, 0.0),
                ),
            )
            row_list.append(new_row * jnp.exp(log_scale))
            previous, current = (current, new_row)
        largest = jnp.maximum(jnp.abs(previous), jnp.abs(current))
        largest = jnp.where(largest > 0.0, largest, 1.0)
        return (
            (previous / largest, current / largest, log_scale + jnp.log(largest)),
            jnp.stack(row_list),
        )

    _, blocks = lax.scan(
        block_step, (zero_state, zero_state, log_start), jnp.arange(degrees // 16, dtype=jnp.int32)
    )
    stacked = blocks.reshape(degrees, orders.shape[0], cos_lat.shape[0])
    return jnp.transpose(stacked, (1, 0, 2))


def fourier_tables(orders):
    longitude = jnp.arange(NLON, dtype=jnp.int32)
    phase_index = longitude[:, None] * orders[None, :] % NLON
    angle_table = phase_index.astype(jnp.float32) * (2.0 * math.pi / NLON)
    cosine_table = jnp.cos(angle_table)
    sine_table = jnp.sin(angle_table)
    forward_table = jnp.stack([cosine_table, -sine_table]).astype(jnp.bfloat16)
    factor = jnp.where(orders == 0, 1.0, 2.0).astype(jnp.float32) / NLON
    inverse_table = jnp.stack(
        [factor[:, None] * cosine_table.T, -factor[:, None] * sine_table.T]
    ).astype(jnp.bfloat16)
    return (forward_table, inverse_table)


def gelu_slope(pre_act):
    return 0.5 * (
        1.0 + jax.scipy.special.erf(pre_act * (1.0 / math.sqrt(2.0)))
    ) + pre_act * jnp.exp(-0.5 * pre_act * pre_act) * (1.0 / math.sqrt(2.0 * math.pi))


def degree_major(matrices, values, lowest_rows, group_size):
    pieces = []
    for group_index, lowest in enumerate(lowest_rows):
        first_row = group_index * group_size
        product = jnp.einsum(
            "klj,kjc->klc",
            matrices[first_row : first_row + group_size, lowest:, :],
            values,
            preferred_element_type=jnp.float32,
        )
        pieces.append(product)
    return jnp.concatenate(pieces, axis=0)


def latitude_major(matrices, values, lowest_rows, group_size):
    pieces = []
    for group_index, lowest in enumerate(lowest_rows):
        first_row = group_index * group_size
        pieces.append(
            jnp.einsum(
                "klj,klc->kjc",
                matrices[first_row : first_row + group_size, lowest:, :],
                values,
                preferred_element_type=jnp.float32,
            )
        )
    return jnp.concatenate(pieces, axis=0)


def shards(saved_input, incoming, spectral_gain, mix_weight, proj_weight):
    devices = lax.axis_size("lat")
    device = lax.axis_index("lat")
    per_device = MODES // devices
    lat_local = saved_input.shape[1]
    channels = saved_input.shape[2]
    column_index = jnp.arange(MODES, dtype=jnp.int32)
    local_index = jnp.arange(per_device, dtype=jnp.int32)
    order_own = device * per_device + local_index
    lowest_rows = [0]
    colatitude = (jnp.arange(NLAT, dtype=jnp.float32) + 0.5) * (math.pi / NLAT)
    quad_weight = quadrature(colatitude)
    forward_table, inverse_table = fourier_tables(column_index)
    legendre = legendre_table(
        order_own.astype(jnp.float32), jnp.cos(colatitude), jnp.sin(colatitude), MODES
    )
    analysis_table = (quad_weight[None, None, :] * legendre).astype(jnp.bfloat16)
    synthesis_table = legendre.astype(jnp.bfloat16)
    grid_field = saved_input[0]
    upstream = incoming[0]
    spectrum = jnp.einsum(
        "jck,pkm->mjpc", grid_field, forward_table, preferred_element_type=jnp.float32
    ).astype(jnp.bfloat16)
    spectrum = spectrum.reshape(MODES, lat_local, 2 * channels)
    coefficients = degree_major(
        analysis_table,
        lax.all_to_all(spectrum, "lat", split_axis=0, concat_axis=1, tiled=True),
        lowest_rows,
        per_device,
    )
    gain_pair = jnp.concatenate([spectral_gain[0], spectral_gain[0]], axis=1)
    scaled = (gain_pair[None, :, :] * coefficients).astype(jnp.bfloat16)
    real_part = mix_weight[0, 0]
    imag_part = mix_weight[0, 1]
    block_weight = jnp.concatenate(
        [
            jnp.concatenate([real_part, imag_part], axis=1),
            jnp.concatenate([-imag_part, real_part], axis=1),
        ],
        axis=0,
    )
    scaled_rows = scaled.reshape(per_device * MODES, 2 * channels)
    mixed_modes = jnp.dot(scaled_rows, block_weight, preferred_element_type=jnp.float32).astype(
        jnp.bfloat16
    )
    mixed_modes = mixed_modes.reshape(per_device, MODES, 2 * channels)
    grid_modes = latitude_major(synthesis_table, mixed_modes, lowest_rows, per_device).astype(
        jnp.bfloat16
    )
    returned = lax.all_to_all(grid_modes, "lat", split_axis=1, concat_axis=0, tiled=True)
    pre_act = jnp.einsum(
        "mjpc,pmk->jck",
        returned.reshape(MODES, lat_local, 2, channels),
        inverse_table,
        preferred_element_type=jnp.float32,
    )
    activated = jax.nn.gelu(pre_act, approximate=False).astype(jnp.bfloat16)
    grad_act = jnp.einsum(
        "cd,jdk->jck", proj_weight[0], upstream, preferred_element_type=jnp.float32
    )
    proj_local = jnp.einsum("jck,jdk->cd", activated, upstream, preferred_element_type=jnp.float32)
    grad_pre = (grad_act * gelu_slope(pre_act)).astype(jnp.bfloat16)
    grad_modes = jnp.einsum(
        "jck,pmk->mjpc", grad_pre, inverse_table, preferred_element_type=jnp.float32
    ).astype(jnp.bfloat16)
    grad_modes = grad_modes.reshape(MODES, lat_local, 2 * channels)
    grad_mixed = degree_major(
        synthesis_table,
        lax.all_to_all(grad_modes, "lat", split_axis=0, concat_axis=1, tiled=True),
        lowest_rows,
        per_device,
    ).astype(jnp.bfloat16)
    grad_rows = grad_mixed.reshape(per_device * MODES, 2 * channels)
    grad_scaled = jnp.dot(grad_rows, block_weight.T, preferred_element_type=jnp.float32).reshape(
        per_device, MODES, 2 * channels
    )
    block_grad = jnp.einsum("rc,rd->cd", scaled_rows, grad_rows, preferred_element_type=jnp.float32)
    grad_real = block_grad[:channels, :channels] + block_grad[channels:, channels:]
    grad_imag = block_grad[:channels, channels:] - block_grad[channels:, :channels]
    gain_sum = jnp.sum(grad_scaled * coefficients, axis=0)
    gain_local = gain_sum[:, :channels] + gain_sum[:, channels:]
    grad_coeffs = (gain_pair[None, :, :] * grad_scaled).astype(jnp.bfloat16)
    grad_spectrum = latitude_major(analysis_table, grad_coeffs, lowest_rows, per_device).astype(
        jnp.bfloat16
    )
    grad_back = lax.all_to_all(grad_spectrum, "lat", split_axis=1, concat_axis=0, tiled=True)
    grad_field = upstream.astype(jnp.float32) + jnp.einsum(
        "mjpc,pkm->jck",
        grad_back.reshape(MODES, lat_local, 2, channels),
        forward_table,
        preferred_element_type=jnp.float32,
    )
    outgoing = grad_field.astype(jnp.bfloat16)
    received = from_behind(outgoing, "section", -1)
    proj_total = lax.psum(proj_local.astype(jnp.bfloat16), "lat").astype(jnp.float32)
    real_total, imag_total, gain_total = (
        lax.psum(grad_real.astype(jnp.bfloat16), "lat").astype(jnp.float32),
        lax.psum(grad_imag.astype(jnp.bfloat16), "lat").astype(jnp.float32),
        lax.psum(gain_local.astype(jnp.bfloat16), "lat").astype(jnp.float32),
    )
    grid_scale = 1.0 / math.sqrt(NLAT * NLON)
    mode_scale = 1.0 / math.sqrt(MODES)
    grad_w2 = grid_scale * proj_total
    grad_mix = grid_scale * jnp.stack([real_total, imag_total])
    grad_gain = mode_scale * gain_total
    return (received[None], grad_w2[None], grad_mix[None], grad_gain[None])


def solution(mesh):
    in_specs = (
        P("section", "lat", None, None),
        P("section", "lat", None, None),
        P("section", None, None),
        P("section", None, None, None),
        P("section", None, None),
    )
    out_specs = (
        P("section", "lat", None, None),
        P("section", None, None),
        P("section", None, None, None),
        P("section", None, None),
    )
    return jax.shard_map(shards, mesh=mesh, in_specs=in_specs, out_specs=out_specs, check_vma=False)
```

profile of v0, /device:TPU:6, one launch (start us, length us, event | category | flops | bytes accessed | tf_op | source)
XLA Modules:
  0.0 638.1 jit_solution(12271798083731310552)
XLA Ops:
  15.8 5.2 copy.60
  21.0 9.0 %all-to-all-start = ((bf16[384,12,384]{2,1,0:T(8,128)(2,1)}), bf16[384,12,384]{2,1,0:T(8,128)(2,1)}, u32[]{:S(2)}, u32[]{:S(2)}) async-start(bf16[384,12,384]{2,1,0:T(8,128)(2,1)} %copy.60), calls=%async_computation | async-start | bytes 9437184 | tf_op jit(solution)/shard_map/all_to_all | solution.py:162
  30.3 120.9 %while.23 = (s32[]{:T(128)}, f32[12,384]{1,0:T(8,128)S(1)}, f32[12,384]{1,0:T(8,128)S(1)}, f32[12,384]{1,0:T(8,128)S(1)}, f32[24,16,12,384]{3,2,1,0:T(8,128)}, /...) while((s32[]{:T(128)}, f32[12,384]{1,0:T(8,128)S(1)}, ...), condition=%wide.region_2.3_spmd.clone.clone.clone.clone, body=%wide.region_1.2_spmd.clone.clone.clone.clone.sunk | while | flops 1801326 | bytes 2800101 | solution.py:80
  152.3 9.1 %copy.56 = f32[384,12,384]{0,2,1:T(8,128)} copy(f32[384,12,384]{2,1,0:T(8,128)} %bitcast.550) | data formatting | bytes 14155776 | tf_op jit(solution)/shard_map/reshape | solution.py:83
  169.0 6.8 %all_to_all.51 = bf16[12,384,384]{2,1,0:T(8,128)(2,1)} reshape(bf16[12,32,12,384]{3,2,1,0:T(8,128)(2,1)} %copy.62) | data formatting | bytes 7077888 | tf_op jit(solution)/shard_map/all_to_all | solution.py:162
  175.7 9.7 %multiply_convert_fusion.1 = (bf16[12,384,384]{2,1,0:T(8,128)(2,1)S(1)}, f32[12,384,384]{2,1,0:T(8,128)}) fusion(f32[384,384]{1,0:T(8,128)} %copy.57, bf16[12,384,384]{2,1,0:T(8,128)(2,1)} %all_to_all.51, f32[384,12,384]{0,2,1:T(8,128)} %copy.56, f32[384]{0:T(512)S(1)} %subtract_multiply_fusion), kind=kOutput, calls=%fused_computation.203 | convolution fusion | flops 1366032384 | bytes 21825024 | tf_op jit(solution)/shard_map/klj,kjc->klc/dot_general | solution.py:111
  188.3 7.5 %convolution_convert_fusion.2 = bf16[12,384,384]{2,1,0:T(8,128)(2,1)S(1)} fusion(bf16[12,384,384]{2,1,0:T(8,128)(2,1)S(1)} %bitcast.554, f32[384,12,384]{2,1,0:T(8,128)} %bitcast.551), kind=kOutput, calls=%fused_computation.226 | convolution fusion | flops 1360723968 | bytes 14155776 | tf_op jit(solution)/shard_map/klj,klc->kjc/dot_general | solution.py:126
  200.2 7.6 %all-to-all-start.1 = ((bf16[12,384,384]{2,0,1:T(8,128)(2,1)}), bf16[12,384,384]{2,0,1:T(8,128)(2,1)}, u32[]{:S(2)}, u32[]{:S(2)}) async-start(bf16[12,384,384]{2,0,1:T(8,128)(2,1)} %copy.65), calls=%async_computation.1 | async-start | bytes 9437184 | tf_op jit(solution)/shard_map/all_to_all | solution.py:185
  207.8 5.3 multiply_convert_fusion.6
  213.1 54.4 %all-to-all-done.1 = bf16[12,384,384]{2,0,1:T(8,128)(2,1)} async-done(((bf16[12,384,384]{2,0,1:T(8,128)(2,1)}), bf16[12,384,384]{2,0,1:T(8,128)(2,1)}, u32[]{:S(2)}, u32[]{:S(2)}) %all-to-all-start.1) | async-done | bytes 3538976 | tf_op jit(solution)/shard_map/all_to_all | solution.py:185
  267.5 5.6 copy.67
  273.1 12.0 %reshape.1584 = bf16[384,12,2,192]{3,2,1,0:T(2,128)(2,1)} reshape(bf16[32,12,12,384]{3,2,1,0:T(8,128)(2,1)} %copy.67) | data formatting | bytes 7077888 | tf_op jit(solution)/shard_map/reshape | solution.py:188
  285.1 9.2 %fusion.72 = f32[12,192,768,1]{2,1,3,0:T(8,128)} fusion(bf16[384,12,2,192]{3,2,1,0:T(2,128)(2,1)} %reshape.1584, bf16[1,384,768]{2,1,0:T(8,128)(2,1)S(1)} %get-tuple-element.512, bf16[1,384,768]{2,1,0:T(8,128)(2,1)S(1)} %get-tuple-element.513), kind=kOutput, calls=%fused_computation.208 | convolution fusion | flops 2718498816 | bytes 11796480 | tf_op jit(solution)/shard_map/mjpc,pmk->jck/dot_general | solution.py:186
  294.3 9.7 %convert_bitcast_fusion = bf16[384,12,2,192]{0,3,1,2:T(8,128)(2,1)} fusion(f32[12,192,768,1]{2,1,3,0:T(8,128)} %fusion.72, bf16[1,12,192,768]{3,2,1,0:T(8,128)(2,1)} %param.8, bf16[1,384,768]{2,1,0:T(8,128)(2,1)S(1)} %get-tuple-element.512, bf16[1,384,768]{2,1,0:T(8,128)(2,1)S(1)} %get-tuple-element.513, bf16[1,192,192]{2,1,0:T(8,128)(2,1)S(1)} %copy-done.21), kind=kOutput, calls=%fused_computation.221 | convolution fusion | flops 3419209728 | bytes 15409152 | tf_op jit(solution)/shard_map/jck,pmk->mjpc/dot_general | solution.py:198
  311.6 61.2 %all_to_all.66 = bf16[384,12,384]{2,1,0:T(8,128)(2,1)S(1)} all-to-all(bf16[384,12,384]{2,1,0:T(8,128)(2,1)} %copy.70), channel_id=1, replica_groups=mesh['section'=4,'lat'=32] {'lat'}, dimensions={0} | all-to-all | bytes 7077888 | tf_op jit(solution)/shard_map/all_to_all | solution.py:204
  375.6 6.8 %all_to_all.58 = bf16[12,384,384]{2,1,0:T(8,128)(2,1)} reshape(bf16[12,32,12,384]{3,2,1,0:T(8,128)(2,1)} %copy.72) | data formatting | bytes 7077888 | tf_op jit(solution)/shard_map/all_to_all | solution.py:204
  382.4 7.9 %convolution_convert_fusion.1 = bf16[12,384,384]{2,1,0:T(8,128)(2,1)S(1)} fusion(bf16[12,384,384]{2,1,0:T(8,128)(2,1)} %all_to_all.58, f32[384,12,384]{2,1,0:T(8,128)} %bitcast.552), kind=kOutput, calls=%fused_computation.225 | convolution fusion | flops 1360723968 | bytes 14155776 | tf_op jit(solution)/shard_map/klj,kjc->klc/dot_general | solution.py:111
  390.3 8.9 %multiply_reduce_fusion = (f32[384,384]{1,0:T(8,128)}, f32[12,384,384]{2,1,0:T(8,128)}) fusion(f32[12,384,384]{2,1,0:T(8,128)} %get-tuple-element.505, bf16[12,384,384]{2,1,0:T(8,128)(2,1)S(1)} %convolution_convert_fusion.1, bf16[192,192]{1,0:T(8,128)(2,1)S(1)} %copy-done.18, bf16[192,192]{1,0:T(8,128)(2,1)S(1)} %copy-done.14, ...), kind=kOutput, calls=%fused_computation.185 | convolution fusion | flops 1363525632 | bytes 18505728 | tf_op jit(solution)/shard_map/dot_general | solution.py:209
  399.3 6.2 fusion.90
  407.8 60.9 %all_to_all.67 = bf16[12,384,384]{2,0,1:T(8,128)(2,1)S(1)} all-to-all(bf16[12,384,384]{2,0,1:T(8,128)(2,1)S(1)} %copy.73), channel_id=1, replica_groups=mesh['section'=4,'lat'=32] {'lat'}, dimensions={1} | all-to-all | bytes 7077888 | tf_op jit(solution)/shard_map/all_to_all | solution.py:221
  472.1 12.1 %reshape.1586 = bf16[384,12,2,192]{3,2,1,0:T(2,128)(2,1)} reshape(bf16[32,12,12,384]{3,2,1,0:T(8,128)(2,1)} %copy.75) | data formatting | bytes 7077888 | tf_op jit(solution)/shard_map/reshape | solution.py:224
  484.2 10.0 %fusion.55 = bf16[12,192,768]{2,1,0:T(8,128)(2,1)} fusion(bf16[1,12,192,768]{3,2,1,0:T(8,128)(2,1)} %param.8, bf16[384,12,2,192]{3,2,1,0:T(2,128)(2,1)} %reshape.1586, bf16[1,768,384]{2,1,0:T(8,128)(2,1)S(1)} %copy-done.9, bf16[1,768,384]{2,1,0:T(8,128)(2,1)S(1)} %copy-done.11), kind=kOutput, calls=%fused_computation.176 | convolution fusion | flops 2723807232 | bytes 11796480 | tf_op jit(solution)/shard_map/mjpc,pkm->jck/dot_general | solution.py:222
  495.1 18.9 %fusion.118 = bf16[192,192]{1,0:T(8,128)(2,1)} fusion(bf16[1,12,192,768]{3,2,1,0:T(8,128)(2,1)S(1)} %copy-done.20, f32[12,192,768,1]{2,1,3,0:T(8,128)} %fusion.72), kind=kOutput, calls=%fused_computation.253 | convolution fusion | flops 794529792 | bytes 10690560 | tf_op jit(solution)/shard_map/jck,jdk->cd/dot_general | solution.py:196
  517.8 102.4 %all-reduce.3.cloned.1.call-done = (bf16[192,192]{1,0:T(8,128)(2,1)}, bf16[1,1,192,192]{3,2,1,0:T(8,128)(2,1)}, bf16[1,1,192,192]{3,2,1,0:T(8,128)(2,1)}, bf16[384,192]{1,0:T(8,128)(2,1)}) async-done(((bf16[192,192]{1,0:T(8,128)(2,1)}, bf16[1,1,192,192]{3,2,1,0:T(8,128)(2,1)}, bf16[1,1,192,192]{3,2,1,0:T(8,128)(2,1)}, bf16[384,192]{1,0:T(8,128)(2,1)}), (bf16[192,192]{1,0:T(8,128)(2,1)}, ...) | async-done | bytes 368656 | tf_op jit(solution)/shard_map/psum | solution.py:230
  (1555 shorter events, 149.7 us)
Async XLA Ops:
  21.0 142.9 %all-to-all-start = ((bf16[384,12,384]{2,1,0:T(8,128)(2,1)}), bf16[384,12,384]{2,1,0:T(8,128)(2,1)}, u32[]{:S(2)}, u32[]{:S(2)}) async-start(bf16[384,12,384]{2,1,0:T(8,128)(2,1)} %copy.60), calls=%async_computation | async-start | bytes 9437184 | tf_op jit(solution)/shard_map/all_to_all | solution.py:162
  30.3 120.9 %copy-start.19 = (f32[1,384,192]{1,2,0:T(8,128)S(1)}, f32[1,384,192]{1,2,0:T(8,128)}, u32[]{:S(2)}) copy-start(f32[1,384,192]{1,2,0:T(8,128)} %param.9) | copy-start | bytes 884740
  152.3 10.2 %copy-start.12 = (bf16[1,2,192,192]{3,2,1,0:T(8,128)(2,1)S(1)}, bf16[1,2,192,192]{3,2,1,0:T(8,128)(2,1)}, u32[]{:S(2)}) copy-start(bf16[1,2,192,192]{3,2,1,0:T(8,128)(2,1)} %param.10) | copy-start | bytes 442372
  175.7 9.7 %copy-start.13 = (bf16[192,192]{1,0:T(8,128)(2,1)S(1)}, bf16[192,192]{1,0:T(8,128)(2,1)}, u32[]{:S(2)}) copy-start(bf16[192,192]{1,0:T(8,128)(2,1)} %fusion.185) | copy-start | bytes 221188
  175.7 9.7 %copy-start.15 = (bf16[192,192]{1,0:T(8,128)(2,1)S(1)}, bf16[192,192]{1,0:T(8,128)(2,1)}, u32[]{:S(2)}) copy-start(bf16[192,192]{1,0:T(8,128)(2,1)} %get-tuple-element.502) | copy-start | bytes 221188
  175.7 9.7 %copy-start.17 = (bf16[192,192]{1,0:T(8,128)(2,1)S(1)}, bf16[192,192]{1,0:T(8,128)(2,1)}, u32[]{:S(2)}) copy-start(bf16[192,192]{1,0:T(8,128)(2,1)} %get-tuple-element.503) | copy-start | bytes 221188
  185.4 10.4 %copy-start.2 = (bf16[12,384,384]{2,1,0:T(8,128)(2,1)}, bf16[12,384,384]{2,1,0:T(8,128)(2,1)S(1)}, u32[]{:S(2)}) copy-start(bf16[12,384,384]{2,1,0:T(8,128)(2,1)S(1)} %get-tuple-element.504) | copy-start | bytes 10616836
  200.2 67.4 %all-to-all-start.1 = ((bf16[12,384,384]{2,0,1:T(8,128)(2,1)}), bf16[12,384,384]{2,0,1:T(8,128)(2,1)}, u32[]{:S(2)}, u32[]{:S(2)}) async-start(bf16[12,384,384]{2,0,1:T(8,128)(2,1)} %copy.65), calls=%async_computation.1 | async-start | bytes 9437184 | tf_op jit(solution)/shard_map/all_to_all | solution.py:185
  207.8 412.4 %all-reduce.3.cloned.1.call-start = ((), (), s32[]{:S(2)}) async-start(), calls=%async_computation.4 | async-start | bytes 983040 | tf_op jit(solution)/shard_map/psum | solution.py:230
  285.1 9.2 %copy-start.21 = (bf16[1,192,192]{2,1,0:T(8,128)(2,1)S(1)}, bf16[1,192,192]{2,1,0:T(8,128)(2,1)}, u32[]{:S(2)}) copy-start(bf16[1,192,192]{2,1,0:T(8,128)(2,1)} %param.11) | copy-start | bytes 221188
  382.4 7.9 %copy-start.14 = (bf16[192,192]{1,0:T(8,128)(2,1)S(1)}, bf16[192,192]{1,0:T(8,128)(2,1)}, u32[]{:S(2)}) copy-start(bf16[192,192]{1,0:T(8,128)(2,1)} %fusion.185) | copy-start | bytes 221188
  382.4 7.9 %copy-start.16 = (bf16[192,192]{1,0:T(8,128)(2,1)S(1)}, bf16[192,192]{1,0:T(8,128)(2,1)}, u32[]{:S(2)}) copy-start(bf16[192,192]{1,0:T(8,128)(2,1)} %get-tuple-element.502) | copy-start | bytes 221188
  382.4 8.0 %copy-start.18 = (bf16[192,192]{1,0:T(8,128)(2,1)S(1)}, bf16[192,192]{1,0:T(8,128)(2,1)}, u32[]{:S(2)}) copy-start(bf16[192,192]{1,0:T(8,128)(2,1)} %get-tuple-element.503) | copy-start | bytes 221188
  382.4 16.9 %slice-start = ((s8[7077888]{0:T(1024)(128)(4,1)}), s8[4194304]{0:T(1024)(128)(4,1)S(1)}, s32[]{:S(2)}) async-start(s8[7077888]{0:T(1024)(128)(4,1)} %bitcast.543), calls=%async_computation.5 | async-start | bytes 8388608
  390.3 9.0 %copy-start.4 = (bf16[12,384,384]{2,1,0:T(8,128)(2,1)}, bf16[12,384,384]{2,1,0:T(8,128)(2,1)S(1)}, u32[]{:S(2)}) copy-start(bf16[12,384,384]{2,1,0:T(8,128)(2,1)S(1)} %convolution_convert_fusion.1) | copy-start | bytes 10616836
  390.3 9.0 %slice-start.1 = ((s8[7077888]{0:T(1024)(128)(4,1)}), s8[2883584]{0:T(1024)(128)(4,1)S(1)}, s32[]{:S(2)}) async-start(s8[7077888]{0:T(1024)(128)(4,1)} %bitcast.543), calls=%async_computation.6 | async-start | bytes 5767168
  390.3 9.0 %copy-start.6 = (f32[384,384]{1,0:T(8,128)S(1)}, f32[384,384]{1,0:T(8,128)}, u32[]{:S(2)}) copy-start(f32[384,384]{1,0:T(8,128)} %copy.57) | copy-start | bytes 1769476
  472.1 12.1 %copy-start.9 = (bf16[1,768,384]{2,1,0:T(8,128)(2,1)S(1)}, bf16[1,768,384]{2,1,0:T(8,128)(2,1)}, u32[]{:S(2)}) copy-start(bf16[1,768,384]{2,1,0:T(8,128)(2,1)} %copy-done.8) | copy-start | bytes 1769476
  472.1 12.1 %copy-start.11 = (bf16[1,768,384]{2,1,0:T(8,128)(2,1)S(1)}, bf16[1,768,384]{2,1,0:T(8,128)(2,1)}, u32[]{:S(2)}) copy-start(bf16[1,768,384]{2,1,0:T(8,128)(2,1)} %copy-done.10) | copy-start | bytes 1769476
  484.2 10.9 %copy-start.20 = (bf16[1,12,192,768]{3,2,1,0:T(8,128)(2,1)S(1)}, bf16[1,12,192,768]{3,2,1,0:T(8,128)(2,1)}, u32[]{:S(2)}) copy-start(bf16[1,12,192,768]{3,2,1,0:T(8,128)(2,1)} %param.8) | copy-start | bytes 10616836
  494.2 19.8 %copy-start.3 = (bf16[12,384,384]{2,1,0:T(8,128)(2,1)S(1)}, bf16[12,384,384]{2,1,0:T(8,128)(2,1)}, u32[]{:S(2)}) copy-start(bf16[12,384,384]{2,1,0:T(8,128)(2,1)} %copy-done.2) | copy-start | bytes 10616836
  494.2 19.8 %copy-start.5 = (bf16[12,384,384]{2,1,0:T(8,128)(2,1)S(1)}, bf16[12,384,384]{2,1,0:T(8,128)(2,1)}, u32[]{:S(2)}) copy-start(bf16[12,384,384]{2,1,0:T(8,128)(2,1)} %copy-done.4) | copy-start | bytes 10616836
  494.3 132.8 %collective-permute-start = (bf16[12,192,768]{2,1,0:T(8,128)(2,1)}, bf16[12,192,768]{2,1,0:T(8,128)(2,1)}, u32[]{:S(2)}, u32[]{:S(2)}) collective-permute-start(bf16[12,192,768]{2,1,0:T(8,128)(2,1)} %fusion.55), channel_id=1, source_target_pairs={{0,96},{32,0},{64,32},{96,64},{1,97},{33,1},{65,33},{97,65},{2,98}... | collective-permute-start | bytes 10616840 | tf_op jit(solution)/shard_map/ppermute | solution.py:19
  514.0 117.0 %copy-start.1 = (bf16[1,12,192,768]{3,2,1,0:T(8,128)(2,1)S(1)}, bf16[1,12,192,768]{3,2,1,0:T(8,128)(2,1)}, u32[]{:S(2)}) copy-start(bf16[1,12,192,768]{3,2,1,0:T(8,128)(2,1)} %param.7) | copy-start | bytes 10616836
  (4 other events, 14.3 us)
Sparse Core Ops, SparseCore 0:
  517.9 102.2 all-reduce.2
where the time goes:
time: 644 us; the launch traced here: 638 us
  waiting for transfers between devices  157 us (24%)
  local copies, waits for them, and re-layouts  124 us (19%)
  blocking collectives  122 us (19%)
  matrix products  96.1 us (15%)
  other arithmetic  79.5 us (12%)
  loops' own time  27.6 us (4%)
  starting transfers between devices  17.5 us (3%)
  between operations  14.6 us (2%)
    psum x1, waiting for transfers between devices, shards(): lax.psum(proj_local.astype(jnp.bfloat16), 'lat').astype(jnp.float32)  102 us
    all_to_all x1, blocking collectives, shards(): lax.all_to_all(grad_modes, 'lat', split_axis=0, concat_axis=1, tiled=True)  61.2 us
    all_to_all x1, blocking collectives, shards(): lax.all_to_all(grad_spectrum, 'lat', split_axis=1, concat_axis=0, tiled=T...  60.9 us
    all_to_all x1, waiting for transfers between devices, shards(): lax.all_to_all(grid_modes, 'lat', split_axis=1, concat_axis=0, tiled=True)  54.4 us
    while x360, other arithmetic  40.4 us
    another operation x1, loops' own time, legendre_table(): lax.scan(block_step, (zero_state, zero_state, log_start), jnp.arange(degr...  27.6 us
    dot_general x1, matrix products, shards(): jnp.einsum('jck,jdk->cd', activated, upstream, preferred_element_type=jnp...  18.9 us
    dynamic_update_slice x24, local copies, waits for them, and re-layouts, legendre_table(): lax.scan(block_step, (zero_state, zero_state, log_start), jnp.arange(degr...  18.9 us
  transfers between devices with their start and end apart: 4, of which 2 were waited for; matrix products, arithmetic and copies ran while one was open for 22% of the time, Pallas kernels for 0%

commit v1 on v0

v1 whole, which is shorter than its diff:
```python
import functools
import math

import jax
import jax.numpy as jnp
import ml_dtypes
import numpy as np
from jax import lax
from jax.experimental import pallas as pl
from jax.experimental.pallas import tpu as pltpu
from jax.sharding import PartitionSpec as P

NLAT = 384
NLON = 768
MODES = 384
C = 192
DEVICES = 32
LAT_LOCAL = 12
ORDERS = 12
GROUPS = 3
GROUP_ORDERS = 4
HALF = 64
LANES = 128
TILE = 16
TILES = 9
GROUP_TILES = 3
SPAN = DEVICES * TILE
VMEM_LIMIT = 56 * 1024 * 1024
F32 = jnp.float32
BF16 = jnp.bfloat16
NT = (((1,), (1,)), ((), ()))

PAIRS = ((0, 0), (1, 0), (1, 1), (2, 1), (2, 2), (3, 2))


def degrees_of(group):
    return MODES - LANES * group


def params(**extra):
    return pltpu.CompilerParams(vmem_limit_bytes=VMEM_LIMIT, **extra)


def cost(flops, bytes_accessed, transcendentals=0):
    return pl.CostEstimate(
        flops=int(flops), bytes_accessed=int(bytes_accessed), transcendentals=int(transcendentals)
    )


def dot(left, right):
    return jnp.dot(left, right, preferred_element_type=F32)


def dot_nt(left, right):
    return lax.dot_general(left, right, NT, preferred_element_type=F32)


def order_rows(group):
    device = np.arange(DEVICES)[:, None]
    local = np.arange(GROUP_ORDERS)[None, :] + GROUP_ORDERS * group
    return (DEVICES * local + device).reshape(-1)


def fourier_rows(orders):
    phase = (orders[:, None] * np.arange(NLON)[None, :]) % NLON
    angle = phase * (2.0 * math.pi / NLON)
    return np.cos(angle), -np.sin(angle)


def forward_groups():
    tables = []
    for group in range(GROUPS):
        cosine, sine = fourier_rows(order_rows(group))
        tables.append(np.concatenate([cosine, sine], axis=0))
    return np.stack(tables).astype(np.float32).astype(ml_dtypes.bfloat16)


def inverse_rows():
    device = np.arange(DEVICES)[:, None]
    orders = (DEVICES * np.arange(ORDERS)[None, :] + device).reshape(-1)
    factor = np.where(orders == 0, 1.0, 2.0)[:, None] / NLON
    cosine, sine = fourier_rows(orders)
    table = np.concatenate([factor * cosine, factor * sine], axis=0)
    return table.astype(np.float32).astype(ml_dtypes.bfloat16)


def spread_tables():
    rows = np.arange(SPAN)
    source, inner = rows // TILE, rows % TILE
    tables = np.zeros((len(PAIRS), SPAN, NLAT), np.float32)
    for index, (order, tile) in enumerate(PAIRS):
        lat = TILE * tile + inner - LAT_LOCAL * order
        valid = (lat >= 0) & (lat < LAT_LOCAL)
        tables[index, rows[valid], (source * LAT_LOCAL + lat)[valid]] = 1.0
    return tables.astype(ml_dtypes.bfloat16)


def log_starts():
    table = np.zeros((DEVICES, TILE, LANES), np.float32)
    numbers = np.zeros((DEVICES, TILE, LANES), np.float32)
    for device in range(DEVICES):
        for local in range(ORDERS):
            order = DEVICES * local + device
            numbers[device, local] = order
            table[device, local] = 0.5 * math.log((2.0 * order + 1.0) / 2.0) + 0.5 * (
                math.lgamma(order + 0.5) - math.lgamma(0.5) - math.lgamma(order + 1.0)
            )
    return table, numbers


def latitude_rows():
    colatitude = (np.arange(NLAT) + 0.5) * (math.pi / NLAT)
    harmonic = np.arange(1, NLAT // 2 + 1)
    terms = np.cos(2.0 * harmonic[None, :] * colatitude[:, None]) / (4.0 * harmonic**2 - 1.0)
    weight = 2.0 / NLAT * (1.0 - 2.0 * np.sum(terms, axis=1))
    rows = np.stack([np.cos(colatitude), np.log(np.sin(colatitude)), weight])
    return np.concatenate([rows, np.zeros((5, NLAT))]).astype(np.float32)


def legendre_kernel(start_ref, order_ref, lat_ref, out_ref):
    order = jnp.concatenate([order_ref[...]] * 3, axis=1)
    cosine = jnp.broadcast_to(lat_ref[0:1, :], (TILE, NLAT))
    log_sin = jnp.broadcast_to(lat_ref[1:2, :], (TILE, NLAT))
    log_start = jnp.concatenate([start_ref[...]] * 3, axis=1) + order * log_sin
    narrow = order_ref[...]
    narrow_square = narrow * narrow
    second_factor = jnp.concatenate([jnp.sqrt(2.0 * narrow + 3.0)] * 3, axis=1)
    zeros = jnp.zeros((TILE, NLAT), F32)

    def block(index, state):
        previous, current, log_scale = state
        scale = jnp.exp(log_scale)
        for inner in range(16):
            row = index * 16 + inner
            degree = row.astype(F32)
            lower = degree - 1.0
            up = jnp.sqrt(
                jnp.maximum(4.0 * degree * degree - 1.0, 1.0)
                / jnp.maximum(degree * degree - narrow_square, 1.0)
            )
            down = jnp.sqrt(
                jnp.maximum(lower * lower - narrow_square, 0.0)
                / jnp.maximum(4.0 * lower * lower - 1.0, 1.0)
            )
            up = jnp.concatenate([up] * 3, axis=1)
            down = jnp.concatenate([down] * 3, axis=1)
            general = up * (cosine * current - down * previous)
            second = second_factor * cosine * current
            new_row = jnp.where(
                degree == order,
                1.0,
                jnp.where(
                    degree == order + 1.0, second, jnp.where(degree > order + 1.0, general, 0.0)
                ),
            )
            out_ref[row] = new_row * scale
            previous, current = current, new_row
        largest = jnp.maximum(jnp.abs(previous), jnp.abs(current))
        largest = jnp.where(largest > 0.0, largest, 1.0)
        return previous / largest, current / largest, log_scale + jnp.log(largest)

    lax.fori_loop(0, MODES // 16, block, (zeros, zeros, log_start))


def legendre_rows(start, order, lat):
    return pl.pallas_call(
        legendre_kernel,
        out_shape=jax.ShapeDtypeStruct((MODES, TILE, NLAT), F32),
        compiler_params=params(),
        cost_estimate=cost(MODES * TILE * NLAT * 25, MODES * TILE * NLAT * 4),
        name="legendre_rows",
    )(start, order, lat)


def expand_kernel(group, rows_ref, lat_ref, spread_ref, a_ref, s_ref, at_ref, st_ref):
    weight = lat_ref[2:3, :]
    for local in range(GROUP_ORDERS):
        legendre = rows_ref[:, GROUP_ORDERS * group + local, :]
        synthesis = legendre.astype(BF16)
        analysis = (weight * legendre).astype(BF16)
        for index, (order, _) in enumerate(PAIRS):
            if order != local:
                continue
            spread = spread_ref[index]
            a_ref[index] = dot_nt(analysis, spread).astype(BF16)
            s_ref[index] = dot_nt(synthesis, spread).astype(BF16)
            at_ref[index] = dot_nt(spread, analysis).astype(BF16)
            st_ref[index] = dot_nt(spread, synthesis).astype(BF16)


def expand_tables(group, rows, lat, spread):
    degrees = degrees_of(group)
    pairs = len(PAIRS)
    flat = jax.ShapeDtypeStruct((pairs, degrees, SPAN), BF16)
    turned = jax.ShapeDtypeStruct((pairs, SPAN, degrees), BF16)
    flat_spec = pl.BlockSpec((pairs, LANES, SPAN), lambda b: (0, b, 0))
    turned_spec = pl.BlockSpec((pairs, SPAN, LANES), lambda b: (0, 0, b))
    return pl.pallas_call(
        functools.partial(expand_kernel, group),
        grid=(degrees // LANES,),
        in_specs=[
            pl.BlockSpec((LANES, TILE, NLAT), lambda b: (b + group, 0, 0)),
            pl.BlockSpec((8, NLAT), lambda b: (0, 0)),
            pl.BlockSpec((pairs, SPAN, NLAT), lambda b: (0, 0, 0)),
        ],
        out_specs=[flat_spec, flat_spec, turned_spec, turned_spec],
        out_shape=[flat, flat, turned, turned],
        compiler_params=params(),
        cost_estimate=cost(
            8 * pairs * degrees * SPAN * NLAT, degrees * TILE * NLAT * 4 + pairs * degrees * SPAN * 8
        ),
        name=f"expand_tables_{group}",
    )(rows, lat, spread)


def half_lanes(shape):
    return lax.broadcasted_iota(jnp.int32, shape, 1) < HALF


def spectrum_kernel(field_ref, table_ref, out_ref, scratch):
    step = pl.program_id(0)
    rows = DEVICES * GROUP_ORDERS
    low = half_lanes((rows, LANES))
    for inner in range(4):
        product = dot_nt(table_ref[...], field_ref[inner])
        real, imag = product[:rows], product[rows:]
        real_a, imag_a = real[:, :LANES], imag[:, :LANES]
        tiles = (
            jnp.where(low, real_a, pltpu.roll(imag_a, HALF, 1)),
            jnp.where(low, pltpu.roll(real_a, HALF, 1), imag_a),
            jnp.concatenate([real[:, LANES:], imag[:, LANES:]], axis=1),
        )
        for index, tile in enumerate(tiles):
            scratch[index, pl.ds(step * 4 + inner, rows, stride=LAT_LOCAL), :] = tile

    @pl.when(step == LAT_LOCAL // 4 - 1)
    def _():
        for index in range(GROUPS):
            out_ref[:, index * LANES : (index + 1) * LANES] = scratch[index].astype(BF16)


def spectrum_rows(field, table):
    rows = DEVICES * GROUP_ORDERS * LAT_LOCAL
    return pl.pallas_call(
        spectrum_kernel,
        grid=(LAT_LOCAL // 4,),
        in_specs=[
            pl.BlockSpec((4, C, NLON), lambda b: (b, 0, 0)),
            pl.BlockSpec((2 * DEVICES * GROUP_ORDERS, NLON), lambda b: (0, 0)),
        ],
        out_specs=pl.BlockSpec((rows, 2 * C), lambda b: (0, 0)),
        out_shape=jax.ShapeDtypeStruct((rows, 2 * C), BF16),
        scratch_shapes=[pltpu.VMEM((GROUPS, rows, LANES), F32)],
        compiler_params=params(),
        cost_estimate=cost(
            2 * LAT_LOCAL * C * NLON * 256, LAT_LOCAL * C * NLON * 2 + rows * 2 * C * 2
        ),
        name="spectrum_rows",
    )(field, table)


def spectral_kernel(
    group, recv_ref, a_ref, st_ref, gain_ref, mix_ref, *rest
):
    outs = rest[-5:]
    coef_ref, scaled_ref = outs[0], outs[1]
    out_refs = outs[2:]
    degrees = degrees_of(group)
    tiles = [recv_ref[:, tile].reshape(SPAN, 2 * C) for tile in range(GROUP_TILES)]
    mixed = []
    for local in range(GROUP_ORDERS):
        coef = None
        for index, (order, tile) in enumerate(PAIRS):
            if order == local:
                part = dot(a_ref[index], tiles[tile])
                coef = part if coef is None else coef + part
        rows = slice(local * degrees, (local + 1) * degrees)
        coef_ref[rows, :] = coef
        scaled = (gain_ref[LANES * group :, :] * coef).astype(BF16)
        scaled_ref[rows, :] = scaled
        mixed.append(dot(scaled, mix_ref[...]).astype(BF16))
    for tile in range(GROUP_TILES):
        grid = (
            dot(st_ref[2 * tile], mixed[tile]) + dot(st_ref[2 * tile + 1], mixed[tile + 1])
        ).astype(BF16)
        for index, out_ref in enumerate(out_refs):
            out_ref[:, tile] = grid[:, index * LANES : (index + 1) * LANES].reshape(
                DEVICES, TILE, LANES
            )


def whole(shape):
    return pl.BlockSpec(shape, lambda *_: (0,) * len(shape))


def spectral_forward(group, recv, a, st, gain, mix, earlier):
    degrees = degrees_of(group)
    rows = GROUP_ORDERS * degrees
    pairs = len(PAIRS)
    payload = jax.ShapeDtypeStruct((DEVICES, TILES, TILE, LANES), BF16)
    payload_spec = pl.BlockSpec(
        (DEVICES, GROUP_TILES, TILE, LANES), lambda b: (0, group, 0, 0)
    )
    return pl.pallas_call(
        functools.partial(spectral_kernel, group),
        grid=(1,),
        in_specs=[
            whole((DEVICES, GROUP_TILES, TILE, 2 * C)),
            whole((pairs, degrees, SPAN)),
            whole((pairs, SPAN, degrees)),
            whole((MODES, 2 * C)),
            whole((2 * C, 2 * C)),
        ]
        + [pl.BlockSpec(memory_space=pl.ANY)] * len(earlier),
        out_specs=[whole((rows, 2 * C)), whole((rows, 2 * C))] + [payload_spec] * 3,
        out_shape=[
            jax.ShapeDtypeStruct((rows, 2 * C), F32),
            jax.ShapeDtypeStruct((rows, 2 * C), BF16),
        ]
        + [payload] * 3,
        input_output_aliases={5 + index: 2 + index for index in range(len(earlier))},
        compiler_params=params(),
        cost_estimate=cost(
            2 * rows * 2 * C * (2 * 768 + 384), rows * SPAN * 6 + rows * 2 * C * 6 + SPAN * 48 * 48
        ),
        name=f"spectral_forward_{group}",
    )(recv, a, st, gain, mix, *earlier)


def grid_kernel(
    recv_ref, up_ref, turned_ref, proj_ref, table_ref, turned_table_ref,
    out_ref, grad_ref, scratch, out_scratch, act_scratch, pre_scratch,
):
    step = pl.program_id(0)
    low = half_lanes((MODES, LANES))
    block = 128

    @pl.when(step == 0)
    def _():
        scratch[...] = recv_ref[...].astype(F32)
        grad_ref[...] = jnp.zeros_like(grad_ref)

    columns = []
    for pair in range(2):
        first = scratch[pl.ds(step * 4 + 2 * pair, MODES, stride=LAT_LOCAL), :]
        second = scratch[pl.ds(step * 4 + 2 * pair + 1, MODES, stride=LAT_LOCAL), :]
        real = jnp.where(low, first, pltpu.roll(second, HALF, 1))
        imag = jnp.where(low, pltpu.roll(first, HALF, 1), second)
        columns.append(jnp.concatenate([real, imag], axis=0).astype(BF16))
    modes = jnp.concatenate(columns, axis=1)
    low_block = half_lanes((block, LANES))
    for part in range(NLON // block):
        rows = slice(part * block, (part + 1) * block)
        pre = dot(turned_table_ref[rows, :], modes)
        grad_act = jnp.concatenate(
            [
                jnp.where(
                    low_block,
                    dot(turned_ref[2 * pair, rows, :], proj_ref[...]),
                    dot(turned_ref[2 * pair + 1, rows, :], proj_ref[...]),
                )
                for pair in range(2)
            ],
            axis=1,
        )
        cumulative = 0.5 * (1.0 + lax.erf(pre * (1.0 / math.sqrt(2.0))))
        slope = cumulative + pre * jnp.exp(-0.5 * pre * pre) * (1.0 / math.sqrt(2.0 * math.pi))
        act_scratch[rows, :] = (pre * cumulative).astype(BF16)
        pre_scratch[rows, :] = (grad_act * slope).astype(BF16)
    low_grad = half_lanes((C, LANES))
    for pair in range(2):
        lanes = slice(pair * LANES, (pair + 1) * LANES)
        act = act_scratch[:, lanes]
        grad_ref[...] += jnp.where(
            low_grad, dot(up_ref[2 * pair], act), dot(up_ref[2 * pair + 1], act)
        )
    grad_modes = dot(table_ref[...], pre_scratch[...])
    for pair in range(2):
        lanes = slice(pair * LANES, (pair + 1) * LANES)
        real, imag = grad_modes[:MODES, lanes], grad_modes[MODES:, lanes]
        out_scratch[pl.ds(step * 4 + 2 * pair, MODES, stride=LAT_LOCAL), :] = jnp.where(
            low, real, pltpu.roll(imag, HALF, 1)
        )
        out_scratch[pl.ds(step * 4 + 2 * pair + 1, MODES, stride=LAT_LOCAL), :] = jnp.where(
            low, pltpu.roll(real, HALF, 1), imag
        )

    @pl.when(step == LAT_LOCAL // 4 - 1)
    def _():
        out_ref[...] = out_scratch[...].astype(BF16)


def grid_stage(recv, up, turned, proj, table, turned_table):
    rows = MODES * LAT_LOCAL
    return pl.pallas_call(
        grid_kernel,
        grid=(LAT_LOCAL // 4,),
        in_specs=[
            whole((rows, LANES)),
            pl.BlockSpec((4, C, NLON), lambda b: (b, 0, 0)),
            pl.BlockSpec((4, NLON, C), lambda b: (b, 0, 0)),
            whole((C, LANES)),
            whole((2 * MODES, NLON)),
            whole((NLON, 2 * MODES)),
        ],
        out_specs=[whole((rows, LANES)), whole((C, LANES))],
        out_shape=[
            jax.ShapeDtypeStruct((rows, LANES), BF16),
            jax.ShapeDtypeStruct((C, LANES), F32),
        ],
        scratch_shapes=[
            pltpu.VMEM((rows, LANES), F32),
            pltpu.VMEM((rows, LANES), F32),
            pltpu.VMEM((NLON, 2 * LANES), BF16),
            pltpu.VMEM((NLON, 2 * LANES), BF16),
        ],
        compiler_params=params(),
        cost_estimate=cost(
            2 * LAT_LOCAL * HALF * NLON * (2 * 768 + 4 * 192) + LAT_LOCAL * HALF * NLON * 60,
            2 * LAT_LOCAL * C * NLON * 2 + 2 * rows * LANES * 2 + 4 * 768 * 768,
            LAT_LOCAL * HALF * NLON * 2,
        ),
        name="grid_stage",
    )(recv, up, turned, proj, table, turned_table)


def backward_kernel(group, recv_a, recv_b, recv_c, s_ref, gain_ref, mix_ref, mixed_ref, coeff_ref):
    degrees = degrees_of(group)
    tiles = [
        jnp.concatenate(
            [ref[:, tile].reshape(SPAN, LANES) for ref in (recv_a, recv_b, recv_c)], axis=1
        )
        for tile in range(GROUP_TILES)
    ]
    for local in range(GROUP_ORDERS):
        total = None
        for index, (order, tile) in enumerate(PAIRS):
            if order == local:
                part = dot(s_ref[index], tiles[tile])
                total = part if total is None else total + part
        rows = slice(local * degrees, (local + 1) * degrees)
        mixed = total.astype(BF16)
        mixed_ref[rows, :] = mixed
        scaled = dot_nt(mixed, mix_ref[...])
        coeff_ref[rows, :] = (gain_ref[LANES * group :, :] * scaled).astype(BF16)


def spectral_backward(group, recv, s, gain, mix):
    degrees = degrees_of(group)
    rows = GROUP_ORDERS * degrees
    recv_spec = pl.BlockSpec((DEVICES, GROUP_TILES, TILE, LANES), lambda b: (0, group, 0, 0))
    result = jax.ShapeDtypeStruct((rows, 2 * C), BF16)
    return pl.pallas_call(
        functools.partial(backward_kernel, group),
        grid=(1,),
        in_specs=[recv_spec] * 3
        + [whole((len(PAIRS), degrees, SPAN)), whole((MODES, 2 * C)), whole((2 * C, 2 * C))],
        out_specs=[whole((rows, 2 * C))] * 2,
        out_shape=[result] * 2,
        compiler_params=params(),
        cost_estimate=cost(
            2 * rows * 2 * C * (768 + 384), rows * SPAN * 3 + rows * 2 * C * 4 + SPAN * 48 * 48
        ),
        name=f"spectral_backward_{group}",
    )(*recv, s, gain, mix)


def synthesis_kernel(group, coeff_ref, at_ref, out_ref):
    degrees = degrees_of(group)
    for tile in range(GROUP_TILES):
        first = coeff_ref[tile * degrees : (tile + 1) * degrees, :]
        second = coeff_ref[(tile + 1) * degrees : (tile + 2) * degrees, :]
        out = dot(at_ref[2 * tile], first) + dot(at_ref[2 * tile + 1], second)
        out_ref[:, tile] = out.astype(BF16).reshape(DEVICES, TILE, 2 * C)


def analysis_back(group, coeffs, at):
    degrees = degrees_of(group)
    rows = GROUP_ORDERS * degrees
    shape = (DEVICES, GROUP_TILES, TILE, 2 * C)
    return pl.pallas_call(
        functools.partial(synthesis_kernel, group),
        grid=(1,),
        in_specs=[whole((rows, 2 * C)), whole((len(PAIRS), SPAN, degrees))],
        out_specs=whole(shape),
        out_shape=jax.ShapeDtypeStruct(shape, BF16),
        compiler_params=params(),
        cost_estimate=cost(
            2 * rows * 2 * C * 768, rows * SPAN * 3 + rows * 2 * C * 2 + SPAN * 48 * 48
        ),
        name=f"analysis_back_{group}",
    )(coeffs, at)


def weight_kernel(group, scaled_ref, mixed_ref, coef_ref, mix_ref, block_ref, gain_ref):
    degrees = degrees_of(group)
    block_ref[...] = lax.dot_general(
        scaled_ref[...], mixed_ref[...], (((0,), (0,)), ((), ())), preferred_element_type=F32
    )
    total = None
    for local in range(GROUP_ORDERS):
        rows = slice(local * degrees, (local + 1) * degrees)
        part = dot_nt(mixed_ref[rows, :], mix_ref[...]) * coef_ref[rows, :]
        total = part if total is None else total + part
    gain_ref[...] = total


def weight_grads(group, scaled, mixed, coef, mix):
    degrees = degrees_of(group)
    rows = GROUP_ORDERS * degrees
    return pl.pallas_call(
        functools.partial(weight_kernel, group),
        out_shape=[
            jax.ShapeDtypeStruct((2 * C, 2 * C), F32),
            jax.ShapeDtypeStruct((degrees, 2 * C), F32),
        ],
        compiler_params=params(),
        cost_estimate=cost(2 * rows * 2 * C * 2 * 384, rows * 2 * C * 8),
        name=f"weight_grads_{group}",
    )(scaled, mixed, coef, mix)


def field_kernel(recv_ref, table_ref, base_ref, out_ref, scratch):
    step = pl.program_id(0)
    orders = DEVICES * GROUP_ORDERS

    @pl.when(step == 0)
    def _():
        for index in range(GROUPS):
            scratch[index] = recv_ref[:, index * LANES : (index + 1) * LANES].astype(F32)

    for inner in range(4):
        real, imag = [], []
        for index in range(GROUPS):
            rows = scratch[index, pl.ds(step * 4 + inner, orders, stride=LAT_LOCAL), :]
            turned = rows.T.astype(BF16)
            real.append(turned[:HALF])
            imag.append(turned[HALF:])
        left = jnp.concatenate(
            [jnp.concatenate(real, axis=0), jnp.concatenate(imag, axis=0)], axis=1
        )
        total = base_ref[inner].astype(F32) + dot(left, table_ref[...])
        out_ref[inner] = total.astype(out_ref.dtype)


def field_stage(recv, table, base, kind):
    rows = DEVICES * GROUP_ORDERS * LAT_LOCAL
    block = pl.BlockSpec((4, C, NLON), lambda b: (b, 0, 0))
    return pl.pallas_call(
        field_kernel,
        grid=(LAT_LOCAL // 4,),
        in_specs=[whole((rows, 2 * C)), whole((2 * DEVICES * GROUP_ORDERS, NLON)), block],
        out_specs=block,
        out_shape=jax.ShapeDtypeStruct((LAT_LOCAL, C, NLON), kind),
        scratch_shapes=[pltpu.VMEM((GROUPS, rows, LANES), F32)],
        compiler_params=params(),
        cost_estimate=cost(
            2 * LAT_LOCAL * C * NLON * 256, LAT_LOCAL * C * NLON * 7 + rows * 2 * C * 2
        ),
        name="field_stage",
    )(recv, table, base)


def exchange(payload):
    return lax.all_to_all(payload, "lat", split_axis=0, concat_axis=0, tiled=True)


def shards(saved_input, incoming, spectral_gain, mix_weight, proj_weight):
    device = lax.axis_index("lat")
    section_count = lax.axis_size("section")
    shift = [(source, (source - 1) % section_count) for source in range(section_count)]

    forward = jnp.asarray(forward_groups())
    inverse_np = inverse_rows()
    inverse = jnp.asarray(inverse_np)
    inverse_turned = jnp.asarray(np.ascontiguousarray(inverse_np.T))
    spread = jnp.asarray(spread_tables())
    lat = jnp.asarray(latitude_rows())
    starts, numbers = log_starts()
    start = lax.dynamic_index_in_dim(jnp.asarray(starts), device, 0, keepdims=False)
    order = lax.dynamic_index_in_dim(jnp.asarray(numbers), device, 0, keepdims=False)

    field = saved_input[0]
    upstream = incoming[0]
    upstream_next = lax.ppermute(upstream, "section", shift)
    turned = jnp.swapaxes(upstream, 1, 2)
    gain = jnp.broadcast_to(
        spectral_gain[0].reshape(MODES, GROUPS, 1, HALF), (MODES, GROUPS, 2, HALF)
    ).reshape(MODES, 2 * C)
    real, imag = mix_weight[0, 0], mix_weight[0, 1]
    mix = (
        jnp.stack([jnp.stack([real, imag]), jnp.stack([-imag, real])])
        .reshape(2, 2, GROUPS, HALF, GROUPS, HALF)
        .transpose(2, 0, 3, 4, 1, 5)
        .reshape(2 * C, 2 * C)
    )
    proj = proj_weight[0].T.reshape(C, GROUPS, 1, HALF)
    proj = jnp.broadcast_to(proj, (C, GROUPS, 2, HALF)).transpose(1, 0, 2, 3)
    proj = proj.reshape(GROUPS, C, LANES)

    group_rows = GROUP_ORDERS * LAT_LOCAL
    received = []
    for group in range(GROUPS):
        rows = spectrum_rows(field, forward[group])
        received.append(exchange(rows.reshape(DEVICES, group_rows, 2 * C)))
    legendre = legendre_rows(start, order, lat)
    tables = [expand_tables(group, legendre, lat, spread) for group in range(GROUPS)]

    coefs, scaleds, payloads = [], [], []
    for group in range(GROUPS):
        coef, scaled, *payloads = spectral_forward(
            group,
            received[group].reshape(DEVICES, GROUP_TILES, TILE, 2 * C),
            tables[group][0],
            tables[group][3],
            gain,
            mix,
            payloads,
        )
        coefs.append(coef)
        scaleds.append(scaled)

    back, proj_parts = [], []
    for block in range(GROUPS):
        recv = exchange(payloads[block].reshape(DEVICES, ORDERS * LAT_LOCAL, LANES))
        rows, proj_part = grid_stage(
            recv.reshape(MODES * LAT_LOCAL, LANES),
            upstream,
            turned,
            proj[block],
            inverse,
            inverse_turned,
        )
        proj_parts.append(proj_part[:, :HALF] + proj_part[:, HALF:])
        back.append(
            exchange(rows.reshape(DEVICES, ORDERS * LAT_LOCAL, LANES)).reshape(
                DEVICES, TILES, TILE, LANES
            )
        )
    proj_local = jnp.concatenate(proj_parts, axis=1).T
    proj_total = lax.psum(proj_local.astype(BF16), "lat").astype(F32)

    base = upstream_next
    mixeds = [None] * GROUPS
    for group in reversed(range(GROUPS)):
        mixeds[group], coeffs = spectral_backward(group, back, tables[group][1], gain, mix)
        moved = lax.ppermute(coeffs, "section", shift)
        rows = exchange(
            analysis_back(group, moved, tables[group][2]).reshape(DEVICES, group_rows, 2 * C)
        )
        base = field_stage(
            rows.reshape(DEVICES * group_rows, 2 * C),
            forward[group],
            base,
            BF16 if group == 0 else F32,
        )

    block_grad, gain_sum = None, None
    for group in reversed(range(GROUPS)):
        part, gain_part = weight_grads(group, scaleds[group], mixeds[group], coefs[group], mix)
        block_grad = part if block_grad is None else block_grad + part
        gain_part = jnp.pad(gain_part, ((LANES * group, 0), (0, 0)))
        gain_sum = gain_part if gain_sum is None else gain_sum + gain_part
    block_grad = block_grad.reshape(GROUPS, 2, HALF, GROUPS, 2, HALF)
    grad_real = (block_grad[:, 0, :, :, 0] + block_grad[:, 1, :, :, 1]).reshape(C, C)
    grad_imag = (block_grad[:, 0, :, :, 1] - block_grad[:, 1, :, :, 0]).reshape(C, C)
    gain_local = gain_sum.reshape(MODES, GROUPS, 2, HALF).sum(axis=2).reshape(MODES, C)

    real_total, imag_total, gain_total = (
        lax.psum(grad_real.astype(BF16), "lat").astype(F32),
        lax.psum(grad_imag.astype(BF16), "lat").astype(F32),
        lax.psum(gain_local.astype(BF16), "lat").astype(F32),
    )
    grid_scale = 1.0 / math.sqrt(NLAT * NLON)
    mode_scale = 1.0 / math.sqrt(MODES)
    grad_w2 = grid_scale * proj_total
    grad_mix = grid_scale * jnp.stack([real_total, imag_total])
    grad_gain = mode_scale * gain_total
    return (base[None], grad_w2[None], grad_mix[None], grad_gain[None])


def solution(mesh):
    in_specs = (
        P("section", "lat", None, None),
        P("section", "lat", None, None),
        P("section", None, None),
        P("section", None, None, None),
        P("section", None, None),
    )
    out_specs = (
        P("section", "lat", None, None),
        P("section", None, None),
        P("section", None, None, None),
        P("section", None, None),
    )
    return jax.shard_map(shards, mesh=mesh, in_specs=in_specs, out_specs=out_specs, check_vma=False)
```

time: 644 us -> 573 us (0.89)
  Pallas kernels: 0 us -> 164 us
  local copies, waits for them, and re-layouts: 124 us -> 27.3 us
  matrix products: 96.1 us -> 0 us
  waiting for transfers between devices: 157 us -> 234 us
  other arithmetic: 79.5 us -> 8.18 us
  blocking collectives: 122 us -> 73.2 us
  loops' own time: 27.6 us -> 0 us
  starting transfers between devices: 17.5 us -> 43.5 us
    pallas_call x0 -> x25, Pallas kernels: none -> 164 us  [the longest x3 31.3 us: expand_tables(): pl.pallas_call(functools.partial(expand_kernel, group), grid=(degrees //...]
    dot_general x12 -> x0, matrix products: 96.1 us -> none  [the longest x1 18.9 us: shards(): jnp.einsum('jck,jdk->cd', activated, upstream, preferred_element_type=jnp...]
    ppermute x1 -> x4, waiting for transfers between devices: 0.01 us -> 83.6 us  [the longest x3 83.6 us: shards(): moved = lax.ppermute(coeffs, 'section', shift)]
    all_to_all x2 -> x3, blocking collectives: 122 us -> 73.2 us  [exchange(): lax.all_to_all(payload, 'lat', split_axis=0, concat_axis=0, tiled=True)]
    reshape x5 -> x3, local copies, waits for them, and re-layouts: 43.5 us -> 2.94 us  [the longest x1 1.11 us: shards(): mix = jnp.stack([jnp.stack([real, imag]), jnp.stack([-imag, real])]).resh...]
    while x360 -> x0, other arithmetic: 40.4 us -> none
    all_to_all x6 -> x0, local copies, waits for them, and re-layouts: 30.4 us -> none  [the longest x2 11.8 us: shards(): lax.all_to_all(spectrum, 'lat', split_axis=0, concat_axis=1, tiled=True)]
    another operation x1 -> x0, loops' own time: 27.6 us -> none  [legendre_table(): lax.scan(block_step, (zero_state, zero_state, log_start), jnp.arange(degr...]
  transfers between devices with their start and end apart: 4 -> 14, of which waited for: 2 -> 9; matrix products, arithmetic and copies ran while one was open for 22% -> 5% of each run, Pallas kernels for 0% -> 25%
where the time goes in v1:
time: 573 us; the launch traced here: 565 us
  waiting for transfers between devices  234 us (41%)
  Pallas kernels  164 us (29%)
  blocking collectives  73.2 us (13%)
  starting transfers between devices  43.5 us (8%)
  local copies, waits for them, and re-layouts  27.3 us (5%)
  between operations  14.8 us (3%)
  other arithmetic  8.18 us (1%)
    psum x1, waiting for transfers between devices, shards(): proj_total = lax.psum(proj_local.astype(BF16), 'lat').astype(F32)  107 us
    ppermute x3, waiting for transfers between devices, shards(): moved = lax.ppermute(coeffs, 'section', shift)  83.6 us
    all_to_all x3, blocking collectives, exchange(): lax.all_to_all(payload, 'lat', split_axis=0, concat_axis=0, tiled=True)  73.2 us
    all_to_all x9, waiting for transfers between devices, exchange(): lax.all_to_all(payload, 'lat', split_axis=0, concat_axis=0, tiled=True)  43.2 us
    all_to_all x9, starting transfers between devices, exchange(): lax.all_to_all(payload, 'lat', split_axis=0, concat_axis=0, tiled=True)  41.7 us
    pallas_call x3, Pallas kernels, expand_tables(): pl.pallas_call(functools.partial(expand_kernel, group), grid=(degrees //...  31.3 us
    pallas_call x3, Pallas kernels, grid_stage(): pl.pallas_call(grid_kernel, grid=(LAT_LOCAL // 4,), in_specs=[whole((rows...  29 us
    pallas_call x3, Pallas kernels, field_stage(): pl.pallas_call(field_kernel, grid=(LAT_LOCAL // 4,), in_specs=[whole((row...  21.5 us
  transfers between devices with their start and end apart: 14, of which 9 were waited for; matrix products, arithmetic and copies ran while one was open for 5% of the time, Pallas kernels for 25%

profile of v1, /device:TPU:6, one launch (start us, length us, event | category | flops | bytes accessed | tf_op | source)
XLA Modules:
  0.0 565.3 jit_solution(12189787224176872951)
XLA Ops:
  12.4 8.3 %all-to-all-start.1 = ((bf16[32,48,384]{2,1,0:T(8,128)(2,1)}), bf16[32,48,384]{2,1,0:T(8,128)(2,1)S(1)}, u32[]{:S(2)}, u32[]{:S(2)}) async-start(bf16[32,48,384]{2,1,0:T(8,128)(2,1)} %bitcast.88), calls=%async_computation.1 | async-start | bytes 2359296 | tf_op jit(solution)/shard_map/all_to_all | solution.py:565
  26.0 13.8 %all-to-all-done.1 = bf16[32,48,384]{2,1,0:T(8,128)(2,1)S(1)} async-done(((bf16[32,48,384]{2,1,0:T(8,128)(2,1)}), bf16[32,48,384]{2,1,0:T(8,128)(2,1)S(1)}, u32[]{:S(2)}, u32[]{:S(2)}) %all-to-all-start.1) | async-done | bytes 1179680 | tf_op jit(solution)/shard_map/all_to_all | solution.py:565
  54.0 9.7 %all-to-all-done.2 = bf16[32,48,384]{2,1,0:T(8,128)(2,1)S(1)} async-done(((bf16[32,48,384]{2,1,0:T(8,128)(2,1)}), bf16[32,48,384]{2,1,0:T(8,128)(2,1)S(1)}, u32[]{:S(2)}, u32[]{:S(2)}) %all-to-all-start.2) | async-done | bytes 1179680 | tf_op jit(solution)/shard_map/all_to_all | solution.py:565
  70.5 10.8 %legendre_rows.1.rows_ref = f32[384,16,384]{2,1,0:T(8,128)} custom-call(f32[16,128]{1,0:T(8,128)} %get-tuple-element.116.start_ref, f32[16,128]{1,0:T(8,128)} %get-tuple-element.115.order_ref, f32[8,384]{1,0:T(8,128)} %constant.39.clone.lat_ref), custom_call_target="tpu_custom_call" | custom-call | flops 58982400 | bytes 9437184 | tf_op jit(solution)/shard_map/legendre_rows/pallas_call | solution.py:166
  81.3 7.0 %expand_tables_2.1 = (bf16[6,128,512]{2,1,0:T(8,128)(2,1)}, bf16[6,128,512]{2,1,0:T(8,128)(2,1)}, bf16[6,512,128]{2,1,0:T(8,128)(2,1)}, bf16[6,512,128]{2,1,0:T(8,128)(2,1)}) custom-call(f32[384,16,384]{2,1,0:T(8,128)} %legendre_rows.1.rows_ref, f32[8,384]{1,0:T(8,128)} %constant.39.clone.lat_ref, bf16[6,512,384]{2,1,0:T(8,128)(2,1)} %constant.38.clone.spread_ref), custom_call_target="tpu_custom_call" | custom-call | flops 1207959552 | bytes 6291456 | tf_op jit(solution)/shard_map/expand_tables_2/pallas_call | solution.py:198
  88.3 10.5 %expand_tables_1.1 = (bf16[6,256,512]{2,1,0:T(8,128)(2,1)}, bf16[6,256,512]{2,1,0:T(8,128)(2,1)}, bf16[6,512,256]{2,1,0:T(8,128)(2,1)}, bf16[6,512,256]{2,1,0:T(8,128)(2,1)}) custom-call(f32[384,16,384]{2,1,0:T(8,128)} %legendre_rows.1.rows_ref, f32[8,384]{1,0:T(8,128)} %constant.39.clone.lat_ref, bf16[6,512,384]{2,1,0:T(8,128)(2,1)} %constant.38.clone.spread_ref), custom_call_target="tpu_custom_call" | custom-call | flops 2415919104 | bytes 12582912 | tf_op jit(solution)/shard_map/expand_tables_1/pallas_call | solution.py:198
  98.8 13.8 %expand_tables_0.1 = (bf16[6,384,512]{2,1,0:T(8,128)(2,1)}, bf16[6,384,512]{2,1,0:T(8,128)(2,1)}, bf16[6,512,384]{2,1,0:T(8,128)(2,1)}, bf16[6,512,384]{2,1,0:T(8,128)(2,1)}) custom-call(f32[384,16,384]{2,1,0:T(8,128)} %legendre_rows.1.rows_ref, f32[8,384]{1,0:T(8,128)} %constant.39.clone.lat_ref, bf16[6,512,384]{2,1,0:T(8,128)(2,1)} %constant.38.clone.spread_ref), custom_call_target="tpu_custom_call" | custom-call | flops 3623878656 | bytes 18874368 | tf_op jit(solution)/shard_map/expand_tables_0/pallas_call | solution.py:198
  112.6 7.7 %spectral_forward_0.1 = (f32[1536,384]{1,0:T(8,128)}, bf16[1536,384]{1,0:T(8,128)(2,1)}, bf16[32,9,16,128]{3,2,1,0:T(8,128)(2,1)}, bf16[32,9,16,128]{3,2,1,0:T(8,128)(2,1)}, bf16[32,9,16,128]{3,2,1,0:T(8,128)(2,1)}) custom-call(bf16[32,3,16,384]{3,2,1,0:T(8,128)(2,1)} %bitcast.95, bf16[6,384,512]{2,1,0:T(8,128)(2,1)} %get-tuple-element.53.a_ref, ...), custom_call_target="tpu_custom_call" | custom-call | flops 2264924160 | bytes 9437184 | tf_op jit(solution)/shard_map/spectral_forward_0/pallas_call | solution.py:304
  132.3 26.8 %all_to_all.60 = bf16[32,144,128]{2,1,0:T(8,128)(2,1)} all-to-all(bf16[32,144,128]{2,1,0:T(8,128)(2,1)} %bitcast.76), channel_id=1, replica_groups=mesh['section'=4,'lat'=32] {'lat'}, dimensions={0} | all-to-all | bytes 2359296 | tf_op jit(solution)/shard_map/all_to_all | solution.py:565
  159.1 22.7 %all_to_all.61 = bf16[32,144,128]{2,1,0:T(8,128)(2,1)} all-to-all(bf16[32,144,128]{2,1,0:T(8,128)(2,1)S(1)} %bitcast.77), channel_id=1, replica_groups=mesh['section'=4,'lat'=32] {'lat'}, dimensions={0} | all-to-all | bytes 2359296 | tf_op jit(solution)/shard_map/all_to_all | solution.py:565
  185.8 6.3 %copy.36.turned_ref = bf16[12,768,192]{2,1,0:T(8,128)(2,1)} copy(bf16[12,768,192]{1,2,0:T(8,128)(2,1)} %bitcast.15) | data formatting | bytes 7077888 | tf_op jit(solution)/shard_map/transpose | solution.py:586
  192.8 9.6 %grid_stage.3 = (bf16[4608,128]{1,0:T(8,128)(2,1)}, f32[192,128]{1,0:T(8,128)}) custom-call(bf16[4608,128]{1,0:T(8,128)(2,1)} %bitcast.83, bf16[12,192,768]{2,1,0:T(8,128)(2,1)} %bitcast.14.up_ref, bf16[12,768,192]{2,1,0:T(8,128)(2,1)} %copy.36.turned_ref, bf16[192,128]{1,0:T(8,128)(2,1)} %copy.37.proj_ref, bf16[768,768]{1,0:T(8,128)(2,1)} %constant.36.clone.table_ref, ...), custom_call_target="tpu_custom_call" | custom-call | flops 2753298432 | bytes 11796480 | tf_op jit(solution)/shard_map/grid_stage/pallas_call | solution.py:395
  211.8 9.7 %grid_stage.4 = (bf16[4608,128]{1,0:T(8,128)(2,1)}, f32[192,128]{1,0:T(8,128)}) custom-call(bf16[4608,128]{1,0:T(8,128)(2,1)} %bitcast.82, bf16[12,192,768]{2,1,0:T(8,128)(2,1)} %bitcast.14.up_ref, bf16[12,768,192]{2,1,0:T(8,128)(2,1)} %copy.36.turned_ref, bf16[192,128]{1,0:T(8,128)(2,1)} %copy.39.proj_ref, bf16[768,768]{1,0:T(8,128)(2,1)} %constant.36.clone.table_ref, ...), custom_call_target="tpu_custom_call" | custom-call | flops 2753298432 | bytes 11796480 | tf_op jit(solution)/shard_map/grid_stage/pallas_call | solution.py:395
  221.4 8.7 %all-to-all-done.4 = bf16[32,144,128]{2,1,0:T(8,128)(2,1)S(1)} async-done(((bf16[32,144,128]{2,1,0:T(8,128)(2,1)}), bf16[32,144,128]{2,1,0:T(8,128)(2,1)S(1)}, u32[]{:S(2)}, u32[]{:S(2)}) %all-to-all-start.4) | async-done | bytes 1179680 | tf_op jit(solution)/shard_map/all_to_all | solution.py:565
  235.8 9.7 %grid_stage.5 = (bf16[4608,128]{1,0:T(8,128)(2,1)}, f32[192,128]{1,0:T(8,128)}) custom-call(bf16[4608,128]{1,0:T(8,128)(2,1)} %bitcast.81, bf16[12,192,768]{2,1,0:T(8,128)(2,1)} %bitcast.14.up_ref, bf16[12,768,192]{2,1,0:T(8,128)(2,1)} %copy.36.turned_ref, bf16[192,128]{1,0:T(8,128)(2,1)} %copy.41.proj_ref, bf16[768,768]{1,0:T(8,128)(2,1)} %constant.36.clone.table_ref, ...), custom_call_target="tpu_custom_call" | custom-call | flops 2753298432 | bytes 11796480 | tf_op jit(solution)/shard_map/grid_stage/pallas_call | solution.py:395
  245.5 8.6 %all-to-all-done.6 = bf16[32,144,128]{2,1,0:T(8,128)(2,1)S(1)} async-done(((bf16[32,144,128]{2,1,0:T(8,128)(2,1)}), bf16[32,144,128]{2,1,0:T(8,128)(2,1)S(1)}, u32[]{:S(2)}, u32[]{:S(2)}) %all-to-all-start.6) | async-done | bytes 1179680 | tf_op jit(solution)/shard_map/all_to_all | solution.py:565
  254.1 23.7 %all_to_all.62 = bf16[32,144,128]{2,1,0:T(8,128)(2,1)} all-to-all(bf16[32,144,128]{2,1,0:T(8,128)(2,1)} %bitcast.98), channel_id=1, replica_groups=mesh['section'=4,'lat'=32] {'lat'}, dimensions={0} | all-to-all | bytes 2359296 | tf_op jit(solution)/shard_map/all_to_all | solution.py:565
  282.9 12.0 %collective-permute-done.2.coeff_ref = bf16[512,384]{1,0:T(8,128)(2,1)S(1)} collective-permute-done((bf16[512,384]{1,0:T(8,128)(2,1)}, bf16[512,384]{1,0:T(8,128)(2,1)S(1)}, u32[]{:S(2)}, u32[]{:S(2)}) %collective-permute-start.2) | collective-permute-done | bytes 393248 | tf_op jit(solution)/shard_map/ppermute | solution.py:647
  323.4 64.2 %collective-permute-done.1.coeff_ref = bf16[1024,384]{1,0:T(8,128)(2,1)S(1)} collective-permute-done((bf16[1024,384]{1,0:T(8,128)(2,1)}, bf16[1024,384]{1,0:T(8,128)(2,1)S(1)}, u32[]{:S(2)}, u32[]{:S(2)}) %collective-permute-start.1) | collective-permute-done | bytes 786464 | tf_op jit(solution)/shard_map/ppermute | solution.py:647
  404.8 7.4 %collective-permute-done.coeff_ref = bf16[1536,384]{1,0:T(8,128)(2,1)} collective-permute-done((bf16[1536,384]{1,0:T(8,128)(2,1)}, bf16[1536,384]{1,0:T(8,128)(2,1)}, u32[]{:S(2)}, u32[]{:S(2)}) %collective-permute-start) | collective-permute-done | bytes 1179680 | tf_op jit(solution)/shard_map/ppermute | solution.py:647
  423.8 107.5 %all-reduce.5.cloned.1.call-done = (bf16[192,192]{0,1:T(8,128)(2,1)}, bf16[1,1,192,192]{3,2,1,0:T(8,128)(2,1)}, bf16[1,1,192,192]{3,2,1,0:T(8,128)(2,1)}, bf16[384,192]{0,1:T(8,128)(2,1)}) async-done(((bf16[192,192]{0,1:T(8,128)(2,1)}, bf16[1,1,192,192]{3,2,1,0:T(8,128)(2,1)}, bf16[1,1,192,192]{3,2,1,0:T(8,128)(2,1)}, bf16[384,192]{0,1:T(8,128)(2,1)}), (bf16[192,192]{0,1:T(8,128)(2,1)}, ...) | async-done | bytes 368656 | tf_op jit(solution)/shard_map/psum | solution.py:641
  535.5 6.5 %field_stage.3.base_ref = f32[12,192,768]{2,1,0:T(8,128)} custom-call(bf16[1536,384]{1,0:T(8,128)(2,1)} %bitcast.78, bf16[256,768]{1,0:T(8,128)(2,1)} %constant.52.table_ref, bf16[12,192,768]{2,1,0:T(8,128)(2,1)} %collective-permute-done.3.base_ref), custom_call_target="tpu_custom_call" | custom-call | flops 905969664 | bytes 13565952 | tf_op jit(solution)/shard_map/field_stage/pallas_call | solution.py:549
  542.0 8.1 %field_stage.4.base_ref = f32[12,192,768]{2,1,0:T(8,128)} custom-call(bf16[1536,384]{1,0:T(8,128)(2,1)} %bitcast.91, bf16[256,768]{1,0:T(8,128)(2,1)} %constant.54.table_ref, f32[12,192,768]{2,1,0:T(8,128)} %field_stage.3.base_ref), custom_call_target="tpu_custom_call" | custom-call | flops 905969664 | bytes 13565952 | tf_op jit(solution)/shard_map/field_stage/pallas_call | solution.py:549
  551.1 6.9 %field_stage.5 = bf16[12,192,768]{2,1,0:T(8,128)(2,1)} custom-call(bf16[1536,384]{1,0:T(8,128)(2,1)} %bitcast.80, bf16[256,768]{1,0:T(8,128)(2,1)} %constant.56.table_ref, f32[12,192,768]{2,1,0:T(8,128)} %field_stage.4.base_ref), custom_call_target="tpu_custom_call" | custom-call | flops 905969664 | bytes 13565952 | tf_op jit(solution)/shard_map/field_stage/pallas_call | solution.py:549
  (115 shorter events, 130.6 us)
Async XLA Ops:
  7.2 184.9 %copy-start = (bf16[1,192,192]{2,1,0:T(8,128)(2,1)S(1)}, bf16[1,192,192]{2,1,0:T(8,128)(2,1)}, u32[]{:S(2)}) copy-start(bf16[1,192,192]{2,1,0:T(8,128)(2,1)} %param.16) | copy-start | bytes 221188
  12.4 27.4 %all-to-all-start.1 = ((bf16[32,48,384]{2,1,0:T(8,128)(2,1)}), bf16[32,48,384]{2,1,0:T(8,128)(2,1)S(1)}, u32[]{:S(2)}, u32[]{:S(2)}) async-start(bf16[32,48,384]{2,1,0:T(8,128)(2,1)} %bitcast.88), calls=%async_computation.1 | async-start | bytes 2359296 | tf_op jit(solution)/shard_map/all_to_all | solution.py:565
  39.8 5.0 copy-start.21
  40.8 23.0 %all-to-all-start.2 = ((bf16[32,48,384]{2,1,0:T(8,128)(2,1)}), bf16[32,48,384]{2,1,0:T(8,128)(2,1)S(1)}, u32[]{:S(2)}, u32[]{:S(2)}) async-start(bf16[32,48,384]{2,1,0:T(8,128)(2,1)} %bitcast.87), calls=%async_computation.2 | async-start | bytes 2359296 | tf_op jit(solution)/shard_map/all_to_all | solution.py:565
  64.8 61.7 %all-to-all-start = ((bf16[32,48,384]{2,1,0:T(8,128)(2,1)}), bf16[32,48,384]{2,1,0:T(8,128)(2,1)S(1)}, u32[]{:S(2)}, u32[]{:S(2)}) async-start(bf16[32,48,384]{2,1,0:T(8,128)(2,1)} %bitcast.85), calls=%async_computation | async-start | bytes 2359296 | tf_op jit(solution)/shard_map/all_to_all | solution.py:565
  132.3 26.8 %copy-start.4 = (bf16[32,9,16,128]{3,2,1,0:T(8,128)(2,1)S(1)}, bf16[32,9,16,128]{3,2,1,0:T(8,128)(2,1)}, u32[]{:S(2)}) copy-start(bf16[32,9,16,128]{3,2,1,0:T(8,128)(2,1)} %get-tuple-element.63) | copy-start | bytes 3538948
  181.8 23.0 %all-to-all-start.7 = ((bf16[32,144,128]{2,1,0:T(8,128)(2,1)}), bf16[32,144,128]{2,1,0:T(8,128)(2,1)S(1)}, u32[]{:S(2)}, u32[]{:S(2)}) async-start(bf16[32,144,128]{2,1,0:T(8,128)(2,1)} %bitcast.28), calls=%async_computation.7 | async-start | bytes 2359296 | tf_op jit(solution)/shard_map/all_to_all | solution.py:565
  205.8 24.2 %all-to-all-start.4 = ((bf16[32,144,128]{2,1,0:T(8,128)(2,1)}), bf16[32,144,128]{2,1,0:T(8,128)(2,1)S(1)}, u32[]{:S(2)}, u32[]{:S(2)}) async-start(bf16[32,144,128]{2,1,0:T(8,128)(2,1)} %bitcast.97), calls=%async_computation.4 | async-start | bytes 2359296 | tf_op jit(solution)/shard_map/all_to_all | solution.py:565
  231.1 23.0 %all-to-all-start.6 = ((bf16[32,144,128]{2,1,0:T(8,128)(2,1)}), bf16[32,144,128]{2,1,0:T(8,128)(2,1)S(1)}, u32[]{:S(2)}, u32[]{:S(2)}) async-start(bf16[32,144,128]{2,1,0:T(8,128)(2,1)} %bitcast.96), calls=%async_computation.6 | async-start | bytes 2359296 | tf_op jit(solution)/shard_map/all_to_all | solution.py:565
  254.1 23.7 %copy-start.3 = (bf16[32,144,128]{2,1,0:T(8,128)(2,1)}, bf16[32,144,128]{2,1,0:T(8,128)(2,1)S(1)}, u32[]{:S(2)}) copy-start(bf16[32,144,128]{2,1,0:T(8,128)(2,1)S(1)} %all-to-all-done.6) | copy-start | bytes 3538948
  281.5 13.4 %collective-permute-start.2 = (bf16[512,384]{1,0:T(8,128)(2,1)}, bf16[512,384]{1,0:T(8,128)(2,1)S(1)}, u32[]{:S(2)}, u32[]{:S(2)}) collective-permute-start(bf16[512,384]{1,0:T(8,128)(2,1)} %get-tuple-element.74), channel_id=1, source_target_pairs={{0,96},{32,0},{64,32},{96,64},{1,97},{33,1},{65,33},{97,65},{2,98}... | collective-permute-start | bytes 1179656 | tf_op jit(solution)/shard_map/ppermute | solution.py:647
  282.3 253.1 %collective-permute-start.3 = (bf16[12,192,768]{2,1,0:T(8,128)(2,1)}, bf16[12,192,768]{2,1,0:T(8,128)(2,1)}, u32[]{:S(2)}, u32[]{:S(2)}) collective-permute-start(bf16[12,192,768]{2,1,0:T(8,128)(2,1)} %bitcast.14.up_ref), channel_id=1, source_target_pairs={{0,96},{32,0},{64,32},{96,64},{1,97},{33,1},{65,33},{97,65},{2,98}... | collective-permute-start | bytes 10616840 | tf_op jit(solution)/shard_map/ppermute | solution.py:585
  298.7 4.1 copy-start.20
  298.7 93.4 %all-to-all-start.11 = ((bf16[32,48,384]{2,1,0:T(8,128)(2,1)}), bf16[32,48,384]{2,1,0:T(8,128)(2,1)S(1)}, u32[]{:S(2)}, u32[]{:S(2)}) async-start(bf16[32,48,384]{2,1,0:T(8,128)(2,1)} %bitcast.89), calls=%async_computation.11 | async-start | bytes 2359296 | tf_op jit(solution)/shard_map/all_to_all | solution.py:565
  302.9 4.8 copy-start.19
  302.9 4.9 copy-start.18
  307.7 79.9 %collective-permute-start.1 = (bf16[1024,384]{1,0:T(8,128)(2,1)}, bf16[1024,384]{1,0:T(8,128)(2,1)S(1)}, u32[]{:S(2)}, u32[]{:S(2)}) collective-permute-start(bf16[1024,384]{1,0:T(8,128)(2,1)} %get-tuple-element.71), channel_id=1, source_target_pairs={{0,96},{32,0},{64,32},{96,64},{1,97},{33,1},{65,33},{97,65},{2,98}... | collective-permute-start | bytes 2359304 | tf_op jit(solution)/shard_map/ppermute | solution.py:647
  314.3 97.8 %collective-permute-start = (bf16[1536,384]{1,0:T(8,128)(2,1)}, bf16[1536,384]{1,0:T(8,128)(2,1)}, u32[]{:S(2)}, u32[]{:S(2)}) collective-permute-start(bf16[1536,384]{1,0:T(8,128)(2,1)} %get-tuple-element.68), channel_id=1, source_target_pairs={{0,96},{32,0},{64,32},{96,64},{1,97},{33,1},{65,33},{97,65},{2,98}... | collective-permute-start | bytes 3538952 | tf_op jit(solution)/shard_map/ppermute | solution.py:647
  393.2 23.6 %all-to-all-start.10 = ((bf16[32,48,384]{2,1,0:T(8,128)(2,1)}), bf16[32,48,384]{2,1,0:T(8,128)(2,1)S(1)}, u32[]{:S(2)}, u32[]{:S(2)}) async-start(bf16[32,48,384]{2,1,0:T(8,128)(2,1)} %bitcast.86), calls=%async_computation.10 | async-start | bytes 2359296 | tf_op jit(solution)/shard_map/all_to_all | solution.py:565
  416.8 5.0 copy-start.13
  416.8 5.1 copy-start.16
  417.8 132.2 %all-to-all-start.9 = ((bf16[32,48,384]{2,1,0:T(8,128)(2,1)}), bf16[32,48,384]{2,1,0:T(8,128)(2,1)S(1)}, u32[]{:S(2)}, u32[]{:S(2)}) async-start(bf16[32,48,384]{2,1,0:T(8,128)(2,1)} %bitcast.90), calls=%async_computation.9 | async-start | bytes 2359296 | tf_op jit(solution)/shard_map/all_to_all | solution.py:565
  421.8 109.5 %all-reduce.5.cloned.1.call-start = ((), (), s32[]{:S(2)}) async-start(), calls=%async_computation.12 | async-start | bytes 884736 | tf_op jit(solution)/shard_map/psum | solution.py:641
  551.1 6.9 %copy-start.1 = (bf16[1,192,192]{2,1,0:T(8,128)(2,1)S(1)}, bf16[1,192,192]{2,1,0:T(8,128)(2,1)}, u32[]{:S(2)}) copy-start(bf16[1,192,192]{2,1,0:T(8,128)(2,1)} %param.16) | copy-start | bytes 221188
  (14 other events, 20.5 us)
Sparse Core Ops, SparseCore 0:
  426.9 104.3 all-reduce.4

commit v2 on v1

v2 whole, which is shorter than its diff:
```python
import functools
import math

import jax
import jax.numpy as jnp
import ml_dtypes
import numpy as np
from jax import lax
from jax.experimental import pallas as pl
from jax.experimental.pallas import tpu as pltpu
from jax.sharding import PartitionSpec as P

NLAT = 384
NLON = 768
MODES = 384
C = 192
DEVICES = 32
LAT_LOCAL = 12
ORDERS = 12
GROUPS = 3
GROUP_ORDERS = 4
HALF = 64
LANES = 128
TILE = 16
TILES = 9
GROUP_TILES = 3
SPAN = DEVICES * TILE
LAT_BLOCKS = 4
BLOCK_LATS = NLAT // LAT_BLOCKS
VMEM_LIMIT = 56 * 1024 * 1024
F32 = jnp.float32
BF16 = jnp.bfloat16
NT = (((1,), (1,)), ((), ()))

PAIRS = ((0, 0), (1, 0), (1, 1), (2, 1), (2, 2), (3, 2))


def degrees_of(group):
    return MODES - LANES * group


def half_lanes(shape):
    return lax.broadcasted_iota(jnp.int32, shape, 1) < HALF


def dot(left, right):
    return jnp.dot(left, right, preferred_element_type=F32)


def dot_nt(left, right):
    return lax.dot_general(left, right, NT, preferred_element_type=F32)


def whole(shape):
    return pl.BlockSpec(shape, lambda *_: (0,) * len(shape))


def call(kernel, inputs, in_specs, out_specs, out_shape, grid, flops, after=(), aliases=None, **extra):
    count = len(inputs)

    def body(*refs):
        kernel(*refs[:count], *refs[count + len(after) :])

    outs = jax.tree.leaves(out_shape)
    moved = sum(value.size * value.dtype.itemsize for value in list(inputs) + outs)
    return pl.pallas_call(
        body,
        grid=grid,
        in_specs=list(in_specs) + [pl.BlockSpec(memory_space=pl.ANY)] * len(after),
        out_specs=out_specs,
        out_shape=out_shape,
        input_output_aliases=aliases or {},
        compiler_params=pltpu.CompilerParams(vmem_limit_bytes=VMEM_LIMIT),
        cost_estimate=pl.CostEstimate(
            flops=int(flops), bytes_accessed=int(moved), transcendentals=0
        ),
        **extra,
    )(*inputs, *after)


def order_rows(first, count):
    device = np.arange(DEVICES)[:, None]
    local = np.arange(GROUP_ORDERS * count)[None, :] + GROUP_ORDERS * first
    return (DEVICES * local + device).reshape(-1)


def fourier_rows(orders):
    phase = (orders[:, None] * np.arange(NLON)[None, :]) % NLON
    angle = phase * (2.0 * math.pi / NLON)
    return np.cos(angle), -np.sin(angle)


def forward_rows(first, count):
    cosine, sine = fourier_rows(order_rows(first, count))
    table = np.concatenate([cosine, sine], axis=0)
    return jnp.asarray(table.astype(np.float32).astype(ml_dtypes.bfloat16))


def inverse_rows():
    device = np.arange(DEVICES)[:, None]
    orders = (DEVICES * np.arange(ORDERS)[None, :] + device).reshape(-1)
    factor = np.where(orders == 0, 1.0, 2.0)[:, None] / NLON
    cosine, sine = fourier_rows(orders)
    table = np.concatenate([factor * cosine, factor * sine], axis=0)
    return table.astype(np.float32).astype(ml_dtypes.bfloat16)


def spread_tables():
    rows = np.arange(LANES)
    source, inner = rows // TILE, rows % TILE
    tables = np.zeros((len(PAIRS), LANES, LANES), np.float32)
    for index, (order, tile) in enumerate(PAIRS):
        lat = TILE * tile + inner - LAT_LOCAL * order
        valid = (lat >= 0) & (lat < LAT_LOCAL)
        tables[index, (source * LAT_LOCAL + lat)[valid], rows[valid]] = 1.0
    flat = jnp.asarray(tables.astype(ml_dtypes.bfloat16))
    turned = jnp.asarray(np.swapaxes(tables, 1, 2).astype(ml_dtypes.bfloat16))
    return flat, turned


def log_starts():
    table = np.zeros((DEVICES, TILE, LANES), np.float32)
    numbers = np.zeros((DEVICES, TILE, LANES), np.float32)
    for device in range(DEVICES):
        for local in range(ORDERS):
            order = DEVICES * local + device
            numbers[device, local] = order
            table[device, local] = 0.5 * math.log((2.0 * order + 1.0) / 2.0) + 0.5 * (
                math.lgamma(order + 0.5) - math.lgamma(0.5) - math.lgamma(order + 1.0)
            )
    return table, numbers


def latitude_rows():
    colatitude = (np.arange(NLAT) + 0.5) * (math.pi / NLAT)
    harmonic = np.arange(1, NLAT // 2 + 1)
    terms = np.cos(2.0 * harmonic[None, :] * colatitude[:, None]) / (4.0 * harmonic**2 - 1.0)
    weight = 2.0 / NLAT * (1.0 - 2.0 * np.sum(terms, axis=1))
    rows = np.stack([np.cos(colatitude), np.log(np.sin(colatitude)), weight])
    rows = np.concatenate([rows, np.zeros((5, NLAT))]).reshape(8, LAT_BLOCKS, BLOCK_LATS)
    rows = np.pad(rows, ((0, 0), (0, 0), (0, LANES - BLOCK_LATS)))
    return rows.reshape(8, SPAN).astype(np.float32)


def legendre_rows(start_ref, order_ref, lat_ref, rows_ref):
    order = jnp.concatenate([order_ref[...]] * LAT_BLOCKS, axis=1)
    cosine = jnp.broadcast_to(lat_ref[0:1, :], (TILE, SPAN))
    log_sin = jnp.broadcast_to(lat_ref[1:2, :], (TILE, SPAN))
    log_start = jnp.concatenate([start_ref[...]] * LAT_BLOCKS, axis=1) + order * log_sin
    narrow = order_ref[...]
    narrow_square = narrow * narrow
    second_factor = jnp.concatenate([jnp.sqrt(2.0 * narrow + 3.0)] * LAT_BLOCKS, axis=1)
    zeros = jnp.zeros((TILE, SPAN), F32)

    def block(index, state):
        previous, current, log_scale = state
        scale = jnp.exp(log_scale)
        for inner in range(16):
            row = index * 16 + inner
            degree = row.astype(F32)
            lower = degree - 1.0
            up = jnp.sqrt(
                jnp.maximum(4.0 * degree * degree - 1.0, 1.0)
                / jnp.maximum(degree * degree - narrow_square, 1.0)
            )
            down = jnp.sqrt(
                jnp.maximum(lower * lower - narrow_square, 0.0)
                / jnp.maximum(4.0 * lower * lower - 1.0, 1.0)
            )
            up = jnp.concatenate([up] * LAT_BLOCKS, axis=1)
            down = jnp.concatenate([down] * LAT_BLOCKS, axis=1)
            general = up * (cosine * current - down * previous)
            second = second_factor * cosine * current
            new_row = jnp.where(
                degree == order,
                1.0,
                jnp.where(
                    degree == order + 1.0, second, jnp.where(degree > order + 1.0, general, 0.0)
                ),
            )
            scaled = new_row * scale
            for part in range(LAT_BLOCKS):
                rows_ref[part, row] = scaled[:, part * LANES : (part + 1) * LANES]
            previous, current = current, new_row
        largest = jnp.maximum(jnp.abs(previous), jnp.abs(current))
        largest = jnp.where(largest > 0.0, largest, 1.0)
        return previous / largest, current / largest, log_scale + jnp.log(largest)

    lax.fori_loop(0, MODES // 16, block, (zeros, zeros, log_start))


def table_kernel(start_ref, order_ref, lat_ref, flat_ref, turned_ref, *rest):
    outs, rows_ref, buffers, sems = rest[:12], rest[12], rest[13:25], rest[25]
    legendre_rows(start_ref, order_ref, lat_ref, rows_ref)
    copies = []
    for group in range(GROUPS):
        ahead_flat, ahead_turned, behind_flat, behind_turned = buffers[4 * group : 4 * group + 4]

        def part_step(part, carry):
            lats = pl.ds(pl.multiple_of(part * LANES, LANES), LANES)
            weight = lat_ref[2:3, lats]
            for local in range(GROUP_ORDERS):
                legendre = rows_ref[part, LANES * group :, GROUP_ORDERS * group + local, :]
                synthesis = legendre.astype(BF16)
                analysis = (weight * legendre).astype(BF16)
                pairs = [index for index, (order, _) in enumerate(PAIRS) if order == local]
                flat = jnp.concatenate([flat_ref[index] for index in pairs], axis=1)
                turned = jnp.concatenate([turned_ref[index] for index in pairs], axis=0)
                products = (
                    dot(analysis, flat).astype(BF16),
                    dot_nt(turned, synthesis).astype(BF16),
                    dot(synthesis, flat).astype(BF16),
                    dot_nt(turned, analysis).astype(BF16),
                )
                for place, index in enumerate(pairs):
                    cut = slice(place * LANES, (place + 1) * LANES)
                    ahead_flat[index, :, lats] = products[0][:, cut]
                    ahead_turned[index, lats, :] = products[1][cut]
                    behind_flat[index, :, lats] = products[2][:, cut]
                    behind_turned[index, lats, :] = products[3][cut]
            return carry

        lax.fori_loop(0, LAT_BLOCKS, part_step, 0)
        for place in range(4):
            at = 4 * group + place
            copy = pltpu.make_async_copy(buffers[at], outs[at], sems.at[at])
            copy.start()
            copies.append(copy)
    for copy in copies:
        copy.wait()


def legendre_tables(start, order, lat, flat, turned, after):
    shapes = []
    for group in range(GROUPS):
        degrees = degrees_of(group)
        shapes += [(len(PAIRS), degrees, SPAN), (len(PAIRS), SPAN, degrees)] * 2
    inputs = (start, order, lat, flat, turned)
    return call(
        table_kernel,
        inputs,
        [whole(value.shape) for value in inputs],
        [pl.BlockSpec(memory_space=pl.ANY)] * len(shapes),
        [jax.ShapeDtypeStruct(shape, BF16) for shape in shapes],
        (1,),
        16 * sum(math.prod(shape) for shape in shapes) * 8,
        after,
        scratch_shapes=[pltpu.VMEM((LAT_BLOCKS, MODES, TILE, LANES), F32)]
        + [pltpu.VMEM(shape, BF16) for shape in shapes]
        + [pltpu.SemaphoreType.DMA((len(shapes),))],
        name="legendre_tables",
    )


def spectrum_kernel(field_ref, table_ref, out_ref, scratch):
    step = pl.program_id(0)
    rows = table_ref.shape[0] // 2
    low = half_lanes((rows, LANES))
    for inner in range(4):
        product = dot_nt(table_ref[...], field_ref[inner])
        real, imag = product[:rows], product[rows:]
        real_a, imag_a = real[:, :LANES], imag[:, :LANES]
        tiles = (
            jnp.where(low, real_a, pltpu.roll(imag_a, HALF, 1)),
            jnp.where(low, pltpu.roll(real_a, HALF, 1), imag_a),
            jnp.concatenate([real[:, LANES:], imag[:, LANES:]], axis=1),
        )
        for index, tile in enumerate(tiles):
            scratch[index, pl.ds(step * 4 + inner, rows, stride=LAT_LOCAL), :] = tile

    @pl.when(step == LAT_LOCAL // 4 - 1)
    def _():
        for index in range(GROUPS):
            out_ref[:, index * LANES : (index + 1) * LANES] = scratch[index].astype(BF16)


def spectrum_rows(field, table, after=()):
    rows = table.shape[0] // 2 * LAT_LOCAL
    return call(
        spectrum_kernel,
        (field, table),
        [pl.BlockSpec((4, C, NLON), lambda b: (b, 0, 0)), whole(table.shape)],
        whole((rows, 2 * C)),
        jax.ShapeDtypeStruct((rows, 2 * C), BF16),
        (LAT_LOCAL // 4,),
        2 * LAT_LOCAL * C * NLON * table.shape[0],
        after,
        scratch_shapes=[pltpu.VMEM((GROUPS, rows, LANES), F32)],
        name="spectrum_rows",
    )


def pair_sum(local, table_ref, tiles):
    total = None
    for index, (order, tile) in enumerate(PAIRS):
        if order == local:
            part = dot(table_ref[index], tiles[tile])
            total = part if total is None else total + part
    return total


def spectral_kernel(recv_ref, *refs):
    a_refs, st_refs = refs[0:3], refs[3:6]
    gain_ref, mix_ref = refs[6:8]
    scaled_outs, payload_ref = refs[8:11], refs[11]
    recv, payload = refs[12:14]
    a_buffers, st_buffers, scaled_buffers = refs[14:17], refs[17:20], refs[20:23]
    in_sems, out_sems = refs[23:25]
    schedule = (2, 0, 1)
    arrivals, departures = {}, []
    for group in schedule:
        tiles = pl.ds(GROUP_TILES * group, GROUP_TILES)
        arrivals[group] = [
            pltpu.make_async_copy(recv_ref.at[:, tiles], recv.at[group], in_sems.at[group, 0]),
            pltpu.make_async_copy(a_refs[group], a_buffers[group], in_sems.at[group, 1]),
            pltpu.make_async_copy(st_refs[group], st_buffers[group], in_sems.at[group, 2]),
        ]
        for copy in arrivals[group]:
            copy.start()
    for group in schedule:
        degrees = degrees_of(group)
        for copy in arrivals[group]:
            copy.wait()
        tiles = [recv[group, :, tile].reshape(SPAN, 2 * C) for tile in range(GROUP_TILES)]
        mixed = []
        for local in range(GROUP_ORDERS):
            rows = slice(local * degrees, (local + 1) * degrees)
            coef = pair_sum(local, a_buffers[group], tiles)
            scaled = (gain_ref[LANES * group :, :] * coef).astype(BF16)
            scaled_buffers[group][rows, :] = scaled
            mixed.append(dot(scaled, mix_ref[...]).astype(BF16))
        for tile in range(GROUP_TILES):
            grid = dot(st_buffers[group][2 * tile], mixed[tile]) + dot(
                st_buffers[group][2 * tile + 1], mixed[tile + 1]
            )
            payload[group, :, tile] = grid.astype(BF16).reshape(DEVICES, TILE, 2 * C)
        tiles = pl.ds(GROUP_TILES * group, GROUP_TILES)
        copies = (
            pltpu.make_async_copy(
                payload.at[group], payload_ref.at[:, tiles], out_sems.at[group, 0]
            ),
            pltpu.make_async_copy(
                scaled_buffers[group], scaled_outs[group], out_sems.at[group, 1]
            ),
        )
        for copy in copies:
            copy.start()
            departures.append(copy)
    for copy in departures:
        copy.wait()


def spectral_forward(recv, a, st, gain, mix, after=()):
    shapes = [(GROUP_ORDERS * degrees_of(group), 2 * C) for group in range(GROUPS)]
    held = pl.BlockSpec(memory_space=pl.ANY)
    slots = (GROUPS, DEVICES, GROUP_TILES, TILE, 2 * C)
    return call(
        spectral_kernel,
        (recv, *a, *st, gain, mix),
        [held] * 7 + [whole(gain.shape), whole(mix.shape)],
        [held] * 4,
        [jax.ShapeDtypeStruct(shape, BF16) for shape in shapes]
        + [jax.ShapeDtypeStruct(recv.shape, BF16)],
        (1,),
        sum(2 * rows * 2 * C * (2 * 768 + 384) for rows, _ in shapes),
        after,
        scratch_shapes=[pltpu.VMEM(slots, BF16), pltpu.VMEM(slots, BF16)]
        + [pltpu.VMEM(value.shape, BF16) for value in a]
        + [pltpu.VMEM(value.shape, BF16) for value in st]
        + [pltpu.VMEM(shape, BF16) for shape in shapes]
        + [pltpu.SemaphoreType.DMA((GROUPS, 3)), pltpu.SemaphoreType.DMA((GROUPS, 2))],
        name="spectral_forward",
    )


def grid_kernel(
    recv_ref, up_ref, turned_ref, proj_ref, table_ref, turned_table_ref,
    out_ref, grad_ref, scratch, out_scratch, act_scratch, pre_scratch,
):
    step = pl.program_id(1)
    low = half_lanes((MODES, LANES))
    block = 128

    @pl.when(step == 0)
    def _():
        scratch[...] = recv_ref[...].astype(F32)
        grad_ref[...] = jnp.zeros_like(grad_ref)

    columns = []
    for pair in range(2):
        first = scratch[pl.ds(step * 4 + 2 * pair, MODES, stride=LAT_LOCAL), :]
        second = scratch[pl.ds(step * 4 + 2 * pair + 1, MODES, stride=LAT_LOCAL), :]
        real = jnp.where(low, first, pltpu.roll(second, HALF, 1))
        imag = jnp.where(low, pltpu.roll(first, HALF, 1), second)
        columns.append(jnp.concatenate([real, imag], axis=0).astype(BF16))
    modes = jnp.concatenate(columns, axis=1)
    low_block = half_lanes((block, LANES))
    for part in range(NLON // block):
        rows = slice(part * block, (part + 1) * block)
        pre = dot(turned_table_ref[rows, :], modes)
        grad_act = jnp.concatenate(
            [
                jnp.where(
                    low_block,
                    dot(turned_ref[2 * pair, rows, :], proj_ref[...]),
                    dot(turned_ref[2 * pair + 1, rows, :], proj_ref[...]),
                )
                for pair in range(2)
            ],
            axis=1,
        )
        cumulative = 0.5 * (1.0 + lax.erf(pre * (1.0 / math.sqrt(2.0))))
        slope = cumulative + pre * jnp.exp(-0.5 * pre * pre) * (1.0 / math.sqrt(2.0 * math.pi))
        act_scratch[rows, :] = (pre * cumulative).astype(BF16)
        pre_scratch[rows, :] = (grad_act * slope).astype(BF16)
    low_grad = half_lanes((C, LANES))
    for pair in range(2):
        lanes = slice(pair * LANES, (pair + 1) * LANES)
        act = act_scratch[:, lanes]
        grad_ref[...] += jnp.where(
            low_grad, dot(up_ref[2 * pair], act), dot(up_ref[2 * pair + 1], act)
        )
    grad_modes = dot(table_ref[...], pre_scratch[...])
    for pair in range(2):
        lanes = slice(pair * LANES, (pair + 1) * LANES)
        real, imag = grad_modes[:MODES, lanes], grad_modes[MODES:, lanes]
        out_scratch[pl.ds(step * 4 + 2 * pair, MODES, stride=LAT_LOCAL), :] = jnp.where(
            low, real, pltpu.roll(imag, HALF, 1)
        )
        out_scratch[pl.ds(step * 4 + 2 * pair + 1, MODES, stride=LAT_LOCAL), :] = jnp.where(
            low, pltpu.roll(real, HALF, 1), imag
        )

    @pl.when(step == LAT_LOCAL // 4 - 1)
    def _():
        out_ref[...] = out_scratch[...].astype(BF16)


def grid_stage(first, blocks, recv, up, turned, proj, table, turned_table, after=()):
    rows = MODES * LAT_LOCAL
    lanes_spec = pl.BlockSpec((rows, LANES), lambda q, b: (0, q))
    grad_spec = pl.BlockSpec((C, LANES), lambda q, b: (0, q))
    return call(
        grid_kernel,
        (recv, up, turned, proj, table, turned_table),
        [
            pl.BlockSpec((rows, LANES), lambda q, b: (0, q + first)),
            pl.BlockSpec((4, C, NLON), lambda q, b: (b, 0, 0)),
            pl.BlockSpec((4, NLON, C), lambda q, b: (b, 0, 0)),
            pl.BlockSpec((C, LANES), lambda q, b: (0, q + first)),
            whole(table.shape),
            whole(turned_table.shape),
        ],
        [lanes_spec, grad_spec],
        [
            jax.ShapeDtypeStruct((rows, LANES * blocks), BF16),
            jax.ShapeDtypeStruct((C, LANES * blocks), F32),
        ],
        (blocks, LAT_LOCAL // 4),
        blocks * LAT_LOCAL * HALF * NLON * (4 * 768 + 8 * 192 + 60),
        after,
        scratch_shapes=[
            pltpu.VMEM((rows, LANES), F32),
            pltpu.VMEM((rows, LANES), F32),
            pltpu.VMEM((NLON, 2 * LANES), BF16),
            pltpu.VMEM((NLON, 2 * LANES), BF16),
        ],
        name=f"grid_stage_{blocks}",
    )


def backward_kernel(group, small_ref, large_ref, s_ref, gain_ref, mix_ref, mixed_ref, coeff_ref):
    degrees = degrees_of(group)
    tiles = [
        jnp.concatenate(
            [
                small_ref[:, tile].reshape(SPAN, LANES),
                large_ref[:, tile].reshape(SPAN, 2 * LANES),
            ],
            axis=1,
        )
        for tile in range(GROUP_TILES)
    ]
    for local in range(GROUP_ORDERS):
        rows = slice(local * degrees, (local + 1) * degrees)
        mixed = pair_sum(local, s_ref, tiles).astype(BF16)
        mixed_ref[rows, :] = mixed
        scaled = dot_nt(mixed, mix_ref[...])
        coeffs = (gain_ref[LANES * group :, :] * scaled).astype(BF16)
        coeff_ref[packed_rows(degrees, local), :] = coeffs[DEVICES * local :]


def packed_rows(degrees, local):
    first = sum(degrees - DEVICES * other for other in range(local))
    return slice(first, first + degrees - DEVICES * local)


def spectral_backward(group, small, large, s, gain, mix, after=()):
    degrees = degrees_of(group)
    rows = GROUP_ORDERS * degrees
    packed = packed_rows(degrees, GROUP_ORDERS - 1).stop
    return call(
        functools.partial(backward_kernel, group),
        (small, large, s, gain, mix),
        [
            pl.BlockSpec((DEVICES, GROUP_TILES, TILE, lanes), lambda b: (0, group, 0, 0))
            for lanes in (LANES, 2 * LANES)
        ]
        + [whole(s.shape), whole(gain.shape), whole(mix.shape)],
        [whole((rows, 2 * C)), whole((packed, 2 * C))],
        [
            jax.ShapeDtypeStruct((rows, 2 * C), BF16),
            jax.ShapeDtypeStruct((packed, 2 * C), BF16),
        ],
        (1,),
        2 * rows * 2 * C * (768 + 384),
        after,
        name=f"spectral_backward_{group}",
    )


def hold_kernel(value_ref, out_ref):
    pass


def hold(value, after):
    held = pl.BlockSpec(memory_space=pl.ANY)
    return call(
        hold_kernel,
        (value,),
        [held],
        held,
        jax.ShapeDtypeStruct(value.shape, value.dtype),
        (1,),
        0,
        after,
        aliases={0: 0},
        name="hold",
    )


def synthesis_kernel(group, packed_ref, at_ref, *rest):
    out_ref, coeff_ref = rest[-2:]
    rest = rest[:-1]
    degrees = degrees_of(group)
    for local in range(GROUP_ORDERS):
        first = local * degrees
        skipped = DEVICES * local
        if local:
            coeff_ref[first : first + skipped, :] = jnp.zeros((skipped, 2 * C), BF16)
        coeff_ref[first + skipped : first + degrees, :] = packed_ref[
            packed_rows(degrees, local), :
        ]
    for tile in range(GROUP_TILES):
        first = coeff_ref[tile * degrees : (tile + 1) * degrees, :]
        second = coeff_ref[(tile + 1) * degrees : (tile + 2) * degrees, :]
        out = dot(at_ref[2 * tile], first) + dot(at_ref[2 * tile + 1], second)
        out_ref[:, tile] = out.astype(BF16).reshape(DEVICES, TILE, 2 * C)
    if len(rest) == 2:
        out_ref[:, GROUP_TILES] = rest[0][...]


def analysis_back(group, coeffs, at, tiles, extra=(), after=()):
    degrees = degrees_of(group)
    rows = GROUP_ORDERS * degrees
    block = GROUP_TILES + len(extra)
    return call(
        functools.partial(synthesis_kernel, group),
        (coeffs, at, *extra),
        [whole(coeffs.shape), whole(at.shape)] + [whole(value.shape) for value in extra],
        whole((DEVICES, block, TILE, 2 * C)),
        jax.ShapeDtypeStruct((DEVICES, tiles, TILE, 2 * C), BF16),
        (1,),
        2 * rows * 2 * C * 768,
        after,
        scratch_shapes=[pltpu.VMEM((rows, 2 * C), BF16)],
        name=f"analysis_back_{group}",
    )


def fold(tile):
    return tile + pltpu.roll(tile, HALF, 1)


def weight_kernel(*refs):
    scaled_refs, mixed_refs = refs[:3], refs[3:6]
    mix_ref, factor_ref, proj_small, proj_large, out_ref, gain, packed, spaced = refs[6:]
    block = None
    for scaled_ref, mixed_ref in zip(scaled_refs, mixed_refs):
        part = lax.dot_general(
            scaled_ref[...], mixed_ref[...], (((0,), (0,)), ((), ())), preferred_element_type=F32
        )
        block = part if block is None else block + part
    for group in range(GROUPS):
        degrees = degrees_of(group)
        total = None
        for local in range(GROUP_ORDERS):
            rows = slice(local * degrees, (local + 1) * degrees)
            part = dot_nt(mixed_refs[group][rows, :], mix_ref[...])
            part = part * scaled_refs[group][rows, :].astype(F32)
            total = part if total is None else total + part
        if group == 0:
            gain[...] = total
        else:
            gain[LANES * group :, :] += total
    gain[...] = gain[...] / factor_ref[...]
    low = half_lanes((HALF, LANES))
    low_gain = half_lanes((C, LANES))
    low_proj = half_lanes((C // 2, LANES))
    for index in range(GROUPS):
        lanes = slice(index * LANES, (index + 1) * LANES)
        for row_block in range(GROUPS):
            start = row_block * LANES
            first = block[start : start + HALF, lanes]
            second = pltpu.roll(block[start + HALF : start + LANES, lanes], HALF, 1)
            packed[index, row_block * HALF : (row_block + 1) * HALF, :] = jnp.where(
                low, first + second, first - second
            )
        packed[index, C : 2 * C, :] = jnp.where(
            low_gain, fold(gain[:C, lanes]), fold(gain[C:, lanes])
        )
        if index == 0:
            proj = fold(proj_small[...])
        else:
            proj = fold(proj_large[:, (index - 1) * LANES : index * LANES])
        packed[index, 2 * C :, :] = jnp.where(low_proj, proj[: C // 2], proj[C // 2 :])
        for row in range(TILE - 1):
            spaced[index, pl.ds(row, DEVICES, stride=TILE), :] = packed[
                index, row * DEVICES : (row + 1) * DEVICES, :
            ]
        spaced[index, pl.ds(TILE - 1, DEVICES, stride=TILE), :] = jnp.zeros((DEVICES, LANES), F32)
        out_ref[:, :, lanes] = spaced[index].astype(BF16).reshape(DEVICES, TILE, LANES)


def weight_grads(scaleds, mixeds, mix, gain, proj_small, proj_large, after=()):
    out = (DEVICES, TILE, 2 * C)
    inputs = (*scaleds, *mixeds, mix, gain, proj_small, proj_large)
    return call(
        weight_kernel,
        inputs,
        [whole(value.shape) for value in inputs],
        whole(out),
        jax.ShapeDtypeStruct(out, BF16),
        (1,),
        sum(4 * value.shape[0] * 2 * C * 2 * C for value in scaleds),
        after,
        scratch_shapes=[
            pltpu.VMEM((MODES, 2 * C), F32),
            pltpu.VMEM((GROUPS, 15 * DEVICES, LANES), F32),
            pltpu.VMEM((GROUPS, TILE * DEVICES, LANES), F32),
        ],
        name="weight_grads",
    )


def total_kernel(recv_ref, payload_ref, out_ref):
    total = jnp.sum(recv_ref[:, 0].astype(F32), axis=0)
    out_ref[:, 0] = jnp.broadcast_to(total.astype(BF16)[None], (DEVICES, TILE, 2 * C))


def attach_totals(recv, payload):
    spec = pl.BlockSpec((DEVICES, 1, TILE, 2 * C), lambda b: (0, GROUP_TILES, 0, 0))
    return call(
        total_kernel,
        (recv, payload),
        [spec, pl.BlockSpec(memory_space=pl.ANY)],
        spec,
        jax.ShapeDtypeStruct(payload.shape, BF16),
        (1,),
        DEVICES * TILE * 2 * C,
        aliases={1: 0},
        name="attach_totals",
    )


def unpack_kernel(recv_ref, proj_ref, mix_ref, gain_ref, spaced, packed):
    grid_scale = 1.0 / math.sqrt(NLAT * NLON)
    mode_scale = 1.0 / math.sqrt(MODES)
    lows, highs = [], []
    for index in range(GROUPS):
        lanes = slice(index * LANES, (index + 1) * LANES)
        spaced[index] = recv_ref[:, 0, :, lanes].reshape(DEVICES * TILE, LANES).astype(F32)
        for row in range(TILE - 1):
            packed[index, row * DEVICES : (row + 1) * DEVICES, :] = spaced[
                index, pl.ds(row, DEVICES, stride=TILE), :
            ]
        lows.append(packed[index, :, :HALF])
        highs.append(packed[index, :, HALF:])
    low = jnp.concatenate(lows, axis=1)
    high = jnp.concatenate(highs, axis=1)
    mix_ref[0] = grid_scale * low[:C]
    mix_ref[1] = grid_scale * high[:C]
    gain = jnp.concatenate([low[C : 2 * C], high[C : 2 * C]], axis=0)
    gain_ref[...] = mode_scale * gain.T
    proj = jnp.concatenate([low[2 * C :], high[2 * C :]], axis=0)
    proj_ref[...] = grid_scale * proj.T


def unpack_totals(recv, after=()):
    shapes = ((C, C), (2, C, C), (C, MODES))
    return call(
        unpack_kernel,
        (recv,),
        [pl.BlockSpec((DEVICES, 1, TILE, 2 * C), lambda b: (0, GROUP_TILES, 0, 0))],
        [whole(shape) for shape in shapes],
        [jax.ShapeDtypeStruct(shape, F32) for shape in shapes],
        (1,),
        4 * MODES * C,
        after,
        scratch_shapes=[
            pltpu.VMEM((GROUPS, TILE * DEVICES, LANES), F32),
            pltpu.VMEM((GROUPS, 15 * DEVICES, LANES), F32),
        ],
        name="unpack_totals",
    )


def field_kernel(recv_ref, table_ref, base_ref, out_ref, scratch):
    step = pl.program_id(0)
    orders = DEVICES * GROUP_ORDERS
    rows = orders * LAT_LOCAL

    @pl.when(step == 0)
    def _():
        for index in range(GROUPS):
            lanes = slice(index * LANES, (index + 1) * LANES)
            values = recv_ref[:, :, :, lanes].astype(F32)
            scratch[index] = values.reshape(rows, LANES)

    lefts = []
    for inner in range(4):
        real, imag = [], []
        for index in range(GROUPS):
            values = scratch[index, pl.ds(step * 4 + inner, orders, stride=LAT_LOCAL), :]
            turned = values.T.astype(BF16)
            real.append(turned[:HALF])
            imag.append(turned[HALF:])
        lefts.append(
            jnp.concatenate(
                [jnp.concatenate(real, axis=0), jnp.concatenate(imag, axis=0)], axis=1
            )
        )
    product = dot(jnp.concatenate(lefts, axis=0), table_ref[...])
    for inner in range(4):
        total = base_ref[inner].astype(F32) + product[inner * C : (inner + 1) * C]
        out_ref[inner] = total.astype(out_ref.dtype)


def field_stage(recv, table, base, kind, after=()):
    rows = DEVICES * GROUP_ORDERS * LAT_LOCAL
    block = pl.BlockSpec((4, C, NLON), lambda b: (b, 0, 0))
    return call(
        field_kernel,
        (recv, table, base),
        [
            pl.BlockSpec((DEVICES, GROUP_TILES, TILE, 2 * C), lambda b: (0, 0, 0, 0)),
            whole(table.shape),
            block,
        ],
        block,
        jax.ShapeDtypeStruct((LAT_LOCAL, C, NLON), kind),
        (LAT_LOCAL // 4,),
        2 * LAT_LOCAL * C * NLON * 256,
        after,
        scratch_shapes=[pltpu.VMEM((GROUPS, rows, LANES), F32)],
        name="field_stage",
    )


def exchange(payload):
    tiles, lanes = payload.shape[1], payload.shape[3]
    flat = payload.reshape(DEVICES, tiles * TILE, lanes)
    moved = lax.all_to_all(flat, "lat", split_axis=0, concat_axis=0, tiled=True)
    return moved.reshape(DEVICES, tiles, TILE, lanes)


def shards(saved_input, incoming, spectral_gain, mix_weight, proj_weight):
    device = lax.axis_index("lat")
    section_count = lax.axis_size("section")
    shift = [(source, (source - 1) % section_count) for source in range(section_count)]

    forward_all = forward_rows(0, GROUPS)
    forward = [forward_rows(group, 1) for group in range(GROUPS)]
    inverse_np = inverse_rows()
    inverse = jnp.asarray(inverse_np)
    inverse_turned = jnp.asarray(np.ascontiguousarray(inverse_np.T))
    spread, spread_turned = spread_tables()
    lat = jnp.asarray(latitude_rows())
    starts, numbers = log_starts()
    start = lax.dynamic_index_in_dim(jnp.asarray(starts), device, 0, keepdims=False)
    order = lax.dynamic_index_in_dim(jnp.asarray(numbers), device, 0, keepdims=False)

    field = saved_input[0]
    upstream = incoming[0]
    upstream_next = lax.ppermute(upstream, "section", shift)
    turned = jnp.swapaxes(upstream, 1, 2)
    gain = jnp.broadcast_to(
        spectral_gain[0].reshape(MODES, GROUPS, 1, HALF), (MODES, GROUPS, 2, HALF)
    ).reshape(MODES, 2 * C)
    real, imag = mix_weight[0, 0], mix_weight[0, 1]
    mix = (
        jnp.stack([jnp.stack([real, imag]), jnp.stack([-imag, real])])
        .reshape(2, 2, GROUPS, HALF, GROUPS, HALF)
        .transpose(2, 0, 3, 4, 1, 5)
        .reshape(2 * C, 2 * C)
    )
    proj = jnp.broadcast_to(
        proj_weight[0].T.reshape(C, GROUPS, 1, HALF), (C, GROUPS, 2, HALF)
    ).reshape(C, 2 * C)

    rows = MODES * LAT_LOCAL
    spectrum = spectrum_rows(field, forward_all)
    recv = exchange(spectrum.reshape(DEVICES, TILES, TILE, 2 * C))
    tables = legendre_tables(start, order, lat, spread, spread_turned, (spectrum,))
    behind = [tables[4 * group + 2 : 4 * group + 4] for group in range(GROUPS)]
    *scaleds, payload = spectral_forward(
        recv, tables[0::4], tables[1::4], gain, mix, (turned, proj)
    )
    recv = exchange(payload).reshape(rows, 2 * C)
    small_rows, proj_small = grid_stage(
        0, 1, recv, upstream, turned, proj, inverse, inverse_turned, (upstream_next,)
    )
    small = exchange(small_rows.reshape(DEVICES, TILES, TILE, LANES))
    large, proj_large = grid_stage(
        1, 2, recv, upstream, turned, proj, inverse, inverse_turned, (small_rows,)
    )
    large = exchange(large.reshape(DEVICES, TILES, TILE, 2 * LANES))

    mixeds, moved = [None] * GROUPS, [None] * GROUPS
    mixeds[2], coeffs_2 = spectral_backward(2, small, large, behind[2][0], gain, mix)
    moved[2] = lax.ppermute(coeffs_2, "section", shift)
    mixeds[1], coeffs_1 = spectral_backward(1, small, large, behind[1][0], gain, mix, (coeffs_2,))
    moved[1] = lax.ppermute(hold(coeffs_1, (moved[2],)), "section", shift)

    out_2 = analysis_back(2, moved[2], behind[2][1], GROUP_TILES, after=(coeffs_1,))
    mixeds[0], coeffs_0 = spectral_backward(0, small, large, behind[0][0], gain, mix, (out_2,))
    moved[0] = lax.ppermute(coeffs_0, "section", shift)
    recv_2 = exchange(out_2)
    partial_grads = weight_grads(
        scaleds, mixeds, mix, gain, proj_small, proj_large, after=(out_2, coeffs_0)
    )
    out_1 = analysis_back(1, moved[1], behind[1][1], GROUP_TILES + 1, (partial_grads,))
    recv_1 = exchange(out_1)
    out_0 = analysis_back(0, moved[0], behind[0][1], GROUP_TILES + 1, after=(out_1,))
    base = field_stage(recv_2, forward[2], upstream_next, F32, (out_0,))
    out_0 = attach_totals(recv_1, out_0)
    recv_0 = exchange(out_0)
    base = field_stage(recv_1, forward[1], base, F32, (out_0,))
    grad_w2, grad_mix, grad_gain = unpack_totals(recv_0)
    received = field_stage(recv_0, forward[0], base, BF16)
    return (
        received[None],
        grad_w2[None],
        grad_mix[None],
        jnp.swapaxes(grad_gain, 0, 1)[None],
    )


def solution(mesh):
    in_specs = (
        P("section", "lat", None, None),
        P("section", "lat", None, None),
        P("section", None, None),
        P("section", None, None, None),
        P("section", None, None),
    )
    out_specs = (
        P("section", "lat", None, None),
        P("section", None, None),
        P("section", None, None, None),
        P("section", None, None),
    )
    return jax.shard_map(shards, mesh=mesh, in_specs=in_specs, out_specs=out_specs, check_vma=False)
```

time: 573 us -> 365 us (0.64)
  waiting for transfers between devices: 234 us -> 93.6 us
  Pallas kernels: 164 us -> 129 us
  between operations: 14.8 us -> 1.2 us
  starting transfers between devices: 43.5 us -> 33.1 us
  blocking collectives: 73.2 us -> 63.8 us
  local copies, waits for them, and re-layouts: 27.3 us -> 35 us
    psum x1 -> x0, waiting for transfers between devices: 107 us -> none  [shards(): proj_total = lax.psum(proj_local.astype(BF16), 'lat').astype(F32)]
    ppermute x3, waiting for transfers between devices: 83.6 us -> 35.4 us  [the longest x1 26.1 us: shards(): moved[0] = lax.ppermute(coeffs_0, 'section', shift)]
    pallas_call x25 -> x18, Pallas kernels: 164 us -> 129 us  [call(): pl.pallas_call(body, grid=grid, in_specs=list(in_specs) + [pl.BlockSpec(m...]
    all_to_all x9 -> x5, starting transfers between devices: 41.7 us -> 31.3 us  [exchange(): moved = lax.all_to_all(flat, 'lat', split_axis=0, concat_axis=0, tiled=True)]
    all_to_all x3 -> x2, blocking collectives: 73.2 us -> 63.8 us  [exchange(): moved = lax.all_to_all(flat, 'lat', split_axis=0, concat_axis=0, tiled=True)]
    all_to_all x9 -> x5, waiting for transfers between devices: 43.2 us -> 52.2 us  [exchange(): moved = lax.all_to_all(flat, 'lat', split_axis=0, concat_axis=0, tiled=True)]
    ppermute x1, waiting for transfers between devices: 0.01 us -> 6.11 us  [shards(): upstream_next = lax.ppermute(upstream, 'section', shift)]
  transfers between devices with their start and end apart: 14 -> 9, of which waited for: 9 -> 7; matrix products, arithmetic and copies ran while one was open for 5% -> 8% of each run, Pallas kernels for 25% -> 25%
where the time goes in v2:
time: 365 us; the launch traced here: 359 us
  Pallas kernels  129 us (35%)
  waiting for transfers between devices  93.6 us (26%)
  blocking collectives  63.8 us (17%)
  local copies, waits for them, and re-layouts  35 us (10%)
  starting transfers between devices  33.1 us (9%)
  other arithmetic  3.68 us (1%)
    pallas_call x18, Pallas kernels, call(): pl.pallas_call(body, grid=grid, in_specs=list(in_specs) + [pl.BlockSpec(m...  129 us
    all_to_all x2, blocking collectives, exchange(): moved = lax.all_to_all(flat, 'lat', split_axis=0, concat_axis=0, tiled=True)  63.8 us
    all_to_all x5, waiting for transfers between devices, exchange(): moved = lax.all_to_all(flat, 'lat', split_axis=0, concat_axis=0, tiled=True)  52.2 us
    all_to_all x5, starting transfers between devices, exchange(): moved = lax.all_to_all(flat, 'lat', split_axis=0, concat_axis=0, tiled=True)  31.3 us
    ppermute x1, waiting for transfers between devices, shards(): moved[0] = lax.ppermute(coeffs_0, 'section', shift)  26.1 us
    unnamed x19, local copies, waits for them, and re-layouts  11.1 us
  transfers between devices with their start and end apart: 9, of which 7 were waited for; matrix products, arithmetic and copies ran while one was open for 8% of the time, Pallas kernels for 25%

profile of v2, /device:TPU:6, one launch (start us, length us, event | category | flops | bytes accessed | tf_op | source)
XLA Modules:
  0.0 359.0 jit_solution(15721386277741990540)
XLA Ops:
  0.6 8.6 %spectrum_rows.1.refs_5_ = bf16[4608,384]{1,0:T(8,128)(2,1)} custom-call(bf16[12,192,768]{2,1,0:T(8,128)(2,1)} %bitcast.67, bf16[768,768]{1,0:T(8,128)(2,1)} %constant.34.clone.refs_1_), custom_call_target="tpu_custom_call" | custom-call | flops 2717908992 | bytes 8257536 | tf_op jit(solution)/shard_map/spectrum_rows/pallas_call | solution.py:66
  9.3 8.3 %all-to-all-start = ((bf16[32,144,384]{2,1,0:T(8,128)(2,1)}), bf16[32,144,384]{2,1,0:T(8,128)(2,1)S(1)}, u32[]{:S(2)}, u32[]{:S(2)}) async-start(bf16[32,144,384]{2,1,0:T(8,128)(2,1)} %bitcast.58), calls=%async_computation | async-start | bytes 7077888 | tf_op jit(solution)/shard_map/all_to_all | solution.py:773
  35.1 6.4 %copy.33.refs_9_.refs_2_ = bf16[12,768,192]{2,1,0:T(8,128)(2,1)} copy(bf16[12,768,192]{1,2,0:T(8,128)(2,1)} %bitcast.9) | data formatting | bytes 7077888 | tf_op jit(solution)/shard_map/transpose | solution.py:796
  46.1 23.6 %legendre_tables.1 = (bf16[6,384,512]{2,1,0:T(8,128)(2,1)}, bf16[6,512,384]{2,1,0:T(8,128)(2,1)}, bf16[6,384,512]{2,1,0:T(8,128)(2,1)}, bf16[6,512,384]{2,1,0:T(...) custom-call(f32[16,128]{1,0:T(8,128)} %get-tuple-element.65.refs_0_,, ...), custom_call_target="tpu_custom_call" | custom-call | flops 1207959552 | bytes 19300352 | tf_op jit(solution)/shard_map/legendre_tables/pallas_call | solution.py:66
  71.5 12.6 %spectral_forward.1 = (bf16[1536,384]{1,0:T(8,128)(2,1)}, bf16[1024,384]{1,0:T(8,128)(2,1)}, bf16[512,384]{1,0:T(8,128)(2,1)}, bf16[32,9,16,384]{3,2,1,0:T(8,128)(2,1)}) custom-call(bf16[32,9,16,384]{3,2,1,0:T(8,128)(2,1)} %bitcast.56, bf16[6,384,512]{2,1,0:T(8,128)(2,1)} %get-tuple-element.33.refs_1_, bf16[6,256,512]{2,1,0:T(8,128)(2,1)} %get-tuple-element.34.refs_2_, ...), custom_call_target="tpu_custom_call" | custom-call | flops 4529848320 | bytes 19759104 | tf_op jit(solution)/shard_map/spectral_forward/pallas_call | solution.py:66
  84.2 7.6 %all-to-all-start.1 = ((bf16[32,144,384]{2,1,0:T(8,128)(2,1)}), bf16[32,144,384]{2,1,0:T(8,128)(2,1)S(1)}, u32[]{:S(2)}, u32[]{:S(2)}) async-start(bf16[32,144,384]{2,1,0:T(8,128)(2,1)} %bitcast.59), calls=%async_computation.1 | async-start | bytes 7077888 | tf_op jit(solution)/shard_map/all_to_all | solution.py:773
  91.8 6.1 %collective-permute-done.refs_6_.refs_2_ = bf16[12,192,768]{2,1,0:T(8,128)(2,1)} collective-permute-done((bf16[12,192,768]{2,1,0:T(8,128)(2,1)}, bf16[12,192,768]{2,1,0:T(8,128)(2,1)}, u32[]{:S(2)}, u32[]{:S(2)}) %collective-permute-start) | collective-permute-done | bytes 3538976 | tf_op jit(solution)/shard_map/ppermute | solution.py:795
  97.9 40.1 %all-to-all-done.1 = bf16[32,144,384]{2,1,0:T(8,128)(2,1)S(1)} async-done(((bf16[32,144,384]{2,1,0:T(8,128)(2,1)}), bf16[32,144,384]{2,1,0:T(8,128)(2,1)S(1)}, u32[]{:S(2)}, u32[]{:S(2)}) %all-to-all-start.1) | async-done | bytes 3538976 | tf_op jit(solution)/shard_map/all_to_all | solution.py:773
  139.8 9.7 %grid_stage_1.1 = (bf16[4608,128]{1,0:T(8,128)(2,1)}, f32[192,128]{1,0:T(8,128)}) custom-call(bf16[4608,384]{1,0:T(8,128)(2,1)} %bitcast.49, bf16[12,192,768]{2,1,0:T(8,128)(2,1)} %bitcast.8.refs_1_, bf16[12,768,192]{2,1,0:T(8,128)(2,1)} %copy.33.refs_9_.refs_2_, bf16[192,384]{1,0:T(8,128)(2,1)} %copy.34.refs_10_.refs_3_, ...), custom_call_target="tpu_custom_call" | custom-call | flops 2753298432 | bytes 14401536 | tf_op jit(solution)/shard_map/grid_stage_1/pallas_call | solution.py:66
  153.4 16.1 %grid_stage_2.1 = (bf16[4608,256]{1,0:T(8,128)(2,1)}, f32[192,256]{1,0:T(8,128)}) custom-call(bf16[4608,384]{1,0:T(8,128)(2,1)} %bitcast.50, bf16[12,192,768]{2,1,0:T(8,128)(2,1)} %bitcast.8.refs_1_, bf16[12,768,192]{2,1,0:T(8,128)(2,1)} %copy.33.refs_9_.refs_2_, bf16[192,384]{1,0:T(8,128)(2,1)} %copy.34.refs_10_.refs_3_, ...), custom_call_target="tpu_custom_call" | custom-call | flops 5506596864 | bytes 15679488 | tf_op jit(solution)/shard_map/grid_stage_2/pallas_call | solution.py:66
  172.4 36.2 %all_to_all.35 = bf16[32,144,256]{2,1,0:T(8,128)(2,1)} all-to-all(bf16[32,144,256]{2,1,0:T(8,128)(2,1)} %bitcast.61), channel_id=1, replica_groups=mesh['section'=4,'lat'=32] {'lat'}, dimensions={0} | all-to-all | bytes 4718592 | tf_op jit(solution)/shard_map/all_to_all | solution.py:773
  212.8 4.7 %spectral_backward_1.1 = (bf16[1024,384]{1,0:T(8,128)(2,1)}, bf16[832,384]{1,0:T(8,128)(2,1)}) custom-call(bf16[32,9,16,128]{3,2,1,0:T(8,128)(2,1)} %bitcast.47, bf16[32,9,16,256]{3,2,1,0:T(8,128)(2,1)} %bitcast.43, bf16[6,256,512]{2,1,0:T(8,128)(2,1)} %get-tuple-element.42.refs_2_, f32[384,384]{1,0:T(8,128)} %copy.32.refs_7_.refs_3_, ...), custom_call_target="tpu_custom_call" | custom-call | flops 905969664 | bytes 7421952 | tf_op jit(solution)/shard_map/spectral_backward_1/pallas_call | solution.py:66
  217.5 4.4 %collective-permute-done.1.refs_1_.refs_0_ = bf16[320,384]{1,0:T(8,128)(2,1)S(1)} collective-permute-done((bf16[320,384]{1,0:T(8,128)(2,1)}, bf16[320,384]{1,0:T(8,128)(2,1)S(1)}, u32[]{:S(2)}, u32[]{:S(2)}) %collective-permute-start.1) | collective-permute-done | bytes 245792 | tf_op jit(solution)/shard_map/ppermute | solution.py:831
  225.9 5.7 %spectral_backward_0.1 = (bf16[1536,384]{1,0:T(8,128)(2,1)}, bf16[1344,384]{1,0:T(8,128)(2,1)}) custom-call(bf16[32,9,16,128]{3,2,1,0:T(8,128)(2,1)} %bitcast.48, bf16[32,9,16,256]{3,2,1,0:T(8,128)(2,1)} %bitcast.44, bf16[6,384,512]{2,1,0:T(8,128)(2,1)} %get-tuple-element.50.refs_2_, f32[384,384]{1,0:T(8,128)} %copy.32.refs_7_.refs_3_, ...), custom_call_target="tpu_custom_call" | custom-call | flops 1358954496 | bytes 8994816 | tf_op jit(solution)/shard_map/spectral_backward_0/pallas_call | solution.py:66
  231.6 6.7 %weight_grads.1.refs_2_ = bf16[32,16,384]{2,1,0:T(8,128)(2,1)} custom-call(bf16[1536,384]{1,0:T(8,128)(2,1)} %get-tuple-element.47.refs_0_, bf16[1024,384]{1,0:T(8,128)(2,1)} %get-tuple-element.48.refs_1_, bf16[512,384]{1,0:T(8,128)(2,1)} %get-tuple-element.49.refs_2_, bf16[1536,384]{1,0:T(8,128)(2,1)} %get-tuple-element.52.refs_3_, ...), custom_call_target="tpu_custom_call" | custom-call | flops 1811939328 | bytes 6291456 | tf_op jit(solution)/shard_map/weight_grads/pallas_call | solution.py:66
  238.3 4.9 %collective-permute-done.2.refs_0_ = bf16[832,384]{1,0:T(8,128)(2,1)S(1)} collective-permute-done((bf16[832,384]{1,0:T(8,128)(2,1)}, bf16[832,384]{1,0:T(8,128)(2,1)S(1)}, u32[]{:S(2)}, u32[]{:S(2)}) %collective-permute-start.2) | collective-permute-done | bytes 639008 | tf_op jit(solution)/shard_map/ppermute | solution.py:833
  247.8 27.7 %all_to_all.36 = bf16[32,64,384]{2,1,0:T(8,128)(2,1)} all-to-all(bf16[32,64,384]{2,1,0:T(8,128)(2,1)} %bitcast.55), channel_id=1, replica_groups=mesh['section'=4,'lat'=32] {'lat'}, dimensions={0} | all-to-all | bytes 3145728 | tf_op jit(solution)/shard_map/all_to_all | solution.py:773
  279.6 26.1 %collective-permute-done.3.refs_0_ = bf16[1344,384]{1,0:T(8,128)(2,1)S(1)} collective-permute-done((bf16[1344,384]{1,0:T(8,128)(2,1)S(1)}, bf16[1344,384]{1,0:T(8,128)(2,1)S(1)}, u32[]{:S(2)}, u32[]{:S(2)}) %collective-permute-start.3) | collective-permute-done | bytes 1032224 | tf_op jit(solution)/shard_map/ppermute | solution.py:837
  306.7 4.6 %analysis_back_0.1.refs_3_ = bf16[32,4,16,384]{3,2,1,0:T(8,128)(2,1)} custom-call(bf16[1344,384]{1,0:T(8,128)(2,1)} %copy-done.5, bf16[6,512,384]{2,1,0:T(8,128)(2,1)} %get-tuple-element.58.refs_1_, bf16[32,4,16,384]{3,2,1,0:T(8,128)(2,1)} %analysis_back_1.1.refs_2_), custom_call_target="tpu_custom_call" | custom-call | flops 905969664 | bytes 4964352 | tf_op jit(solution)/shard_map/analysis_back_0/pallas_call | solution.py:66
  316.9 7.4 %all-to-all-start.5 = ((bf16[32,64,384]{2,1,0:T(8,128)(2,1)}), bf16[32,64,384]{2,1,0:T(8,128)(2,1)S(1)}, u32[]{:S(2)}, u32[]{:S(2)}) async-start(bf16[32,64,384]{2,1,0:T(8,128)(2,1)} %bitcast.45), calls=%async_computation.5 | async-start | bytes 3145728 | tf_op jit(solution)/shard_map/all_to_all | solution.py:773
  324.3 6.6 %field_stage.3.refs_2_ = f32[12,192,768]{2,1,0:T(8,128)} custom-call(bf16[32,3,16,384]{3,2,1,0:T(8,128)(2,1)} %bitcast.57, bf16[256,768]{1,0:T(8,128)(2,1)} %constant.37.clone.refs_1_, bf16[12,192,768]{2,1,0:T(8,128)(2,1)} %collective-permute-done.refs_6_.refs_2_, bf16[32,4,16,384]{3,2,1,0:T(8,128)(2,1)} %analysis_back_0.1.refs_3_), custom_call_target="tpu_custom_call" | custom-call | flops 905969664 | bytes 12189696 | tf_op jit(solution)/shard_map/field_stage/pallas_call | solution.py:66
  330.9 8.2 %field_stage.4.refs_2_ = f32[12,192,768]{2,1,0:T(8,128)} custom-call(bf16[32,4,16,384]{3,2,1,0:T(8,128)(2,1)} %bitcast.54, bf16[256,768]{1,0:T(8,128)(2,1)} %constant.36.clone.refs_1_, f32[12,192,768]{2,1,0:T(8,128)} %field_stage.3.refs_2_, bf16[32,4,16,384]{3,2,1,0:T(8,128)(2,1)} %attach_totals.1.refs_3_), custom_call_target="tpu_custom_call" | custom-call | flops 905969664 | bytes 16121856 | tf_op jit(solution)/shard_map/field_stage/pallas_call | solution.py:66
  339.1 9.2 %all-to-all-done.5 = bf16[32,64,384]{2,1,0:T(8,128)(2,1)S(1)} async-done(((bf16[32,64,384]{2,1,0:T(8,128)(2,1)}), bf16[32,64,384]{2,1,0:T(8,128)(2,1)S(1)}, u32[]{:S(2)}, u32[]{:S(2)}) %all-to-all-start.5) | async-done | bytes 1572896 | tf_op jit(solution)/shard_map/all_to_all | solution.py:773
  351.7 6.9 %field_stage.5 = bf16[12,192,768]{2,1,0:T(8,128)(2,1)} custom-call(bf16[32,4,16,384]{3,2,1,0:T(8,128)(2,1)} %bitcast.52, bf16[256,768]{1,0:T(8,128)(2,1)} %constant.35.clone.refs_1_, f32[12,192,768]{2,1,0:T(8,128)} %field_stage.4.refs_2_), custom_call_target="tpu_custom_call" | custom-call | flops 905969664 | bytes 12582912 | tf_op jit(solution)/shard_map/field_stage/pallas_call | solution.py:66
  (46 shorter events, 59.6 us)
Async XLA Ops:
  9.3 60.5 %all-to-all-start = ((bf16[32,144,384]{2,1,0:T(8,128)(2,1)}), bf16[32,144,384]{2,1,0:T(8,128)(2,1)S(1)}, u32[]{:S(2)}, u32[]{:S(2)}) async-start(bf16[32,144,384]{2,1,0:T(8,128)(2,1)} %bitcast.58), calls=%async_computation | async-start | bytes 7077888 | tf_op jit(solution)/shard_map/all_to_all | solution.py:773
  17.6 80.3 %collective-permute-start = (bf16[12,192,768]{2,1,0:T(8,128)(2,1)}, bf16[12,192,768]{2,1,0:T(8,128)(2,1)}, u32[]{:S(2)}, u32[]{:S(2)}) collective-permute-start(bf16[12,192,768]{2,1,0:T(8,128)(2,1)} %bitcast.8.refs_1_), channel_id=1, source_target_pairs={{0,96},{32,0},{64,32},{96,64},{1,97},{33,1},{65,33},{97,65},{2,98}... | collective-permute-start | bytes 10616840 | tf_op jit(solution)/shard_map/ppermute | solution.py:795
  69.7 1.8 copy-start.3
  84.2 53.8 %all-to-all-start.1 = ((bf16[32,144,384]{2,1,0:T(8,128)(2,1)}), bf16[32,144,384]{2,1,0:T(8,128)(2,1)S(1)}, u32[]{:S(2)}, u32[]{:S(2)}) async-start(bf16[32,144,384]{2,1,0:T(8,128)(2,1)} %bitcast.59), calls=%async_computation.1 | async-start | bytes 7077888 | tf_op jit(solution)/shard_map/all_to_all | solution.py:773
  138.0 1.8 copy-start.1
  149.4 23.0 %all-to-all-start.2 = ((bf16[32,144,128]{2,1,0:T(8,128)(2,1)}), bf16[32,144,128]{2,1,0:T(8,128)(2,1)S(1)}, u32[]{:S(2)}, u32[]{:S(2)}) async-start(bf16[32,144,128]{2,1,0:T(8,128)(2,1)} %bitcast.63), calls=%async_computation.2 | async-start | bytes 2359296 | tf_op jit(solution)/shard_map/all_to_all | solution.py:773
  172.4 36.2 %copy-start = (bf16[32,144,128]{2,1,0:T(8,128)(2,1)}, bf16[32,144,128]{2,1,0:T(8,128)(2,1)S(1)}, u32[]{:S(2)}) copy-start(bf16[32,144,128]{2,1,0:T(8,128)(2,1)S(1)} %all-to-all-done.2) | copy-start | bytes 3538948
  212.3 9.6 %collective-permute-start.1 = (bf16[320,384]{1,0:T(8,128)(2,1)}, bf16[320,384]{1,0:T(8,128)(2,1)S(1)}, u32[]{:S(2)}, u32[]{:S(2)}) collective-permute-start(bf16[320,384]{1,0:T(8,128)(2,1)} %get-tuple-element.44.refs_5_), channel_id=1, source_target_pairs={{0,96},{32,0},{64,32},{96,64},{1,97},{33,1},{65,33},{97,65},{2,98}... | collective-permute-start | bytes 737288 | tf_op jit(solution)/shard_map/ppermute | solution.py:831
  221.9 0.7 copy-start.7
  225.7 17.5 %collective-permute-start.2 = (bf16[832,384]{1,0:T(8,128)(2,1)}, bf16[832,384]{1,0:T(8,128)(2,1)S(1)}, u32[]{:S(2)}, u32[]{:S(2)}) collective-permute-start(bf16[832,384]{1,0:T(8,128)(2,1)} %hold.1), channel_id=1, source_target_pairs={{0,96},{32,0},{64,32},{96,64},{1,97},{33,1},{65,33},{97,65},{2,98}... | collective-permute-start | bytes 1916936 | tf_op jit(solution)/shard_map/ppermute | solution.py:833
  243.1 0.8 copy-start.8
  275.5 4.1 %copy-start.6 = (bf16[1344,384]{1,0:T(8,128)(2,1)S(1)}, bf16[1344,384]{1,0:T(8,128)(2,1)}, u32[]{:S(2)}) copy-start(bf16[1344,384]{1,0:T(8,128)(2,1)} %get-tuple-element.57.refs_11_) | copy-start | bytes 3096580
  275.5 40.4 %all-to-all-start.6 = ((bf16[32,48,384]{2,1,0:T(8,128)(2,1)}), bf16[32,48,384]{2,1,0:T(8,128)(2,1)S(1)}, u32[]{:S(2)}, u32[]{:S(2)}) async-start(bf16[32,48,384]{2,1,0:T(8,128)(2,1)} %bitcast.24), calls=%async_computation.6 | async-start | bytes 2359296 | tf_op jit(solution)/shard_map/all_to_all | solution.py:773
  279.6 26.2 %collective-permute-start.3 = (bf16[1344,384]{1,0:T(8,128)(2,1)S(1)}, bf16[1344,384]{1,0:T(8,128)(2,1)S(1)}, u32[]{:S(2)}, u32[]{:S(2)}) collective-permute-start(bf16[1344,384]{1,0:T(8,128)(2,1)S(1)} %copy-done.6), channel_id=1, source_target_pairs={{0,96},{32,0},{64,32},{96,64},{1,97},{33,1},{65,33},{97,65},{2,98}... | collective-permute-start | bytes 3096584 | tf_op jit(solution)/shard_map/ppermute | solution.py:837
  305.7 1.0 copy-start.5
  315.9 1.1 copy-start.4
  316.9 31.3 %all-to-all-start.5 = ((bf16[32,64,384]{2,1,0:T(8,128)(2,1)}), bf16[32,64,384]{2,1,0:T(8,128)(2,1)S(1)}, u32[]{:S(2)}, u32[]{:S(2)}) async-start(bf16[32,64,384]{2,1,0:T(8,128)(2,1)} %bitcast.45), calls=%async_computation.5 | async-start | bytes 3145728 | tf_op jit(solution)/shard_map/all_to_all | solution.py:773
  348.3 1.2 copy-start.2

commit v3 on v2

--- a/solution.py
+++ b/solution.py
@@ -55,14 +55,12 @@
     return pl.BlockSpec(shape, lambda *_: (0,) * len(shape))
 
 
-def call(kernel, inputs, in_specs, out_specs, out_shape, grid, flops, after=(), aliases=None, **extra):
+def call(kernel, inputs, in_specs, out_specs, out_shape, grid, after=(), aliases=None, **extra):
     count = len(inputs)
 
     def body(*refs):
         kernel(*refs[:count], *refs[count + len(after) :])
 
-    outs = jax.tree.leaves(out_shape)
-    moved = sum(value.size * value.dtype.itemsize for value in list(inputs) + outs)
     return pl.pallas_call(
         body,
         grid=grid,
@@ -71,9 +69,7 @@
         out_shape=out_shape,
         input_output_aliases=aliases or {},
         compiler_params=pltpu.CompilerParams(vmem_limit_bytes=VMEM_LIMIT),
-        cost_estimate=pl.CostEstimate(
-            flops=int(flops), bytes_accessed=int(moved), transcendentals=0
-        ),
+        cost_estimate=pl.CostEstimate(flops=1, bytes_accessed=1, transcendentals=0),
         **extra,
     )(*inputs, *after)
 
@@ -243,12 +239,49 @@
         [pl.BlockSpec(memory_space=pl.ANY)] * len(shapes),
         [jax.ShapeDtypeStruct(shape, BF16) for shape in shapes],
         (1,),
-        16 * sum(math.prod(shape) for shape in shapes) * 8,
         after,
         scratch_shapes=[pltpu.VMEM((LAT_BLOCKS, MODES, TILE, LANES), F32)]
         + [pltpu.VMEM(shape, BF16) for shape in shapes]
         + [pltpu.SemaphoreType.DMA((len(shapes),))],
         name="legendre_tables",
+    )
+
+
+def blocks_of(value):
+    return [value[:, index * HALF : (index + 1) * HALF] for index in range(GROUPS)]
+
+
+def interleave(first, second):
+    pairs = zip(blocks_of(first), blocks_of(second))
+    return jnp.concatenate([block for pair in pairs for block in pair], axis=1)
+
+
+def prepare_kernel(gain_ref, mix_ref, proj_ref, gain_out, mix_out, proj_out):
+    gain = gain_ref[...].T
+    gain_out[...] = interleave(gain, gain)
+    real, imag = mix_ref[0].astype(F32), mix_ref[1].astype(F32)
+    upper, lower = interleave(real, imag), interleave(-imag, real)
+    for index in range(GROUPS):
+        rows = slice(index * HALF, (index + 1) * HALF)
+        start = index * LANES
+        mix_out[start : start + HALF, :] = upper[rows].astype(BF16)
+        mix_out[start + HALF : start + LANES, :] = lower[rows].astype(BF16)
+    proj = proj_ref[...].astype(F32).T
+    proj_out[...] = interleave(proj, proj).astype(BF16)
+
+
+def prepare(gain, mix, proj, after):
+    shapes = ((MODES, 2 * C), (2 * C, 2 * C), (C, 2 * C))
+    kinds = (F32, BF16, BF16)
+    return call(
+        prepare_kernel,
+        (gain, mix, proj),
+        [whole(gain.shape), whole(mix.shape), whole(proj.shape)],
+        [whole(shape) for shape in shapes],
+        [jax.ShapeDtypeStruct(shape, kind) for shape, kind in zip(shapes, kinds)],
+        (1,),
+        after,
+        name="prepare",
     )
 
 
@@ -283,7 +316,6 @@
         whole((rows, 2 * C)),
         jax.ShapeDtypeStruct((rows, 2 * C), BF16),
         (LAT_LOCAL // 4,),
-        2 * LAT_LOCAL * C * NLON * table.shape[0],
         after,
         scratch_shapes=[pltpu.VMEM((GROUPS, rows, LANES), F32)],
         name="spectrum_rows",
@@ -362,7 +394,6 @@
         [jax.ShapeDtypeStruct(shape, BF16) for shape in shapes]
         + [jax.ShapeDtypeStruct(recv.shape, BF16)],
         (1,),
-        sum(2 * rows * 2 * C * (2 * 768 + 384) for rows, _ in shapes),
         after,
         scratch_shapes=[pltpu.VMEM(slots, BF16), pltpu.VMEM(slots, BF16)]
         + [pltpu.VMEM(value.shape, BF16) for value in a]
@@ -457,7 +488,6 @@
             jax.ShapeDtypeStruct((C, LANES * blocks), F32),
         ],
         (blocks, LAT_LOCAL // 4),
-        blocks * LAT_LOCAL * HALF * NLON * (4 * 768 + 8 * 192 + 60),
         after,
         scratch_shapes=[
             pltpu.VMEM((rows, LANES), F32),
@@ -513,7 +543,6 @@
             jax.ShapeDtypeStruct((packed, 2 * C), BF16),
         ],
         (1,),
-        2 * rows * 2 * C * (768 + 384),
         after,
         name=f"spectral_backward_{group}",
     )
@@ -532,7 +561,6 @@
         held,
         jax.ShapeDtypeStruct(value.shape, value.dtype),
         (1,),
-        0,
         after,
         aliases={0: 0},
         name="hold",
@@ -571,7 +599,6 @@
         whole((DEVICES, block, TILE, 2 * C)),
         jax.ShapeDtypeStruct((DEVICES, tiles, TILE, 2 * C), BF16),
         (1,),
-        2 * rows * 2 * C * 768,
         after,
         scratch_shapes=[pltpu.VMEM((rows, 2 * C), BF16)],
         name=f"analysis_back_{group}",
@@ -642,7 +669,6 @@
         whole(out),
         jax.ShapeDtypeStruct(out, BF16),
         (1,),
-        sum(4 * value.shape[0] * 2 * C * 2 * C for value in scaleds),
         after,
         scratch_shapes=[
             pltpu.VMEM((MODES, 2 * C), F32),
@@ -667,7 +693,6 @@
         spec,
         jax.ShapeDtypeStruct(payload.shape, BF16),
         (1,),
-        DEVICES * TILE * 2 * C,
         aliases={1: 0},
         name="attach_totals",
     )
@@ -705,7 +730,6 @@
         [whole(shape) for shape in shapes],
         [jax.ShapeDtypeStruct(shape, F32) for shape in shapes],
         (1,),
-        4 * MODES * C,
         after,
         scratch_shapes=[
             pltpu.VMEM((GROUPS, TILE * DEVICES, LANES), F32),
@@ -760,7 +784,6 @@
         block,
         jax.ShapeDtypeStruct((LAT_LOCAL, C, NLON), kind),
         (LAT_LOCAL // 4,),
-        2 * LAT_LOCAL * C * NLON * 256,
         after,
         scratch_shapes=[pltpu.VMEM((GROUPS, rows, LANES), F32)],
         name="field_stage",
@@ -794,23 +817,12 @@
     upstream = incoming[0]
     upstream_next = lax.ppermute(upstream, "section", shift)
     turned = jnp.swapaxes(upstream, 1, 2)
-    gain = jnp.broadcast_to(
-        spectral_gain[0].reshape(MODES, GROUPS, 1, HALF), (MODES, GROUPS, 2, HALF)
-    ).reshape(MODES, 2 * C)
-    real, imag = mix_weight[0, 0], mix_weight[0, 1]
-    mix = (
-        jnp.stack([jnp.stack([real, imag]), jnp.stack([-imag, real])])
-        .reshape(2, 2, GROUPS, HALF, GROUPS, HALF)
-        .transpose(2, 0, 3, 4, 1, 5)
-        .reshape(2 * C, 2 * C)
-    )
-    proj = jnp.broadcast_to(
-        proj_weight[0].T.reshape(C, GROUPS, 1, HALF), (C, GROUPS, 2, HALF)
-    ).reshape(C, 2 * C)
-
     rows = MODES * LAT_LOCAL
     spectrum = spectrum_rows(field, forward_all)
     recv = exchange(spectrum.reshape(DEVICES, TILES, TILE, 2 * C))
+    gain, mix, proj = prepare(
+        jnp.swapaxes(spectral_gain[0], 0, 1), mix_weight[0], proj_weight[0], (spectrum,)
+    )
     tables = legendre_tables(start, order, lat, spread, spread_turned, (spectrum,))
     behind = [tables[4 * group + 2 : 4 * group + 4] for group in range(GROUPS)]
     *scaleds, payload = spectral_forward(
@@ -828,24 +840,23 @@
 
     mixeds, moved = [None] * GROUPS, [None] * GROUPS
     mixeds[2], coeffs_2 = spectral_backward(2, small, large, behind[2][0], gain, mix)
-    moved[2] = lax.ppermute(coeffs_2, "section", shift)
-    mixeds[1], coeffs_1 = spectral_backward(1, small, large, behind[1][0], gain, mix, (coeffs_2,))
-    moved[1] = lax.ppermute(hold(coeffs_1, (moved[2],)), "section", shift)
-
-    out_2 = analysis_back(2, moved[2], behind[2][1], GROUP_TILES, after=(coeffs_1,))
-    mixeds[0], coeffs_0 = spectral_backward(0, small, large, behind[0][0], gain, mix, (out_2,))
-    moved[0] = lax.ppermute(coeffs_0, "section", shift)
+    out_2 = analysis_back(2, coeffs_2, behind[2][1], GROUP_TILES)
     recv_2 = exchange(out_2)
+    mixeds[1], coeffs_1 = spectral_backward(1, small, large, behind[1][0], gain, mix, (out_2,))
+    moved[1] = lax.ppermute(coeffs_1, "section", shift)
+    mixeds[0], coeffs_0 = spectral_backward(0, small, large, behind[0][0], gain, mix, (coeffs_1,))
     partial_grads = weight_grads(
-        scaleds, mixeds, mix, gain, proj_small, proj_large, after=(out_2, coeffs_0)
-    )
+        scaleds, mixeds, mix, gain, proj_small, proj_large, after=(coeffs_0,)
+    )
+    moved[0] = lax.ppermute(hold(coeffs_0, (moved[1], partial_grads)), "section", shift)
     out_1 = analysis_back(1, moved[1], behind[1][1], GROUP_TILES + 1, (partial_grads,))
-    recv_1 = exchange(out_1)
+    recv_1 = exchange(hold(out_1, (recv_2,)))
     out_0 = analysis_back(0, moved[0], behind[0][1], GROUP_TILES + 1, after=(out_1,))
-    base = field_stage(recv_2, forward[2], upstream_next, F32, (out_0,))
+    moved_2 = lax.ppermute(hold(recv_2, (moved[0],)), "section", shift)
     out_0 = attach_totals(recv_1, out_0)
+    base = field_stage(recv_1, forward[1], upstream_next, F32, (out_0,))
     recv_0 = exchange(out_0)
-    base = field_stage(recv_1, forward[1], base, F32, (out_0,))
+    base = field_stage(moved_2, forward[2], base, F32)
     grad_w2, grad_mix, grad_gain = unpack_totals(recv_0)
     received = field_stage(recv_0, forward[0], base, BF16)
     return (

time: 365 us -> 339 us (0.929); the launches traced: 359 us -> 337 us
  blocking collectives: 63.8 us -> 36.2 us
  waiting for transfers between devices: 93.6 us -> 117 us
  local copies, waits for them, and re-layouts: 35 us -> 14.3 us
  starting transfers between devices: 33.1 us -> 38.4 us
  other arithmetic: 3.68 us -> 0 us
    all_to_all x2 -> x1, blocking collectives: 63.8 us -> 36.2 us  [exchange(): moved = lax.all_to_all(flat, 'lat', split_axis=0, concat_axis=0, tiled=True)]
    ppermute x3, waiting for transfers between devices: 35.4 us -> 54 us  [the longest x1 26.4 us: shards(): lax.ppermute(hold(coeffs_0, (moved[1], partial_grads)), 'section', shift)]
    ppermute x1, waiting for transfers between devices: 6.11 us -> 16.3 us  [shards(): upstream_next = lax.ppermute(upstream, 'section', shift)]
    reshape x3 -> x0, local copies, waits for them, and re-layouts: 6.05 us -> none  [the longest x1 2.22 us: shards(): mix = jnp.stack([jnp.stack([real, imag]), jnp.stack([-imag, real])]).resh...]
    all_to_all x5 -> x6, waiting for transfers between devices: 52.2 us -> 46.4 us  [exchange(): moved = lax.all_to_all(flat, 'lat', split_axis=0, concat_axis=0, tiled=True)]
    all_to_all x5 -> x6, starting transfers between devices: 31.3 us -> 36.3 us  [exchange(): moved = lax.all_to_all(flat, 'lat', split_axis=0, concat_axis=0, tiled=True)]
    pallas_call x18 -> x21, Pallas kernels: 129 us -> 131 us  [call(): pl.pallas_call(body, grid=grid, in_specs=list(in_specs) + [pl.BlockSpec(m...]
    unnamed x19 -> x17, local copies, waits for them, and re-layouts: 11.1 us -> 8.99 us
  transfers between devices with their start and end apart: 9 -> 10, of which waited for: 7 -> 7; matrix products, arithmetic and copies ran while one was open for 8% -> 2% of each run, Pallas kernels for 25% -> 28%
where the time goes in v3:
time: 339 us; the launch traced here: 337 us
  Pallas kernels  131 us (39%)
  waiting for transfers between devices  117 us (35%)
  starting transfers between devices  38.4 us (11%)
  blocking collectives  36.2 us (11%)
  local copies, waits for them, and re-layouts  14.3 us (4%)
    pallas_call x21, Pallas kernels, call(): pl.pallas_call(body, grid=grid, in_specs=list(in_specs) + [pl.BlockSpec(m...  131 us
    all_to_all x6, waiting for transfers between devices, exchange(): moved = lax.all_to_all(flat, 'lat', split_axis=0, concat_axis=0, tiled=True)  46.4 us
    all_to_all x6, starting transfers between devices, exchange(): moved = lax.all_to_all(flat, 'lat', split_axis=0, concat_axis=0, tiled=True)  36.3 us
    all_to_all x1, blocking collectives, exchange(): moved = lax.all_to_all(flat, 'lat', split_axis=0, concat_axis=0, tiled=True)  36.2 us
    ppermute x1, waiting for transfers between devices, shards(): lax.ppermute(hold(coeffs_0, (moved[1], partial_grads)), 'section', shift)  26.4 us
    ppermute x1, waiting for transfers between devices, shards(): moved_2 = lax.ppermute(hold(recv_2, (moved[0],)), 'section', shift)  22.9 us
    ppermute x1, waiting for transfers between devices, shards(): upstream_next = lax.ppermute(upstream, 'section', shift)  16.3 us
    unnamed x17, local copies, waits for them, and re-layouts  8.99 us
  transfers between devices with their start and end apart: 10, of which 7 were waited for; matrix products, arithmetic and copies ran while one was open for 2% of the time, Pallas kernels for 28%

profile of v3, /device:TPU:6, one launch (start us, length us, event | category | flops | bytes accessed | tf_op | source)
XLA Modules:
  0.0 337.3 jit_solution(9803722473242413308)
XLA Ops:
  0.6 8.6 %spectrum_rows.1.refs_5_.refs_3_ = bf16[4608,384]{1,0:T(8,128)(2,1)} custom-call(bf16[12,192,768]{2,1,0:T(8,128)(2,1)} %bitcast.56, bf16[768,768]{1,0:T(8,128)(2,1)} %constant.34.clone.refs_1_), custom_call_target="tpu_custom_call" | custom-call | flops 1 | bytes 1 | tf_op jit(solution)/shard_map/spectrum_rows/pallas_call | solution.py:64
  9.3 8.7 %all-to-all-start = ((bf16[32,144,384]{2,1,0:T(8,128)(2,1)}), bf16[32,144,384]{2,1,0:T(8,128)(2,1)}, u32[]{:S(2)}, u32[]{:S(2)}) async-start(bf16[32,144,384]{2,1,0:T(8,128)(2,1)} %bitcast.33), calls=%async_computation | async-start | bytes 7077888 | tf_op jit(solution)/shard_map/all_to_all | solution.py:796
  22.8 23.6 %legendre_tables.1 = (bf16[6,384,512]{2,1,0:T(8,128)(2,1)}, bf16[6,512,384]{2,1,0:T(8,128)(2,1)}, bf16[6,384,512]{2,1,0:T(8,128)(2,1)}, bf16[6,512,384]{2,1,0:T(...) custom-call(f32[16,128]{1,0:T(8,128)} %get-tuple-element.69.refs_0_,, ...), custom_call_target="tpu_custom_call" | custom-call | flops 1 | bytes 1 | tf_op jit(solution)/shard_map/legendre_tables/pallas_call | solution.py:64
  46.4 4.0 %copy.24.refs_9_.refs_2_ = bf16[12,768,192]{2,1,0:T(8,128)(2,1)} copy(bf16[12,768,192]{1,2,0:T(8,128)(2,1)S(1)} %bitcast.40) | data formatting | bytes 7077888 | tf_op jit(solution)/shard_map/transpose | solution.py:819
  50.4 13.8 %all-to-all-done = bf16[32,144,384]{2,1,0:T(8,128)(2,1)} async-done(((bf16[32,144,384]{2,1,0:T(8,128)(2,1)}), bf16[32,144,384]{2,1,0:T(8,128)(2,1)}, u32[]{:S(2)}, u32[]{:S(2)}) %all-to-all-start) | async-done | bytes 3538976 | tf_op jit(solution)/shard_map/all_to_all | solution.py:796
  64.2 12.6 %spectral_forward.1 = (bf16[1536,384]{1,0:T(8,128)(2,1)}, bf16[1024,384]{1,0:T(8,128)(2,1)}, bf16[512,384]{1,0:T(8,128)(2,1)}, bf16[32,9,16,384]{3,2,1,0:T(8,128)(2,1)}) custom-call(bf16[32,9,16,384]{3,2,1,0:T(8,128)(2,1)} %bitcast.2.refs_0_, bf16[6,384,512]{2,1,0:T(8,128)(2,1)} %get-tuple-element.36.refs_1_, ...), custom_call_target="tpu_custom_call" | custom-call | flops 1 | bytes 1 | tf_op jit(solution)/shard_map/spectral_forward/pallas_call | solution.py:64
  76.8 5.1 %all-to-all-start.1 = ((bf16[32,144,384]{2,1,0:T(8,128)(2,1)}), bf16[32,144,384]{2,1,0:T(8,128)(2,1)}, u32[]{:S(2)}, u32[]{:S(2)}) async-start(bf16[32,144,384]{2,1,0:T(8,128)(2,1)} %bitcast.54), calls=%async_computation.1 | async-start | bytes 7077888 | tf_op jit(solution)/shard_map/all_to_all | solution.py:796
  81.9 16.3 %collective-permute-done.refs_6_.refs_2_ = bf16[12,192,768]{2,1,0:T(8,128)(2,1)} collective-permute-done((bf16[12,192,768]{2,1,0:T(8,128)(2,1)S(1)}, bf16[12,192,768]{2,1,0:T(8,128)(2,1)}, u32[]{:S(2)}, u32[]{:S(2)}) %collective-permute-start) | collective-permute-done | bytes 3538976 | tf_op jit(solution)/shard_map/ppermute | solution.py:818
  98.2 29.6 %all-to-all-done.1 = bf16[32,144,384]{2,1,0:T(8,128)(2,1)} async-done(((bf16[32,144,384]{2,1,0:T(8,128)(2,1)}), bf16[32,144,384]{2,1,0:T(8,128)(2,1)}, u32[]{:S(2)}, u32[]{:S(2)}) %all-to-all-start.1) | async-done | bytes 3538976 | tf_op jit(solution)/shard_map/all_to_all | solution.py:796
  127.9 9.7 %grid_stage_1.1 = (bf16[4608,128]{1,0:T(8,128)(2,1)}, f32[192,128]{1,0:T(8,128)}) custom-call(bf16[4608,384]{1,0:T(8,128)(2,1)} %bitcast.12.refs_0_, bf16[12,192,768]{2,1,0:T(8,128)(2,1)} %bitcast.37, bf16[12,768,192]{2,1,0:T(8,128)(2,1)} %copy.24.refs_9_.refs_2_, bf16[192,384]{1,0:T(8,128)(2,1)} %get-tuple-element.44.refs_10_.refs_3_, ...), custom_call_target="tpu_custom_call" | custom-call | flops 1 | bytes 1 | tf_op jit(solution)/shard_map/grid_stage_1/pallas_call | solution.py:64
  141.5 16.1 %grid_stage_2.1 = (bf16[4608,256]{1,0:T(8,128)(2,1)}, f32[192,256]{1,0:T(8,128)}) custom-call(bf16[4608,384]{1,0:T(8,128)(2,1)} %bitcast.12.refs_0_, bf16[12,192,768]{2,1,0:T(8,128)(2,1)} %bitcast.38, bf16[12,768,192]{2,1,0:T(8,128)(2,1)} %copy.24.refs_9_.refs_2_, bf16[192,384]{1,0:T(8,128)(2,1)} %get-tuple-element.44.refs_10_.refs_3_, ...), custom_call_target="tpu_custom_call" | custom-call | flops 1 | bytes 1 | tf_op jit(solution)/shard_map/grid_stage_2/pallas_call | solution.py:64
  160.5 36.2 %all_to_all.35 = bf16[32,144,256]{2,1,0:T(8,128)(2,1)} all-to-all(bf16[32,144,256]{2,1,0:T(8,128)(2,1)} %bitcast.57), channel_id=1, replica_groups=mesh['section'=4,'lat'=32] {'lat'}, dimensions={0} | all-to-all | bytes 4718592 | tf_op jit(solution)/shard_map/all_to_all | solution.py:796
  207.4 4.7 %spectral_backward_1.1 = (bf16[1024,384]{1,0:T(8,128)(2,1)}, bf16[832,384]{1,0:T(8,128)(2,1)}) custom-call(bf16[32,9,16,128]{3,2,1,0:T(8,128)(2,1)} %bitcast.43, bf16[32,9,16,256]{3,2,1,0:T(8,128)(2,1)} %bitcast.35, bf16[6,256,512]{2,1,0:T(8,128)(2,1)} %get-tuple-element.48.refs_2_, f32[384,384]{1,0:T(8,128)} %get-tuple-element.42.refs_7_.refs_3_, ...), custom_call_target="tpu_custom_call" | custom-call | flops 1 | bytes 1 | tf_op jit(solution)/shard_map/spectral_backward_1/pallas_call | solution.py:64
  212.9 5.6 %spectral_backward_0.1 = (bf16[1536,384]{1,0:T(8,128)(2,1)}, bf16[1344,384]{1,0:T(8,128)(2,1)}) custom-call(bf16[32,9,16,128]{3,2,1,0:T(8,128)(2,1)} %bitcast.44, bf16[32,9,16,256]{3,2,1,0:T(8,128)(2,1)} %bitcast.36, bf16[6,384,512]{2,1,0:T(8,128)(2,1)} %get-tuple-element.57.refs_2_, f32[384,384]{1,0:T(8,128)} %get-tuple-element.42.refs_7_.refs_3_, ...), custom_call_target="tpu_custom_call" | custom-call | flops 1 | bytes 1 | tf_op jit(solution)/shard_map/spectral_backward_0/pallas_call | solution.py:64
  218.5 6.7 %weight_grads.1.refs_2_ = bf16[32,16,384]{2,1,0:T(8,128)(2,1)} custom-call(bf16[1536,384]{1,0:T(8,128)(2,1)} %get-tuple-element.54.refs_0_, bf16[1024,384]{1,0:T(8,128)(2,1)} %get-tuple-element.55.refs_1_, bf16[512,384]{1,0:T(8,128)(2,1)} %get-tuple-element.56.refs_2_, bf16[1536,384]{1,0:T(8,128)(2,1)} %get-tuple-element.58.refs_3_, ...), custom_call_target="tpu_custom_call" | custom-call | flops 1 | bytes 1 | tf_op jit(solution)/shard_map/weight_grads/pallas_call | solution.py:64
  225.3 4.7 %collective-permute-done.1.refs_0_.refs_1_ = bf16[832,384]{1,0:T(8,128)(2,1)S(1)} collective-permute-done((bf16[832,384]{1,0:T(8,128)(2,1)}, bf16[832,384]{1,0:T(8,128)(2,1)S(1)}, u32[]{:S(2)}, u32[]{:S(2)}) %collective-permute-start.1) | collective-permute-done | bytes 639008 | tf_op jit(solution)/shard_map/ppermute | solution.py:846
  238.4 7.4 %all-to-all-start.5 = ((bf16[32,64,384]{2,1,0:T(8,128)(2,1)}), bf16[32,64,384]{2,1,0:T(8,128)(2,1)S(1)}, u32[]{:S(2)}, u32[]{:S(2)}) async-start(bf16[32,64,384]{2,1,0:T(8,128)(2,1)} %bitcast.49), calls=%async_computation.5 | async-start | bytes 3145728 | tf_op jit(solution)/shard_map/all_to_all | solution.py:796
  245.8 26.4 %collective-permute-done.2.refs_0_.refs_1_ = bf16[1344,384]{1,0:T(8,128)(2,1)S(1)} collective-permute-done((bf16[1344,384]{1,0:T(8,128)(2,1)}, bf16[1344,384]{1,0:T(8,128)(2,1)S(1)}, u32[]{:S(2)}, u32[]{:S(2)}) %collective-permute-start.2) | collective-permute-done | bytes 1032224 | tf_op jit(solution)/shard_map/ppermute | solution.py:851
  273.3 4.6 %analysis_back_0.1.refs_1_ = bf16[32,4,16,384]{3,2,1,0:T(8,128)(2,1)} custom-call(bf16[1344,384]{1,0:T(8,128)(2,1)} %copy-done.5, bf16[6,512,384]{2,1,0:T(8,128)(2,1)} %get-tuple-element.64.refs_1_, bf16[32,4,16,384]{3,2,1,0:T(8,128)(2,1)} %analysis_back_1.1.refs_2_), custom_call_target="tpu_custom_call" | custom-call | flops 1 | bytes 1 | tf_op jit(solution)/shard_map/analysis_back_0/pallas_call | solution.py:64
  280.9 7.3 %all-to-all-start.6 = ((bf16[32,64,384]{2,1,0:T(8,128)(2,1)}), bf16[32,64,384]{2,1,0:T(8,128)(2,1)S(1)}, u32[]{:S(2)}, u32[]{:S(2)}) async-start(bf16[32,64,384]{2,1,0:T(8,128)(2,1)} %bitcast.41), calls=%async_computation.6 | async-start | bytes 3145728 | tf_op jit(solution)/shard_map/all_to_all | solution.py:796
  288.3 6.6 %field_stage.3.refs_2_ = f32[12,192,768]{2,1,0:T(8,128)} custom-call(bf16[32,4,16,384]{3,2,1,0:T(8,128)(2,1)} %bitcast.48, bf16[256,768]{1,0:T(8,128)(2,1)} %constant.36.clone.refs_1_, bf16[12,192,768]{2,1,0:T(8,128)(2,1)} %collective-permute-done.refs_6_.refs_2_, bf16[32,4,16,384]{3,2,1,0:T(8,128)(2,1)} %attach_totals.1.refs_3_), custom_call_target="tpu_custom_call" | custom-call | flops 1 | bytes 1 | tf_op jit(solution)/shard_map/field_stage/pallas_call | solution.py:64
  294.9 22.9 %collective-permute-done.3.refs_0_ = bf16[32,3,16,384]{3,2,1,0:T(8,128)(2,1)S(1)} collective-permute-done((bf16[32,3,16,384]{3,2,1,0:T(8,128)(2,1)}, bf16[32,3,16,384]{3,2,1,0:T(8,128)(2,1)S(1)}, u32[]{:S(2)}, u32[]{:S(2)}) %collective-permute-start.3) | collective-permute-done | bytes 1179680 | tf_op jit(solution)/shard_map/ppermute | solution.py:855
  318.9 8.2 %field_stage.4.refs_2_ = f32[12,192,768]{2,1,0:T(8,128)} custom-call(bf16[32,3,16,384]{3,2,1,0:T(8,128)(2,1)} %copy-done.7, bf16[256,768]{1,0:T(8,128)(2,1)} %constant.37.clone.refs_1_, f32[12,192,768]{2,1,0:T(8,128)} %field_stage.3.refs_2_), custom_call_target="tpu_custom_call" | custom-call | flops 1 | bytes 1 | tf_op jit(solution)/shard_map/field_stage/pallas_call | solution.py:64
  330.5 6.9 %field_stage.5 = bf16[12,192,768]{2,1,0:T(8,128)(2,1)} custom-call(bf16[32,4,16,384]{3,2,1,0:T(8,128)(2,1)} %bitcast.46, bf16[256,768]{1,0:T(8,128)(2,1)} %constant.35.clone.refs_1_, f32[12,192,768]{2,1,0:T(8,128)} %field_stage.4.refs_2_), custom_call_target="tpu_custom_call" | custom-call | flops 1 | bytes 1 | tf_op jit(solution)/shard_map/field_stage/pallas_call | solution.py:64
  (37 shorter events, 40.3 us)
Async XLA Ops:
  9.3 8.7 %copy-start = (bf16[1,12,192,768]{3,2,1,0:T(8,128)(2,1)S(1)}, bf16[1,12,192,768]{3,2,1,0:T(8,128)(2,1)}, u32[]{:S(2)}) copy-start(bf16[1,12,192,768]{3,2,1,0:T(8,128)(2,1)} %param.17) | copy-start | bytes 10616836
  9.3 54.9 %all-to-all-start = ((bf16[32,144,384]{2,1,0:T(8,128)(2,1)}), bf16[32,144,384]{2,1,0:T(8,128)(2,1)}, u32[]{:S(2)}, u32[]{:S(2)}) async-start(bf16[32,144,384]{2,1,0:T(8,128)(2,1)} %bitcast.33), calls=%async_computation | async-start | bytes 7077888 | tf_op jit(solution)/shard_map/all_to_all | solution.py:796
  18.0 80.2 %collective-permute-start = (bf16[12,192,768]{2,1,0:T(8,128)(2,1)S(1)}, bf16[12,192,768]{2,1,0:T(8,128)(2,1)}, u32[]{:S(2)}, u32[]{:S(2)}) collective-permute-start(bf16[12,192,768]{2,1,0:T(8,128)(2,1)S(1)} %bitcast.39), channel_id=1, source_target_pairs={{0,96},{32,0},{64,32},{96,64},{1,97},{33,1},{65,33},{97,65},{2,98}... | collective-permute-start | bytes 10616840 | tf_op jit(solution)/shard_map/ppermute | solution.py:818
  76.8 51.1 %all-to-all-start.1 = ((bf16[32,144,384]{2,1,0:T(8,128)(2,1)}), bf16[32,144,384]{2,1,0:T(8,128)(2,1)}, u32[]{:S(2)}, u32[]{:S(2)}) async-start(bf16[32,144,384]{2,1,0:T(8,128)(2,1)} %bitcast.54), calls=%async_computation.1 | async-start | bytes 7077888 | tf_op jit(solution)/shard_map/all_to_all | solution.py:796
  137.6 23.0 %all-to-all-start.2 = ((bf16[32,144,128]{2,1,0:T(8,128)(2,1)}), bf16[32,144,128]{2,1,0:T(8,128)(2,1)S(1)}, u32[]{:S(2)}, u32[]{:S(2)}) async-start(bf16[32,144,128]{2,1,0:T(8,128)(2,1)} %bitcast.53), calls=%async_computation.2 | async-start | bytes 2359296 | tf_op jit(solution)/shard_map/all_to_all | solution.py:796
  160.5 36.2 %copy-start.1 = (bf16[32,144,128]{2,1,0:T(8,128)(2,1)}, bf16[32,144,128]{2,1,0:T(8,128)(2,1)S(1)}, u32[]{:S(2)}) copy-start(bf16[32,144,128]{2,1,0:T(8,128)(2,1)S(1)} %all-to-all-done.2) | copy-start | bytes 3538948
  203.4 33.9 %all-to-all-start.4 = ((bf16[32,48,384]{2,1,0:T(8,128)(2,1)}), bf16[32,48,384]{2,1,0:T(8,128)(2,1)S(1)}, u32[]{:S(2)}, u32[]{:S(2)}) async-start(bf16[32,48,384]{2,1,0:T(8,128)(2,1)} %bitcast.50), calls=%async_computation.4 | async-start | bytes 2359296 | tf_op jit(solution)/shard_map/all_to_all | solution.py:796
  212.1 17.9 %collective-permute-start.1 = (bf16[832,384]{1,0:T(8,128)(2,1)}, bf16[832,384]{1,0:T(8,128)(2,1)S(1)}, u32[]{:S(2)}, u32[]{:S(2)}) collective-permute-start(bf16[832,384]{1,0:T(8,128)(2,1)} %get-tuple-element.52.refs_5_), channel_id=1, source_target_pairs={{0,96},{32,0},{64,32},{96,64},{1,97},{33,1},{65,33},{97,65},{2,98}... | collective-permute-start | bytes 1916936 | tf_op jit(solution)/shard_map/ppermute | solution.py:846
  229.9 0.8 copy-start.6
  237.4 1.0 copy-start.4
  238.4 39.5 %all-to-all-start.5 = ((bf16[32,64,384]{2,1,0:T(8,128)(2,1)}), bf16[32,64,384]{2,1,0:T(8,128)(2,1)S(1)}, u32[]{:S(2)}, u32[]{:S(2)}) async-start(bf16[32,64,384]{2,1,0:T(8,128)(2,1)} %bitcast.49), calls=%async_computation.5 | async-start | bytes 3145728 | tf_op jit(solution)/shard_map/all_to_all | solution.py:796
  245.7 26.5 %collective-permute-start.2 = (bf16[1344,384]{1,0:T(8,128)(2,1)}, bf16[1344,384]{1,0:T(8,128)(2,1)S(1)}, u32[]{:S(2)}, u32[]{:S(2)}) collective-permute-start(bf16[1344,384]{1,0:T(8,128)(2,1)} %hold.4), channel_id=1, source_target_pairs={{0,96},{32,0},{64,32},{96,64},{1,97},{33,1},{65,33},{97,65},{2,98}... | collective-permute-start | bytes 3096584 | tf_op jit(solution)/shard_map/ppermute | solution.py:851
  272.2 1.0 copy-start.5
  277.9 1.1 copy-start.3
  280.9 46.1 %all-to-all-start.6 = ((bf16[32,64,384]{2,1,0:T(8,128)(2,1)}), bf16[32,64,384]{2,1,0:T(8,128)(2,1)S(1)}, u32[]{:S(2)}, u32[]{:S(2)}) async-start(bf16[32,64,384]{2,1,0:T(8,128)(2,1)} %bitcast.41), calls=%async_computation.6 | async-start | bytes 3145728 | tf_op jit(solution)/shard_map/all_to_all | solution.py:796
  288.2 29.6 %collective-permute-start.3 = (bf16[32,3,16,384]{3,2,1,0:T(8,128)(2,1)}, bf16[32,3,16,384]{3,2,1,0:T(8,128)(2,1)S(1)}, u32[]{:S(2)}, u32[]{:S(2)}) collective-permute-start(bf16[32,3,16,384]{3,2,1,0:T(8,128)(2,1)} %hold.5), channel_id=1, source_target_pairs={{0,96},{32,0},{64,32},{96,64},{1,97},{33,1},{65,33},{97,65},{2,98}... | collective-permute-start | bytes 3538952 | tf_op jit(solution)/shard_map/ppermute | solution.py:855
  317.8 1.0 copy-start.7
  327.0 1.2 copy-start.2

commit v4 on v3

--- a/solution.py
+++ b/solution.py
@@ -27,7 +27,7 @@
 SPAN = DEVICES * TILE
 LAT_BLOCKS = 4
 BLOCK_LATS = NLAT // LAT_BLOCKS
-VMEM_LIMIT = 56 * 1024 * 1024
+MIB = 1024 * 1024
 F32 = jnp.float32
 BF16 = jnp.bfloat16
 NT = (((1,), (1,)), ((), ()))
@@ -43,6 +43,18 @@
     return lax.broadcasted_iota(jnp.int32, shape, 1) < HALF
 
 
+def packed_rows(group):
+    rows, first = [], 0
+    for local in range(GROUP_ORDERS):
+        rows.append(slice(first, first + degrees_of(group) - DEVICES * local))
+        first = rows[-1].stop
+    return rows
+
+
+PACKED = [packed_rows(group)[-1].stop for group in range(GROUPS)]
+BASES = [sum(PACKED[:group]) for group in range(GROUPS)]
+
+
 def dot(left, right):
     return jnp.dot(left, right, preferred_element_type=F32)
 
@@ -52,10 +64,15 @@
 
 
 def whole(shape):
-    return pl.BlockSpec(shape, lambda *_: (0,) * len(shape))
-
-
-def call(kernel, inputs, in_specs, out_specs, out_shape, grid, after=(), aliases=None, **extra):
+    return pl.BlockSpec(shape, lambda *_: (0,) * len(shape), pipeline_mode=pl.Buffered(1))
+
+
+HELD = pl.BlockSpec(memory_space=pltpu.HBM)
+
+
+def call(
+    kernel, inputs, in_specs, out_specs, out_shape, grid, after=(), aliases=None, vmem=56, **extra
+):
     count = len(inputs)
 
     def body(*refs):
@@ -68,7 +85,7 @@
         out_specs=out_specs,
         out_shape=out_shape,
         input_output_aliases=aliases or {},
-        compiler_params=pltpu.CompilerParams(vmem_limit_bytes=VMEM_LIMIT),
+        compiler_params=pltpu.CompilerParams(vmem_limit_bytes=vmem * MIB),
         cost_estimate=pl.CostEstimate(flops=1, bytes_accessed=1, transcendentals=0),
         **extra,
     )(*inputs, *after)
@@ -236,7 +253,7 @@
         table_kernel,
         inputs,
         [whole(value.shape) for value in inputs],
-        [pl.BlockSpec(memory_space=pl.ANY)] * len(shapes),
+        [HELD] * len(shapes),
         [jax.ShapeDtypeStruct(shape, BF16) for shape in shapes],
         (1,),
         after,
@@ -326,7 +343,7 @@
     total = None
     for index, (order, tile) in enumerate(PAIRS):
         if order == local:
-            part = dot(table_ref[index], tiles[tile])
+            part = dot(table_ref[index, DEVICES * local :, :], tiles[tile])
             total = part if total is None else total + part
     return total
 
@@ -334,10 +351,9 @@
 def spectral_kernel(recv_ref, *refs):
     a_refs, st_refs = refs[0:3], refs[3:6]
     gain_ref, mix_ref = refs[6:8]
-    scaled_outs, payload_ref = refs[8:11], refs[11]
-    recv, payload = refs[12:14]
-    a_buffers, st_buffers, scaled_buffers = refs[14:17], refs[17:20], refs[20:23]
-    in_sems, out_sems = refs[23:25]
+    scaled_ref, payload_ref, recv, payload = refs[8:12]
+    a_buffers, st_buffers, scaled_buffers = refs[12:15], refs[15:18], refs[18:21]
+    in_sems, out_sems = refs[21:23]
     schedule = (2, 0, 1)
     arrivals, departures = {}, []
     for group in schedule:
@@ -350,17 +366,20 @@
         for copy in arrivals[group]:
             copy.start()
     for group in schedule:
-        degrees = degrees_of(group)
         for copy in arrivals[group]:
             copy.wait()
         tiles = [recv[group, :, tile].reshape(SPAN, 2 * C) for tile in range(GROUP_TILES)]
         mixed = []
         for local in range(GROUP_ORDERS):
-            rows = slice(local * degrees, (local + 1) * degrees)
+            skipped = DEVICES * local
             coef = pair_sum(local, a_buffers[group], tiles)
-            scaled = (gain_ref[LANES * group :, :] * coef).astype(BF16)
-            scaled_buffers[group][rows, :] = scaled
-            mixed.append(dot(scaled, mix_ref[...]).astype(BF16))
+            scaled = (gain_ref[LANES * group + skipped :, :] * coef).astype(BF16)
+            scaled_buffers[group][packed_rows(group)[local], :] = scaled
+            product = dot(scaled, mix_ref[...]).astype(BF16)
+            if skipped:
+                zeros = jnp.zeros((skipped, 2 * C), BF16)
+                product = jnp.concatenate([zeros, product], axis=0)
+            mixed.append(product)
         for tile in range(GROUP_TILES):
             grid = dot(st_buffers[group][2 * tile], mixed[tile]) + dot(
                 st_buffers[group][2 * tile + 1], mixed[tile + 1]
@@ -372,7 +391,9 @@
                 payload.at[group], payload_ref.at[:, tiles], out_sems.at[group, 0]
             ),
             pltpu.make_async_copy(
-                scaled_buffers[group], scaled_outs[group], out_sems.at[group, 1]
+                scaled_buffers[group],
+                scaled_ref.at[pl.ds(BASES[group], PACKED[group])],
+                out_sems.at[group, 1],
             ),
         )
         for copy in copies:
@@ -383,25 +404,37 @@
 
 
 def spectral_forward(recv, a, st, gain, mix, after=()):
-    shapes = [(GROUP_ORDERS * degrees_of(group), 2 * C) for group in range(GROUPS)]
-    held = pl.BlockSpec(memory_space=pl.ANY)
     slots = (GROUPS, DEVICES, GROUP_TILES, TILE, 2 * C)
     return call(
         spectral_kernel,
         (recv, *a, *st, gain, mix),
-        [held] * 7 + [whole(gain.shape), whole(mix.shape)],
-        [held] * 4,
-        [jax.ShapeDtypeStruct(shape, BF16) for shape in shapes]
-        + [jax.ShapeDtypeStruct(recv.shape, BF16)],
+        [HELD] * 7 + [whole(gain.shape), whole(mix.shape)],
+        [HELD] * 2,
+        [
+            jax.ShapeDtypeStruct((sum(PACKED), 2 * C), BF16),
+            jax.ShapeDtypeStruct(recv.shape, BF16),
+        ],
         (1,),
         after,
         scratch_shapes=[pltpu.VMEM(slots, BF16), pltpu.VMEM(slots, BF16)]
         + [pltpu.VMEM(value.shape, BF16) for value in a]
         + [pltpu.VMEM(value.shape, BF16) for value in st]
-        + [pltpu.VMEM(shape, BF16) for shape in shapes]
+        + [pltpu.VMEM((rows, 2 * C), BF16) for rows in PACKED]
         + [pltpu.SemaphoreType.DMA((GROUPS, 3)), pltpu.SemaphoreType.DMA((GROUPS, 2))],
         name="spectral_forward",
     )
+
+
+def normal_cumulative(value, bell):
+    denominator = 1.0 + (0.3275911 / math.sqrt(2.0)) * jnp.abs(value)
+    inverse = pl.reciprocal(denominator, approx=True)
+    inverse = inverse * (2.0 - denominator * inverse)
+    series = 0.5 * 1.061405429 * inverse - 0.5 * 1.453152027
+    series = series * inverse + 0.5 * 1.421413741
+    series = series * inverse - 0.5 * 0.284496736
+    series = series * inverse + 0.5 * 0.254829592
+    tail = series * inverse * bell
+    return jnp.where(value < 0.0, tail, 1.0 - tail)
 
 
 def grid_kernel(
@@ -440,8 +473,9 @@
             ],
             axis=1,
         )
-        cumulative = 0.5 * (1.0 + lax.erf(pre * (1.0 / math.sqrt(2.0))))
-        slope = cumulative + pre * jnp.exp(-0.5 * pre * pre) * (1.0 / math.sqrt(2.0 * math.pi))
+        bell = jnp.exp(-0.5 * pre * pre)
+        cumulative = normal_cumulative(pre, bell)
+        slope = cumulative + pre * bell * (1.0 / math.sqrt(2.0 * math.pi))
         act_scratch[rows, :] = (pre * cumulative).astype(BF16)
         pre_scratch[rows, :] = (grad_act * slope).astype(BF16)
     low_grad = half_lanes((C, LANES))
@@ -499,52 +533,53 @@
     )
 
 
-def backward_kernel(group, small_ref, large_ref, s_ref, gain_ref, mix_ref, mixed_ref, coeff_ref):
-    degrees = degrees_of(group)
-    tiles = [
-        jnp.concatenate(
-            [
-                small_ref[:, tile].reshape(SPAN, LANES),
-                large_ref[:, tile].reshape(SPAN, 2 * LANES),
-            ],
-            axis=1,
-        )
-        for tile in range(GROUP_TILES)
+def backward_kernel(groups, *refs):
+    recv_ref, table_refs, out_ref = refs[0], refs[1 : 1 + len(groups)], refs[1 + len(groups)]
+    buffers, sems = refs[2 + len(groups) : -1], refs[-1]
+    copies = [
+        pltpu.make_async_copy(table_refs[place], buffers[place], sems.at[place])
+        for place in range(len(groups))
     ]
-    for local in range(GROUP_ORDERS):
-        rows = slice(local * degrees, (local + 1) * degrees)
-        mixed = pair_sum(local, s_ref, tiles).astype(BF16)
-        mixed_ref[rows, :] = mixed
-        scaled = dot_nt(mixed, mix_ref[...])
-        coeffs = (gain_ref[LANES * group :, :] * scaled).astype(BF16)
-        coeff_ref[packed_rows(degrees, local), :] = coeffs[DEVICES * local :]
-
-
-def packed_rows(degrees, local):
-    first = sum(degrees - DEVICES * other for other in range(local))
-    return slice(first, first + degrees - DEVICES * local)
-
-
-def spectral_backward(group, small, large, s, gain, mix, after=()):
-    degrees = degrees_of(group)
-    rows = GROUP_ORDERS * degrees
-    packed = packed_rows(degrees, GROUP_ORDERS - 1).stop
-    return call(
-        functools.partial(backward_kernel, group),
-        (small, large, s, gain, mix),
+    for copy in copies:
+        copy.start()
+    lanes = recv_ref.shape[-1]
+    first = 0
+    for place, group in enumerate(groups):
+        start = GROUP_TILES * place
+        tiles = [
+            recv_ref[:, start + tile].reshape(SPAN, lanes) for tile in range(GROUP_TILES)
+        ]
+        copies[place].wait()
+        for local, rows in enumerate(packed_rows(group)):
+            mixed = pair_sum(local, buffers[place], tiles).astype(BF16)
+            out_ref[first + rows.start : first + rows.stop, :] = mixed
+        first += PACKED[group]
+
+
+def spectral_backward(groups, recv, tables, after=()):
+    lanes = recv.shape[-1]
+    tiles = GROUP_TILES * len(groups)
+    block = groups[0] if len(groups) == 1 else 0
+    out = (sum(PACKED[group] for group in groups), lanes)
+    return call(
+        functools.partial(backward_kernel, groups),
+        (recv, *tables),
         [
-            pl.BlockSpec((DEVICES, GROUP_TILES, TILE, lanes), lambda b: (0, group, 0, 0))
-            for lanes in (LANES, 2 * LANES)
+            pl.BlockSpec(
+                (DEVICES, tiles, TILE, lanes),
+                lambda b: (0, block, 0, 0),
+                pipeline_mode=pl.Buffered(1),
+            )
         ]
-        + [whole(s.shape), whole(gain.shape), whole(mix.shape)],
-        [whole((rows, 2 * C)), whole((packed, 2 * C))],
-        [
-            jax.ShapeDtypeStruct((rows, 2 * C), BF16),
-            jax.ShapeDtypeStruct((packed, 2 * C), BF16),
-        ],
+        + [HELD] * len(groups),
+        whole(out),
+        jax.ShapeDtypeStruct(out, BF16),
         (1,),
         after,
-        name=f"spectral_backward_{group}",
+        scratch_shapes=[pltpu.VMEM(table.shape, BF16) for table in tables]
+        + [pltpu.SemaphoreType.DMA((len(groups),))],
+        vmem=20,
+        name="spectral_backward_" + "_".join(str(group) for group in groups),
     )
 
 
@@ -563,44 +598,60 @@
         (1,),
         after,
         aliases={0: 0},
+        vmem=1,
         name="hold",
     )
 
 
-def synthesis_kernel(group, packed_ref, at_ref, *rest):
-    out_ref, coeff_ref = rest[-2:]
-    rest = rest[:-1]
+def synthesis_kernel(group, table_ref, small_ref, large_ref, gain_ref, mix_ref, *refs):
+    extra, (out_ref, coeff_ref, at_ref, part_ref, sems) = refs[:-5], refs[-5:]
     degrees = degrees_of(group)
-    for local in range(GROUP_ORDERS):
+    copies = (
+        pltpu.make_async_copy(
+            small_ref.at[pl.ds(BASES[group], PACKED[group])], part_ref, sems.at[0]
+        ),
+        pltpu.make_async_copy(table_ref, at_ref, sems.at[1]),
+    )
+    for copy in copies:
+        copy.start()
+    copies[0].wait()
+    for local, rows in enumerate(packed_rows(group)):
         first = local * degrees
         skipped = DEVICES * local
-        if local:
+        mixed = jnp.concatenate([part_ref[rows, :], large_ref[rows, :]], axis=1)
+        scaled = dot_nt(mixed, mix_ref[...])
+        if skipped:
             coeff_ref[first : first + skipped, :] = jnp.zeros((skipped, 2 * C), BF16)
-        coeff_ref[first + skipped : first + degrees, :] = packed_ref[
-            packed_rows(degrees, local), :
-        ]
+        coeff_ref[first + skipped : first + degrees, :] = (
+            gain_ref[LANES * group + skipped :, :] * scaled
+        ).astype(BF16)
+    copies[1].wait()
     for tile in range(GROUP_TILES):
         first = coeff_ref[tile * degrees : (tile + 1) * degrees, :]
         second = coeff_ref[(tile + 1) * degrees : (tile + 2) * degrees, :]
         out = dot(at_ref[2 * tile], first) + dot(at_ref[2 * tile + 1], second)
         out_ref[:, tile] = out.astype(BF16).reshape(DEVICES, TILE, 2 * C)
-    if len(rest) == 2:
-        out_ref[:, GROUP_TILES] = rest[0][...]
-
-
-def analysis_back(group, coeffs, at, tiles, extra=(), after=()):
-    degrees = degrees_of(group)
-    rows = GROUP_ORDERS * degrees
-    block = GROUP_TILES + len(extra)
+    if extra:
+        out_ref[:, GROUP_TILES] = extra[0][...]
+
+
+def analysis_back(group, at, small, large, gain, mix, tiles, extra=(), after=()):
+    inputs = (at, small, large, gain, mix, *extra)
     return call(
         functools.partial(synthesis_kernel, group),
-        (coeffs, at, *extra),
-        [whole(coeffs.shape), whole(at.shape)] + [whole(value.shape) for value in extra],
-        whole((DEVICES, block, TILE, 2 * C)),
+        inputs,
+        [HELD] * 2 + [whole(value.shape) for value in inputs[2:]],
+        whole((DEVICES, GROUP_TILES + len(extra), TILE, 2 * C)),
         jax.ShapeDtypeStruct((DEVICES, tiles, TILE, 2 * C), BF16),
         (1,),
         after,
-        scratch_shapes=[pltpu.VMEM((rows, 2 * C), BF16)],
+        scratch_shapes=[
+            pltpu.VMEM((GROUP_ORDERS * degrees_of(group), 2 * C), BF16),
+            pltpu.VMEM(at.shape, BF16),
+            pltpu.VMEM((PACKED[group], LANES), BF16),
+            pltpu.SemaphoreType.DMA((2,)),
+        ],
+        vmem=20,
         name=f"analysis_back_{group}",
     )
 
@@ -609,27 +660,29 @@
     return tile + pltpu.roll(tile, HALF, 1)
 
 
-def weight_kernel(*refs):
-    scaled_refs, mixed_refs = refs[:3], refs[3:6]
-    mix_ref, factor_ref, proj_small, proj_large, out_ref, gain, packed, spaced = refs[6:]
+def weight_kernel(held_ref, small_ref, *refs):
+    large_refs, (mix_ref, factor_ref, proj_small, proj_large) = refs[:3], refs[3:7]
+    out_ref, gain, packed, spaced, scaled_ref, sem = refs[7:]
+    copy = pltpu.make_async_copy(held_ref, scaled_ref, sem)
+    copy.start()
+    copy.wait()
     block = None
-    for scaled_ref, mixed_ref in zip(scaled_refs, mixed_refs):
+    for group in range(GROUPS):
+        rows = slice(BASES[group], BASES[group] + PACKED[group])
+        mixed = jnp.concatenate([small_ref[rows, :], large_refs[group][...]], axis=1)
         part = lax.dot_general(
-            scaled_ref[...], mixed_ref[...], (((0,), (0,)), ((), ())), preferred_element_type=F32
+            scaled_ref[rows, :], mixed, (((0,), (0,)), ((), ())), preferred_element_type=F32
         )
         block = part if block is None else block + part
-    for group in range(GROUPS):
-        degrees = degrees_of(group)
-        total = None
-        for local in range(GROUP_ORDERS):
-            rows = slice(local * degrees, (local + 1) * degrees)
-            part = dot_nt(mixed_refs[group][rows, :], mix_ref[...])
-            part = part * scaled_refs[group][rows, :].astype(F32)
-            total = part if total is None else total + part
-        if group == 0:
-            gain[...] = total
-        else:
-            gain[LANES * group :, :] += total
+        for local, rows in enumerate(packed_rows(group)):
+            here = slice(BASES[group] + rows.start, BASES[group] + rows.stop)
+            mixed = jnp.concatenate([small_ref[here, :], large_refs[group][rows, :]], axis=1)
+            part = dot_nt(mixed, mix_ref[...]) * scaled_ref[here, :].astype(F32)
+            first = LANES * group + DEVICES * local
+            if first:
+                gain[first:, :] += part
+            else:
+                gain[...] = part
     gain[...] = gain[...] / factor_ref[...]
     low = half_lanes((HALF, LANES))
     low_gain = half_lanes((C, LANES))
@@ -659,13 +712,13 @@
         out_ref[:, :, lanes] = spaced[index].astype(BF16).reshape(DEVICES, TILE, LANES)
 
 
-def weight_grads(scaleds, mixeds, mix, gain, proj_small, proj_large, after=()):
+def weight_grads(scaled, small, large, mix, gain, proj_small, proj_large, after=()):
     out = (DEVICES, TILE, 2 * C)
-    inputs = (*scaleds, *mixeds, mix, gain, proj_small, proj_large)
+    inputs = (scaled, small, *large, mix, gain, proj_small, proj_large)
     return call(
         weight_kernel,
         inputs,
-        [whole(value.shape) for value in inputs],
+        [HELD] + [whole(value.shape) for value in inputs[1:]],
         whole(out),
         jax.ShapeDtypeStruct(out, BF16),
         (1,),
@@ -674,7 +727,10 @@
             pltpu.VMEM((MODES, 2 * C), F32),
             pltpu.VMEM((GROUPS, 15 * DEVICES, LANES), F32),
             pltpu.VMEM((GROUPS, TILE * DEVICES, LANES), F32),
+            pltpu.VMEM(scaled.shape, BF16),
+            pltpu.SemaphoreType.DMA,
         ],
+        vmem=24,
         name="weight_grads",
     )
 
@@ -694,6 +750,7 @@
         jax.ShapeDtypeStruct(payload.shape, BF16),
         (1,),
         aliases={1: 0},
+        vmem=8,
         name="attach_totals",
     )
 
@@ -735,21 +792,24 @@
             pltpu.VMEM((GROUPS, TILE * DEVICES, LANES), F32),
             pltpu.VMEM((GROUPS, 15 * DEVICES, LANES), F32),
         ],
+        vmem=12,
         name="unpack_totals",
     )
 
 
-def field_kernel(recv_ref, table_ref, base_ref, out_ref, scratch):
+def field_kernel(*refs):
+    recv_refs, (table_ref, base_ref, out_ref, scratch) = refs[:-4], refs[-4:]
     step = pl.program_id(0)
     orders = DEVICES * GROUP_ORDERS
-    rows = orders * LAT_LOCAL
+    rows = orders * LAT_LOCAL // len(recv_refs)
 
     @pl.when(step == 0)
     def _():
         for index in range(GROUPS):
             lanes = slice(index * LANES, (index + 1) * LANES)
-            values = recv_ref[:, :, :, lanes].astype(F32)
-            scratch[index] = values.reshape(rows, LANES)
+            for place, recv_ref in enumerate(recv_refs):
+                values = recv_ref[:, :, :, lanes].astype(F32)
+                scratch[index, place * rows : (place + 1) * rows] = values.reshape(rows, LANES)
 
     lefts = []
     for inner in range(4):
@@ -770,22 +830,27 @@
         out_ref[inner] = total.astype(out_ref.dtype)
 
 
-def field_stage(recv, table, base, kind, after=()):
+def field_stage(recv, table, base, after=()):
     rows = DEVICES * GROUP_ORDERS * LAT_LOCAL
     block = pl.BlockSpec((4, C, NLON), lambda b: (b, 0, 0))
     return call(
         field_kernel,
-        (recv, table, base),
+        (*recv, table, base),
         [
-            pl.BlockSpec((DEVICES, GROUP_TILES, TILE, 2 * C), lambda b: (0, 0, 0, 0)),
-            whole(table.shape),
-            block,
-        ],
+            pl.BlockSpec(
+                (DEVICES // len(recv), GROUP_TILES, TILE, 2 * C),
+                lambda b: (0, 0, 0, 0),
+                pipeline_mode=pl.Buffered(1),
+            )
+        ]
+        * len(recv)
+        + [whole(table.shape), block],
         block,
-        jax.ShapeDtypeStruct((LAT_LOCAL, C, NLON), kind),
+        jax.ShapeDtypeStruct((LAT_LOCAL, C, NLON), BF16),
         (LAT_LOCAL // 4,),
         after,
         scratch_shapes=[pltpu.VMEM((GROUPS, rows, LANES), F32)],
+        vmem=20,
         name="field_stage",
     )
 
@@ -823,14 +888,28 @@
     gain, mix, proj = prepare(
         jnp.swapaxes(spectral_gain[0], 0, 1), mix_weight[0], proj_weight[0], (spectrum,)
     )
+    gain_next, mix_next, _ = prepare(
+        lax.ppermute(jnp.swapaxes(spectral_gain[0], 0, 1), "section", shift),
+        lax.ppermute(mix_weight[0], "section", shift),
+        proj_weight[0],
+        (spectrum,),
+    )
     tables = legendre_tables(start, order, lat, spread, spread_turned, (spectrum,))
     behind = [tables[4 * group + 2 : 4 * group + 4] for group in range(GROUPS)]
-    *scaleds, payload = spectral_forward(
+    scaled, payload = spectral_forward(
         recv, tables[0::4], tables[1::4], gain, mix, (turned, proj)
     )
     recv = exchange(payload).reshape(rows, 2 * C)
     small_rows, proj_small = grid_stage(
-        0, 1, recv, upstream, turned, proj, inverse, inverse_turned, (upstream_next,)
+        0,
+        1,
+        recv,
+        upstream,
+        turned,
+        proj,
+        inverse,
+        inverse_turned,
+        (upstream_next, gain_next, mix_next),
     )
     small = exchange(small_rows.reshape(DEVICES, TILES, TILE, LANES))
     large, proj_large = grid_stage(
@@ -839,26 +918,50 @@
     large = exchange(large.reshape(DEVICES, TILES, TILE, 2 * LANES))
 
     mixeds, moved = [None] * GROUPS, [None] * GROUPS
-    mixeds[2], coeffs_2 = spectral_backward(2, small, large, behind[2][0], gain, mix)
-    out_2 = analysis_back(2, coeffs_2, behind[2][1], GROUP_TILES)
+    every = tuple(range(GROUPS))
+    mixed_small = spectral_backward(every, small, [table[0] for table in behind])
+    moved_small = lax.ppermute(mixed_small, "section", shift)
+    mixed_2 = spectral_backward((2,), large, [behind[2][0]], (moved_small,))
+    moved_2 = lax.ppermute(mixed_2, "section", shift)
+    out_2 = analysis_back(
+        2, behind[2][1], moved_small, moved_2, gain_next, mix_next, GROUP_TILES
+    )
     recv_2 = exchange(out_2)
-    mixeds[1], coeffs_1 = spectral_backward(1, small, large, behind[1][0], gain, mix, (out_2,))
-    moved[1] = lax.ppermute(coeffs_1, "section", shift)
-    mixeds[0], coeffs_0 = spectral_backward(0, small, large, behind[0][0], gain, mix, (coeffs_1,))
+    mixed_1 = spectral_backward((1,), large, [behind[1][0]], (out_2,))
+    moved_1 = lax.ppermute(mixed_1, "section", shift)
+    mixed_0 = spectral_backward((0,), large, [behind[0][0]], (mixed_1,))
+    moved_0 = lax.ppermute(mixed_0, "section", shift)
     partial_grads = weight_grads(
-        scaleds, mixeds, mix, gain, proj_small, proj_large, after=(coeffs_0,)
-    )
-    moved[0] = lax.ppermute(hold(coeffs_0, (moved[1], partial_grads)), "section", shift)
-    out_1 = analysis_back(1, moved[1], behind[1][1], GROUP_TILES + 1, (partial_grads,))
-    recv_1 = exchange(hold(out_1, (recv_2,)))
-    out_0 = analysis_back(0, moved[0], behind[0][1], GROUP_TILES + 1, after=(out_1,))
-    moved_2 = lax.ppermute(hold(recv_2, (moved[0],)), "section", shift)
+        scaled, mixed_small, (mixed_0, mixed_1, mixed_2), mix, gain, proj_small, proj_large
+    )
+    out_1 = analysis_back(
+        1,
+        behind[1][1],
+        moved_small,
+        moved_1,
+        gain_next,
+        mix_next,
+        GROUP_TILES + 1,
+        (partial_grads,),
+    )
+    out_1 = hold(out_1, (recv_2,))
+    recv_1 = exchange(out_1)
+    out_0 = analysis_back(
+        0,
+        behind[0][1],
+        moved_small,
+        moved_0,
+        gain_next,
+        mix_next,
+        GROUP_TILES + 1,
+        after=(recv_2,),
+    )
     out_0 = attach_totals(recv_1, out_0)
-    base = field_stage(recv_1, forward[1], upstream_next, F32, (out_0,))
     recv_0 = exchange(out_0)
-    base = field_stage(moved_2, forward[2], base, F32)
+    base = field_stage((recv_2,), forward[2], upstream_next, (out_0,))
+    base = field_stage((recv_1,), forward[1], base)
     grad_w2, grad_mix, grad_gain = unpack_totals(recv_0)
-    received = field_stage(recv_0, forward[0], base, BF16)
+    received = field_stage((recv_0,), forward[0], base)
     return (
         received[None],
         grad_w2[None],

time: 339 us -> 313 us (0.923)
  blocking collectives: 36.2 us -> 0 us
  Pallas kernels: 131 us -> 104 us
  local copies, waits for them, and re-layouts: 14.3 us -> 27.4 us
  waiting for transfers between devices: 117 us -> 130 us
  starting transfers between devices: 38.4 us -> 46.4 us
    all_to_all x1 -> x0, blocking collectives: 36.2 us -> none  [exchange(): moved = lax.all_to_all(flat, 'lat', split_axis=0, concat_axis=0, tiled=True)]
    pallas_call x21, Pallas kernels: 131 us -> 104 us  [call(): pl.pallas_call(body, grid=grid, in_specs=list(in_specs) + [pl.BlockSpec(m...]
    ppermute x3 -> x6, waiting for transfers between devices: 54 us -> 74.2 us  [the longest x1 26.1 us: shards(): lax.ppermute(mix_weight[0], 'section', shift)]
    ppermute x1, waiting for transfers between devices: 16.3 us -> 0.01 us  [shards(): upstream_next = lax.ppermute(upstream, 'section', shift)]
    unnamed x17 -> x76, local copies, waits for them, and re-layouts: 8.99 us -> 19.8 us
    all_to_all x6 -> x7, waiting for transfers between devices: 46.4 us -> 55.3 us  [exchange(): moved = lax.all_to_all(flat, 'lat', split_axis=0, concat_axis=0, tiled=True)]
    all_to_all x6 -> x7, starting transfers between devices: 36.3 us -> 41.6 us  [exchange(): moved = lax.all_to_all(flat, 'lat', split_axis=0, concat_axis=0, tiled=True)]
  transfers between devices with their start and end apart: 10 -> 14, of which waited for: 7 -> 10; matrix products, arithmetic and copies ran while one was open for 2% -> 2% of each run, Pallas kernels for 28% -> 24%
where the time goes in v4:
time: 313 us; the launch traced here: 309 us
  waiting for transfers between devices  130 us (42%)
  Pallas kernels  104 us (33%)
  starting transfers between devices  46.4 us (15%)
  local copies, waits for them, and re-layouts  27.4 us (9%)
    pallas_call x21, Pallas kernels, call(): pl.pallas_call(body, grid=grid, in_specs=list(in_specs) + [pl.BlockSpec(m...  104 us
    all_to_all x7, waiting for transfers between devices, exchange(): moved = lax.all_to_all(flat, 'lat', split_axis=0, concat_axis=0, tiled=True)  55.3 us
    all_to_all x7, starting transfers between devices, exchange(): moved = lax.all_to_all(flat, 'lat', split_axis=0, concat_axis=0, tiled=True)  41.6 us
    ppermute x1, waiting for transfers between devices, shards(): lax.ppermute(mix_weight[0], 'section', shift)  26.1 us
    unnamed x76, local copies, waits for them, and re-layouts  19.8 us
    ppermute x1, waiting for transfers between devices, shards(): moved_0 = lax.ppermute(mixed_0, 'section', shift)  19 us
    ppermute x1, waiting for transfers between devices, shards(): moved_small = lax.ppermute(mixed_small, 'section', shift)  16.1 us
    ppermute x1, waiting for transfers between devices, shards(): moved_1 = lax.ppermute(mixed_1, 'section', shift)  7.98 us
  transfers between devices with their start and end apart: 14, of which 10 were waited for; matrix products, arithmetic and copies ran while one was open for 2% of the time, Pallas kernels for 24%

profile of v4, /device:TPU:6, one launch (start us, length us, event | category | flops | bytes accessed | tf_op | source)
XLA Modules:
  0.0 309.0 jit_solution(6510993739071896427)
XLA Ops:
  0.6 8.6 %spectrum_rows.1.refs_5_.refs_3_ = bf16[4608,384]{1,0:T(8,128)(2,1)} custom-call(bf16[12,192,768]{2,1,0:T(8,128)(2,1)} %bitcast.51, bf16[768,768]{1,0:T(8,128)(2,1)} %constant.34.clone.refs_1_), custom_call_target="tpu_custom_call" | custom-call | flops 1 | bytes 1 | tf_op jit(solution)/shard_map/spectrum_rows/pallas_call | solution.py:81
  9.3 8.4 %all-to-all-start = ((bf16[32,144,384]{2,1,0:T(8,128)(2,1)}), bf16[32,144,384]{2,1,0:T(8,128)(2,1)}, u32[]{:S(2)}, u32[]{:S(2)}) async-start(bf16[32,144,384]{2,1,0:T(8,128)(2,1)} %bitcast.43), calls=%async_computation | async-start | bytes 7077888 | tf_op jit(solution)/shard_map/all_to_all | solution.py:861
  22.5 23.6 %legendre_tables.1 = (bf16[6,384,512]{2,1,0:T(8,128)(2,1)}, bf16[6,512,384]{2,1,0:T(8,128)(2,1)}, bf16[6,384,512]{2,1,0:T(8,128)(2,1)}, bf16[6,512,384]{2,1,0:T(...) custom-call(f32[16,128]{1,0:T(8,128)} %get-tuple-element.57.refs_0_,, ...), custom_call_target="tpu_custom_call" | custom-call | flops 1 | bytes 1 | tf_op jit(solution)/shard_map/legendre_tables/pallas_call | solution.py:81
  46.1 6.3 %copy.22.refs_9_.refs_2_ = bf16[12,768,192]{2,1,0:T(8,128)(2,1)} copy(bf16[12,768,192]{1,2,0:T(8,128)(2,1)} %bitcast.45) | data formatting | bytes 7077888 | tf_op jit(solution)/shard_map/transpose | solution.py:884
  52.4 11.5 %all-to-all-done = bf16[32,144,384]{2,1,0:T(8,128)(2,1)} async-done(((bf16[32,144,384]{2,1,0:T(8,128)(2,1)}), bf16[32,144,384]{2,1,0:T(8,128)(2,1)}, u32[]{:S(2)}, u32[]{:S(2)}) %all-to-all-start) | async-done | bytes 3538976 | tf_op jit(solution)/shard_map/all_to_all | solution.py:861
  63.9 12.1 %spectral_forward.1 = (bf16[2496,384]{1,0:T(8,128)(2,1)}, bf16[32,9,16,384]{3,2,1,0:T(8,128)(2,1)}) custom-call(bf16[32,9,16,384]{3,2,1,0:T(8,128)(2,1)} %bitcast.4.refs_0_, bf16[6,384,512]{2,1,0:T(8,128)(2,1)} %get-tuple-element.31.refs_1_, bf16[6,256,512]{2,1,0:T(8,128)(2,1)} %get-tuple-element.32.refs_2_, bf16[6,128,512]{2,1,0:T(8,128)(2,1)} %get-tuple-element.33.refs_3_, ...), custom_call_target="tpu_custom_call" | custom-call | flops 1 | bytes 1 | tf_op jit(solution)/shard_map/spectral_forward/pallas_call | solution.py:81
  76.0 4.9 %all-to-all-start.1 = ((bf16[32,144,384]{2,1,0:T(8,128)(2,1)}), bf16[32,144,384]{2,1,0:T(8,128)(2,1)}, u32[]{:S(2)}, u32[]{:S(2)}) async-start(bf16[32,144,384]{2,1,0:T(8,128)(2,1)} %bitcast.49), calls=%async_computation.1 | async-start | bytes 7077888 | tf_op jit(solution)/shard_map/all_to_all | solution.py:861
  82.5 26.1 %collective-permute-done.2.refs_1_ = bf16[2,192,192]{2,1,0:T(8,128)(2,1)S(1)} collective-permute-done((bf16[2,192,192]{2,1,0:T(8,128)(2,1)}, bf16[2,192,192]{2,1,0:T(8,128)(2,1)S(1)}, u32[]{:S(2)}, u32[]{:S(2)}) %collective-permute-start.2) | collective-permute-done | bytes 147488 | tf_op jit(solution)/shard_map/ppermute | solution.py:893
  112.4 14.7 %all-to-all-done.1 = bf16[32,144,384]{2,1,0:T(8,128)(2,1)} async-done(((bf16[32,144,384]{2,1,0:T(8,128)(2,1)}), bf16[32,144,384]{2,1,0:T(8,128)(2,1)}, u32[]{:S(2)}, u32[]{:S(2)}) %all-to-all-start.1) | async-done | bytes 3538976 | tf_op jit(solution)/shard_map/all_to_all | solution.py:861
  127.1 10.2 %grid_stage_1.1 = (bf16[4608,128]{1,0:T(8,128)(2,1)}, f32[192,128]{1,0:T(8,128)}) custom-call(bf16[4608,384]{1,0:T(8,128)(2,1)} %bitcast.12.refs_0_, bf16[12,192,768]{2,1,0:T(8,128)(2,1)} %bitcast.46, bf16[12,768,192]{2,1,0:T(8,128)(2,1)} %copy.22.refs_9_.refs_2_, bf16[192,384]{1,0:T(8,128)(2,1)} %get-tuple-element.39.refs_10_.refs_3_, ...), custom_call_target="tpu_custom_call" | custom-call | flops 1 | bytes 1 | tf_op jit(solution)/shard_map/grid_stage_1/pallas_call | solution.py:81
  137.3 3.9 %all-to-all-start.2 = ((bf16[32,144,128]{2,1,0:T(8,128)(2,1)}), bf16[32,144,128]{2,1,0:T(8,128)(2,1)S(1)}, u32[]{:S(2)}, u32[]{:S(2)}) async-start(bf16[32,144,128]{2,1,0:T(8,128)(2,1)} %bitcast.48), calls=%async_computation.2 | async-start | bytes 2359296 | tf_op jit(solution)/shard_map/all_to_all | solution.py:861
  141.2 17.1 %grid_stage_2.1 = (bf16[4608,256]{1,0:T(8,128)(2,1)}, f32[192,256]{1,0:T(8,128)}) custom-call(bf16[4608,384]{1,0:T(8,128)(2,1)} %bitcast.12.refs_0_, bf16[12,192,768]{2,1,0:T(8,128)(2,1)} %bitcast.47, bf16[12,768,192]{2,1,0:T(8,128)(2,1)} %copy.22.refs_9_.refs_2_, bf16[192,384]{1,0:T(8,128)(2,1)} %get-tuple-element.39.refs_10_.refs_3_, ...), custom_call_target="tpu_custom_call" | custom-call | flops 1 | bytes 1 | tf_op jit(solution)/shard_map/grid_stage_2/pallas_call | solution.py:81
  160.3 5.5 %all-to-all-start.3 = ((bf16[32,144,256]{2,1,0:T(8,128)(2,1)}), bf16[32,144,256]{2,1,0:T(8,128)(2,1)S(1)}, u32[]{:S(2)}, u32[]{:S(2)}) async-start(bf16[32,144,256]{2,1,0:T(8,128)(2,1)} %bitcast.52), calls=%async_computation.3 | async-start | bytes 4718592 | tf_op jit(solution)/shard_map/all_to_all | solution.py:861
  173.7 16.1 %collective-permute-done.3.refs_2_.refs_1_ = bf16[2496,128]{1,0:T(8,128)(2,1)S(1)} collective-permute-done((bf16[2496,128]{1,0:T(8,128)(2,1)S(1)}, bf16[2496,128]{1,0:T(8,128)(2,1)S(1)}, u32[]{:S(2)}, u32[]{:S(2)}) %collective-permute-start.3) | collective-permute-done | bytes 639008 | tf_op jit(solution)/shard_map/ppermute | solution.py:923
  189.8 9.1 %all-to-all-done.3 = bf16[32,144,256]{2,1,0:T(8,128)(2,1)S(1)} async-done(((bf16[32,144,256]{2,1,0:T(8,128)(2,1)}), bf16[32,144,256]{2,1,0:T(8,128)(2,1)S(1)}, u32[]{:S(2)}, u32[]{:S(2)}) %all-to-all-start.3) | async-done | bytes 2359328 | tf_op jit(solution)/shard_map/all_to_all | solution.py:861
  202.1 5.0 %collective-permute-done.4.refs_2_ = bf16[320,256]{1,0:T(8,128)(2,1)S(1)} collective-permute-done((bf16[320,256]{1,0:T(8,128)(2,1)S(1)}, bf16[320,256]{1,0:T(8,128)(2,1)S(1)}, u32[]{:S(2)}, u32[]{:S(2)}) %collective-permute-start.4) | collective-permute-done | bytes 163872 | tf_op jit(solution)/shard_map/ppermute | solution.py:925
  209.8 3.9 %all-to-all-start.4 = ((bf16[32,48,384]{2,1,0:T(8,128)(2,1)}), bf16[32,48,384]{2,1,0:T(8,128)(2,1)S(1)}, u32[]{:S(2)}, u32[]{:S(2)}) async-start(bf16[32,48,384]{2,1,0:T(8,128)(2,1)} %bitcast.41), calls=%async_computation.4 | async-start | bytes 2359296 | tf_op jit(solution)/shard_map/all_to_all | solution.py:861
  222.7 8.0 %collective-permute-done.5.refs_2_ = bf16[832,256]{1,0:T(8,128)(2,1)S(1)} collective-permute-done((bf16[832,256]{1,0:T(8,128)(2,1)S(1)}, bf16[832,256]{1,0:T(8,128)(2,1)S(1)}, u32[]{:S(2)}, u32[]{:S(2)}) %collective-permute-start.5) | collective-permute-done | bytes 426016 | tf_op jit(solution)/shard_map/ppermute | solution.py:931
  233.9 7.4 %all-to-all-start.5 = ((bf16[32,64,384]{2,1,0:T(8,128)(2,1)}), bf16[32,64,384]{2,1,0:T(8,128)(2,1)S(1)}, u32[]{:S(2)}, u32[]{:S(2)}) async-start(bf16[32,64,384]{2,1,0:T(8,128)(2,1)} %bitcast.20), calls=%async_computation.5 | async-start | bytes 3145728 | tf_op jit(solution)/shard_map/all_to_all | solution.py:861
  241.4 19.0 %collective-permute-done.6.refs_2_ = bf16[1344,256]{1,0:T(8,128)(2,1)S(1)} collective-permute-done((bf16[1344,256]{1,0:T(8,128)(2,1)}, bf16[1344,256]{1,0:T(8,128)(2,1)S(1)}, u32[]{:S(2)}, u32[]{:S(2)}) %collective-permute-start.6) | collective-permute-done | bytes 688160 | tf_op jit(solution)/shard_map/ppermute | solution.py:933
  264.1 3.9 %analysis_back_0.1.refs_1_ = bf16[32,4,16,384]{3,2,1,0:T(8,128)(2,1)} custom-call(bf16[6,512,384]{2,1,0:T(8,128)(2,1)S(1)} %copy-done.23, bf16[2496,128]{1,0:T(8,128)(2,1)S(1)} %copy-done.7, bf16[1344,256]{1,0:T(8,128)(2,1)S(1)} %collective-permute-done.6.refs_2_, f32[384,384]{1,0:T(8,128)S(1)} %copy-done.12, bf16[384,384]{1,0:T(8,128)(2,1)S(1)} %copy-done.17, ...), custom_call_target="tpu_custom_call" | custom-call | flops 1 | bytes 1 | tf_op jit(solution)/shard_map/analysis_back_0/pallas_call | solution.py:81
  269.3 7.5 %all-to-all-start.6 = ((bf16[32,64,384]{2,1,0:T(8,128)(2,1)}), bf16[32,64,384]{2,1,0:T(8,128)(2,1)}, u32[]{:S(2)}, u32[]{:S(2)}) async-start(bf16[32,64,384]{2,1,0:T(8,128)(2,1)} %bitcast.22), calls=%async_computation.6 | async-start | bytes 3145728 | tf_op jit(solution)/shard_map/all_to_all | solution.py:861
  282.7 18.1 %all-to-all-done.6 = bf16[32,64,384]{2,1,0:T(8,128)(2,1)} async-done(((bf16[32,64,384]{2,1,0:T(8,128)(2,1)}), bf16[32,64,384]{2,1,0:T(8,128)(2,1)}, u32[]{:S(2)}, u32[]{:S(2)}) %all-to-all-start.6) | async-done | bytes 1572896 | tf_op jit(solution)/shard_map/all_to_all | solution.py:861
  304.0 4.5 %field_stage.5 = bf16[12,192,768]{2,1,0:T(8,128)(2,1)} custom-call(bf16[32,4,16,384]{3,2,1,0:T(8,128)(2,1)} %bitcast.23.refs_0_, bf16[256,768]{1,0:T(8,128)(2,1)S(1)} %copy-done.31, bf16[12,192,768]{2,1,0:T(8,128)(2,1)S(1)} %field_stage.4.refs_2_), custom_call_target="tpu_custom_call" | custom-call | flops 1 | bytes 1 | tf_op jit(solution)/shard_map/field_stage/pallas_call | solution.py:81
  (103 shorter events, 51.9 us)
Async XLA Ops:
  9.3 54.7 %all-to-all-start = ((bf16[32,144,384]{2,1,0:T(8,128)(2,1)}), bf16[32,144,384]{2,1,0:T(8,128)(2,1)}, u32[]{:S(2)}, u32[]{:S(2)}) async-start(bf16[32,144,384]{2,1,0:T(8,128)(2,1)} %bitcast.43), calls=%async_computation | async-start | bytes 7077888 | tf_op jit(solution)/shard_map/all_to_all | solution.py:861
  17.7 94.6 %collective-permute-start = (bf16[12,192,768]{2,1,0:T(8,128)(2,1)}, bf16[12,192,768]{2,1,0:T(8,128)(2,1)S(1)}, u32[]{:S(2)}, u32[]{:S(2)}) collective-permute-start(bf16[12,192,768]{2,1,0:T(8,128)(2,1)} %bitcast.44), channel_id=1, source_target_pairs={{0,96},{32,0},{64,32},{96,64},{1,97},{33,1},{65,33},{97,65},{2,98}... | collective-permute-start | bytes 10616840 | tf_op jit(solution)/shard_map/ppermute | solution.py:883
  76.0 51.1 %all-to-all-start.1 = ((bf16[32,144,384]{2,1,0:T(8,128)(2,1)}), bf16[32,144,384]{2,1,0:T(8,128)(2,1)}, u32[]{:S(2)}, u32[]{:S(2)}) async-start(bf16[32,144,384]{2,1,0:T(8,128)(2,1)} %bitcast.49), calls=%async_computation.1 | async-start | bytes 7077888 | tf_op jit(solution)/shard_map/all_to_all | solution.py:861
  80.9 27.7 %collective-permute-start.1 = (f32[192,384]{1,0:T(8,128)}, f32[192,384]{1,0:T(8,128)S(1)}, u32[]{:S(2)}, u32[]{:S(2)}) collective-permute-start(f32[192,384]{1,0:T(8,128)} %bitcast.56), channel_id=1, source_target_pairs={{0,96},{32,0},{64,32},{96,64},{1,97},{33,1},{65,33},{97,65},{2,98}... | collective-permute-start | bytes 884744 | tf_op jit(solution)/shard_map/ppermute | solution.py:892
  81.8 26.8 %collective-permute-start.2 = (bf16[2,192,192]{2,1,0:T(8,128)(2,1)}, bf16[2,192,192]{2,1,0:T(8,128)(2,1)S(1)}, u32[]{:S(2)}, u32[]{:S(2)}) collective-permute-start(bf16[2,192,192]{2,1,0:T(8,128)(2,1)} %bitcast.58), channel_id=1, source_target_pairs={{0,96},{32,0},{64,32},{96,64},{1,97},{33,1},{65,33},{97,65},{2,98}... | collective-permute-start | bytes 442376 | tf_op jit(solution)/shard_map/ppermute | solution.py:893
  112.3 14.7 %copy-start.2 = (bf16[12,192,768]{2,1,0:T(8,128)(2,1)}, bf16[12,192,768]{2,1,0:T(8,128)(2,1)S(1)}, u32[]{:S(2)}) copy-start(bf16[12,192,768]{2,1,0:T(8,128)(2,1)S(1)} %collective-permute-done.refs_6_.refs_2_) | copy-start | bytes 10616836
  137.3 23.0 %all-to-all-start.2 = ((bf16[32,144,128]{2,1,0:T(8,128)(2,1)}), bf16[32,144,128]{2,1,0:T(8,128)(2,1)S(1)}, u32[]{:S(2)}, u32[]{:S(2)}) async-start(bf16[32,144,128]{2,1,0:T(8,128)(2,1)} %bitcast.48), calls=%async_computation.2 | async-start | bytes 2359296 | tf_op jit(solution)/shard_map/all_to_all | solution.py:861
  160.3 38.6 %all-to-all-start.3 = ((bf16[32,144,256]{2,1,0:T(8,128)(2,1)}), bf16[32,144,256]{2,1,0:T(8,128)(2,1)S(1)}, u32[]{:S(2)}, u32[]{:S(2)}) async-start(bf16[32,144,256]{2,1,0:T(8,128)(2,1)} %bitcast.52), calls=%async_computation.3 | async-start | bytes 4718592 | tf_op jit(solution)/shard_map/all_to_all | solution.py:861
  171.9 17.8 %collective-permute-start.3 = (bf16[2496,128]{1,0:T(8,128)(2,1)S(1)}, bf16[2496,128]{1,0:T(8,128)(2,1)S(1)}, u32[]{:S(2)}, u32[]{:S(2)}) collective-permute-start(bf16[2496,128]{1,0:T(8,128)(2,1)S(1)} %spectral_backward_0_1_2.1.refs_1_), channel_id=1, source_target_pairs={{0,96},{32,0},{64,32},{96,64},{1,97},{33,1},{65,33},{97,65},{2,98}... | collective-permute-start | bytes 1916936 | tf_op jit(solution)/shard_map/ppermute | solution.py:923
  189.8 17.4 %copy-start.6 = (bf16[2496,128]{1,0:T(8,128)(2,1)}, bf16[2496,128]{1,0:T(8,128)(2,1)S(1)}, u32[]{:S(2)}) copy-start(bf16[2496,128]{1,0:T(8,128)(2,1)S(1)} %collective-permute-done.3.refs_2_.refs_1_) | copy-start | bytes 1916932
  200.0 7.2 %copy-start.10 = (f32[384,384]{1,0:T(8,128)S(1)}, f32[384,384]{1,0:T(8,128)}, u32[]{:S(2)}) copy-start(f32[384,384]{1,0:T(8,128)} %get-tuple-element.41.refs_7_.refs_3_) | copy-start | bytes 1769476
  200.0 7.2 %copy-start.15 = (bf16[384,384]{1,0:T(8,128)(2,1)S(1)}, bf16[384,384]{1,0:T(8,128)(2,1)}, u32[]{:S(2)}) copy-start(bf16[384,384]{1,0:T(8,128)(2,1)} %get-tuple-element.42.refs_8_.refs_4_) | copy-start | bytes 884740
  200.0 7.2 %copy-start.28 = (bf16[6,512,128]{2,1,0:T(8,128)(2,1)S(1)}, bf16[6,512,128]{2,1,0:T(8,128)(2,1)}, u32[]{:S(2)}) copy-start(bf16[6,512,128]{2,1,0:T(8,128)(2,1)} %get-tuple-element.48.refs_0_) | copy-start | bytes 2359300
  200.5 6.6 %collective-permute-start.4 = (bf16[320,256]{1,0:T(8,128)(2,1)S(1)}, bf16[320,256]{1,0:T(8,128)(2,1)S(1)}, u32[]{:S(2)}, u32[]{:S(2)}) collective-permute-start(bf16[320,256]{1,0:T(8,128)(2,1)S(1)} %spectral_backward_2.1.refs_4_), channel_id=1, source_target_pairs={{0,96},{32,0},{64,32},{96,64},{1,97},{33,1},{65,33},{97,65},{2,98}... | collective-permute-start | bytes 491528 | tf_op jit(solution)/shard_map/ppermute | solution.py:925
  209.8 24.1 %all-to-all-start.4 = ((bf16[32,48,384]{2,1,0:T(8,128)(2,1)}), bf16[32,48,384]{2,1,0:T(8,128)(2,1)S(1)}, u32[]{:S(2)}, u32[]{:S(2)}) async-start(bf16[32,48,384]{2,1,0:T(8,128)(2,1)} %bitcast.41), calls=%async_computation.4 | async-start | bytes 2359296 | tf_op jit(solution)/shard_map/all_to_all | solution.py:861
  217.3 13.4 %collective-permute-start.5 = (bf16[832,256]{1,0:T(8,128)(2,1)S(1)}, bf16[832,256]{1,0:T(8,128)(2,1)S(1)}, u32[]{:S(2)}, u32[]{:S(2)}) collective-permute-start(bf16[832,256]{1,0:T(8,128)(2,1)S(1)} %spectral_backward_1.1.refs_2_.refs_3_), channel_id=1, source_target_pairs={{0,96},{32,0},{64,32},{96,64},{1,97},{33,1},{65,33},{97,65},{2,98}... | collective-permute-start | bytes 1277960 | tf_op jit(solution)/shard_map/ppermute | solution.py:931
  219.4 11.3 %copy-start.7 = (bf16[2496,128]{1,0:T(8,128)(2,1)S(1)}, bf16[2496,128]{1,0:T(8,128)(2,1)}, u32[]{:S(2)}) copy-start(bf16[2496,128]{1,0:T(8,128)(2,1)} %copy-done.6) | copy-start | bytes 1916932
  219.4 11.3 %copy-start.11 = (f32[384,384]{1,0:T(8,128)S(1)}, f32[384,384]{1,0:T(8,128)}, u32[]{:S(2)}) copy-start(f32[384,384]{1,0:T(8,128)} %get-tuple-element.41.refs_7_.refs_3_) | copy-start | bytes 1769476
  219.4 11.3 %copy-start.16 = (bf16[384,384]{1,0:T(8,128)(2,1)S(1)}, bf16[384,384]{1,0:T(8,128)(2,1)}, u32[]{:S(2)}) copy-start(bf16[384,384]{1,0:T(8,128)(2,1)} %get-tuple-element.42.refs_8_.refs_4_) | copy-start | bytes 884740
  219.4 11.3 %copy-start.26 = (bf16[6,512,256]{2,1,0:T(8,128)(2,1)S(1)}, bf16[6,512,256]{2,1,0:T(8,128)(2,1)}, u32[]{:S(2)}) copy-start(bf16[6,512,256]{2,1,0:T(8,128)(2,1)} %get-tuple-element.30.refs_0_) | copy-start | bytes 4718596
  233.9 34.1 %all-to-all-start.5 = ((bf16[32,64,384]{2,1,0:T(8,128)(2,1)}), bf16[32,64,384]{2,1,0:T(8,128)(2,1)S(1)}, u32[]{:S(2)}, u32[]{:S(2)}) async-start(bf16[32,64,384]{2,1,0:T(8,128)(2,1)} %bitcast.20), calls=%async_computation.5 | async-start | bytes 3145728 | tf_op jit(solution)/shard_map/all_to_all | solution.py:861
  241.3 19.1 %collective-permute-start.6 = (bf16[1344,256]{1,0:T(8,128)(2,1)}, bf16[1344,256]{1,0:T(8,128)(2,1)S(1)}, u32[]{:S(2)}, u32[]{:S(2)}) collective-permute-start(bf16[1344,256]{1,0:T(8,128)(2,1)} %copy-done.20), channel_id=1, source_target_pairs={{0,96},{32,0},{64,32},{96,64},{1,97},{33,1},{65,33},{97,65},{2,98}... | collective-permute-start | bytes 2064392 | tf_op jit(solution)/shard_map/ppermute | solution.py:933
  269.3 7.5 %copy-start.33 = (bf16[256,768]{1,0:T(8,128)(2,1)S(1)}, bf16[256,768]{1,0:T(8,128)(2,1)}, u32[]{:S(2)}) copy-start(bf16[256,768]{1,0:T(8,128)(2,1)} %constant.37.clone.refs_1_) | copy-start | bytes 1179652
  269.3 31.4 %all-to-all-start.6 = ((bf16[32,64,384]{2,1,0:T(8,128)(2,1)}), bf16[32,64,384]{2,1,0:T(8,128)(2,1)}, u32[]{:S(2)}, u32[]{:S(2)}) async-start(bf16[32,64,384]{2,1,0:T(8,128)(2,1)} %bitcast.22), calls=%async_computation.6 | async-start | bytes 3145728 | tf_op jit(solution)/shard_map/all_to_all | solution.py:861
  (28 other events, 43.2 us)

commit v5 on v4

--- a/solution.py
+++ b/solution.py
@@ -340,12 +340,17 @@
 
 
 def pair_sum(local, table_ref, tiles):
-    total = None
-    for index, (order, tile) in enumerate(PAIRS):
-        if order == local:
-            part = dot(table_ref[index, DEVICES * local :, :], tiles[tile])
-            total = part if total is None else total + part
-    return total
+    pairs = [(index, tile) for index, (order, tile) in enumerate(PAIRS) if order == local]
+    left = [table_ref[index, DEVICES * local :, :] for index, _ in pairs]
+    right = [tiles[tile] for _, tile in pairs]
+    if len(pairs) == 1:
+        return dot(left[0], right[0])
+    return dot(jnp.concatenate(left, axis=1), jnp.concatenate(right, axis=0))
+
+
+def tile_sum(tile, table_ref, first, second):
+    left = jnp.concatenate([table_ref[2 * tile], table_ref[2 * tile + 1]], axis=1)
+    return dot(left, jnp.concatenate([first, second], axis=0))
 
 
 def spectral_kernel(recv_ref, *refs):
@@ -381,9 +386,7 @@
                 product = jnp.concatenate([zeros, product], axis=0)
             mixed.append(product)
         for tile in range(GROUP_TILES):
-            grid = dot(st_buffers[group][2 * tile], mixed[tile]) + dot(
-                st_buffers[group][2 * tile + 1], mixed[tile + 1]
-            )
+            grid = tile_sum(tile, st_buffers[group], mixed[tile], mixed[tile + 1])
             payload[group, :, tile] = grid.astype(BF16).reshape(DEVICES, TILE, 2 * C)
         tiles = pl.ds(GROUP_TILES * group, GROUP_TILES)
         copies = (
@@ -629,7 +632,7 @@
     for tile in range(GROUP_TILES):
         first = coeff_ref[tile * degrees : (tile + 1) * degrees, :]
         second = coeff_ref[(tile + 1) * degrees : (tile + 2) * degrees, :]
-        out = dot(at_ref[2 * tile], first) + dot(at_ref[2 * tile + 1], second)
+        out = tile_sum(tile, at_ref, first, second)
         out_ref[:, tile] = out.astype(BF16).reshape(DEVICES, TILE, 2 * C)
     if extra:
         out_ref[:, GROUP_TILES] = extra[0][...]
@@ -755,13 +758,13 @@
     )
 
 
-def unpack_kernel(recv_ref, proj_ref, mix_ref, gain_ref, spaced, packed):
+def unpack_totals(recv_ref, proj_ref, mix_ref, gain_ref, spaced, packed):
     grid_scale = 1.0 / math.sqrt(NLAT * NLON)
     mode_scale = 1.0 / math.sqrt(MODES)
     lows, highs = [], []
     for index in range(GROUPS):
         lanes = slice(index * LANES, (index + 1) * LANES)
-        spaced[index] = recv_ref[:, 0, :, lanes].reshape(DEVICES * TILE, LANES).astype(F32)
+        spaced[index] = recv_ref[:, GROUP_TILES, :, lanes].reshape(DEVICES * TILE, LANES).astype(F32)
         for row in range(TILE - 1):
             packed[index, row * DEVICES : (row + 1) * DEVICES, :] = spaced[
                 index, pl.ds(row, DEVICES, stride=TILE), :
@@ -778,38 +781,20 @@
     proj_ref[...] = grid_scale * proj.T
 
 
-def unpack_totals(recv, after=()):
-    shapes = ((C, C), (2, C, C), (C, MODES))
-    return call(
-        unpack_kernel,
-        (recv,),
-        [pl.BlockSpec((DEVICES, 1, TILE, 2 * C), lambda b: (0, GROUP_TILES, 0, 0))],
-        [whole(shape) for shape in shapes],
-        [jax.ShapeDtypeStruct(shape, F32) for shape in shapes],
-        (1,),
-        after,
-        scratch_shapes=[
-            pltpu.VMEM((GROUPS, TILE * DEVICES, LANES), F32),
-            pltpu.VMEM((GROUPS, 15 * DEVICES, LANES), F32),
-        ],
-        vmem=12,
-        name="unpack_totals",
-    )
-
-
-def field_kernel(*refs):
-    recv_refs, (table_ref, base_ref, out_ref, scratch) = refs[:-4], refs[-4:]
+def field_kernel(recv_ref, table_ref, base_ref, out_ref, *refs):
+    totals, (scratch, *unpacking) = refs[:3] if len(refs) > 1 else (), refs[3:] or refs
     step = pl.program_id(0)
     orders = DEVICES * GROUP_ORDERS
-    rows = orders * LAT_LOCAL // len(recv_refs)
+    rows = orders * LAT_LOCAL
 
     @pl.when(step == 0)
     def _():
         for index in range(GROUPS):
             lanes = slice(index * LANES, (index + 1) * LANES)
-            for place, recv_ref in enumerate(recv_refs):
-                values = recv_ref[:, :, :, lanes].astype(F32)
-                scratch[index, place * rows : (place + 1) * rows] = values.reshape(rows, LANES)
+            values = recv_ref[:, :GROUP_TILES, :, lanes].astype(F32)
+            scratch[index] = values.reshape(rows, LANES)
+        if totals:
+            unpack_totals(recv_ref, *totals, *unpacking)
 
     lefts = []
     for inner in range(4):
@@ -830,27 +815,36 @@
         out_ref[inner] = total.astype(out_ref.dtype)
 
 
-def field_stage(recv, table, base, after=()):
+def field_stage(recv, table, base, unpacked=False, after=()):
     rows = DEVICES * GROUP_ORDERS * LAT_LOCAL
     block = pl.BlockSpec((4, C, NLON), lambda b: (b, 0, 0))
+    tiles = GROUP_TILES + int(unpacked)
+    totals = ((C, C), (2, C, C), (C, MODES)) if unpacked else ()
+    scratch_shapes = [pltpu.VMEM((GROUPS, rows, LANES), F32)]
+    if unpacked:
+        scratch_shapes += [
+            pltpu.VMEM((GROUPS, TILE * DEVICES, LANES), F32),
+            pltpu.VMEM((GROUPS, 15 * DEVICES, LANES), F32),
+        ]
     return call(
         field_kernel,
-        (*recv, table, base),
+        (recv, table, base),
         [
             pl.BlockSpec(
-                (DEVICES // len(recv), GROUP_TILES, TILE, 2 * C),
+                (DEVICES, tiles, TILE, 2 * C),
                 lambda b: (0, 0, 0, 0),
                 pipeline_mode=pl.Buffered(1),
-            )
-        ]
-        * len(recv)
-        + [whole(table.shape), block],
-        block,
-        jax.ShapeDtypeStruct((LAT_LOCAL, C, NLON), BF16),
+            ),
+            whole(table.shape),
+            block,
+        ],
+        [block] + [whole(shape) for shape in totals],
+        [jax.ShapeDtypeStruct((LAT_LOCAL, C, NLON), BF16)]
+        + [jax.ShapeDtypeStruct(shape, F32) for shape in totals],
         (LAT_LOCAL // 4,),
         after,
-        scratch_shapes=[pltpu.VMEM((GROUPS, rows, LANES), F32)],
-        vmem=20,
+        scratch_shapes=scratch_shapes,
+        vmem=24 if unpacked else 20,
         name="field_stage",
     )
 
@@ -927,13 +921,25 @@
         2, behind[2][1], moved_small, moved_2, gain_next, mix_next, GROUP_TILES
     )
     recv_2 = exchange(out_2)
-    mixed_1 = spectral_backward((1,), large, [behind[1][0]], (out_2,))
-    moved_1 = lax.ppermute(mixed_1, "section", shift)
-    mixed_0 = spectral_backward((0,), large, [behind[0][0]], (mixed_1,))
+    mixed_0 = spectral_backward((0,), large, [behind[0][0]], (out_2,))
     moved_0 = lax.ppermute(mixed_0, "section", shift)
+    mixed_1 = spectral_backward((1,), large, [behind[1][0]], (mixed_0,))
+    moved_1 = lax.ppermute(hold(mixed_1, (moved_0,)), "section", shift)
     partial_grads = weight_grads(
         scaled, mixed_small, (mixed_0, mixed_1, mixed_2), mix, gain, proj_small, proj_large
     )
+    out_0 = analysis_back(
+        0,
+        behind[0][1],
+        moved_small,
+        moved_0,
+        gain_next,
+        mix_next,
+        GROUP_TILES + 1,
+        (partial_grads,),
+    )
+    out_0 = hold(out_0, (recv_2,))
+    recv_0 = exchange(out_0)
     out_1 = analysis_back(
         1,
         behind[1][1],
@@ -942,26 +948,13 @@
         gain_next,
         mix_next,
         GROUP_TILES + 1,
-        (partial_grads,),
-    )
-    out_1 = hold(out_1, (recv_2,))
+        after=(recv_2,),
+    )
+    out_1 = attach_totals(recv_0, out_1)
     recv_1 = exchange(out_1)
-    out_0 = analysis_back(
-        0,
-        behind[0][1],
-        moved_small,
-        moved_0,
-        gain_next,
-        mix_next,
-        GROUP_TILES + 1,
-        after=(recv_2,),
-    )
-    out_0 = attach_totals(recv_1, out_0)
-    recv_0 = exchange(out_0)
-    base = field_stage((recv_2,), forward[2], upstream_next, (out_0,))
-    base = field_stage((recv_1,), forward[1], base)
-    grad_w2, grad_mix, grad_gain = unpack_totals(recv_0)
-    received = field_stage((recv_0,), forward[0], base)
+    (base,) = field_stage(recv_2, forward[2], upstream_next, after=(out_1,))
+    (base,) = field_stage(recv_0, forward[0], base)
+    received, grad_w2, grad_mix, grad_gain = field_stage(recv_1, forward[1], base, True)
     return (
         received[None],
         grad_w2[None],

time: 313 us -> 310 us (level)
    ppermute x1, waiting for transfers between devices: 7.98 us -> 13.4 us  [shards(): moved_1 = lax.ppermute(hold(mixed_1, (moved_0,)), 'section', shift)]
    ppermute x1, waiting for transfers between devices: 19 us -> 13.7 us  [shards(): moved_0 = lax.ppermute(mixed_0, 'section', shift)]
    unnamed x76 -> x84, local copies, waits for them, and re-layouts: 19.8 us -> 22.7 us
  transfers between devices with their start and end apart: 14 -> 14, of which waited for: 10 -> 11; matrix products, arithmetic and copies ran while one was open for 2% -> 2% of each run, Pallas kernels for 24% -> 24%
where the time goes in v5:
time: 310 us; the launch traced here: 309 us
  waiting for transfers between devices  132 us (43%)
  Pallas kernels  102 us (33%)
  starting transfers between devices  44 us (14%)
  local copies, waits for them, and re-layouts  30.2 us (10%)
    pallas_call x21, Pallas kernels, call(): pl.pallas_call(body, grid=grid, in_specs=list(in_specs) + [pl.BlockSpec(m...  102 us
    all_to_all x7, waiting for transfers between devices, exchange(): moved = lax.all_to_all(flat, 'lat', split_axis=0, concat_axis=0, tiled=True)  57.2 us
    all_to_all x7, starting transfers between devices, exchange(): moved = lax.all_to_all(flat, 'lat', split_axis=0, concat_axis=0, tiled=True)  39.3 us
    ppermute x1, waiting for transfers between devices, shards(): lax.ppermute(mix_weight[0], 'section', shift)  26.6 us
    unnamed x84, local copies, waits for them, and re-layouts  22.7 us
    ppermute x1, waiting for transfers between devices, shards(): moved_small = lax.ppermute(mixed_small, 'section', shift)  16.1 us
    ppermute x1, waiting for transfers between devices, shards(): moved_0 = lax.ppermute(mixed_0, 'section', shift)  13.7 us
    ppermute x1, waiting for transfers between devices, shards(): moved_1 = lax.ppermute(hold(mixed_1, (moved_0,)), 'section', shift)  13.4 us
  transfers between devices with their start and end apart: 14, of which 11 were waited for; matrix products, arithmetic and copies ran while one was open for 2% of the time, Pallas kernels for 24%

profile of v5, /device:TPU:6, one launch (start us, length us, event | category | flops | bytes accessed | tf_op | source)
XLA Modules:
  0.0 308.9 jit_solution(8132065357034460335)
XLA Ops:
  0.6 8.6 %spectrum_rows.1.refs_5_.refs_3_ = bf16[4608,384]{1,0:T(8,128)(2,1)} custom-call(bf16[12,192,768]{2,1,0:T(8,128)(2,1)} %bitcast.50, bf16[768,768]{1,0:T(8,128)(2,1)} %constant.34.clone.refs_1_), custom_call_target="tpu_custom_call" | custom-call | flops 1 | bytes 1 | tf_op jit(solution)/shard_map/spectrum_rows/pallas_call | solution.py:81
  9.3 8.4 %all-to-all-start = ((bf16[32,144,384]{2,1,0:T(8,128)(2,1)}), bf16[32,144,384]{2,1,0:T(8,128)(2,1)}, u32[]{:S(2)}, u32[]{:S(2)}) async-start(bf16[32,144,384]{2,1,0:T(8,128)(2,1)} %bitcast.43), calls=%async_computation | async-start | bytes 7077888 | tf_op jit(solution)/shard_map/all_to_all | solution.py:855
  22.5 23.6 %legendre_tables.1 = (bf16[6,384,512]{2,1,0:T(8,128)(2,1)}, bf16[6,512,384]{2,1,0:T(8,128)(2,1)}, bf16[6,384,512]{2,1,0:T(8,128)(2,1)}, bf16[6,512,384]{2,1,0:T(...) custom-call(f32[16,128]{1,0:T(8,128)} %get-tuple-element.59.refs_0_,, ...), custom_call_target="tpu_custom_call" | custom-call | flops 1 | bytes 1 | tf_op jit(solution)/shard_map/legendre_tables/pallas_call | solution.py:81
  46.1 6.3 %copy.23.refs_9_.refs_2_ = bf16[12,768,192]{2,1,0:T(8,128)(2,1)} copy(bf16[12,768,192]{1,2,0:T(8,128)(2,1)} %bitcast.45) | data formatting | bytes 7077888 | tf_op jit(solution)/shard_map/transpose | solution.py:878
  52.4 11.5 %all-to-all-done = bf16[32,144,384]{2,1,0:T(8,128)(2,1)} async-done(((bf16[32,144,384]{2,1,0:T(8,128)(2,1)}), bf16[32,144,384]{2,1,0:T(8,128)(2,1)}, u32[]{:S(2)}, u32[]{:S(2)}) %all-to-all-start) | async-done | bytes 3538976 | tf_op jit(solution)/shard_map/all_to_all | solution.py:855
  63.9 11.7 %spectral_forward.1 = (bf16[2496,384]{1,0:T(8,128)(2,1)}, bf16[32,9,16,384]{3,2,1,0:T(8,128)(2,1)}) custom-call(bf16[32,9,16,384]{3,2,1,0:T(8,128)(2,1)} %bitcast.4.refs_0_, bf16[6,384,512]{2,1,0:T(8,128)(2,1)} %get-tuple-element.32.refs_1_, bf16[6,256,512]{2,1,0:T(8,128)(2,1)} %get-tuple-element.33.refs_2_, bf16[6,128,512]{2,1,0:T(8,128)(2,1)} %get-tuple-element.34.refs_3_, ...), custom_call_target="tpu_custom_call" | custom-call | flops 1 | bytes 1 | tf_op jit(solution)/shard_map/spectral_forward/pallas_call | solution.py:81
  75.6 4.9 %all-to-all-start.1 = ((bf16[32,144,384]{2,1,0:T(8,128)(2,1)}), bf16[32,144,384]{2,1,0:T(8,128)(2,1)}, u32[]{:S(2)}, u32[]{:S(2)}) async-start(bf16[32,144,384]{2,1,0:T(8,128)(2,1)} %bitcast.49), calls=%async_computation.1 | async-start | bytes 7077888 | tf_op jit(solution)/shard_map/all_to_all | solution.py:855
  82.0 26.6 %collective-permute-done.2.refs_1_ = bf16[2,192,192]{2,1,0:T(8,128)(2,1)S(1)} collective-permute-done((bf16[2,192,192]{2,1,0:T(8,128)(2,1)}, bf16[2,192,192]{2,1,0:T(8,128)(2,1)S(1)}, u32[]{:S(2)}, u32[]{:S(2)}) %collective-permute-start.2) | collective-permute-done | bytes 147488 | tf_op jit(solution)/shard_map/ppermute | solution.py:887
  112.4 14.3 %all-to-all-done.1 = bf16[32,144,384]{2,1,0:T(8,128)(2,1)} async-done(((bf16[32,144,384]{2,1,0:T(8,128)(2,1)}), bf16[32,144,384]{2,1,0:T(8,128)(2,1)}, u32[]{:S(2)}, u32[]{:S(2)}) %all-to-all-start.1) | async-done | bytes 3538976 | tf_op jit(solution)/shard_map/all_to_all | solution.py:855
  126.7 10.2 %grid_stage_1.1 = (bf16[4608,128]{1,0:T(8,128)(2,1)}, f32[192,128]{1,0:T(8,128)}) custom-call(bf16[4608,384]{1,0:T(8,128)(2,1)} %bitcast.12.refs_0_, bf16[12,192,768]{2,1,0:T(8,128)(2,1)} %bitcast.46, bf16[12,768,192]{2,1,0:T(8,128)(2,1)} %copy.23.refs_9_.refs_2_, bf16[192,384]{1,0:T(8,128)(2,1)} %get-tuple-element.40.refs_10_.refs_3_, ...), custom_call_target="tpu_custom_call" | custom-call | flops 1 | bytes 1 | tf_op jit(solution)/shard_map/grid_stage_1/pallas_call | solution.py:81
  136.9 3.9 %all-to-all-start.2 = ((bf16[32,144,128]{2,1,0:T(8,128)(2,1)}), bf16[32,144,128]{2,1,0:T(8,128)(2,1)S(1)}, u32[]{:S(2)}, u32[]{:S(2)}) async-start(bf16[32,144,128]{2,1,0:T(8,128)(2,1)} %bitcast.48), calls=%async_computation.2 | async-start | bytes 2359296 | tf_op jit(solution)/shard_map/all_to_all | solution.py:855
  140.9 17.1 %grid_stage_2.1 = (bf16[4608,256]{1,0:T(8,128)(2,1)}, f32[192,256]{1,0:T(8,128)}) custom-call(bf16[4608,384]{1,0:T(8,128)(2,1)} %bitcast.12.refs_0_, bf16[12,192,768]{2,1,0:T(8,128)(2,1)} %bitcast.47, bf16[12,768,192]{2,1,0:T(8,128)(2,1)} %copy.23.refs_9_.refs_2_, bf16[192,384]{1,0:T(8,128)(2,1)} %get-tuple-element.40.refs_10_.refs_3_, ...), custom_call_target="tpu_custom_call" | custom-call | flops 1 | bytes 1 | tf_op jit(solution)/shard_map/grid_stage_2/pallas_call | solution.py:81
  159.9 5.5 %all-to-all-start.3 = ((bf16[32,144,256]{2,1,0:T(8,128)(2,1)}), bf16[32,144,256]{2,1,0:T(8,128)(2,1)S(1)}, u32[]{:S(2)}, u32[]{:S(2)}) async-start(bf16[32,144,256]{2,1,0:T(8,128)(2,1)} %bitcast.51), calls=%async_computation.3 | async-start | bytes 4718592 | tf_op jit(solution)/shard_map/all_to_all | solution.py:855
  173.3 16.1 %collective-permute-done.3.refs_2_.refs_1_ = bf16[2496,128]{1,0:T(8,128)(2,1)S(1)} collective-permute-done((bf16[2496,128]{1,0:T(8,128)(2,1)S(1)}, bf16[2496,128]{1,0:T(8,128)(2,1)S(1)}, u32[]{:S(2)}, u32[]{:S(2)}) %collective-permute-start.3) | collective-permute-done | bytes 639008 | tf_op jit(solution)/shard_map/ppermute | solution.py:917
  189.4 9.1 %all-to-all-done.3 = bf16[32,144,256]{2,1,0:T(8,128)(2,1)S(1)} async-done(((bf16[32,144,256]{2,1,0:T(8,128)(2,1)}), bf16[32,144,256]{2,1,0:T(8,128)(2,1)S(1)}, u32[]{:S(2)}, u32[]{:S(2)}) %all-to-all-start.3) | async-done | bytes 2359328 | tf_op jit(solution)/shard_map/all_to_all | solution.py:855
  201.7 5.0 %collective-permute-done.4.refs_2_ = bf16[320,256]{1,0:T(8,128)(2,1)S(1)} collective-permute-done((bf16[320,256]{1,0:T(8,128)(2,1)S(1)}, bf16[320,256]{1,0:T(8,128)(2,1)S(1)}, u32[]{:S(2)}, u32[]{:S(2)}) %collective-permute-start.4) | collective-permute-done | bytes 163872 | tf_op jit(solution)/shard_map/ppermute | solution.py:919
  209.1 3.9 %all-to-all-start.4 = ((bf16[32,48,384]{2,1,0:T(8,128)(2,1)}), bf16[32,48,384]{2,1,0:T(8,128)(2,1)S(1)}, u32[]{:S(2)}, u32[]{:S(2)}) async-start(bf16[32,48,384]{2,1,0:T(8,128)(2,1)} %bitcast.41), calls=%async_computation.4 | async-start | bytes 2359296 | tf_op jit(solution)/shard_map/all_to_all | solution.py:855
  222.5 13.7 %collective-permute-done.5.refs_2_.refs_1_ = bf16[1344,256]{1,0:T(8,128)(2,1)S(1)} collective-permute-done((bf16[1344,256]{1,0:T(8,128)(2,1)S(1)}, bf16[1344,256]{1,0:T(8,128)(2,1)S(1)}, u32[]{:S(2)}, u32[]{:S(2)}) %collective-permute-start.5) | collective-permute-done | bytes 688160 | tf_op jit(solution)/shard_map/ppermute | solution.py:925
  236.2 3.8 %analysis_back_0.1.refs_0_ = bf16[32,4,16,384]{3,2,1,0:T(8,128)(2,1)} custom-call(bf16[6,512,384]{2,1,0:T(8,128)(2,1)S(1)} %copy-done.27, bf16[2496,128]{1,0:T(8,128)(2,1)S(1)} %copy-done.7, bf16[1344,256]{1,0:T(8,128)(2,1)S(1)} %collective-permute-done.5.refs_2_.refs_1_, f32[384,384]{1,0:T(8,128)S(1)} %copy-done.11, bf16[384,384]{1,0:T(8,128)(2,1)S(1)} %copy-done.16, ...), custom_call_target="tpu_custom_call" | custom-call | flops 1 | bytes 1 | tf_op jit(solution)/shard_map/analysis_back_0/pallas_call | solution.py:81
  240.8 7.4 %all-to-all-start.5 = ((bf16[32,64,384]{2,1,0:T(8,128)(2,1)}), bf16[32,64,384]{2,1,0:T(8,128)(2,1)S(1)}, u32[]{:S(2)}, u32[]{:S(2)}) async-start(bf16[32,64,384]{2,1,0:T(8,128)(2,1)} %bitcast.20), calls=%async_computation.5 | async-start | bytes 3145728 | tf_op jit(solution)/shard_map/all_to_all | solution.py:855
  251.1 13.4 %collective-permute-done.6.refs_2_ = bf16[832,256]{1,0:T(8,128)(2,1)S(1)} collective-permute-done((bf16[832,256]{1,0:T(8,128)(2,1)}, bf16[832,256]{1,0:T(8,128)(2,1)S(1)}, u32[]{:S(2)}, u32[]{:S(2)}) %collective-permute-start.6) | collective-permute-done | bytes 426016 | tf_op jit(solution)/shard_map/ppermute | solution.py:927
  273.4 5.3 %all-to-all-start.6 = ((bf16[32,64,384]{2,1,0:T(8,128)(2,1)}), bf16[32,64,384]{2,1,0:T(8,128)(2,1)}, u32[]{:S(2)}, u32[]{:S(2)}) async-start(bf16[32,64,384]{2,1,0:T(8,128)(2,1)} %bitcast.22), calls=%async_computation.6 | async-start | bytes 3145728 | tf_op jit(solution)/shard_map/all_to_all | solution.py:855
  284.6 18.1 %all-to-all-done.6 = bf16[32,64,384]{2,1,0:T(8,128)(2,1)} async-done(((bf16[32,64,384]{2,1,0:T(8,128)(2,1)}), bf16[32,64,384]{2,1,0:T(8,128)(2,1)}, u32[]{:S(2)}, u32[]{:S(2)}) %all-to-all-start.6) | async-done | bytes 1572896 | tf_op jit(solution)/shard_map/all_to_all | solution.py:855
  303.7 5.2 %field_stage.5 = (bf16[12,192,768]{2,1,0:T(8,128)(2,1)}, f32[192,192]{1,0:T(8,128)}, f32[2,192,192]{2,1,0:T(8,128)}, f32[192,384]{1,0:T(8,128)}) custom-call(bf16[32,4,16,384]{3,2,1,0:T(8,128)(2,1)} %bitcast.23.refs_0_, bf16[256,768]{1,0:T(8,128)(2,1)S(1)} %copy-done.37, bf16[12,192,768]{2,1,0:T(8,128)(2,1)S(1)} %field_stage.4.refs_2_), custom_call_target="tpu_custom_call" | custom-call | flops 1 | bytes 1 | tf_op jit(solution)/shard_map/field_stage/pallas_call | solution.py:81
  (111 shorter events, 54.1 us)
Async XLA Ops:
  9.3 54.7 %all-to-all-start = ((bf16[32,144,384]{2,1,0:T(8,128)(2,1)}), bf16[32,144,384]{2,1,0:T(8,128)(2,1)}, u32[]{:S(2)}, u32[]{:S(2)}) async-start(bf16[32,144,384]{2,1,0:T(8,128)(2,1)} %bitcast.43), calls=%async_computation | async-start | bytes 7077888 | tf_op jit(solution)/shard_map/all_to_all | solution.py:855
  17.7 94.7 %collective-permute-start = (bf16[12,192,768]{2,1,0:T(8,128)(2,1)}, bf16[12,192,768]{2,1,0:T(8,128)(2,1)S(1)}, u32[]{:S(2)}, u32[]{:S(2)}) collective-permute-start(bf16[12,192,768]{2,1,0:T(8,128)(2,1)} %bitcast.44), channel_id=1, source_target_pairs={{0,96},{32,0},{64,32},{96,64},{1,97},{33,1},{65,33},{97,65},{2,98}... | collective-permute-start | bytes 10616840 | tf_op jit(solution)/shard_map/ppermute | solution.py:877
  75.6 51.1 %all-to-all-start.1 = ((bf16[32,144,384]{2,1,0:T(8,128)(2,1)}), bf16[32,144,384]{2,1,0:T(8,128)(2,1)}, u32[]{:S(2)}, u32[]{:S(2)}) async-start(bf16[32,144,384]{2,1,0:T(8,128)(2,1)} %bitcast.49), calls=%async_computation.1 | async-start | bytes 7077888 | tf_op jit(solution)/shard_map/all_to_all | solution.py:855
  80.5 28.1 %collective-permute-start.1 = (f32[192,384]{1,0:T(8,128)}, f32[192,384]{1,0:T(8,128)S(1)}, u32[]{:S(2)}, u32[]{:S(2)}) collective-permute-start(f32[192,384]{1,0:T(8,128)} %bitcast.55), channel_id=1, source_target_pairs={{0,96},{32,0},{64,32},{96,64},{1,97},{33,1},{65,33},{97,65},{2,98}... | collective-permute-start | bytes 884744 | tf_op jit(solution)/shard_map/ppermute | solution.py:886
  81.4 27.2 %collective-permute-start.2 = (bf16[2,192,192]{2,1,0:T(8,128)(2,1)}, bf16[2,192,192]{2,1,0:T(8,128)(2,1)S(1)}, u32[]{:S(2)}, u32[]{:S(2)}) collective-permute-start(bf16[2,192,192]{2,1,0:T(8,128)(2,1)} %bitcast.57), channel_id=1, source_target_pairs={{0,96},{32,0},{64,32},{96,64},{1,97},{33,1},{65,33},{97,65},{2,98}... | collective-permute-start | bytes 442376 | tf_op jit(solution)/shard_map/ppermute | solution.py:887
  112.4 14.3 %copy-start.2 = (bf16[12,192,768]{2,1,0:T(8,128)(2,1)}, bf16[12,192,768]{2,1,0:T(8,128)(2,1)S(1)}, u32[]{:S(2)}) copy-start(bf16[12,192,768]{2,1,0:T(8,128)(2,1)S(1)} %collective-permute-done.refs_6_.refs_2_) | copy-start | bytes 10616836
  136.9 23.0 %all-to-all-start.2 = ((bf16[32,144,128]{2,1,0:T(8,128)(2,1)}), bf16[32,144,128]{2,1,0:T(8,128)(2,1)S(1)}, u32[]{:S(2)}, u32[]{:S(2)}) async-start(bf16[32,144,128]{2,1,0:T(8,128)(2,1)} %bitcast.48), calls=%async_computation.2 | async-start | bytes 2359296 | tf_op jit(solution)/shard_map/all_to_all | solution.py:855
  159.9 38.6 %all-to-all-start.3 = ((bf16[32,144,256]{2,1,0:T(8,128)(2,1)}), bf16[32,144,256]{2,1,0:T(8,128)(2,1)S(1)}, u32[]{:S(2)}, u32[]{:S(2)}) async-start(bf16[32,144,256]{2,1,0:T(8,128)(2,1)} %bitcast.51), calls=%async_computation.3 | async-start | bytes 4718592 | tf_op jit(solution)/shard_map/all_to_all | solution.py:855
  171.6 17.8 %collective-permute-start.3 = (bf16[2496,128]{1,0:T(8,128)(2,1)S(1)}, bf16[2496,128]{1,0:T(8,128)(2,1)S(1)}, u32[]{:S(2)}, u32[]{:S(2)}) collective-permute-start(bf16[2496,128]{1,0:T(8,128)(2,1)S(1)} %spectral_backward_0_1_2.1.refs_1_), channel_id=1, source_target_pairs={{0,96},{32,0},{64,32},{96,64},{1,97},{33,1},{65,33},{97,65},{2,98}... | collective-permute-start | bytes 1916936 | tf_op jit(solution)/shard_map/ppermute | solution.py:917
  189.4 17.4 %copy-start.6 = (bf16[2496,128]{1,0:T(8,128)(2,1)}, bf16[2496,128]{1,0:T(8,128)(2,1)S(1)}, u32[]{:S(2)}) copy-start(bf16[2496,128]{1,0:T(8,128)(2,1)S(1)} %collective-permute-done.3.refs_2_.refs_1_) | copy-start | bytes 1916932
  199.6 7.1 %copy-start.10 = (f32[384,384]{1,0:T(8,128)S(1)}, f32[384,384]{1,0:T(8,128)}, u32[]{:S(2)}) copy-start(f32[384,384]{1,0:T(8,128)} %get-tuple-element.42.refs_7_.refs_3_) | copy-start | bytes 1769476
  199.6 7.1 %copy-start.15 = (bf16[384,384]{1,0:T(8,128)(2,1)S(1)}, bf16[384,384]{1,0:T(8,128)(2,1)}, u32[]{:S(2)}) copy-start(bf16[384,384]{1,0:T(8,128)(2,1)} %get-tuple-element.43.refs_8_.refs_4_) | copy-start | bytes 884740
  199.6 7.2 %copy-start.32 = (bf16[6,512,128]{2,1,0:T(8,128)(2,1)S(1)}, bf16[6,512,128]{2,1,0:T(8,128)(2,1)}, u32[]{:S(2)}) copy-start(bf16[6,512,128]{2,1,0:T(8,128)(2,1)} %get-tuple-element.49.refs_0_) | copy-start | bytes 2359300
  200.2 6.6 %collective-permute-start.4 = (bf16[320,256]{1,0:T(8,128)(2,1)S(1)}, bf16[320,256]{1,0:T(8,128)(2,1)S(1)}, u32[]{:S(2)}, u32[]{:S(2)}) collective-permute-start(bf16[320,256]{1,0:T(8,128)(2,1)S(1)} %spectral_backward_2.1.refs_4_), channel_id=1, source_target_pairs={{0,96},{32,0},{64,32},{96,64},{1,97},{33,1},{65,33},{97,65},{2,98}... | collective-permute-start | bytes 491528 | tf_op jit(solution)/shard_map/ppermute | solution.py:919
  209.1 31.7 %all-to-all-start.4 = ((bf16[32,48,384]{2,1,0:T(8,128)(2,1)}), bf16[32,48,384]{2,1,0:T(8,128)(2,1)S(1)}, u32[]{:S(2)}, u32[]{:S(2)}) async-start(bf16[32,48,384]{2,1,0:T(8,128)(2,1)} %bitcast.41), calls=%async_computation.4 | async-start | bytes 2359296 | tf_op jit(solution)/shard_map/all_to_all | solution.py:855
  217.1 19.0 %collective-permute-start.5 = (bf16[1344,256]{1,0:T(8,128)(2,1)S(1)}, bf16[1344,256]{1,0:T(8,128)(2,1)S(1)}, u32[]{:S(2)}, u32[]{:S(2)}) collective-permute-start(bf16[1344,256]{1,0:T(8,128)(2,1)S(1)} %spectral_backward_0.1.refs_2_), channel_id=1, source_target_pairs={{0,96},{32,0},{64,32},{96,64},{1,97},{33,1},{65,33},{97,65},{2,98}... | collective-permute-start | bytes 2064392 | tf_op jit(solution)/shard_map/ppermute | solution.py:925
  219.2 17.0 %copy-start.7 = (bf16[2496,128]{1,0:T(8,128)(2,1)S(1)}, bf16[2496,128]{1,0:T(8,128)(2,1)}, u32[]{:S(2)}) copy-start(bf16[2496,128]{1,0:T(8,128)(2,1)} %copy-done.6) | copy-start | bytes 1916932
  219.2 17.0 %copy-start.11 = (f32[384,384]{1,0:T(8,128)S(1)}, f32[384,384]{1,0:T(8,128)}, u32[]{:S(2)}) copy-start(f32[384,384]{1,0:T(8,128)} %get-tuple-element.42.refs_7_.refs_3_) | copy-start | bytes 1769476
  219.2 17.0 %copy-start.16 = (bf16[384,384]{1,0:T(8,128)(2,1)S(1)}, bf16[384,384]{1,0:T(8,128)(2,1)}, u32[]{:S(2)}) copy-start(bf16[384,384]{1,0:T(8,128)(2,1)} %get-tuple-element.43.refs_8_.refs_4_) | copy-start | bytes 884740
  219.2 17.0 %copy-start.27 = (bf16[6,512,384]{2,1,0:T(8,128)(2,1)S(1)}, bf16[6,512,384]{2,1,0:T(8,128)(2,1)}, u32[]{:S(2)}) copy-start(bf16[6,512,384]{2,1,0:T(8,128)(2,1)} %get-tuple-element.31.refs_0_) | copy-start | bytes 7077892
  240.8 31.3 %all-to-all-start.5 = ((bf16[32,64,384]{2,1,0:T(8,128)(2,1)}), bf16[32,64,384]{2,1,0:T(8,128)(2,1)S(1)}, u32[]{:S(2)}, u32[]{:S(2)}) async-start(bf16[32,64,384]{2,1,0:T(8,128)(2,1)} %bitcast.20), calls=%async_computation.5 | async-start | bytes 3145728 | tf_op jit(solution)/shard_map/all_to_all | solution.py:855
  250.3 14.2 %copy-start.12 = (f32[384,384]{1,0:T(8,128)S(1)}, f32[384,384]{1,0:T(8,128)}, u32[]{:S(2)}) copy-start(f32[384,384]{1,0:T(8,128)} %get-tuple-element.42.refs_7_.refs_3_) | copy-start | bytes 1769476
  251.1 13.4 %collective-permute-start.6 = (bf16[832,256]{1,0:T(8,128)(2,1)}, bf16[832,256]{1,0:T(8,128)(2,1)S(1)}, u32[]{:S(2)}, u32[]{:S(2)}) collective-permute-start(bf16[832,256]{1,0:T(8,128)(2,1)} %copy-done.20), channel_id=1, source_target_pairs={{0,96},{32,0},{64,32},{96,64},{1,97},{33,1},{65,33},{97,65},{2,98}... | collective-permute-start | bytes 1277960 | tf_op jit(solution)/shard_map/ppermute | solution.py:927
  273.4 29.2 %all-to-all-start.6 = ((bf16[32,64,384]{2,1,0:T(8,128)(2,1)}), bf16[32,64,384]{2,1,0:T(8,128)(2,1)}, u32[]{:S(2)}, u32[]{:S(2)}) async-start(bf16[32,64,384]{2,1,0:T(8,128)(2,1)} %bitcast.22), calls=%async_computation.6 | async-start | bytes 3145728 | tf_op jit(solution)/shard_map/all_to_all | solution.py:855
  (32 other events, 50.0 us)

commit v6 on v5

--- a/solution.py
+++ b/solution.py
@@ -306,17 +306,17 @@
     step = pl.program_id(0)
     rows = table_ref.shape[0] // 2
     low = half_lanes((rows, LANES))
-    for inner in range(4):
-        product = dot_nt(table_ref[...], field_ref[inner])
-        real, imag = product[:rows], product[rows:]
-        real_a, imag_a = real[:, :LANES], imag[:, :LANES]
-        tiles = (
-            jnp.where(low, real_a, pltpu.roll(imag_a, HALF, 1)),
-            jnp.where(low, pltpu.roll(real_a, HALF, 1), imag_a),
-            jnp.concatenate([real[:, LANES:], imag[:, LANES:]], axis=1),
-        )
-        for index, tile in enumerate(tiles):
-            scratch[index, pl.ds(step * 4 + inner, rows, stride=LAT_LOCAL), :] = tile
+    fields = field_ref[...].reshape(4 * C, NLON)
+    product = dot_nt(table_ref[...], fields)
+    for block in range(4 * GROUPS):
+        inner, index = block // GROUPS, block % GROUPS
+        lanes = slice(block // 2 * LANES, (block // 2 + 1) * LANES)
+        real, imag = product[:rows, lanes], product[rows:, lanes]
+        if block % 2:
+            tile = jnp.where(low, pltpu.roll(real, HALF, 1), imag)
+        else:
+            tile = jnp.where(low, real, pltpu.roll(imag, HALF, 1))
+        scratch[index, pl.ds(step * 4 + inner, rows, stride=LAT_LOCAL), :] = tile
 
     @pl.when(step == LAT_LOCAL // 4 - 1)
     def _():
@@ -339,13 +339,15 @@
     )
 
 
-def pair_sum(local, table_ref, tiles):
-    pairs = [(index, tile) for index, (order, tile) in enumerate(PAIRS) if order == local]
-    left = [table_ref[index, DEVICES * local :, :] for index, _ in pairs]
-    right = [tiles[tile] for _, tile in pairs]
-    if len(pairs) == 1:
-        return dot(left[0], right[0])
-    return dot(jnp.concatenate(left, axis=1), jnp.concatenate(right, axis=0))
+def order_sums(group, table_ref, tiles):
+    totals = [None] * GROUP_ORDERS
+    for tile in range(GROUP_TILES):
+        left = [table_ref[2 * tile + place, DEVICES * (tile + place) :, :] for place in range(2)]
+        product = dot(jnp.concatenate(left, axis=0), tiles[tile])
+        middle = left[0].shape[0]
+        for order, part in ((tile, product[:middle]), (tile + 1, product[middle:])):
+            totals[order] = part if totals[order] is None else totals[order] + part
+    return totals
 
 
 def tile_sum(tile, table_ref, first, second):
@@ -374,17 +376,19 @@
         for copy in arrivals[group]:
             copy.wait()
         tiles = [recv[group, :, tile].reshape(SPAN, 2 * C) for tile in range(GROUP_TILES)]
+        held = scaled_buffers[group]
+        for local, coef in enumerate(order_sums(group, a_buffers[group], tiles)):
+            skipped = DEVICES * local
+            held[packed_rows(group)[local], :] = (
+                gain_ref[LANES * group + skipped :, :] * coef
+            ).astype(BF16)
+        product = dot(held[...], mix_ref[...]).astype(BF16)
         mixed = []
-        for local in range(GROUP_ORDERS):
-            skipped = DEVICES * local
-            coef = pair_sum(local, a_buffers[group], tiles)
-            scaled = (gain_ref[LANES * group + skipped :, :] * coef).astype(BF16)
-            scaled_buffers[group][packed_rows(group)[local], :] = scaled
-            product = dot(scaled, mix_ref[...]).astype(BF16)
-            if skipped:
-                zeros = jnp.zeros((skipped, 2 * C), BF16)
-                product = jnp.concatenate([zeros, product], axis=0)
-            mixed.append(product)
+        for local, rows in enumerate(packed_rows(group)):
+            zeros = jnp.zeros((DEVICES * local, 2 * C), BF16)
+            mixed.append(
+                jnp.concatenate([zeros, product[rows]], axis=0) if local else product[rows]
+            )
         for tile in range(GROUP_TILES):
             grid = tile_sum(tile, st_buffers[group], mixed[tile], mixed[tile + 1])
             payload[group, :, tile] = grid.astype(BF16).reshape(DEVICES, TILE, 2 * C)
@@ -483,11 +487,10 @@
         pre_scratch[rows, :] = (grad_act * slope).astype(BF16)
     low_grad = half_lanes((C, LANES))
     for pair in range(2):
-        lanes = slice(pair * LANES, (pair + 1) * LANES)
-        act = act_scratch[:, lanes]
-        grad_ref[...] += jnp.where(
-            low_grad, dot(up_ref[2 * pair], act), dot(up_ref[2 * pair + 1], act)
-        )
+        act = act_scratch[:, pair * LANES : (pair + 1) * LANES]
+        ups = up_ref[2 * pair : 2 * pair + 2].reshape(2 * C, NLON)
+        grads = dot(ups, act)
+        grad_ref[...] += jnp.where(low_grad, grads[:C], grads[C:])
     grad_modes = dot(table_ref[...], pre_scratch[...])
     for pair in range(2):
         lanes = slice(pair * LANES, (pair + 1) * LANES)
@@ -548,20 +551,20 @@
     lanes = recv_ref.shape[-1]
     first = 0
     for place, group in enumerate(groups):
-        start = GROUP_TILES * place
+        start = GROUP_TILES * group if recv_ref.shape[1] == TILES else 0
         tiles = [
             recv_ref[:, start + tile].reshape(SPAN, lanes) for tile in range(GROUP_TILES)
         ]
         copies[place].wait()
-        for local, rows in enumerate(packed_rows(group)):
-            mixed = pair_sum(local, buffers[place], tiles).astype(BF16)
-            out_ref[first + rows.start : first + rows.stop, :] = mixed
+        sums = order_sums(group, buffers[place], tiles)
+        for total, rows in zip(sums, packed_rows(group)):
+            out_ref[first + rows.start : first + rows.stop, :] = total.astype(BF16)
         first += PACKED[group]
 
 
 def spectral_backward(groups, recv, tables, after=()):
     lanes = recv.shape[-1]
-    tiles = GROUP_TILES * len(groups)
+    tiles = GROUP_TILES if len(groups) == 1 else TILES
     block = groups[0] if len(groups) == 1 else 0
     out = (sum(PACKED[group] for group in groups), lanes)
     return call(
@@ -606,8 +609,8 @@
     )
 
 
-def synthesis_kernel(group, table_ref, small_ref, large_ref, gain_ref, mix_ref, *refs):
-    extra, (out_ref, coeff_ref, at_ref, part_ref, sems) = refs[:-5], refs[-5:]
+def synthesis_kernel(group, large_rows, table_ref, small_ref, large_ref, gain_ref, mix_ref, *refs):
+    out_ref, coeff_ref, at_ref, part_ref, sems = refs[-5:]
     degrees = degrees_of(group)
     copies = (
         pltpu.make_async_copy(
@@ -618,15 +621,14 @@
     for copy in copies:
         copy.start()
     copies[0].wait()
+    product = dot_nt(jnp.concatenate([part_ref[...], large_ref[large_rows, :]], axis=1), mix_ref[...])
     for local, rows in enumerate(packed_rows(group)):
         first = local * degrees
         skipped = DEVICES * local
-        mixed = jnp.concatenate([part_ref[rows, :], large_ref[rows, :]], axis=1)
-        scaled = dot_nt(mixed, mix_ref[...])
         if skipped:
             coeff_ref[first : first + skipped, :] = jnp.zeros((skipped, 2 * C), BF16)
         coeff_ref[first + skipped : first + degrees, :] = (
-            gain_ref[LANES * group + skipped :, :] * scaled
+            gain_ref[LANES * group + skipped :, :] * product[rows]
         ).astype(BF16)
     copies[1].wait()
     for tile in range(GROUP_TILES):
@@ -634,20 +636,19 @@
         second = coeff_ref[(tile + 1) * degrees : (tile + 2) * degrees, :]
         out = tile_sum(tile, at_ref, first, second)
         out_ref[:, tile] = out.astype(BF16).reshape(DEVICES, TILE, 2 * C)
-    if extra:
-        out_ref[:, GROUP_TILES] = extra[0][...]
-
-
-def analysis_back(group, at, small, large, gain, mix, tiles, extra=(), after=()):
-    inputs = (at, small, large, gain, mix, *extra)
-    return call(
-        functools.partial(synthesis_kernel, group),
+
+
+def analysis_back(group, at, small, large, first, gain, mix, tiles, block, payload=(), after=()):
+    inputs = (at, small, large, gain, mix, *payload)
+    return call(
+        functools.partial(synthesis_kernel, group, slice(first, first + PACKED[group])),
         inputs,
-        [HELD] * 2 + [whole(value.shape) for value in inputs[2:]],
-        whole((DEVICES, GROUP_TILES + len(extra), TILE, 2 * C)),
+        [HELD] * 2 + [whole(value.shape) for value in inputs[2:5]] + [HELD] * len(payload),
+        pl.BlockSpec((DEVICES, GROUP_TILES, TILE, 2 * C), lambda b: (0, block, 0, 0)),
         jax.ShapeDtypeStruct((DEVICES, tiles, TILE, 2 * C), BF16),
         (1,),
         after,
+        aliases={5: 0} if payload else {},
         scratch_shapes=[
             pltpu.VMEM((GROUP_ORDERS * degrees_of(group), 2 * C), BF16),
             pltpu.VMEM(at.shape, BF16),
@@ -664,23 +665,23 @@
 
 
 def weight_kernel(held_ref, small_ref, *refs):
-    large_refs, (mix_ref, factor_ref, proj_small, proj_large) = refs[:3], refs[3:7]
-    out_ref, gain, packed, spaced, scaled_ref, sem = refs[7:]
+    first_ref, rest_ref, mix_ref, factor_ref, proj_small, proj_large = refs[:6]
+    out_ref, gain, packed, spaced, scaled_ref, sem = refs[6:]
+    large = (first_ref[...], rest_ref[: PACKED[1], :], rest_ref[PACKED[1] :, :])
     copy = pltpu.make_async_copy(held_ref, scaled_ref, sem)
     copy.start()
     copy.wait()
     block = None
     for group in range(GROUPS):
         rows = slice(BASES[group], BASES[group] + PACKED[group])
-        mixed = jnp.concatenate([small_ref[rows, :], large_refs[group][...]], axis=1)
+        mixed = jnp.concatenate([small_ref[rows, :], large[group]], axis=1)
         part = lax.dot_general(
             scaled_ref[rows, :], mixed, (((0,), (0,)), ((), ())), preferred_element_type=F32
         )
         block = part if block is None else block + part
+        product = dot_nt(mixed, mix_ref[...]) * scaled_ref[rows, :].astype(F32)
         for local, rows in enumerate(packed_rows(group)):
-            here = slice(BASES[group] + rows.start, BASES[group] + rows.stop)
-            mixed = jnp.concatenate([small_ref[here, :], large_refs[group][rows, :]], axis=1)
-            part = dot_nt(mixed, mix_ref[...]) * scaled_ref[here, :].astype(F32)
+            part = product[rows]
             first = LANES * group + DEVICES * local
             if first:
                 gain[first:, :] += part
@@ -712,18 +713,18 @@
                 index, row * DEVICES : (row + 1) * DEVICES, :
             ]
         spaced[index, pl.ds(TILE - 1, DEVICES, stride=TILE), :] = jnp.zeros((DEVICES, LANES), F32)
-        out_ref[:, :, lanes] = spaced[index].astype(BF16).reshape(DEVICES, TILE, LANES)
+        out_ref[:, 0, :, lanes] = spaced[index].astype(BF16).reshape(DEVICES, TILE, LANES)
 
 
 def weight_grads(scaled, small, large, mix, gain, proj_small, proj_large, after=()):
-    out = (DEVICES, TILE, 2 * C)
+    tiles = 2 * GROUP_TILES
     inputs = (scaled, small, *large, mix, gain, proj_small, proj_large)
     return call(
         weight_kernel,
         inputs,
         [HELD] + [whole(value.shape) for value in inputs[1:]],
-        whole(out),
-        jax.ShapeDtypeStruct(out, BF16),
+        pl.BlockSpec((DEVICES, 1, TILE, 2 * C), lambda b: (0, tiles, 0, 0)),
+        jax.ShapeDtypeStruct((DEVICES, tiles + 1, TILE, 2 * C), BF16),
         (1,),
         after,
         scratch_shapes=[
@@ -744,12 +745,15 @@
 
 
 def attach_totals(recv, payload):
-    spec = pl.BlockSpec((DEVICES, 1, TILE, 2 * C), lambda b: (0, GROUP_TILES, 0, 0))
+    def last(value):
+        tile = value.shape[1] - 1
+        return pl.BlockSpec((DEVICES, 1, TILE, 2 * C), lambda b: (0, tile, 0, 0))
+
     return call(
         total_kernel,
         (recv, payload),
-        [spec, pl.BlockSpec(memory_space=pl.ANY)],
-        spec,
+        [last(recv), pl.BlockSpec(memory_space=pl.ANY)],
+        last(payload),
         jax.ShapeDtypeStruct(payload.shape, BF16),
         (1,),
         aliases={1: 0},
@@ -815,7 +819,7 @@
         out_ref[inner] = total.astype(out_ref.dtype)
 
 
-def field_stage(recv, table, base, unpacked=False, after=()):
+def field_stage(recv, at, table, base, unpacked=False, after=()):
     rows = DEVICES * GROUP_ORDERS * LAT_LOCAL
     block = pl.BlockSpec((4, C, NLON), lambda b: (b, 0, 0))
     tiles = GROUP_TILES + int(unpacked)
@@ -832,7 +836,7 @@
         [
             pl.BlockSpec(
                 (DEVICES, tiles, TILE, 2 * C),
-                lambda b: (0, 0, 0, 0),
+                lambda b: (0, at, 0, 0),
                 pipeline_mode=pl.Buffered(1),
             ),
             whole(table.shape),
@@ -915,46 +919,35 @@
     every = tuple(range(GROUPS))
     mixed_small = spectral_backward(every, small, [table[0] for table in behind])
     moved_small = lax.ppermute(mixed_small, "section", shift)
-    mixed_2 = spectral_backward((2,), large, [behind[2][0]], (moved_small,))
-    moved_2 = lax.ppermute(mixed_2, "section", shift)
-    out_2 = analysis_back(
-        2, behind[2][1], moved_small, moved_2, gain_next, mix_next, GROUP_TILES
-    )
-    recv_2 = exchange(out_2)
-    mixed_0 = spectral_backward((0,), large, [behind[0][0]], (out_2,))
-    moved_0 = lax.ppermute(mixed_0, "section", shift)
-    mixed_1 = spectral_backward((1,), large, [behind[1][0]], (mixed_0,))
-    moved_1 = lax.ppermute(hold(mixed_1, (moved_0,)), "section", shift)
-    partial_grads = weight_grads(
-        scaled, mixed_small, (mixed_0, mixed_1, mixed_2), mix, gain, proj_small, proj_large
-    )
+    mixed_rest = spectral_backward((1, 2), large, [behind[1][0], behind[2][0]], (moved_small,))
+    moved_rest = lax.ppermute(mixed_rest, "section", shift)
+    mixed_0 = spectral_backward((0,), large, [behind[0][0]], (mixed_rest,))
+    out_rest = weight_grads(
+        scaled, mixed_small, (mixed_0, mixed_rest), mix, gain, proj_small, proj_large
+    )
+    for block, group in enumerate((1, 2)):
+        out_rest = analysis_back(
+            group,
+            behind[group][1],
+            moved_small,
+            moved_rest,
+            block * PACKED[1],
+            gain_next,
+            mix_next,
+            2 * GROUP_TILES + 1,
+            block,
+            (out_rest,),
+        )
+    moved_0 = lax.ppermute(hold(mixed_0, (moved_rest,)), "section", shift)
+    recv_rest = exchange(out_rest)
     out_0 = analysis_back(
-        0,
-        behind[0][1],
-        moved_small,
-        moved_0,
-        gain_next,
-        mix_next,
-        GROUP_TILES + 1,
-        (partial_grads,),
-    )
-    out_0 = hold(out_0, (recv_2,))
+        0, behind[0][1], moved_small, moved_0, 0, gain_next, mix_next, GROUP_TILES + 1, 0
+    )
+    out_0 = attach_totals(recv_rest, out_0)
     recv_0 = exchange(out_0)
-    out_1 = analysis_back(
-        1,
-        behind[1][1],
-        moved_small,
-        moved_1,
-        gain_next,
-        mix_next,
-        GROUP_TILES + 1,
-        after=(recv_2,),
-    )
-    out_1 = attach_totals(recv_0, out_1)
-    recv_1 = exchange(out_1)
-    (base,) = field_stage(recv_2, forward[2], upstream_next, after=(out_1,))
-    (base,) = field_stage(recv_0, forward[0], base)
-    received, grad_w2, grad_mix, grad_gain = field_stage(recv_1, forward[1], base, True)
+    (base,) = field_stage(recv_rest, 0, forward[1], upstream_next, after=(out_0,))
+    (base,) = field_stage(recv_rest, 1, forward[2], base)
+    received, grad_w2, grad_mix, grad_gain = field_stage(recv_0, 0, forward[0], base, True)
     return (
         received[None],
         grad_w2[None],

time: 310 us -> 304 us (0.981)
  starting transfers between devices: 44 us -> 36.3 us
  local copies, waits for them, and re-layouts: 30.2 us -> 37 us
  Pallas kernels: 102 us -> 98 us
    all_to_all x7 -> x6, starting transfers between devices: 39.3 us -> 31.8 us  [exchange(): moved = lax.all_to_all(flat, 'lat', split_axis=0, concat_axis=0, tiled=True)]
    unnamed x84 -> x82, local copies, waits for them, and re-layouts: 22.7 us -> 29.4 us
    ppermute x3 -> x2, waiting for transfers between devices: 32.1 us -> 28.3 us  [the longest x1 19 us: shards(): moved_0 = lax.ppermute(hold(mixed_0, (moved_rest,)), 'section', shift)]
    pallas_call x21 -> x19, Pallas kernels: 102 us -> 98 us  [call(): pl.pallas_call(body, grid=grid, in_specs=list(in_specs) + [pl.BlockSpec(m...]
    all_to_all x7 -> x6, waiting for transfers between devices: 57.2 us -> 58.6 us  [exchange(): moved = lax.all_to_all(flat, 'lat', split_axis=0, concat_axis=0, tiled=True)]
  transfers between devices with their start and end apart: 14 -> 12, of which waited for: 11 -> 10; matrix products, arithmetic and copies ran while one was open for 2% -> 3% of each run, Pallas kernels for 24% -> 23%
where the time goes in v6:
time: 304 us; the launch traced here: 302 us
  waiting for transfers between devices  130 us (43%)
  Pallas kernels  98 us (32%)
  local copies, waits for them, and re-layouts  37 us (12%)
  starting transfers between devices  36.3 us (12%)
    pallas_call x19, Pallas kernels, call(): pl.pallas_call(body, grid=grid, in_specs=list(in_specs) + [pl.BlockSpec(m...  98 us
    all_to_all x6, waiting for transfers between devices, exchange(): moved = lax.all_to_all(flat, 'lat', split_axis=0, concat_axis=0, tiled=True)  58.6 us
    all_to_all x6, starting transfers between devices, exchange(): moved = lax.all_to_all(flat, 'lat', split_axis=0, concat_axis=0, tiled=True)  31.8 us
    unnamed x82, local copies, waits for them, and re-layouts  29.4 us
    ppermute x1, waiting for transfers between devices, shards(): lax.ppermute(mix_weight[0], 'section', shift)  27 us
    ppermute x1, waiting for transfers between devices, shards(): moved_0 = lax.ppermute(hold(mixed_0, (moved_rest,)), 'section', shift)  19 us
    ppermute x1, waiting for transfers between devices, shards(): moved_small = lax.ppermute(mixed_small, 'section', shift)  16.1 us
    ppermute x1, waiting for transfers between devices, shards(): moved_rest = lax.ppermute(mixed_rest, 'section', shift)  9.28 us
  transfers between devices with their start and end apart: 12, of which 10 were waited for; matrix products, arithmetic and copies ran while one was open for 3% of the time, Pallas kernels for 23%

profile of v6, /device:TPU:6, one launch (start us, length us, event | category | flops | bytes accessed | tf_op | source)
XLA Modules:
  0.0 302.3 jit_solution(10696110694041797620)
XLA Ops:
  0.6 8.1 %spectrum_rows.1.refs_5_.refs_3_ = bf16[4608,384]{1,0:T(8,128)(2,1)} custom-call(bf16[12,192,768]{2,1,0:T(8,128)(2,1)} %bitcast.46, bf16[768,768]{1,0:T(8,128)(2,1)} %constant.34.clone.refs_1_), custom_call_target="tpu_custom_call" | custom-call | flops 1 | bytes 1 | tf_op jit(solution)/shard_map/spectrum_rows/pallas_call | solution.py:81
  8.7 8.4 %all-to-all-start = ((bf16[32,144,384]{2,1,0:T(8,128)(2,1)}), bf16[32,144,384]{2,1,0:T(8,128)(2,1)}, u32[]{:S(2)}, u32[]{:S(2)}) async-start(bf16[32,144,384]{2,1,0:T(8,128)(2,1)} %bitcast.39), calls=%async_computation | async-start | bytes 7077888 | tf_op jit(solution)/shard_map/all_to_all | solution.py:859
  22.0 23.6 %legendre_tables.1 = (bf16[6,384,512]{2,1,0:T(8,128)(2,1)}, bf16[6,512,384]{2,1,0:T(8,128)(2,1)}, bf16[6,384,512]{2,1,0:T(8,128)(2,1)}, bf16[6,512,384]{2,1,0:T(...) custom-call(f32[16,128]{1,0:T(8,128)} %get-tuple-element.59.refs_0_,, ...), custom_call_target="tpu_custom_call" | custom-call | flops 1 | bytes 1 | tf_op jit(solution)/shard_map/legendre_tables/pallas_call | solution.py:81
  45.6 6.3 %copy.24.refs_9_.refs_2_ = bf16[12,768,192]{2,1,0:T(8,128)(2,1)} copy(bf16[12,768,192]{1,2,0:T(8,128)(2,1)} %bitcast.41) | data formatting | bytes 7077888 | tf_op jit(solution)/shard_map/transpose | solution.py:882
  51.8 11.5 %all-to-all-done = bf16[32,144,384]{2,1,0:T(8,128)(2,1)} async-done(((bf16[32,144,384]{2,1,0:T(8,128)(2,1)}), bf16[32,144,384]{2,1,0:T(8,128)(2,1)}, u32[]{:S(2)}, u32[]{:S(2)}) %all-to-all-start) | async-done | bytes 3538976 | tf_op jit(solution)/shard_map/all_to_all | solution.py:859
  63.4 11.4 %spectral_forward.1 = (bf16[2496,384]{1,0:T(8,128)(2,1)}, bf16[32,9,16,384]{3,2,1,0:T(8,128)(2,1)}) custom-call(bf16[32,9,16,384]{3,2,1,0:T(8,128)(2,1)} %bitcast.4.refs_0_, bf16[6,384,512]{2,1,0:T(8,128)(2,1)} %get-tuple-element.32.refs_1_, bf16[6,256,512]{2,1,0:T(8,128)(2,1)} %get-tuple-element.33.refs_2_, bf16[6,128,512]{2,1,0:T(8,128)(2,1)} %get-tuple-element.34.refs_3_, ...), custom_call_target="tpu_custom_call" | custom-call | flops 1 | bytes 1 | tf_op jit(solution)/shard_map/spectral_forward/pallas_call | solution.py:81
  74.8 4.9 %all-to-all-start.1 = ((bf16[32,144,384]{2,1,0:T(8,128)(2,1)}), bf16[32,144,384]{2,1,0:T(8,128)(2,1)}, u32[]{:S(2)}, u32[]{:S(2)}) async-start(bf16[32,144,384]{2,1,0:T(8,128)(2,1)} %bitcast.45), calls=%async_computation.1 | async-start | bytes 7077888 | tf_op jit(solution)/shard_map/all_to_all | solution.py:859
  81.1 27.0 %collective-permute-done.2.refs_1_ = bf16[2,192,192]{2,1,0:T(8,128)(2,1)S(1)} collective-permute-done((bf16[2,192,192]{2,1,0:T(8,128)(2,1)}, bf16[2,192,192]{2,1,0:T(8,128)(2,1)S(1)}, u32[]{:S(2)}, u32[]{:S(2)}) %collective-permute-start.2) | collective-permute-done | bytes 147488 | tf_op jit(solution)/shard_map/ppermute | solution.py:891
  111.8 14.0 %all-to-all-done.1 = bf16[32,144,384]{2,1,0:T(8,128)(2,1)} async-done(((bf16[32,144,384]{2,1,0:T(8,128)(2,1)}), bf16[32,144,384]{2,1,0:T(8,128)(2,1)}, u32[]{:S(2)}, u32[]{:S(2)}) %all-to-all-start.1) | async-done | bytes 3538976 | tf_op jit(solution)/shard_map/all_to_all | solution.py:859
  125.8 9.9 %grid_stage_1.1 = (bf16[4608,128]{1,0:T(8,128)(2,1)}, f32[192,128]{1,0:T(8,128)}) custom-call(bf16[4608,384]{1,0:T(8,128)(2,1)} %bitcast.12.refs_0_, bf16[12,192,768]{2,1,0:T(8,128)(2,1)} %bitcast.42, bf16[12,768,192]{2,1,0:T(8,128)(2,1)} %copy.24.refs_9_.refs_2_, bf16[192,384]{1,0:T(8,128)(2,1)} %get-tuple-element.40.refs_10_.refs_3_, ...), custom_call_target="tpu_custom_call" | custom-call | flops 1 | bytes 1 | tf_op jit(solution)/shard_map/grid_stage_1/pallas_call | solution.py:81
  135.8 3.9 %all-to-all-start.2 = ((bf16[32,144,128]{2,1,0:T(8,128)(2,1)}), bf16[32,144,128]{2,1,0:T(8,128)(2,1)S(1)}, u32[]{:S(2)}, u32[]{:S(2)}) async-start(bf16[32,144,128]{2,1,0:T(8,128)(2,1)} %bitcast.44), calls=%async_computation.2 | async-start | bytes 2359296 | tf_op jit(solution)/shard_map/all_to_all | solution.py:859
  139.7 16.7 %grid_stage_2.1 = (bf16[4608,256]{1,0:T(8,128)(2,1)}, f32[192,256]{1,0:T(8,128)}) custom-call(bf16[4608,384]{1,0:T(8,128)(2,1)} %bitcast.12.refs_0_, bf16[12,192,768]{2,1,0:T(8,128)(2,1)} %bitcast.43, bf16[12,768,192]{2,1,0:T(8,128)(2,1)} %copy.24.refs_9_.refs_2_, bf16[192,384]{1,0:T(8,128)(2,1)} %get-tuple-element.40.refs_10_.refs_3_, ...), custom_call_target="tpu_custom_call" | custom-call | flops 1 | bytes 1 | tf_op jit(solution)/shard_map/grid_stage_2/pallas_call | solution.py:81
  159.8 5.1 %all-to-all-start.3 = ((bf16[32,144,256]{2,1,0:T(8,128)(2,1)}), bf16[32,144,256]{2,1,0:T(8,128)(2,1)S(1)}, u32[]{:S(2)}, u32[]{:S(2)}) async-start(bf16[32,144,256]{2,1,0:T(8,128)(2,1)} %bitcast.47), calls=%async_computation.3 | async-start | bytes 4718592 | tf_op jit(solution)/shard_map/all_to_all | solution.py:859
  170.3 2.8 spectral_backward_0_1_2.1.refs_1_
  174.8 16.1 %collective-permute-done.3.refs_3_.refs_1_ = bf16[2496,128]{1,0:T(8,128)(2,1)S(1)} collective-permute-done((bf16[2496,128]{1,0:T(8,128)(2,1)S(1)}, bf16[2496,128]{1,0:T(8,128)(2,1)S(1)}, u32[]{:S(2)}, u32[]{:S(2)}) %collective-permute-start.3) | collective-permute-done | bytes 639008 | tf_op jit(solution)/shard_map/ppermute | solution.py:921
  190.9 7.0 %all-to-all-done.3 = bf16[32,144,256]{2,1,0:T(8,128)(2,1)S(1)} async-done(((bf16[32,144,256]{2,1,0:T(8,128)(2,1)}), bf16[32,144,256]{2,1,0:T(8,128)(2,1)S(1)}, u32[]{:S(2)}, u32[]{:S(2)}) %all-to-all-start.3) | async-done | bytes 2359328 | tf_op jit(solution)/shard_map/all_to_all | solution.py:859
  204.1 3.2 %weight_grads.1.refs_5_ = bf16[32,7,16,384]{3,2,1,0:T(8,128)(2,1)S(1)} custom-call(bf16[2496,384]{1,0:T(8,128)(2,1)S(1)} %copy-done.30, bf16[2496,128]{1,0:T(8,128)(2,1)S(1)} %copy-done.27, bf16[1344,256]{1,0:T(8,128)(2,1)S(1)} %spectral_backward_0.1.refs_2_.refs_0_, bf16[1152,256]{1,0:T(8,128)(2,1)S(1)} %spectral_backward_1_2.1.refs_2_.refs_3_, ...), custom_call_target="tpu_custom_call" | custom-call | flops 1 | bytes 1 | tf_op jit(solution)/shard_map/weight_grads/pallas_call | solution.py:81
  207.3 9.3 %collective-permute-done.4.refs_2_.refs_1_ = bf16[1152,256]{1,0:T(8,128)(2,1)S(1)} collective-permute-done((bf16[1152,256]{1,0:T(8,128)(2,1)S(1)}, bf16[1152,256]{1,0:T(8,128)(2,1)S(1)}, u32[]{:S(2)}, u32[]{:S(2)}) %collective-permute-start.4) | collective-permute-done | bytes 589856 | tf_op jit(solution)/shard_map/ppermute | solution.py:923
  221.5 4.7 %all-to-all-start.4 = ((bf16[32,112,384]{2,1,0:T(8,128)(2,1)}), bf16[32,112,384]{2,1,0:T(8,128)(2,1)S(1)}, u32[]{:S(2)}, u32[]{:S(2)}) async-start(bf16[32,112,384]{2,1,0:T(8,128)(2,1)} %bitcast.34), calls=%async_computation.4 | async-start | bytes 5505024 | tf_op jit(solution)/shard_map/all_to_all | solution.py:859
  229.2 19.0 %collective-permute-done.5.refs_2_ = bf16[1344,256]{1,0:T(8,128)(2,1)S(1)} collective-permute-done((bf16[1344,256]{1,0:T(8,128)(2,1)}, bf16[1344,256]{1,0:T(8,128)(2,1)S(1)}, u32[]{:S(2)}, u32[]{:S(2)}) %collective-permute-start.5) | collective-permute-done | bytes 688160 | tf_op jit(solution)/shard_map/ppermute | solution.py:941
  254.7 9.0 %all-to-all-done.4 = bf16[32,112,384]{2,1,0:T(8,128)(2,1)S(1)} async-done(((bf16[32,112,384]{2,1,0:T(8,128)(2,1)}), bf16[32,112,384]{2,1,0:T(8,128)(2,1)S(1)}, u32[]{:S(2)}, u32[]{:S(2)}) %all-to-all-start.4) | async-done | bytes 2752544 | tf_op jit(solution)/shard_map/all_to_all | solution.py:859
  266.4 4.8 %all-to-all-start.5 = ((bf16[32,64,384]{2,1,0:T(8,128)(2,1)}), bf16[32,64,384]{2,1,0:T(8,128)(2,1)}, u32[]{:S(2)}, u32[]{:S(2)}) async-start(bf16[32,64,384]{2,1,0:T(8,128)(2,1)} %bitcast.35), calls=%async_computation.5 | async-start | bytes 3145728 | tf_op jit(solution)/shard_map/all_to_all | solution.py:859
  280.4 14.7 %all-to-all-done.5 = bf16[32,64,384]{2,1,0:T(8,128)(2,1)} async-done(((bf16[32,64,384]{2,1,0:T(8,128)(2,1)}), bf16[32,64,384]{2,1,0:T(8,128)(2,1)}, u32[]{:S(2)}, u32[]{:S(2)}) %all-to-all-start.5) | async-done | bytes 1572896 | tf_op jit(solution)/shard_map/all_to_all | solution.py:859
  297.1 5.2 %field_stage.5 = (bf16[12,192,768]{2,1,0:T(8,128)(2,1)}, f32[192,192]{1,0:T(8,128)}, f32[2,192,192]{2,1,0:T(8,128)}, f32[192,384]{1,0:T(8,128)}) custom-call(bf16[32,4,16,384]{3,2,1,0:T(8,128)(2,1)} %bitcast.21.refs_0_, bf16[256,768]{1,0:T(8,128)(2,1)S(1)} %copy-done.36, bf16[12,192,768]{2,1,0:T(8,128)(2,1)S(1)} %copy-done.6), custom_call_target="tpu_custom_call" | custom-call | flops 1 | bytes 1 | tf_op jit(solution)/shard_map/field_stage/pallas_call | solution.py:81
  (103 shorter events, 54.7 us)
Async XLA Ops:
  8.7 54.7 %all-to-all-start = ((bf16[32,144,384]{2,1,0:T(8,128)(2,1)}), bf16[32,144,384]{2,1,0:T(8,128)(2,1)}, u32[]{:S(2)}, u32[]{:S(2)}) async-start(bf16[32,144,384]{2,1,0:T(8,128)(2,1)} %bitcast.39), calls=%async_computation | async-start | bytes 7077888 | tf_op jit(solution)/shard_map/all_to_all | solution.py:859
  17.2 94.6 %collective-permute-start = (bf16[12,192,768]{2,1,0:T(8,128)(2,1)}, bf16[12,192,768]{2,1,0:T(8,128)(2,1)S(1)}, u32[]{:S(2)}, u32[]{:S(2)}) collective-permute-start(bf16[12,192,768]{2,1,0:T(8,128)(2,1)} %bitcast.40), channel_id=1, source_target_pairs={{0,96},{32,0},{64,32},{96,64},{1,97},{33,1},{65,33},{97,65},{2,98}... | collective-permute-start | bytes 10616840 | tf_op jit(solution)/shard_map/ppermute | solution.py:881
  74.8 51.1 %all-to-all-start.1 = ((bf16[32,144,384]{2,1,0:T(8,128)(2,1)}), bf16[32,144,384]{2,1,0:T(8,128)(2,1)}, u32[]{:S(2)}, u32[]{:S(2)}) async-start(bf16[32,144,384]{2,1,0:T(8,128)(2,1)} %bitcast.45), calls=%async_computation.1 | async-start | bytes 7077888 | tf_op jit(solution)/shard_map/all_to_all | solution.py:859
  79.6 28.4 %collective-permute-start.1 = (f32[192,384]{1,0:T(8,128)}, f32[192,384]{1,0:T(8,128)S(1)}, u32[]{:S(2)}, u32[]{:S(2)}) collective-permute-start(f32[192,384]{1,0:T(8,128)} %bitcast.51), channel_id=1, source_target_pairs={{0,96},{32,0},{64,32},{96,64},{1,97},{33,1},{65,33},{97,65},{2,98}... | collective-permute-start | bytes 884744 | tf_op jit(solution)/shard_map/ppermute | solution.py:890
  80.5 27.5 %collective-permute-start.2 = (bf16[2,192,192]{2,1,0:T(8,128)(2,1)}, bf16[2,192,192]{2,1,0:T(8,128)(2,1)S(1)}, u32[]{:S(2)}, u32[]{:S(2)}) collective-permute-start(bf16[2,192,192]{2,1,0:T(8,128)(2,1)} %bitcast.53), channel_id=1, source_target_pairs={{0,96},{32,0},{64,32},{96,64},{1,97},{33,1},{65,33},{97,65},{2,98}... | collective-permute-start | bytes 442376 | tf_op jit(solution)/shard_map/ppermute | solution.py:891
  111.8 14.0 %copy-start.7 = (bf16[12,192,768]{2,1,0:T(8,128)(2,1)}, bf16[12,192,768]{2,1,0:T(8,128)(2,1)S(1)}, u32[]{:S(2)}) copy-start(bf16[12,192,768]{2,1,0:T(8,128)(2,1)S(1)} %collective-permute-done.refs_6_.refs_2_) | copy-start | bytes 10616836
  135.8 23.0 %all-to-all-start.2 = ((bf16[32,144,128]{2,1,0:T(8,128)(2,1)}), bf16[32,144,128]{2,1,0:T(8,128)(2,1)S(1)}, u32[]{:S(2)}, u32[]{:S(2)}) async-start(bf16[32,144,128]{2,1,0:T(8,128)(2,1)} %bitcast.44), calls=%async_computation.2 | async-start | bytes 2359296 | tf_op jit(solution)/shard_map/all_to_all | solution.py:859
  159.8 38.1 %all-to-all-start.3 = ((bf16[32,144,256]{2,1,0:T(8,128)(2,1)}), bf16[32,144,256]{2,1,0:T(8,128)(2,1)S(1)}, u32[]{:S(2)}, u32[]{:S(2)}) async-start(bf16[32,144,256]{2,1,0:T(8,128)(2,1)} %bitcast.47), calls=%async_computation.3 | async-start | bytes 4718592 | tf_op jit(solution)/shard_map/all_to_all | solution.py:859
  173.1 17.8 %collective-permute-start.3 = (bf16[2496,128]{1,0:T(8,128)(2,1)S(1)}, bf16[2496,128]{1,0:T(8,128)(2,1)S(1)}, u32[]{:S(2)}, u32[]{:S(2)}) collective-permute-start(bf16[2496,128]{1,0:T(8,128)(2,1)S(1)} %spectral_backward_0_1_2.1.refs_1_), channel_id=1, source_target_pairs={{0,96},{32,0},{64,32},{96,64},{1,97},{33,1},{65,33},{97,65},{2,98}... | collective-permute-start | bytes 1916936 | tf_op jit(solution)/shard_map/ppermute | solution.py:921
  200.5 2.5 copy-start.10
  201.8 2.2 copy-start.27
  201.8 2.2 copy-start.29
  201.8 2.2 copy-start.30
  201.8 14.7 %collective-permute-start.4 = (bf16[1152,256]{1,0:T(8,128)(2,1)S(1)}, bf16[1152,256]{1,0:T(8,128)(2,1)S(1)}, u32[]{:S(2)}, u32[]{:S(2)}) collective-permute-start(bf16[1152,256]{1,0:T(8,128)(2,1)S(1)} %spectral_backward_1_2.1.refs_2_.refs_3_), channel_id=1, source_target_pairs={{0,96},{32,0},{64,32},{96,64},{1,97},{33,1},{65,33},{97,65},{2,98}... | collective-permute-start | bytes 1769480 | tf_op jit(solution)/shard_map/ppermute | solution.py:923
  204.0 3.3 %copy-start.15 = (bf16[1344,256]{1,0:T(8,128)(2,1)}, bf16[1344,256]{1,0:T(8,128)(2,1)S(1)}, u32[]{:S(2)}) copy-start(bf16[1344,256]{1,0:T(8,128)(2,1)S(1)} %spectral_backward_0.1.refs_2_.refs_0_) | copy-start | bytes 2064388
  204.0 12.5 %copy-start.11 = (f32[384,384]{1,0:T(8,128)S(1)}, f32[384,384]{1,0:T(8,128)}, u32[]{:S(2)}) copy-start(f32[384,384]{1,0:T(8,128)} %get-tuple-element.42.refs_7_.refs_3_) | copy-start | bytes 1769476
  204.0 12.5 %copy-start.22 = (bf16[384,384]{1,0:T(8,128)(2,1)S(1)}, bf16[384,384]{1,0:T(8,128)(2,1)}, u32[]{:S(2)}) copy-start(bf16[384,384]{1,0:T(8,128)(2,1)} %get-tuple-element.43.refs_8_.refs_4_) | copy-start | bytes 884740
  204.1 12.5 %copy-start.31 = (bf16[6,512,256]{2,1,0:T(8,128)(2,1)S(1)}, bf16[6,512,256]{2,1,0:T(8,128)(2,1)}, u32[]{:S(2)}) copy-start(bf16[6,512,256]{2,1,0:T(8,128)(2,1)} %get-tuple-element.49.refs_0_) | copy-start | bytes 4718596
  221.5 42.1 %all-to-all-start.4 = ((bf16[32,112,384]{2,1,0:T(8,128)(2,1)}), bf16[32,112,384]{2,1,0:T(8,128)(2,1)S(1)}, u32[]{:S(2)}, u32[]{:S(2)}) async-start(bf16[32,112,384]{2,1,0:T(8,128)(2,1)} %bitcast.34), calls=%async_computation.4 | async-start | bytes 5505024 | tf_op jit(solution)/shard_map/all_to_all | solution.py:859
  228.3 19.9 %copy-start.12 = (f32[384,384]{1,0:T(8,128)S(1)}, f32[384,384]{1,0:T(8,128)}, u32[]{:S(2)}) copy-start(f32[384,384]{1,0:T(8,128)} %get-tuple-element.42.refs_7_.refs_3_) | copy-start | bytes 1769476
  229.2 19.0 %collective-permute-start.5 = (bf16[1344,256]{1,0:T(8,128)(2,1)}, bf16[1344,256]{1,0:T(8,128)(2,1)S(1)}, u32[]{:S(2)}, u32[]{:S(2)}) collective-permute-start(bf16[1344,256]{1,0:T(8,128)(2,1)} %copy-done.17), channel_id=1, source_target_pairs={{0,96},{32,0},{64,32},{96,64},{1,97},{33,1},{65,33},{97,65},{2,98}... | collective-permute-start | bytes 2064392 | tf_op jit(solution)/shard_map/ppermute | solution.py:941
  266.4 4.8 %copy-start.35 = (bf16[256,768]{1,0:T(8,128)(2,1)S(1)}, bf16[256,768]{1,0:T(8,128)(2,1)}, u32[]{:S(2)}) copy-start(bf16[256,768]{1,0:T(8,128)(2,1)} %constant.36.clone.refs_1_) | copy-start | bytes 1179652
  266.4 28.8 %all-to-all-start.5 = ((bf16[32,64,384]{2,1,0:T(8,128)(2,1)}), bf16[32,64,384]{2,1,0:T(8,128)(2,1)}, u32[]{:S(2)}, u32[]{:S(2)}) async-start(bf16[32,64,384]{2,1,0:T(8,128)(2,1)} %bitcast.35), calls=%async_computation.5 | async-start | bytes 3145728 | tf_op jit(solution)/shard_map/all_to_all | solution.py:859
  276.6 18.5 %copy-start.36 = (bf16[256,768]{1,0:T(8,128)(2,1)S(1)}, bf16[256,768]{1,0:T(8,128)(2,1)}, u32[]{:S(2)}) copy-start(bf16[256,768]{1,0:T(8,128)(2,1)} %constant.35.clone.refs_1_) | copy-start | bytes 1179652
  (29 other events, 42.2 us)

commit v7 on v6

--- a/solution.py
+++ b/solution.py
@@ -645,7 +645,7 @@
         inputs,
         [HELD] * 2 + [whole(value.shape) for value in inputs[2:5]] + [HELD] * len(payload),
         pl.BlockSpec((DEVICES, GROUP_TILES, TILE, 2 * C), lambda b: (0, block, 0, 0)),
-        jax.ShapeDtypeStruct((DEVICES, tiles, TILE, 2 * C), BF16),
+        pltpu.HBM((DEVICES, tiles, TILE, 2 * C), BF16),
         (1,),
         after,
         aliases={5: 0} if payload else {},
@@ -724,7 +724,7 @@
         inputs,
         [HELD] + [whole(value.shape) for value in inputs[1:]],
         pl.BlockSpec((DEVICES, 1, TILE, 2 * C), lambda b: (0, tiles, 0, 0)),
-        jax.ShapeDtypeStruct((DEVICES, tiles + 1, TILE, 2 * C), BF16),
+        pltpu.HBM((DEVICES, tiles + 1, TILE, 2 * C), BF16),
         (1,),
         after,
         scratch_shapes=[
@@ -739,7 +739,8 @@
     )
 
 
-def total_kernel(recv_ref, payload_ref, out_ref):
+def total_kernel(recv_ref, payload_ref, out_ref, token_ref):
+    token_ref[...] = jnp.zeros((8, LANES), F32)
     total = jnp.sum(recv_ref[:, 0].astype(F32), axis=0)
     out_ref[:, 0] = jnp.broadcast_to(total.astype(BF16)[None], (DEVICES, TILE, 2 * C))
 
@@ -753,8 +754,8 @@
         total_kernel,
         (recv, payload),
         [last(recv), pl.BlockSpec(memory_space=pl.ANY)],
-        last(payload),
-        jax.ShapeDtypeStruct(payload.shape, BF16),
+        [last(payload), whole((8, LANES))],
+        [pltpu.HBM(payload.shape, BF16), jax.ShapeDtypeStruct((8, LANES), F32)],
         (1,),
         aliases={1: 0},
         vmem=8,
@@ -843,12 +844,12 @@
             block,
         ],
         [block] + [whole(shape) for shape in totals],
-        [jax.ShapeDtypeStruct((LAT_LOCAL, C, NLON), BF16)]
+        [pltpu.HBM((LAT_LOCAL, C, NLON), BF16)]
         + [jax.ShapeDtypeStruct(shape, F32) for shape in totals],
         (LAT_LOCAL // 4,),
         after,
         scratch_shapes=scratch_shapes,
-        vmem=24 if unpacked else 20,
+        vmem=56 if unpacked else 20,
         name="field_stage",
     )
 
@@ -943,9 +944,9 @@
     out_0 = analysis_back(
         0, behind[0][1], moved_small, moved_0, 0, gain_next, mix_next, GROUP_TILES + 1, 0
     )
-    out_0 = attach_totals(recv_rest, out_0)
+    out_0, token = attach_totals(recv_rest, out_0)
     recv_0 = exchange(out_0)
-    (base,) = field_stage(recv_rest, 0, forward[1], upstream_next, after=(out_0,))
+    (base,) = field_stage(recv_rest, 0, forward[1], upstream_next, after=(token,))
     (base,) = field_stage(recv_rest, 1, forward[2], base)
     received, grad_w2, grad_mix, grad_gain = field_stage(recv_0, 0, forward[0], base, True)
     return (

time: 304 us -> 302 us (level)
  Pallas kernels: 98 us -> 107 us
  local copies, waits for them, and re-layouts: 37 us -> 28.6 us
    pallas_call x19, Pallas kernels: 98 us -> 107 us  [call(): pl.pallas_call(body, grid=grid, in_specs=list(in_specs) + [pl.BlockSpec(m...]
    unnamed x82 -> x68, local copies, waits for them, and re-layouts: 29.4 us -> 21 us
  transfers between devices with their start and end apart: 12 -> 12, of which waited for: 10 -> 10; matrix products, arithmetic and copies ran while one was open for 3% -> 3% of each run, Pallas kernels for 23% -> 25%
where the time goes in v7:
time: 302 us; the launch traced here: 300 us
  waiting for transfers between devices  128 us (42%)
  Pallas kernels  107 us (35%)
  starting transfers between devices  36.3 us (12%)
  local copies, waits for them, and re-layouts  28.6 us (9%)
    pallas_call x19, Pallas kernels, call(): pl.pallas_call(body, grid=grid, in_specs=list(in_specs) + [pl.BlockSpec(m...  107 us
    all_to_all x6, waiting for transfers between devices, exchange(): moved = lax.all_to_all(flat, 'lat', split_axis=0, concat_axis=0, tiled=True)  57.2 us
    all_to_all x6, starting transfers between devices, exchange(): moved = lax.all_to_all(flat, 'lat', split_axis=0, concat_axis=0, tiled=True)  31.8 us
    ppermute x1, waiting for transfers between devices, shards(): lax.ppermute(mix_weight[0], 'section', shift)  27 us
    unnamed x68, local copies, waits for them, and re-layouts  21 us
    ppermute x1, waiting for transfers between devices, shards(): moved_0 = lax.ppermute(hold(mixed_0, (moved_rest,)), 'section', shift)  19 us
    ppermute x1, waiting for transfers between devices, shards(): moved_small = lax.ppermute(mixed_small, 'section', shift)  16.1 us
    ppermute x1, waiting for transfers between devices, shards(): moved_rest = lax.ppermute(mixed_rest, 'section', shift)  8.55 us
  transfers between devices with their start and end apart: 12, of which 10 were waited for; matrix products, arithmetic and copies ran while one was open for 3% of the time, Pallas kernels for 25%

profile of v7, /device:TPU:6, one launch (start us, length us, event | category | flops | bytes accessed | tf_op | source)
XLA Modules:
  0.0 300.3 jit_solution(2603794621147329756)
XLA Ops:
  0.6 8.1 %spectrum_rows.1.refs_5_.refs_3_ = bf16[4608,384]{1,0:T(8,128)(2,1)} custom-call(bf16[12,192,768]{2,1,0:T(8,128)(2,1)} %bitcast.46, bf16[768,768]{1,0:T(8,128)(2,1)} %constant.34.clone.refs_1_), custom_call_target="tpu_custom_call" | custom-call | flops 1 | bytes 1 | tf_op jit(solution)/shard_map/spectrum_rows/pallas_call | solution.py:81
  8.7 8.4 %all-to-all-start = ((bf16[32,144,384]{2,1,0:T(8,128)(2,1)}), bf16[32,144,384]{2,1,0:T(8,128)(2,1)}, u32[]{:S(2)}, u32[]{:S(2)}) async-start(bf16[32,144,384]{2,1,0:T(8,128)(2,1)} %bitcast.37), calls=%async_computation | async-start | bytes 7077888 | tf_op jit(solution)/shard_map/all_to_all | solution.py:860
  22.0 23.6 %legendre_tables.1 = (bf16[6,384,512]{2,1,0:T(8,128)(2,1)}, bf16[6,512,384]{2,1,0:T(8,128)(2,1)}, bf16[6,384,512]{2,1,0:T(8,128)(2,1)}, bf16[6,512,384]{2,1,0:T(...) custom-call(f32[16,128]{1,0:T(8,128)} %get-tuple-element.63.refs_0_,, ...), custom_call_target="tpu_custom_call" | custom-call | flops 1 | bytes 1 | tf_op jit(solution)/shard_map/legendre_tables/pallas_call | solution.py:81
  45.6 6.3 %copy.24.refs_9_.refs_2_ = bf16[12,768,192]{2,1,0:T(8,128)(2,1)} copy(bf16[12,768,192]{1,2,0:T(8,128)(2,1)} %bitcast.40) | data formatting | bytes 7077888 | tf_op jit(solution)/shard_map/transpose | solution.py:883
  51.8 11.5 %all-to-all-done = bf16[32,144,384]{2,1,0:T(8,128)(2,1)} async-done(((bf16[32,144,384]{2,1,0:T(8,128)(2,1)}), bf16[32,144,384]{2,1,0:T(8,128)(2,1)}, u32[]{:S(2)}, u32[]{:S(2)}) %all-to-all-start) | async-done | bytes 3538976 | tf_op jit(solution)/shard_map/all_to_all | solution.py:860
  63.4 11.4 %spectral_forward.1 = (bf16[2496,384]{1,0:T(8,128)(2,1)}, bf16[32,9,16,384]{3,2,1,0:T(8,128)(2,1)}) custom-call(bf16[32,9,16,384]{3,2,1,0:T(8,128)(2,1)} %bitcast.4.refs_0_, bf16[6,384,512]{2,1,0:T(8,128)(2,1)} %get-tuple-element.34.refs_1_, bf16[6,256,512]{2,1,0:T(8,128)(2,1)} %get-tuple-element.35.refs_2_, bf16[6,128,512]{2,1,0:T(8,128)(2,1)} %get-tuple-element.36.refs_3_, ...), custom_call_target="tpu_custom_call" | custom-call | flops 1 | bytes 1 | tf_op jit(solution)/shard_map/spectral_forward/pallas_call | solution.py:81
  74.8 4.8 %all-to-all-start.1 = ((bf16[32,144,384]{2,1,0:T(8,128)(2,1)}), bf16[32,144,384]{2,1,0:T(8,128)(2,1)}, u32[]{:S(2)}, u32[]{:S(2)}) async-start(bf16[32,144,384]{2,1,0:T(8,128)(2,1)} %bitcast.45), calls=%async_computation.1 | async-start | bytes 7077888 | tf_op jit(solution)/shard_map/all_to_all | solution.py:860
  81.1 27.0 %collective-permute-done.2.refs_1_ = bf16[2,192,192]{2,1,0:T(8,128)(2,1)S(1)} collective-permute-done((bf16[2,192,192]{2,1,0:T(8,128)(2,1)}, bf16[2,192,192]{2,1,0:T(8,128)(2,1)S(1)}, u32[]{:S(2)}, u32[]{:S(2)}) %collective-permute-start.2) | collective-permute-done | bytes 147488 | tf_op jit(solution)/shard_map/ppermute | solution.py:892
  111.8 14.0 %all-to-all-done.1 = bf16[32,144,384]{2,1,0:T(8,128)(2,1)} async-done(((bf16[32,144,384]{2,1,0:T(8,128)(2,1)}), bf16[32,144,384]{2,1,0:T(8,128)(2,1)}, u32[]{:S(2)}, u32[]{:S(2)}) %all-to-all-start.1) | async-done | bytes 3538976 | tf_op jit(solution)/shard_map/all_to_all | solution.py:860
  125.8 9.9 %grid_stage_1.1 = (bf16[4608,128]{1,0:T(8,128)(2,1)}, f32[192,128]{1,0:T(8,128)}) custom-call(bf16[4608,384]{1,0:T(8,128)(2,1)} %bitcast.12.refs_0_, bf16[12,192,768]{2,1,0:T(8,128)(2,1)} %bitcast.41, bf16[12,768,192]{2,1,0:T(8,128)(2,1)} %copy.24.refs_9_.refs_2_, bf16[192,384]{1,0:T(8,128)(2,1)} %get-tuple-element.42.refs_10_.refs_3_, ...), custom_call_target="tpu_custom_call" | custom-call | flops 1 | bytes 1 | tf_op jit(solution)/shard_map/grid_stage_1/pallas_call | solution.py:81
  135.8 3.9 %all-to-all-start.2 = ((bf16[32,144,128]{2,1,0:T(8,128)(2,1)}), bf16[32,144,128]{2,1,0:T(8,128)(2,1)S(1)}, u32[]{:S(2)}, u32[]{:S(2)}) async-start(bf16[32,144,128]{2,1,0:T(8,128)(2,1)} %bitcast.44), calls=%async_computation.2 | async-start | bytes 2359296 | tf_op jit(solution)/shard_map/all_to_all | solution.py:860
  139.7 16.7 %grid_stage_2.1 = (bf16[4608,256]{1,0:T(8,128)(2,1)}, f32[192,256]{1,0:T(8,128)}) custom-call(bf16[4608,384]{1,0:T(8,128)(2,1)} %bitcast.12.refs_0_, bf16[12,192,768]{2,1,0:T(8,128)(2,1)} %bitcast.42, bf16[12,768,192]{2,1,0:T(8,128)(2,1)} %copy.24.refs_9_.refs_2_, bf16[192,384]{1,0:T(8,128)(2,1)} %get-tuple-element.42.refs_10_.refs_3_, ...), custom_call_target="tpu_custom_call" | custom-call | flops 1 | bytes 1 | tf_op jit(solution)/shard_map/grid_stage_2/pallas_call | solution.py:81
  159.8 5.0 %all-to-all-start.3 = ((bf16[32,144,256]{2,1,0:T(8,128)(2,1)}), bf16[32,144,256]{2,1,0:T(8,128)(2,1)S(1)}, u32[]{:S(2)}, u32[]{:S(2)}) async-start(bf16[32,144,256]{2,1,0:T(8,128)(2,1)} %bitcast.47), calls=%async_computation.3 | async-start | bytes 4718592 | tf_op jit(solution)/shard_map/all_to_all | solution.py:860
  174.8 16.1 %collective-permute-done.3.refs_3_.refs_1_ = bf16[2496,128]{1,0:T(8,128)(2,1)S(1)} collective-permute-done((bf16[2496,128]{1,0:T(8,128)(2,1)S(1)}, bf16[2496,128]{1,0:T(8,128)(2,1)S(1)}, u32[]{:S(2)}, u32[]{:S(2)}) %collective-permute-start.3) | collective-permute-done | bytes 639008 | tf_op jit(solution)/shard_map/ppermute | solution.py:922
  190.9 7.0 %all-to-all-done.3 = bf16[32,144,256]{2,1,0:T(8,128)(2,1)S(1)} async-done(((bf16[32,144,256]{2,1,0:T(8,128)(2,1)}), bf16[32,144,256]{2,1,0:T(8,128)(2,1)S(1)}, u32[]{:S(2)}, u32[]{:S(2)}) %all-to-all-start.3) | async-done | bytes 2359328 | tf_op jit(solution)/shard_map/all_to_all | solution.py:860
  204.0 3.9 %weight_grads.1.refs_5_ = bf16[32,7,16,384]{3,2,1,0:T(8,128)(2,1)} custom-call(bf16[2496,384]{1,0:T(8,128)(2,1)S(1)} %copy-done.24, bf16[2496,128]{1,0:T(8,128)(2,1)S(1)} %copy-done.21, bf16[1344,256]{1,0:T(8,128)(2,1)S(1)} %spectral_backward_0.1.refs_2_.refs_0_, bf16[1152,256]{1,0:T(8,128)(2,1)S(1)} %spectral_backward_1_2.1.refs_2_.refs_3_, ...), custom_call_target="tpu_custom_call" | custom-call | flops 1 | bytes 1 | tf_op jit(solution)/shard_map/weight_grads/pallas_call | solution.py:81
  208.0 8.5 %collective-permute-done.4.refs_2_.refs_1_ = bf16[1152,256]{1,0:T(8,128)(2,1)S(1)} collective-permute-done((bf16[1152,256]{1,0:T(8,128)(2,1)S(1)}, bf16[1152,256]{1,0:T(8,128)(2,1)S(1)}, u32[]{:S(2)}, u32[]{:S(2)}) %collective-permute-start.4) | collective-permute-done | bytes 589856 | tf_op jit(solution)/shard_map/ppermute | solution.py:924
  221.7 4.7 %all-to-all-start.4 = ((bf16[32,112,384]{2,1,0:T(8,128)(2,1)}), bf16[32,112,384]{2,1,0:T(8,128)(2,1)S(1)}, u32[]{:S(2)}, u32[]{:S(2)}) async-start(bf16[32,112,384]{2,1,0:T(8,128)(2,1)} %bitcast.38), calls=%async_computation.4 | async-start | bytes 5505024 | tf_op jit(solution)/shard_map/all_to_all | solution.py:860
  229.4 19.0 %collective-permute-done.5.refs_2_ = bf16[1344,256]{1,0:T(8,128)(2,1)S(1)} collective-permute-done((bf16[1344,256]{1,0:T(8,128)(2,1)}, bf16[1344,256]{1,0:T(8,128)(2,1)S(1)}, u32[]{:S(2)}, u32[]{:S(2)}) %collective-permute-start.5) | collective-permute-done | bytes 688160 | tf_op jit(solution)/shard_map/ppermute | solution.py:942
  251.1 3.5 %analysis_back_0.1.refs_1_ = bf16[32,4,16,384]{3,2,1,0:T(8,128)(2,1)} custom-call(bf16[6,512,384]{2,1,0:T(8,128)(2,1)S(1)} %copy-done.22, bf16[2496,128]{1,0:T(8,128)(2,1)S(1)} %collective-permute-done.3.refs_3_.refs_1_, bf16[1344,256]{1,0:T(8,128)(2,1)S(1)} %collective-permute-done.5.refs_2_, f32[384,384]{1,0:T(8,128)S(1)} %copy-done.6, ...), custom_call_target="tpu_custom_call" | custom-call | flops 1 | bytes 1 | tf_op jit(solution)/shard_map/analysis_back_0/pallas_call | solution.py:81
  254.7 9.2 %all-to-all-done.4 = bf16[32,112,384]{2,1,0:T(8,128)(2,1)S(1)} async-done(((bf16[32,112,384]{2,1,0:T(8,128)(2,1)}), bf16[32,112,384]{2,1,0:T(8,128)(2,1)S(1)}, u32[]{:S(2)}, u32[]{:S(2)}) %all-to-all-start.4) | async-done | bytes 2752544 | tf_op jit(solution)/shard_map/all_to_all | solution.py:860
  264.8 4.8 %all-to-all-start.5 = ((bf16[32,64,384]{2,1,0:T(8,128)(2,1)}), bf16[32,64,384]{2,1,0:T(8,128)(2,1)}, u32[]{:S(2)}, u32[]{:S(2)}) async-start(bf16[32,64,384]{2,1,0:T(8,128)(2,1)} %bitcast.43), calls=%async_computation.5 | async-start | bytes 3145728 | tf_op jit(solution)/shard_map/all_to_all | solution.py:860
  280.5 13.1 %all-to-all-done.5 = bf16[32,64,384]{2,1,0:T(8,128)(2,1)} async-done(((bf16[32,64,384]{2,1,0:T(8,128)(2,1)}), bf16[32,64,384]{2,1,0:T(8,128)(2,1)}, u32[]{:S(2)}, u32[]{:S(2)}) %all-to-all-start.5) | async-done | bytes 1572896 | tf_op jit(solution)/shard_map/all_to_all | solution.py:860
  293.6 6.7 %field_stage.5 = (bf16[12,192,768]{2,1,0:T(8,128)(2,1)}, f32[192,192]{1,0:T(8,128)}, f32[2,192,192]{2,1,0:T(8,128)}, f32[192,384]{1,0:T(8,128)}) custom-call(bf16[32,4,16,384]{3,2,1,0:T(8,128)(2,1)} %bitcast.21.refs_0_, bf16[256,768]{1,0:T(8,128)(2,1)} %constant.35.clone.refs_1_, bf16[12,192,768]{2,1,0:T(8,128)(2,1)} %field_stage.4.refs_2_), custom_call_target="tpu_custom_call" | custom-call | flops 1 | bytes 1 | tf_op jit(solution)/shard_map/field_stage/pallas_call | solution.py:81
  (89 shorter events, 51.9 us)
Async XLA Ops:
  8.7 54.7 %all-to-all-start = ((bf16[32,144,384]{2,1,0:T(8,128)(2,1)}), bf16[32,144,384]{2,1,0:T(8,128)(2,1)}, u32[]{:S(2)}, u32[]{:S(2)}) async-start(bf16[32,144,384]{2,1,0:T(8,128)(2,1)} %bitcast.37), calls=%async_computation | async-start | bytes 7077888 | tf_op jit(solution)/shard_map/all_to_all | solution.py:860
  17.2 94.7 %collective-permute-start = (bf16[12,192,768]{2,1,0:T(8,128)(2,1)}, bf16[12,192,768]{2,1,0:T(8,128)(2,1)S(1)}, u32[]{:S(2)}, u32[]{:S(2)}) collective-permute-start(bf16[12,192,768]{2,1,0:T(8,128)(2,1)} %bitcast.39), channel_id=1, source_target_pairs={{0,96},{32,0},{64,32},{96,64},{1,97},{33,1},{65,33},{97,65},{2,98}... | collective-permute-start | bytes 10616840 | tf_op jit(solution)/shard_map/ppermute | solution.py:882
  74.8 51.0 %all-to-all-start.1 = ((bf16[32,144,384]{2,1,0:T(8,128)(2,1)}), bf16[32,144,384]{2,1,0:T(8,128)(2,1)}, u32[]{:S(2)}, u32[]{:S(2)}) async-start(bf16[32,144,384]{2,1,0:T(8,128)(2,1)} %bitcast.45), calls=%async_computation.1 | async-start | bytes 7077888 | tf_op jit(solution)/shard_map/all_to_all | solution.py:860
  79.6 28.4 %collective-permute-start.1 = (f32[192,384]{1,0:T(8,128)}, f32[192,384]{1,0:T(8,128)S(1)}, u32[]{:S(2)}, u32[]{:S(2)}) collective-permute-start(f32[192,384]{1,0:T(8,128)} %bitcast.51), channel_id=1, source_target_pairs={{0,96},{32,0},{64,32},{96,64},{1,97},{33,1},{65,33},{97,65},{2,98}... | collective-permute-start | bytes 884744 | tf_op jit(solution)/shard_map/ppermute | solution.py:891
  80.5 27.5 %collective-permute-start.2 = (bf16[2,192,192]{2,1,0:T(8,128)(2,1)}, bf16[2,192,192]{2,1,0:T(8,128)(2,1)S(1)}, u32[]{:S(2)}, u32[]{:S(2)}) collective-permute-start(bf16[2,192,192]{2,1,0:T(8,128)(2,1)} %bitcast.53), channel_id=1, source_target_pairs={{0,96},{32,0},{64,32},{96,64},{1,97},{33,1},{65,33},{97,65},{2,98}... | collective-permute-start | bytes 442376 | tf_op jit(solution)/shard_map/ppermute | solution.py:892
  111.8 14.0 %copy-start.1 = (bf16[12,192,768]{2,1,0:T(8,128)(2,1)}, bf16[12,192,768]{2,1,0:T(8,128)(2,1)S(1)}, u32[]{:S(2)}) copy-start(bf16[12,192,768]{2,1,0:T(8,128)(2,1)S(1)} %collective-permute-done.refs_6_.refs_2_) | copy-start | bytes 10616836
  135.8 23.0 %all-to-all-start.2 = ((bf16[32,144,128]{2,1,0:T(8,128)(2,1)}), bf16[32,144,128]{2,1,0:T(8,128)(2,1)S(1)}, u32[]{:S(2)}, u32[]{:S(2)}) async-start(bf16[32,144,128]{2,1,0:T(8,128)(2,1)} %bitcast.44), calls=%async_computation.2 | async-start | bytes 2359296 | tf_op jit(solution)/shard_map/all_to_all | solution.py:860
  159.8 38.1 %all-to-all-start.3 = ((bf16[32,144,256]{2,1,0:T(8,128)(2,1)}), bf16[32,144,256]{2,1,0:T(8,128)(2,1)S(1)}, u32[]{:S(2)}, u32[]{:S(2)}) async-start(bf16[32,144,256]{2,1,0:T(8,128)(2,1)} %bitcast.47), calls=%async_computation.3 | async-start | bytes 4718592 | tf_op jit(solution)/shard_map/all_to_all | solution.py:860
  173.1 17.8 %collective-permute-start.3 = (bf16[2496,128]{1,0:T(8,128)(2,1)S(1)}, bf16[2496,128]{1,0:T(8,128)(2,1)S(1)}, u32[]{:S(2)}, u32[]{:S(2)}) collective-permute-start(bf16[2496,128]{1,0:T(8,128)(2,1)S(1)} %spectral_backward_0_1_2.1.refs_1_), channel_id=1, source_target_pairs={{0,96},{32,0},{64,32},{96,64},{1,97},{33,1},{65,33},{97,65},{2,98}... | collective-permute-start | bytes 1916936 | tf_op jit(solution)/shard_map/ppermute | solution.py:922
  200.4 2.5 copy-start.4
  201.7 2.2 copy-start.21
  201.8 14.7 %collective-permute-start.4 = (bf16[1152,256]{1,0:T(8,128)(2,1)S(1)}, bf16[1152,256]{1,0:T(8,128)(2,1)S(1)}, u32[]{:S(2)}, u32[]{:S(2)}) collective-permute-start(bf16[1152,256]{1,0:T(8,128)(2,1)S(1)} %spectral_backward_1_2.1.refs_2_.refs_3_), channel_id=1, source_target_pairs={{0,96},{32,0},{64,32},{96,64},{1,97},{33,1},{65,33},{97,65},{2,98}... | collective-permute-start | bytes 1769480 | tf_op jit(solution)/shard_map/ppermute | solution.py:924
  203.9 4.0 %copy-start.9 = (bf16[1344,256]{1,0:T(8,128)(2,1)}, bf16[1344,256]{1,0:T(8,128)(2,1)S(1)}, u32[]{:S(2)}) copy-start(bf16[1344,256]{1,0:T(8,128)(2,1)S(1)} %spectral_backward_0.1.refs_2_.refs_0_) | copy-start | bytes 2064388
  204.0 12.5 %copy-start.5 = (f32[384,384]{1,0:T(8,128)S(1)}, f32[384,384]{1,0:T(8,128)}, u32[]{:S(2)}) copy-start(f32[384,384]{1,0:T(8,128)} %get-tuple-element.44.refs_7_.refs_3_) | copy-start | bytes 1769476
  204.0 12.5 %copy-start.16 = (bf16[384,384]{1,0:T(8,128)(2,1)S(1)}, bf16[384,384]{1,0:T(8,128)(2,1)}, u32[]{:S(2)}) copy-start(bf16[384,384]{1,0:T(8,128)(2,1)} %get-tuple-element.45.refs_8_.refs_4_) | copy-start | bytes 884740
  204.0 12.5 %copy-start.25 = (bf16[6,512,256]{2,1,0:T(8,128)(2,1)S(1)}, bf16[6,512,256]{2,1,0:T(8,128)(2,1)}, u32[]{:S(2)}) copy-start(bf16[6,512,256]{2,1,0:T(8,128)(2,1)} %get-tuple-element.51.refs_0_) | copy-start | bytes 4718596
  216.5 3.0 %copy-start.12 = (bf16[1152,256]{1,0:T(8,128)(2,1)}, bf16[1152,256]{1,0:T(8,128)(2,1)S(1)}, u32[]{:S(2)}) copy-start(bf16[1152,256]{1,0:T(8,128)(2,1)S(1)} %collective-permute-done.4.refs_2_.refs_1_) | copy-start | bytes 1769476
  216.5 3.0 %copy-start.27 = (bf16[6,512,128]{2,1,0:T(8,128)(2,1)S(1)}, bf16[6,512,128]{2,1,0:T(8,128)(2,1)}, u32[]{:S(2)}) copy-start(bf16[6,512,128]{2,1,0:T(8,128)(2,1)} %get-tuple-element.33.refs_0_) | copy-start | bytes 2359300
  221.7 42.2 %all-to-all-start.4 = ((bf16[32,112,384]{2,1,0:T(8,128)(2,1)}), bf16[32,112,384]{2,1,0:T(8,128)(2,1)S(1)}, u32[]{:S(2)}, u32[]{:S(2)}) async-start(bf16[32,112,384]{2,1,0:T(8,128)(2,1)} %bitcast.38), calls=%async_computation.4 | async-start | bytes 5505024 | tf_op jit(solution)/shard_map/all_to_all | solution.py:860
  228.6 19.9 %copy-start.6 = (f32[384,384]{1,0:T(8,128)S(1)}, f32[384,384]{1,0:T(8,128)}, u32[]{:S(2)}) copy-start(f32[384,384]{1,0:T(8,128)} %get-tuple-element.44.refs_7_.refs_3_) | copy-start | bytes 1769476
  229.4 19.0 %collective-permute-start.5 = (bf16[1344,256]{1,0:T(8,128)(2,1)}, bf16[1344,256]{1,0:T(8,128)(2,1)S(1)}, u32[]{:S(2)}, u32[]{:S(2)}) collective-permute-start(bf16[1344,256]{1,0:T(8,128)(2,1)} %copy-done.11), channel_id=1, source_target_pairs={{0,96},{32,0},{64,32},{96,64},{1,97},{33,1},{65,33},{97,65},{2,98}... | collective-permute-start | bytes 2064392 | tf_op jit(solution)/shard_map/ppermute | solution.py:942
  264.8 4.8 %copy-start.29 = (bf16[256,768]{1,0:T(8,128)(2,1)S(1)}, bf16[256,768]{1,0:T(8,128)(2,1)}, u32[]{:S(2)}) copy-start(bf16[256,768]{1,0:T(8,128)(2,1)} %constant.36.clone.refs_1_) | copy-start | bytes 1179652
  264.8 28.8 %all-to-all-start.5 = ((bf16[32,64,384]{2,1,0:T(8,128)(2,1)}), bf16[32,64,384]{2,1,0:T(8,128)(2,1)}, u32[]{:S(2)}, u32[]{:S(2)}) async-start(bf16[32,64,384]{2,1,0:T(8,128)(2,1)} %bitcast.43), calls=%async_computation.5 | async-start | bytes 3145728 | tf_op jit(solution)/shard_map/all_to_all | solution.py:860
  271.7 3.4 %copy-start.28 = (bf16[256,768]{1,0:T(8,128)(2,1)S(1)}, bf16[256,768]{1,0:T(8,128)(2,1)}, u32[]{:S(2)}) copy-start(bf16[256,768]{1,0:T(8,128)(2,1)} %constant.37.clone.refs_1_) | copy-start | bytes 1179652
  (22 other events, 32.0 us)

commit v8 on v7

--- a/solution.py
+++ b/solution.py
@@ -361,7 +361,7 @@
     scaled_ref, payload_ref, recv, payload = refs[8:12]
     a_buffers, st_buffers, scaled_buffers = refs[12:15], refs[15:18], refs[18:21]
     in_sems, out_sems = refs[21:23]
-    schedule = (2, 0, 1)
+    schedule = (2, 1, 0)
     arrivals, departures = {}, []
     for group in schedule:
         tiles = pl.ds(GROUP_TILES * group, GROUP_TILES)
@@ -373,7 +373,7 @@
         for copy in arrivals[group]:
             copy.start()
     for group in schedule:
-        for copy in arrivals[group]:
+        for copy in arrivals[group][:2]:
             copy.wait()
         tiles = [recv[group, :, tile].reshape(SPAN, 2 * C) for tile in range(GROUP_TILES)]
         held = scaled_buffers[group]
@@ -389,6 +389,7 @@
             mixed.append(
                 jnp.concatenate([zeros, product[rows]], axis=0) if local else product[rows]
             )
+        arrivals[group][2].wait()
         for tile in range(GROUP_TILES):
             grid = tile_sum(tile, st_buffers[group], mixed[tile], mixed[tile + 1])
             payload[group, :, tile] = grid.astype(BF16).reshape(DEVICES, TILE, 2 * C)
@@ -445,10 +446,16 @@
 
 
 def grid_kernel(
-    recv_ref, up_ref, turned_ref, proj_ref, table_ref, turned_table_ref,
-    out_ref, grad_ref, scratch, out_scratch, act_scratch, pre_scratch,
+    recv_ref, up_ref, turned_ref, proj_ref, held_ref, turned_table_ref,
+    out_ref, grad_ref, scratch, out_scratch, act_scratch, pre_scratch, table_ref, sem,
 ):
     step = pl.program_id(1)
+    opening = jnp.logical_and(pl.program_id(0) == 0, step == 0)
+
+    @pl.when(opening)
+    def _():
+        pltpu.make_async_copy(held_ref, table_ref, sem).start()
+
     low = half_lanes((MODES, LANES))
     block = 128
 
@@ -491,6 +498,11 @@
         ups = up_ref[2 * pair : 2 * pair + 2].reshape(2 * C, NLON)
         grads = dot(ups, act)
         grad_ref[...] += jnp.where(low_grad, grads[:C], grads[C:])
+
+    @pl.when(opening)
+    def _():
+        pltpu.make_async_copy(held_ref, table_ref, sem).wait()
+
     grad_modes = dot(table_ref[...], pre_scratch[...])
     for pair in range(2):
         lanes = slice(pair * LANES, (pair + 1) * LANES)
@@ -519,7 +531,7 @@
             pl.BlockSpec((4, C, NLON), lambda q, b: (b, 0, 0)),
             pl.BlockSpec((4, NLON, C), lambda q, b: (b, 0, 0)),
             pl.BlockSpec((C, LANES), lambda q, b: (0, q + first)),
-            whole(table.shape),
+            HELD,
             whole(turned_table.shape),
         ],
         [lanes_spec, grad_spec],
@@ -534,6 +546,8 @@
             pltpu.VMEM((rows, LANES), F32),
             pltpu.VMEM((NLON, 2 * LANES), BF16),
             pltpu.VMEM((NLON, 2 * LANES), BF16),
+            pltpu.VMEM(table.shape, BF16),
+            pltpu.SemaphoreType.DMA,
         ],
         name=f"grid_stage_{blocks}",
     )
@@ -609,54 +623,68 @@
     )
 
 
-def synthesis_kernel(group, large_rows, table_ref, small_ref, large_ref, gain_ref, mix_ref, *refs):
-    out_ref, coeff_ref, at_ref, part_ref, sems = refs[-5:]
-    degrees = degrees_of(group)
-    copies = (
-        pltpu.make_async_copy(
-            small_ref.at[pl.ds(BASES[group], PACKED[group])], part_ref, sems.at[0]
-        ),
-        pltpu.make_async_copy(table_ref, at_ref, sems.at[1]),
-    )
-    for copy in copies:
-        copy.start()
-    copies[0].wait()
-    product = dot_nt(jnp.concatenate([part_ref[...], large_ref[large_rows, :]], axis=1), mix_ref[...])
-    for local, rows in enumerate(packed_rows(group)):
-        first = local * degrees
-        skipped = DEVICES * local
-        if skipped:
-            coeff_ref[first : first + skipped, :] = jnp.zeros((skipped, 2 * C), BF16)
-        coeff_ref[first + skipped : first + degrees, :] = (
-            gain_ref[LANES * group + skipped :, :] * product[rows]
-        ).astype(BF16)
-    copies[1].wait()
-    for tile in range(GROUP_TILES):
-        first = coeff_ref[tile * degrees : (tile + 1) * degrees, :]
-        second = coeff_ref[(tile + 1) * degrees : (tile + 2) * degrees, :]
-        out = tile_sum(tile, at_ref, first, second)
-        out_ref[:, tile] = out.astype(BF16).reshape(DEVICES, TILE, 2 * C)
-
-
-def analysis_back(group, at, small, large, first, gain, mix, tiles, block, payload=(), after=()):
-    inputs = (at, small, large, gain, mix, *payload)
-    return call(
-        functools.partial(synthesis_kernel, group, slice(first, first + PACKED[group])),
+def synthesis_kernel(groups, small_ref, large_ref, gain_ref, mix_ref, *refs):
+    count = len(groups)
+    table_refs, refs = refs[:count], refs[-3 * count - 2 :]
+    out_ref, coeff_refs, at_refs = refs[0], refs[1 : 1 + count], refs[1 + count : 1 + 2 * count]
+    part_refs, sems = refs[1 + 2 * count : -1], refs[-1]
+    copies = []
+    for place, group in enumerate(groups):
+        rows = pl.ds(BASES[group], PACKED[group])
+        copies.append(
+            (
+                pltpu.make_async_copy(small_ref.at[rows], part_refs[place], sems.at[0, place]),
+                pltpu.make_async_copy(table_refs[place], at_refs[place], sems.at[1, place]),
+            )
+        )
+    for pair in copies:
+        for copy in pair:
+            copy.start()
+    start = 0
+    for place, group in enumerate(groups):
+        coeff_ref, at_ref = coeff_refs[place], at_refs[place]
+        degrees = degrees_of(group)
+        copies[place][0].wait()
+        large = large_ref[start : start + PACKED[group], :]
+        start += PACKED[group]
+        mixed = jnp.concatenate([part_refs[place][...], large], axis=1)
+        product = dot_nt(mixed, mix_ref[...])
+        for local, rows in enumerate(packed_rows(group)):
+            first = local * degrees
+            skipped = DEVICES * local
+            if skipped:
+                coeff_ref[first : first + skipped, :] = jnp.zeros((skipped, 2 * C), BF16)
+            coeff_ref[first + skipped : first + degrees, :] = (
+                gain_ref[LANES * group + skipped :, :] * product[rows]
+            ).astype(BF16)
+        copies[place][1].wait()
+        for tile in range(GROUP_TILES):
+            first = coeff_ref[tile * degrees : (tile + 1) * degrees, :]
+            second = coeff_ref[(tile + 1) * degrees : (tile + 2) * degrees, :]
+            out = tile_sum(tile, at_ref, first, second).astype(BF16)
+            out_ref[:, GROUP_TILES * place + tile] = out.reshape(DEVICES, TILE, 2 * C)
+
+
+def analysis_back(groups, tables, small, large, gain, mix, tiles, payload=(), after=()):
+    inputs = (small, large, gain, mix, *tables, *payload)
+    count = len(groups)
+    return call(
+        functools.partial(synthesis_kernel, groups),
         inputs,
-        [HELD] * 2 + [whole(value.shape) for value in inputs[2:5]] + [HELD] * len(payload),
-        pl.BlockSpec((DEVICES, GROUP_TILES, TILE, 2 * C), lambda b: (0, block, 0, 0)),
+        [HELD] + [whole(value.shape) for value in inputs[1:4]] + [HELD] * len(inputs[4:]),
+        whole((DEVICES, GROUP_TILES * count, TILE, 2 * C)),
         pltpu.HBM((DEVICES, tiles, TILE, 2 * C), BF16),
         (1,),
         after,
-        aliases={5: 0} if payload else {},
+        aliases={4 + count: 0} if payload else {},
         scratch_shapes=[
-            pltpu.VMEM((GROUP_ORDERS * degrees_of(group), 2 * C), BF16),
-            pltpu.VMEM(at.shape, BF16),
-            pltpu.VMEM((PACKED[group], LANES), BF16),
-            pltpu.SemaphoreType.DMA((2,)),
-        ],
-        vmem=20,
-        name=f"analysis_back_{group}",
+            pltpu.VMEM((GROUP_ORDERS * degrees_of(group), 2 * C), BF16) for group in groups
+        ]
+        + [pltpu.VMEM(table.shape, BF16) for table in tables]
+        + [pltpu.VMEM((PACKED[group], LANES), BF16) for group in groups]
+        + [pltpu.SemaphoreType.DMA((2, count))],
+        vmem=24,
+        name="analysis_back_" + "_".join(str(group) for group in groups),
     )
 
 
@@ -926,23 +954,20 @@
     out_rest = weight_grads(
         scaled, mixed_small, (mixed_0, mixed_rest), mix, gain, proj_small, proj_large
     )
-    for block, group in enumerate((1, 2)):
-        out_rest = analysis_back(
-            group,
-            behind[group][1],
-            moved_small,
-            moved_rest,
-            block * PACKED[1],
-            gain_next,
-            mix_next,
-            2 * GROUP_TILES + 1,
-            block,
-            (out_rest,),
-        )
+    out_rest = analysis_back(
+        (1, 2),
+        [behind[1][1], behind[2][1]],
+        moved_small,
+        moved_rest,
+        gain_next,
+        mix_next,
+        2 * GROUP_TILES + 1,
+        (out_rest,),
+    )
     moved_0 = lax.ppermute(hold(mixed_0, (moved_rest,)), "section", shift)
     recv_rest = exchange(out_rest)
     out_0 = analysis_back(
-        0, behind[0][1], moved_small, moved_0, 0, gain_next, mix_next, GROUP_TILES + 1, 0
+        (0,), [behind[0][1]], moved_small, moved_0, gain_next, mix_next, GROUP_TILES + 1
     )
     out_0, token = attach_totals(recv_rest, out_0)
     recv_0 = exchange(out_0)

time: 302 us -> 301 us (level)
  local copies, waits for them, and re-layouts: 28.6 us -> 24.3 us
    unnamed x68 -> x64, local copies, waits for them, and re-layouts: 21 us -> 16.8 us
    pallas_call x19 -> x18, Pallas kernels: 107 us -> 107 us  [call(): pl.pallas_call(body, grid=grid, in_specs=list(in_specs) + [pl.BlockSpec(m...]
where the time goes in v8:
time: 301 us; the launch traced here: 299 us
  waiting for transfers between devices  130 us (43%)
  Pallas kernels  107 us (36%)
  starting transfers between devices  37.1 us (12%)
  local copies, waits for them, and re-layouts  24.3 us (8%)
    pallas_call x18, Pallas kernels, call(): pl.pallas_call(body, grid=grid, in_specs=list(in_specs) + [pl.BlockSpec(m...  107 us
    all_to_all x6, waiting for transfers between devices, exchange(): moved = lax.all_to_all(flat, 'lat', split_axis=0, concat_axis=0, tiled=True)  59.5 us
    all_to_all x6, starting transfers between devices, exchange(): moved = lax.all_to_all(flat, 'lat', split_axis=0, concat_axis=0, tiled=True)  32.5 us
    ppermute x1, waiting for transfers between devices, shards(): lax.ppermute(mix_weight[0], 'section', shift)  27.4 us
    ppermute x1, waiting for transfers between devices, shards(): moved_0 = lax.ppermute(hold(mixed_0, (moved_rest,)), 'section', shift)  18.8 us
    unnamed x64, local copies, waits for them, and re-layouts  16.8 us
    ppermute x1, waiting for transfers between devices, shards(): moved_small = lax.ppermute(mixed_small, 'section', shift)  16.1 us
    ppermute x1, waiting for transfers between devices, shards(): moved_rest = lax.ppermute(mixed_rest, 'section', shift)  8.53 us
  transfers between devices with their start and end apart: 12, of which 10 were waited for; matrix products, arithmetic and copies ran while one was open for 3% of the time, Pallas kernels for 25%

profile of v8, /device:TPU:6, one launch (start us, length us, event | category | flops | bytes accessed | tf_op | source)
XLA Modules:
  0.0 299.3 jit_solution(16543080734159892825)
XLA Ops:
  0.6 8.1 %spectrum_rows.1.refs_5_.refs_3_ = bf16[4608,384]{1,0:T(8,128)(2,1)} custom-call(bf16[12,192,768]{2,1,0:T(8,128)(2,1)} %bitcast.46, bf16[768,768]{1,0:T(8,128)(2,1)} %constant.34.clone.refs_1_), custom_call_target="tpu_custom_call" | custom-call | flops 1 | bytes 1 | tf_op jit(solution)/shard_map/spectrum_rows/pallas_call | solution.py:81
  8.7 8.4 %all-to-all-start = ((bf16[32,144,384]{2,1,0:T(8,128)(2,1)}), bf16[32,144,384]{2,1,0:T(8,128)(2,1)}, u32[]{:S(2)}, u32[]{:S(2)}) async-start(bf16[32,144,384]{2,1,0:T(8,128)(2,1)} %bitcast.37), calls=%async_computation | async-start | bytes 7077888 | tf_op jit(solution)/shard_map/all_to_all | solution.py:888
  21.9 23.6 %legendre_tables.1 = (bf16[6,384,512]{2,1,0:T(8,128)(2,1)}, bf16[6,512,384]{2,1,0:T(8,128)(2,1)}, bf16[6,384,512]{2,1,0:T(8,128)(2,1)}, bf16[6,512,384]{2,1,0:T(...) custom-call(f32[16,128]{1,0:T(8,128)} %get-tuple-element.63.refs_0_,, ...), custom_call_target="tpu_custom_call" | custom-call | flops 1 | bytes 1 | tf_op jit(solution)/shard_map/legendre_tables/pallas_call | solution.py:81
  45.5 6.3 %copy.23.refs_9_.refs_2_ = bf16[12,768,192]{2,1,0:T(8,128)(2,1)} copy(bf16[12,768,192]{1,2,0:T(8,128)(2,1)} %bitcast.39) | data formatting | bytes 7077888 | tf_op jit(solution)/shard_map/transpose | solution.py:911
  51.8 11.6 %all-to-all-done = bf16[32,144,384]{2,1,0:T(8,128)(2,1)} async-done(((bf16[32,144,384]{2,1,0:T(8,128)(2,1)}), bf16[32,144,384]{2,1,0:T(8,128)(2,1)}, u32[]{:S(2)}, u32[]{:S(2)}) %all-to-all-start) | async-done | bytes 3538976 | tf_op jit(solution)/shard_map/all_to_all | solution.py:888
  63.4 11.0 %spectral_forward.1 = (bf16[2496,384]{1,0:T(8,128)(2,1)}, bf16[32,9,16,384]{3,2,1,0:T(8,128)(2,1)}) custom-call(bf16[32,9,16,384]{3,2,1,0:T(8,128)(2,1)} %bitcast.2.refs_0_, bf16[6,384,512]{2,1,0:T(8,128)(2,1)} %get-tuple-element.33.refs_1_, bf16[6,256,512]{2,1,0:T(8,128)(2,1)} %get-tuple-element.34.refs_2_, bf16[6,128,512]{2,1,0:T(8,128)(2,1)} %get-tuple-element.35.refs_3_, ...), custom_call_target="tpu_custom_call" | custom-call | flops 1 | bytes 1 | tf_op jit(solution)/shard_map/spectral_forward/pallas_call | solution.py:81
  74.4 4.8 %all-to-all-start.1 = ((bf16[32,144,384]{2,1,0:T(8,128)(2,1)}), bf16[32,144,384]{2,1,0:T(8,128)(2,1)}, u32[]{:S(2)}, u32[]{:S(2)}) async-start(bf16[32,144,384]{2,1,0:T(8,128)(2,1)} %bitcast.45), calls=%async_computation.1 | async-start | bytes 7077888 | tf_op jit(solution)/shard_map/all_to_all | solution.py:888
  80.7 27.4 %collective-permute-done.2.refs_1_ = bf16[2,192,192]{2,1,0:T(8,128)(2,1)S(1)} collective-permute-done((bf16[2,192,192]{2,1,0:T(8,128)(2,1)}, bf16[2,192,192]{2,1,0:T(8,128)(2,1)S(1)}, u32[]{:S(2)}, u32[]{:S(2)}) %collective-permute-start.2) | collective-permute-done | bytes 147488 | tf_op jit(solution)/shard_map/ppermute | solution.py:920
  111.9 13.6 %all-to-all-done.1 = bf16[32,144,384]{2,1,0:T(8,128)(2,1)} async-done(((bf16[32,144,384]{2,1,0:T(8,128)(2,1)}), bf16[32,144,384]{2,1,0:T(8,128)(2,1)}, u32[]{:S(2)}, u32[]{:S(2)}) %all-to-all-start.1) | async-done | bytes 3538976 | tf_op jit(solution)/shard_map/all_to_all | solution.py:888
  125.4 10.2 %grid_stage_1.1 = (bf16[4608,128]{1,0:T(8,128)(2,1)}, f32[192,128]{1,0:T(8,128)}) custom-call(bf16[4608,384]{1,0:T(8,128)(2,1)} %bitcast.12.refs_0_, bf16[12,192,768]{2,1,0:T(8,128)(2,1)} %bitcast.40, bf16[12,768,192]{2,1,0:T(8,128)(2,1)} %copy.23.refs_9_.refs_2_, bf16[192,384]{1,0:T(8,128)(2,1)} %get-tuple-element.41.refs_10_.refs_3_, ...), custom_call_target="tpu_custom_call" | custom-call | flops 1 | bytes 1 | tf_op jit(solution)/shard_map/grid_stage_1/pallas_call | solution.py:81
  135.6 4.0 %all-to-all-start.2 = ((bf16[32,144,128]{2,1,0:T(8,128)(2,1)}), bf16[32,144,128]{2,1,0:T(8,128)(2,1)S(1)}, u32[]{:S(2)}, u32[]{:S(2)}) async-start(bf16[32,144,128]{2,1,0:T(8,128)(2,1)} %bitcast.44), calls=%async_computation.2 | async-start | bytes 2359296 | tf_op jit(solution)/shard_map/all_to_all | solution.py:888
  139.6 17.4 %grid_stage_2.1 = (bf16[4608,256]{1,0:T(8,128)(2,1)}, f32[192,256]{1,0:T(8,128)}) custom-call(bf16[4608,384]{1,0:T(8,128)(2,1)} %bitcast.12.refs_0_, bf16[12,192,768]{2,1,0:T(8,128)(2,1)} %bitcast.41, bf16[12,768,192]{2,1,0:T(8,128)(2,1)} %copy.23.refs_9_.refs_2_, bf16[192,384]{1,0:T(8,128)(2,1)} %get-tuple-element.41.refs_10_.refs_3_, ...), custom_call_target="tpu_custom_call" | custom-call | flops 1 | bytes 1 | tf_op jit(solution)/shard_map/grid_stage_2/pallas_call | solution.py:81
  158.6 5.8 %all-to-all-start.3 = ((bf16[32,144,256]{2,1,0:T(8,128)(2,1)}), bf16[32,144,256]{2,1,0:T(8,128)(2,1)S(1)}, u32[]{:S(2)}, u32[]{:S(2)}) async-start(bf16[32,144,256]{2,1,0:T(8,128)(2,1)} %bitcast.47), calls=%async_computation.3 | async-start | bytes 4718592 | tf_op jit(solution)/shard_map/all_to_all | solution.py:888
  173.1 16.1 %collective-permute-done.3.refs_3_.refs_0_ = bf16[2496,128]{1,0:T(8,128)(2,1)S(1)} collective-permute-done((bf16[2496,128]{1,0:T(8,128)(2,1)S(1)}, bf16[2496,128]{1,0:T(8,128)(2,1)S(1)}, u32[]{:S(2)}, u32[]{:S(2)}) %collective-permute-start.3) | collective-permute-done | bytes 639008 | tf_op jit(solution)/shard_map/ppermute | solution.py:950
  189.2 8.3 %all-to-all-done.3 = bf16[32,144,256]{2,1,0:T(8,128)(2,1)S(1)} async-done(((bf16[32,144,256]{2,1,0:T(8,128)(2,1)}), bf16[32,144,256]{2,1,0:T(8,128)(2,1)S(1)}, u32[]{:S(2)}, u32[]{:S(2)}) %all-to-all-start.3) | async-done | bytes 2359328 | tf_op jit(solution)/shard_map/all_to_all | solution.py:888
  203.6 3.9 %weight_grads.1.refs_6_ = bf16[32,7,16,384]{3,2,1,0:T(8,128)(2,1)} custom-call(bf16[2496,384]{1,0:T(8,128)(2,1)S(1)} %copy-done.22, bf16[2496,128]{1,0:T(8,128)(2,1)S(1)} %copy-done.17, bf16[1344,256]{1,0:T(8,128)(2,1)S(1)} %spectral_backward_0.1.refs_2_.refs_0_, bf16[1152,256]{1,0:T(8,128)(2,1)S(1)} %spectral_backward_1_2.1.refs_2_.refs_3_, ...), custom_call_target="tpu_custom_call" | custom-call | flops 1 | bytes 1 | tf_op jit(solution)/shard_map/weight_grads/pallas_call | solution.py:81
  207.6 8.5 %collective-permute-done.4.refs_1_ = bf16[1152,256]{1,0:T(8,128)(2,1)S(1)} collective-permute-done((bf16[1152,256]{1,0:T(8,128)(2,1)S(1)}, bf16[1152,256]{1,0:T(8,128)(2,1)S(1)}, u32[]{:S(2)}, u32[]{:S(2)}) %collective-permute-start.4) | collective-permute-done | bytes 589856 | tf_op jit(solution)/shard_map/ppermute | solution.py:952
  216.1 4.6 %analysis_back_1_2.1 = bf16[32,7,16,384]{3,2,1,0:T(8,128)(2,1)} custom-call(bf16[2496,128]{1,0:T(8,128)(2,1)S(1)} %copy-done.8, bf16[1152,256]{1,0:T(8,128)(2,1)S(1)} %collective-permute-done.4.refs_1_, f32[384,384]{1,0:T(8,128)S(1)} %copy-done.10, bf16[384,384]{1,0:T(8,128)(2,1)S(1)} %copy-done.14, ...), custom_call_target="tpu_custom_call", output_to_operand_aliasing={{}: (6, {})} | custom-call | flops 1 | bytes 1 | tf_op jit(solution)/shard_map/analysis_back_1_2/pallas_call | solution.py:81
  220.7 4.7 %all-to-all-start.4 = ((bf16[32,112,384]{2,1,0:T(8,128)(2,1)}), bf16[32,112,384]{2,1,0:T(8,128)(2,1)S(1)}, u32[]{:S(2)}, u32[]{:S(2)}) async-start(bf16[32,112,384]{2,1,0:T(8,128)(2,1)} %bitcast.42), calls=%async_computation.4 | async-start | bytes 5505024 | tf_op jit(solution)/shard_map/all_to_all | solution.py:888
  226.5 18.8 %collective-permute-done.5.refs_1_ = bf16[1344,256]{1,0:T(8,128)(2,1)S(1)} collective-permute-done((bf16[1344,256]{1,0:T(8,128)(2,1)S(1)}, bf16[1344,256]{1,0:T(8,128)(2,1)S(1)}, u32[]{:S(2)}, u32[]{:S(2)}) %collective-permute-start.5) | collective-permute-done | bytes 688160 | tf_op jit(solution)/shard_map/ppermute | solution.py:967
  251.5 11.4 %all-to-all-done.4 = bf16[32,112,384]{2,1,0:T(8,128)(2,1)S(1)} async-done(((bf16[32,112,384]{2,1,0:T(8,128)(2,1)}), bf16[32,112,384]{2,1,0:T(8,128)(2,1)S(1)}, u32[]{:S(2)}, u32[]{:S(2)}) %all-to-all-start.4) | async-done | bytes 2752544 | tf_op jit(solution)/shard_map/all_to_all | solution.py:888
  263.8 4.8 %all-to-all-start.5 = ((bf16[32,64,384]{2,1,0:T(8,128)(2,1)}), bf16[32,64,384]{2,1,0:T(8,128)(2,1)}, u32[]{:S(2)}, u32[]{:S(2)}) async-start(bf16[32,64,384]{2,1,0:T(8,128)(2,1)} %bitcast.43), calls=%async_computation.5 | async-start | bytes 3145728 | tf_op jit(solution)/shard_map/all_to_all | solution.py:888
  279.6 13.0 %all-to-all-done.5 = bf16[32,64,384]{2,1,0:T(8,128)(2,1)} async-done(((bf16[32,64,384]{2,1,0:T(8,128)(2,1)}), bf16[32,64,384]{2,1,0:T(8,128)(2,1)}, u32[]{:S(2)}, u32[]{:S(2)}) %all-to-all-start.5) | async-done | bytes 1572896 | tf_op jit(solution)/shard_map/all_to_all | solution.py:888
  292.6 6.7 %field_stage.5 = (bf16[12,192,768]{2,1,0:T(8,128)(2,1)}, f32[192,192]{1,0:T(8,128)}, f32[2,192,192]{2,1,0:T(8,128)}, f32[192,384]{1,0:T(8,128)}) custom-call(bf16[32,4,16,384]{3,2,1,0:T(8,128)(2,1)} %bitcast.21.refs_0_, bf16[256,768]{1,0:T(8,128)(2,1)} %constant.35.clone.refs_1_, bf16[12,192,768]{2,1,0:T(8,128)(2,1)} %field_stage.4.refs_2_), custom_call_target="tpu_custom_call" | custom-call | flops 1 | bytes 1 | tf_op jit(solution)/shard_map/field_stage/pallas_call | solution.py:81
  (84 shorter events, 45.4 us)
Async XLA Ops:
  8.7 54.7 %all-to-all-start = ((bf16[32,144,384]{2,1,0:T(8,128)(2,1)}), bf16[32,144,384]{2,1,0:T(8,128)(2,1)}, u32[]{:S(2)}, u32[]{:S(2)}) async-start(bf16[32,144,384]{2,1,0:T(8,128)(2,1)} %bitcast.37), calls=%async_computation | async-start | bytes 7077888 | tf_op jit(solution)/shard_map/all_to_all | solution.py:888
  17.2 94.7 %collective-permute-start = (bf16[12,192,768]{2,1,0:T(8,128)(2,1)}, bf16[12,192,768]{2,1,0:T(8,128)(2,1)S(1)}, u32[]{:S(2)}, u32[]{:S(2)}) collective-permute-start(bf16[12,192,768]{2,1,0:T(8,128)(2,1)} %bitcast.38), channel_id=1, source_target_pairs={{0,96},{32,0},{64,32},{96,64},{1,97},{33,1},{65,33},{97,65},{2,98}... | collective-permute-start | bytes 10616840 | tf_op jit(solution)/shard_map/ppermute | solution.py:910
  74.4 51.0 %all-to-all-start.1 = ((bf16[32,144,384]{2,1,0:T(8,128)(2,1)}), bf16[32,144,384]{2,1,0:T(8,128)(2,1)}, u32[]{:S(2)}, u32[]{:S(2)}) async-start(bf16[32,144,384]{2,1,0:T(8,128)(2,1)} %bitcast.45), calls=%async_computation.1 | async-start | bytes 7077888 | tf_op jit(solution)/shard_map/all_to_all | solution.py:888
  79.2 28.8 %collective-permute-start.1 = (f32[192,384]{1,0:T(8,128)}, f32[192,384]{1,0:T(8,128)S(1)}, u32[]{:S(2)}, u32[]{:S(2)}) collective-permute-start(f32[192,384]{1,0:T(8,128)} %bitcast.51), channel_id=1, source_target_pairs={{0,96},{32,0},{64,32},{96,64},{1,97},{33,1},{65,33},{97,65},{2,98}... | collective-permute-start | bytes 884744 | tf_op jit(solution)/shard_map/ppermute | solution.py:919
  80.1 27.9 %collective-permute-start.2 = (bf16[2,192,192]{2,1,0:T(8,128)(2,1)}, bf16[2,192,192]{2,1,0:T(8,128)(2,1)S(1)}, u32[]{:S(2)}, u32[]{:S(2)}) collective-permute-start(bf16[2,192,192]{2,1,0:T(8,128)(2,1)} %bitcast.53), channel_id=1, source_target_pairs={{0,96},{32,0},{64,32},{96,64},{1,97},{33,1},{65,33},{97,65},{2,98}... | collective-permute-start | bytes 442376 | tf_op jit(solution)/shard_map/ppermute | solution.py:920
  111.9 13.6 %copy-start.1 = (bf16[12,192,768]{2,1,0:T(8,128)(2,1)}, bf16[12,192,768]{2,1,0:T(8,128)(2,1)S(1)}, u32[]{:S(2)}) copy-start(bf16[12,192,768]{2,1,0:T(8,128)(2,1)S(1)} %collective-permute-done.refs_6_.refs_2_) | copy-start | bytes 10616836
  135.6 23.0 %all-to-all-start.2 = ((bf16[32,144,128]{2,1,0:T(8,128)(2,1)}), bf16[32,144,128]{2,1,0:T(8,128)(2,1)S(1)}, u32[]{:S(2)}, u32[]{:S(2)}) async-start(bf16[32,144,128]{2,1,0:T(8,128)(2,1)} %bitcast.44), calls=%async_computation.2 | async-start | bytes 2359296 | tf_op jit(solution)/shard_map/all_to_all | solution.py:888
  158.6 38.9 %all-to-all-start.3 = ((bf16[32,144,256]{2,1,0:T(8,128)(2,1)}), bf16[32,144,256]{2,1,0:T(8,128)(2,1)S(1)}, u32[]{:S(2)}, u32[]{:S(2)}) async-start(bf16[32,144,256]{2,1,0:T(8,128)(2,1)} %bitcast.47), calls=%async_computation.3 | async-start | bytes 4718592 | tf_op jit(solution)/shard_map/all_to_all | solution.py:888
  171.4 17.8 %collective-permute-start.3 = (bf16[2496,128]{1,0:T(8,128)(2,1)S(1)}, bf16[2496,128]{1,0:T(8,128)(2,1)S(1)}, u32[]{:S(2)}, u32[]{:S(2)}) collective-permute-start(bf16[2496,128]{1,0:T(8,128)(2,1)S(1)} %spectral_backward_0_1_2.1.refs_1_), channel_id=1, source_target_pairs={{0,96},{32,0},{64,32},{96,64},{1,97},{33,1},{65,33},{97,65},{2,98}... | collective-permute-start | bytes 1916936 | tf_op jit(solution)/shard_map/ppermute | solution.py:950
  189.2 12.1 %copy-start.7 = (bf16[2496,128]{1,0:T(8,128)(2,1)}, bf16[2496,128]{1,0:T(8,128)(2,1)S(1)}, u32[]{:S(2)}) copy-start(bf16[2496,128]{1,0:T(8,128)(2,1)S(1)} %collective-permute-done.3.refs_3_.refs_0_) | copy-start | bytes 1916932
  201.4 14.7 %collective-permute-start.4 = (bf16[1152,256]{1,0:T(8,128)(2,1)S(1)}, bf16[1152,256]{1,0:T(8,128)(2,1)S(1)}, u32[]{:S(2)}, u32[]{:S(2)}) collective-permute-start(bf16[1152,256]{1,0:T(8,128)(2,1)S(1)} %spectral_backward_1_2.1.refs_2_.refs_3_), channel_id=1, source_target_pairs={{0,96},{32,0},{64,32},{96,64},{1,97},{33,1},{65,33},{97,65},{2,98}... | collective-permute-start | bytes 1769480 | tf_op jit(solution)/shard_map/ppermute | solution.py:952
  203.6 12.5 %copy-start.8 = (bf16[2496,128]{1,0:T(8,128)(2,1)S(1)}, bf16[2496,128]{1,0:T(8,128)(2,1)}, u32[]{:S(2)}) copy-start(bf16[2496,128]{1,0:T(8,128)(2,1)} %copy-done.7) | copy-start | bytes 1916932
  203.6 12.5 %copy-start.10 = (f32[384,384]{1,0:T(8,128)S(1)}, f32[384,384]{1,0:T(8,128)}, u32[]{:S(2)}) copy-start(f32[384,384]{1,0:T(8,128)} %get-tuple-element.43.refs_7_.refs_2_) | copy-start | bytes 1769476
  203.6 12.5 %copy-start.14 = (bf16[384,384]{1,0:T(8,128)(2,1)S(1)}, bf16[384,384]{1,0:T(8,128)(2,1)}, u32[]{:S(2)}) copy-start(bf16[384,384]{1,0:T(8,128)(2,1)} %get-tuple-element.44.refs_8_.refs_3_) | copy-start | bytes 884740
  203.6 12.5 %copy-start.23 = (bf16[6,512,256]{2,1,0:T(8,128)(2,1)S(1)}, bf16[6,512,256]{2,1,0:T(8,128)(2,1)}, u32[]{:S(2)}) copy-start(bf16[6,512,256]{2,1,0:T(8,128)(2,1)} %get-tuple-element.50.refs_4_) | copy-start | bytes 4718596
  203.6 12.5 %copy-start.25 = (bf16[6,512,128]{2,1,0:T(8,128)(2,1)S(1)}, bf16[6,512,128]{2,1,0:T(8,128)(2,1)}, u32[]{:S(2)}) copy-start(bf16[6,512,128]{2,1,0:T(8,128)(2,1)} %get-tuple-element.51.refs_5_) | copy-start | bytes 2359300
  216.1 4.6 %copy-start.19 = (bf16[1152,256]{1,0:T(8,128)(2,1)}, bf16[1152,256]{1,0:T(8,128)(2,1)S(1)}, u32[]{:S(2)}) copy-start(bf16[1152,256]{1,0:T(8,128)(2,1)S(1)} %collective-permute-done.4.refs_1_) | copy-start | bytes 1769476
  220.7 42.2 %all-to-all-start.4 = ((bf16[32,112,384]{2,1,0:T(8,128)(2,1)}), bf16[32,112,384]{2,1,0:T(8,128)(2,1)S(1)}, u32[]{:S(2)}, u32[]{:S(2)}) async-start(bf16[32,112,384]{2,1,0:T(8,128)(2,1)} %bitcast.42), calls=%async_computation.4 | async-start | bytes 5505024 | tf_op jit(solution)/shard_map/all_to_all | solution.py:888
  226.5 18.8 %copy-start.9 = (bf16[2496,128]{1,0:T(8,128)(2,1)S(1)}, bf16[2496,128]{1,0:T(8,128)(2,1)}, u32[]{:S(2)}) copy-start(bf16[2496,128]{1,0:T(8,128)(2,1)} %copy-done.7) | copy-start | bytes 1916932
  226.5 18.8 %copy-start.11 = (f32[384,384]{1,0:T(8,128)S(1)}, f32[384,384]{1,0:T(8,128)}, u32[]{:S(2)}) copy-start(f32[384,384]{1,0:T(8,128)} %get-tuple-element.43.refs_7_.refs_2_) | copy-start | bytes 1769476
  226.5 18.8 %collective-permute-start.5 = (bf16[1344,256]{1,0:T(8,128)(2,1)S(1)}, bf16[1344,256]{1,0:T(8,128)(2,1)S(1)}, u32[]{:S(2)}, u32[]{:S(2)}) collective-permute-start(bf16[1344,256]{1,0:T(8,128)(2,1)S(1)} %hold.1), channel_id=1, source_target_pairs={{0,96},{32,0},{64,32},{96,64},{1,97},{33,1},{65,33},{97,65},{2,98}... | collective-permute-start | bytes 2064392 | tf_op jit(solution)/shard_map/ppermute | solution.py:967
  263.8 4.8 %copy-start.27 = (bf16[256,768]{1,0:T(8,128)(2,1)S(1)}, bf16[256,768]{1,0:T(8,128)(2,1)}, u32[]{:S(2)}) copy-start(bf16[256,768]{1,0:T(8,128)(2,1)} %constant.36.clone.refs_1_) | copy-start | bytes 1179652
  263.8 28.8 %all-to-all-start.5 = ((bf16[32,64,384]{2,1,0:T(8,128)(2,1)}), bf16[32,64,384]{2,1,0:T(8,128)(2,1)}, u32[]{:S(2)}, u32[]{:S(2)}) async-start(bf16[32,64,384]{2,1,0:T(8,128)(2,1)} %bitcast.43), calls=%async_computation.5 | async-start | bytes 3145728 | tf_op jit(solution)/shard_map/all_to_all | solution.py:888
  270.7 3.4 %copy-start.26 = (bf16[256,768]{1,0:T(8,128)(2,1)S(1)}, bf16[256,768]{1,0:T(8,128)(2,1)}, u32[]{:S(2)}) copy-start(bf16[256,768]{1,0:T(8,128)(2,1)} %constant.37.clone.refs_1_) | copy-start | bytes 1179652
  (20 other events, 32.4 us)

commit v9 on v8

--- a/solution.py
+++ b/solution.py
@@ -457,7 +457,7 @@
         pltpu.make_async_copy(held_ref, table_ref, sem).start()
 
     low = half_lanes((MODES, LANES))
-    block = 128
+    block = 256
 
     @pl.when(step == 0)
     def _():
@@ -555,7 +555,7 @@
 
 def backward_kernel(groups, *refs):
     recv_ref, table_refs, out_ref = refs[0], refs[1 : 1 + len(groups)], refs[1 + len(groups)]
-    buffers, sems = refs[2 + len(groups) : -1], refs[-1]
+    buffers, sems = refs[-1 - len(groups) : -1], refs[-1]
     copies = [
         pltpu.make_async_copy(table_refs[place], buffers[place], sems.at[place])
         for place in range(len(groups))
@@ -576,7 +576,7 @@
         first += PACKED[group]
 
 
-def spectral_backward(groups, recv, tables, after=()):
+def spectral_backward(groups, recv, tables, after=(), last=False):
     lanes = recv.shape[-1]
     tiles = GROUP_TILES if len(groups) == 1 else TILES
     block = groups[0] if len(groups) == 1 else 0
@@ -592,15 +592,17 @@
             )
         ]
         + [HELD] * len(groups),
-        whole(out),
-        jax.ShapeDtypeStruct(out, BF16),
+        [whole(out)] + [HELD] * len(groups) * last,
+        [jax.ShapeDtypeStruct(out, BF16)]
+        + [pltpu.HBM(table.shape, BF16) for table in tables] * last,
         (1,),
         after,
+        aliases={1 + place: 1 + place for place in range(len(groups))} if last else {},
         scratch_shapes=[pltpu.VMEM(table.shape, BF16) for table in tables]
         + [pltpu.SemaphoreType.DMA((len(groups),))],
         vmem=20,
         name="spectral_backward_" + "_".join(str(group) for group in groups),
-    )
+    )[0]
 
 
 def hold_kernel(value_ref, out_ref):
@@ -948,7 +950,7 @@
     every = tuple(range(GROUPS))
     mixed_small = spectral_backward(every, small, [table[0] for table in behind])
     moved_small = lax.ppermute(mixed_small, "section", shift)
-    mixed_rest = spectral_backward((1, 2), large, [behind[1][0], behind[2][0]], (moved_small,))
+    mixed_rest = spectral_backward((1, 2), large, [behind[1][0], behind[2][0]], (moved_small,), True)
     moved_rest = lax.ppermute(mixed_rest, "section", shift)
     mixed_0 = spectral_backward((0,), large, [behind[0][0]], (mixed_rest,))
     out_rest = weight_grads(

time: 301 us -> 300 us (level)
    unnamed x64 -> x60, local copies, waits for them, and re-layouts: 16.8 us -> 14.2 us
where the time goes in v9:
time: 300 us; the launch traced here: 298 us
  waiting for transfers between devices  130 us (43%)
  Pallas kernels  108 us (36%)
  starting transfers between devices  37.3 us (12%)
  local copies, waits for them, and re-layouts  21.8 us (7%)
    pallas_call x18, Pallas kernels, call(): pl.pallas_call(body, grid=grid, in_specs=list(in_specs) + [pl.BlockSpec(m...  108 us
    all_to_all x6, waiting for transfers between devices, exchange(): moved = lax.all_to_all(flat, 'lat', split_axis=0, concat_axis=0, tiled=True)  59.2 us
    all_to_all x6, starting transfers between devices, exchange(): moved = lax.all_to_all(flat, 'lat', split_axis=0, concat_axis=0, tiled=True)  32.7 us
    ppermute x1, waiting for transfers between devices, shards(): lax.ppermute(mix_weight[0], 'section', shift)  27.4 us
    ppermute x1, waiting for transfers between devices, shards(): moved_0 = lax.ppermute(hold(mixed_0, (moved_rest,)), 'section', shift)  18.8 us
    ppermute x1, waiting for transfers between devices, shards(): moved_small = lax.ppermute(mixed_small, 'section', shift)  16.1 us
    unnamed x60, local copies, waits for them, and re-layouts  14.2 us
    ppermute x1, waiting for transfers between devices, shards(): moved_rest = lax.ppermute(mixed_rest, 'section', shift)  8.53 us
  transfers between devices with their start and end apart: 12, of which 10 were waited for; matrix products, arithmetic and copies ran while one was open for 3% of the time, Pallas kernels for 25%

profile of v9, /device:TPU:6, one launch (start us, length us, event | category | flops | bytes accessed | tf_op | source)
XLA Modules:
  0.0 298.4 jit_solution(2567026596372861230)
XLA Ops:
  0.6 8.1 %spectrum_rows.1.refs_5_.refs_3_ = bf16[4608,384]{1,0:T(8,128)(2,1)} custom-call(bf16[12,192,768]{2,1,0:T(8,128)(2,1)} %bitcast.46, bf16[768,768]{1,0:T(8,128)(2,1)} %constant.34.clone.refs_1_), custom_call_target="tpu_custom_call" | custom-call | flops 1 | bytes 1 | tf_op jit(solution)/shard_map/spectrum_rows/pallas_call | solution.py:81
  8.7 8.4 %all-to-all-start = ((bf16[32,144,384]{2,1,0:T(8,128)(2,1)}), bf16[32,144,384]{2,1,0:T(8,128)(2,1)}, u32[]{:S(2)}, u32[]{:S(2)}) async-start(bf16[32,144,384]{2,1,0:T(8,128)(2,1)} %bitcast.37), calls=%async_computation | async-start | bytes 7077888 | tf_op jit(solution)/shard_map/all_to_all | solution.py:890
  21.9 23.6 %legendre_tables.1 = (bf16[6,384,512]{2,1,0:T(8,128)(2,1)}, bf16[6,512,384]{2,1,0:T(8,128)(2,1)}, bf16[6,384,512]{2,1,0:T(8,128)(2,1)}, bf16[6,512,384]{2,1,0:T(...) custom-call(f32[16,128]{1,0:T(8,128)} %get-tuple-element.65.refs_0_,, ...), custom_call_target="tpu_custom_call" | custom-call | flops 1 | bytes 1 | tf_op jit(solution)/shard_map/legendre_tables/pallas_call | solution.py:81
  45.6 6.3 %copy.25.refs_9_.refs_2_ = bf16[12,768,192]{2,1,0:T(8,128)(2,1)} copy(bf16[12,768,192]{1,2,0:T(8,128)(2,1)} %bitcast.39) | data formatting | bytes 7077888 | tf_op jit(solution)/shard_map/transpose | solution.py:913
  51.8 11.5 %all-to-all-done = bf16[32,144,384]{2,1,0:T(8,128)(2,1)} async-done(((bf16[32,144,384]{2,1,0:T(8,128)(2,1)}), bf16[32,144,384]{2,1,0:T(8,128)(2,1)}, u32[]{:S(2)}, u32[]{:S(2)}) %all-to-all-start) | async-done | bytes 3538976 | tf_op jit(solution)/shard_map/all_to_all | solution.py:890
  63.4 11.0 %spectral_forward.1 = (bf16[2496,384]{1,0:T(8,128)(2,1)}, bf16[32,9,16,384]{3,2,1,0:T(8,128)(2,1)}) custom-call(bf16[32,9,16,384]{3,2,1,0:T(8,128)(2,1)} %bitcast.2.refs_0_, bf16[6,384,512]{2,1,0:T(8,128)(2,1)} %get-tuple-element.34.refs_1_, bf16[6,256,512]{2,1,0:T(8,128)(2,1)} %get-tuple-element.35.refs_2_, bf16[6,128,512]{2,1,0:T(8,128)(2,1)} %get-tuple-element.36.refs_3_, ...), custom_call_target="tpu_custom_call" | custom-call | flops 1 | bytes 1 | tf_op jit(solution)/shard_map/spectral_forward/pallas_call | solution.py:81
  74.4 4.8 %all-to-all-start.1 = ((bf16[32,144,384]{2,1,0:T(8,128)(2,1)}), bf16[32,144,384]{2,1,0:T(8,128)(2,1)}, u32[]{:S(2)}, u32[]{:S(2)}) async-start(bf16[32,144,384]{2,1,0:T(8,128)(2,1)} %bitcast.45), calls=%async_computation.1 | async-start | bytes 7077888 | tf_op jit(solution)/shard_map/all_to_all | solution.py:890
  80.7 27.4 %collective-permute-done.2.refs_1_ = bf16[2,192,192]{2,1,0:T(8,128)(2,1)S(1)} collective-permute-done((bf16[2,192,192]{2,1,0:T(8,128)(2,1)}, bf16[2,192,192]{2,1,0:T(8,128)(2,1)S(1)}, u32[]{:S(2)}, u32[]{:S(2)}) %collective-permute-start.2) | collective-permute-done | bytes 147488 | tf_op jit(solution)/shard_map/ppermute | solution.py:922
  111.9 13.6 %all-to-all-done.1 = bf16[32,144,384]{2,1,0:T(8,128)(2,1)} async-done(((bf16[32,144,384]{2,1,0:T(8,128)(2,1)}), bf16[32,144,384]{2,1,0:T(8,128)(2,1)}, u32[]{:S(2)}, u32[]{:S(2)}) %all-to-all-start.1) | async-done | bytes 3538976 | tf_op jit(solution)/shard_map/all_to_all | solution.py:890
  125.4 10.3 %grid_stage_1.1 = (bf16[4608,128]{1,0:T(8,128)(2,1)}, f32[192,128]{1,0:T(8,128)}) custom-call(bf16[4608,384]{1,0:T(8,128)(2,1)} %bitcast.12.refs_0_, bf16[12,192,768]{2,1,0:T(8,128)(2,1)} %bitcast.40, bf16[12,768,192]{2,1,0:T(8,128)(2,1)} %copy.25.refs_9_.refs_2_, bf16[192,384]{1,0:T(8,128)(2,1)} %get-tuple-element.42.refs_10_.refs_3_, ...), custom_call_target="tpu_custom_call" | custom-call | flops 1 | bytes 1 | tf_op jit(solution)/shard_map/grid_stage_1/pallas_call | solution.py:81
  135.7 4.0 %all-to-all-start.2 = ((bf16[32,144,128]{2,1,0:T(8,128)(2,1)}), bf16[32,144,128]{2,1,0:T(8,128)(2,1)S(1)}, u32[]{:S(2)}, u32[]{:S(2)}) async-start(bf16[32,144,128]{2,1,0:T(8,128)(2,1)} %bitcast.44), calls=%async_computation.2 | async-start | bytes 2359296 | tf_op jit(solution)/shard_map/all_to_all | solution.py:890
  139.7 17.6 %grid_stage_2.1 = (bf16[4608,256]{1,0:T(8,128)(2,1)}, f32[192,256]{1,0:T(8,128)}) custom-call(bf16[4608,384]{1,0:T(8,128)(2,1)} %bitcast.12.refs_0_, bf16[12,192,768]{2,1,0:T(8,128)(2,1)} %bitcast.41, bf16[12,768,192]{2,1,0:T(8,128)(2,1)} %copy.25.refs_9_.refs_2_, bf16[192,384]{1,0:T(8,128)(2,1)} %get-tuple-element.42.refs_10_.refs_3_, ...), custom_call_target="tpu_custom_call" | custom-call | flops 1 | bytes 1 | tf_op jit(solution)/shard_map/grid_stage_2/pallas_call | solution.py:81
  158.7 6.0 %all-to-all-start.3 = ((bf16[32,144,256]{2,1,0:T(8,128)(2,1)}), bf16[32,144,256]{2,1,0:T(8,128)(2,1)S(1)}, u32[]{:S(2)}, u32[]{:S(2)}) async-start(bf16[32,144,256]{2,1,0:T(8,128)(2,1)} %bitcast.47), calls=%async_computation.3 | async-start | bytes 4718592 | tf_op jit(solution)/shard_map/all_to_all | solution.py:890
  173.4 16.1 %collective-permute-done.3.refs_3_.refs_0_ = bf16[2496,128]{1,0:T(8,128)(2,1)S(1)} collective-permute-done((bf16[2496,128]{1,0:T(8,128)(2,1)S(1)}, bf16[2496,128]{1,0:T(8,128)(2,1)S(1)}, u32[]{:S(2)}, u32[]{:S(2)}) %collective-permute-start.3) | collective-permute-done | bytes 639008 | tf_op jit(solution)/shard_map/ppermute | solution.py:952
  189.5 8.3 %all-to-all-done.3 = bf16[32,144,256]{2,1,0:T(8,128)(2,1)S(1)} async-done(((bf16[32,144,256]{2,1,0:T(8,128)(2,1)}), bf16[32,144,256]{2,1,0:T(8,128)(2,1)S(1)}, u32[]{:S(2)}, u32[]{:S(2)}) %all-to-all-start.3) | async-done | bytes 2359328 | tf_op jit(solution)/shard_map/all_to_all | solution.py:890
  202.7 3.9 %weight_grads.1.refs_6_ = bf16[32,7,16,384]{3,2,1,0:T(8,128)(2,1)} custom-call(bf16[2496,384]{1,0:T(8,128)(2,1)S(1)} %copy-done.20, bf16[2496,128]{1,0:T(8,128)(2,1)S(1)} %copy-done.15, bf16[1344,256]{1,0:T(8,128)(2,1)S(1)} %spectral_backward_0.1.refs_2_.refs_0_, bf16[1152,256]{1,0:T(8,128)(2,1)S(1)} %get-tuple-element.51.refs_2_.refs_3_, ...), custom_call_target="tpu_custom_call" | custom-call | flops 1 | bytes 1 | tf_op jit(solution)/shard_map/weight_grads/pallas_call | solution.py:81
  206.7 8.5 %collective-permute-done.4.refs_1_ = bf16[1152,256]{1,0:T(8,128)(2,1)S(1)} collective-permute-done((bf16[1152,256]{1,0:T(8,128)(2,1)S(1)}, bf16[1152,256]{1,0:T(8,128)(2,1)S(1)}, u32[]{:S(2)}, u32[]{:S(2)}) %collective-permute-start.4) | collective-permute-done | bytes 589856 | tf_op jit(solution)/shard_map/ppermute | solution.py:954
  215.2 4.6 %analysis_back_1_2.1 = bf16[32,7,16,384]{3,2,1,0:T(8,128)(2,1)} custom-call(bf16[2496,128]{1,0:T(8,128)(2,1)S(1)} %copy-done.7, bf16[1152,256]{1,0:T(8,128)(2,1)S(1)} %collective-permute-done.4.refs_1_, f32[384,384]{1,0:T(8,128)S(1)} %copy-done.9, bf16[384,384]{1,0:T(8,128)(2,1)S(1)} %copy-done.12, ...), custom_call_target="tpu_custom_call", output_to_operand_aliasing={{}: (6, {})} | custom-call | flops 1 | bytes 1 | tf_op jit(solution)/shard_map/analysis_back_1_2/pallas_call | solution.py:81
  219.8 4.7 %all-to-all-start.4 = ((bf16[32,112,384]{2,1,0:T(8,128)(2,1)}), bf16[32,112,384]{2,1,0:T(8,128)(2,1)S(1)}, u32[]{:S(2)}, u32[]{:S(2)}) async-start(bf16[32,112,384]{2,1,0:T(8,128)(2,1)} %bitcast.42), calls=%async_computation.4 | async-start | bytes 5505024 | tf_op jit(solution)/shard_map/all_to_all | solution.py:890
  225.6 18.8 %collective-permute-done.5.refs_1_ = bf16[1344,256]{1,0:T(8,128)(2,1)S(1)} collective-permute-done((bf16[1344,256]{1,0:T(8,128)(2,1)S(1)}, bf16[1344,256]{1,0:T(8,128)(2,1)S(1)}, u32[]{:S(2)}, u32[]{:S(2)}) %collective-permute-start.5) | collective-permute-done | bytes 688160 | tf_op jit(solution)/shard_map/ppermute | solution.py:969
  250.6 11.4 %all-to-all-done.4 = bf16[32,112,384]{2,1,0:T(8,128)(2,1)S(1)} async-done(((bf16[32,112,384]{2,1,0:T(8,128)(2,1)}), bf16[32,112,384]{2,1,0:T(8,128)(2,1)S(1)}, u32[]{:S(2)}, u32[]{:S(2)}) %all-to-all-start.4) | async-done | bytes 2752544 | tf_op jit(solution)/shard_map/all_to_all | solution.py:890
  262.9 4.8 %all-to-all-start.5 = ((bf16[32,64,384]{2,1,0:T(8,128)(2,1)}), bf16[32,64,384]{2,1,0:T(8,128)(2,1)}, u32[]{:S(2)}, u32[]{:S(2)}) async-start(bf16[32,64,384]{2,1,0:T(8,128)(2,1)} %bitcast.43), calls=%async_computation.5 | async-start | bytes 3145728 | tf_op jit(solution)/shard_map/all_to_all | solution.py:890
  278.7 13.0 %all-to-all-done.5 = bf16[32,64,384]{2,1,0:T(8,128)(2,1)} async-done(((bf16[32,64,384]{2,1,0:T(8,128)(2,1)}), bf16[32,64,384]{2,1,0:T(8,128)(2,1)}, u32[]{:S(2)}, u32[]{:S(2)}) %all-to-all-start.5) | async-done | bytes 1572896 | tf_op jit(solution)/shard_map/all_to_all | solution.py:890
  291.7 6.7 %field_stage.5 = (bf16[12,192,768]{2,1,0:T(8,128)(2,1)}, f32[192,192]{1,0:T(8,128)}, f32[2,192,192]{2,1,0:T(8,128)}, f32[192,384]{1,0:T(8,128)}) custom-call(bf16[32,4,16,384]{3,2,1,0:T(8,128)(2,1)} %bitcast.21.refs_0_, bf16[256,768]{1,0:T(8,128)(2,1)} %constant.35.clone.refs_1_, bf16[12,192,768]{2,1,0:T(8,128)(2,1)} %field_stage.4.refs_2_), custom_call_target="tpu_custom_call" | custom-call | flops 1 | bytes 1 | tf_op jit(solution)/shard_map/field_stage/pallas_call | solution.py:81
  (80 shorter events, 44.1 us)
Async XLA Ops:
  8.7 54.7 %all-to-all-start = ((bf16[32,144,384]{2,1,0:T(8,128)(2,1)}), bf16[32,144,384]{2,1,0:T(8,128)(2,1)}, u32[]{:S(2)}, u32[]{:S(2)}) async-start(bf16[32,144,384]{2,1,0:T(8,128)(2,1)} %bitcast.37), calls=%async_computation | async-start | bytes 7077888 | tf_op jit(solution)/shard_map/all_to_all | solution.py:890
  17.2 94.7 %collective-permute-start = (bf16[12,192,768]{2,1,0:T(8,128)(2,1)}, bf16[12,192,768]{2,1,0:T(8,128)(2,1)S(1)}, u32[]{:S(2)}, u32[]{:S(2)}) collective-permute-start(bf16[12,192,768]{2,1,0:T(8,128)(2,1)} %bitcast.38), channel_id=1, source_target_pairs={{0,96},{32,0},{64,32},{96,64},{1,97},{33,1},{65,33},{97,65},{2,98}... | collective-permute-start | bytes 10616840 | tf_op jit(solution)/shard_map/ppermute | solution.py:912
  74.4 51.0 %all-to-all-start.1 = ((bf16[32,144,384]{2,1,0:T(8,128)(2,1)}), bf16[32,144,384]{2,1,0:T(8,128)(2,1)}, u32[]{:S(2)}, u32[]{:S(2)}) async-start(bf16[32,144,384]{2,1,0:T(8,128)(2,1)} %bitcast.45), calls=%async_computation.1 | async-start | bytes 7077888 | tf_op jit(solution)/shard_map/all_to_all | solution.py:890
  79.2 28.8 %collective-permute-start.1 = (f32[192,384]{1,0:T(8,128)}, f32[192,384]{1,0:T(8,128)S(1)}, u32[]{:S(2)}, u32[]{:S(2)}) collective-permute-start(f32[192,384]{1,0:T(8,128)} %bitcast.51), channel_id=1, source_target_pairs={{0,96},{32,0},{64,32},{96,64},{1,97},{33,1},{65,33},{97,65},{2,98}... | collective-permute-start | bytes 884744 | tf_op jit(solution)/shard_map/ppermute | solution.py:921
  80.1 27.9 %collective-permute-start.2 = (bf16[2,192,192]{2,1,0:T(8,128)(2,1)}, bf16[2,192,192]{2,1,0:T(8,128)(2,1)S(1)}, u32[]{:S(2)}, u32[]{:S(2)}) collective-permute-start(bf16[2,192,192]{2,1,0:T(8,128)(2,1)} %bitcast.53), channel_id=1, source_target_pairs={{0,96},{32,0},{64,32},{96,64},{1,97},{33,1},{65,33},{97,65},{2,98}... | collective-permute-start | bytes 442376 | tf_op jit(solution)/shard_map/ppermute | solution.py:922
  111.9 13.6 %copy-start.1 = (bf16[12,192,768]{2,1,0:T(8,128)(2,1)}, bf16[12,192,768]{2,1,0:T(8,128)(2,1)S(1)}, u32[]{:S(2)}) copy-start(bf16[12,192,768]{2,1,0:T(8,128)(2,1)S(1)} %collective-permute-done.refs_6_.refs_2_) | copy-start | bytes 10616836
  135.7 23.0 %all-to-all-start.2 = ((bf16[32,144,128]{2,1,0:T(8,128)(2,1)}), bf16[32,144,128]{2,1,0:T(8,128)(2,1)S(1)}, u32[]{:S(2)}, u32[]{:S(2)}) async-start(bf16[32,144,128]{2,1,0:T(8,128)(2,1)} %bitcast.44), calls=%async_computation.2 | async-start | bytes 2359296 | tf_op jit(solution)/shard_map/all_to_all | solution.py:890
  158.7 39.0 %all-to-all-start.3 = ((bf16[32,144,256]{2,1,0:T(8,128)(2,1)}), bf16[32,144,256]{2,1,0:T(8,128)(2,1)S(1)}, u32[]{:S(2)}, u32[]{:S(2)}) async-start(bf16[32,144,256]{2,1,0:T(8,128)(2,1)} %bitcast.47), calls=%async_computation.3 | async-start | bytes 4718592 | tf_op jit(solution)/shard_map/all_to_all | solution.py:890
  171.6 17.8 %collective-permute-start.3 = (bf16[2496,128]{1,0:T(8,128)(2,1)S(1)}, bf16[2496,128]{1,0:T(8,128)(2,1)S(1)}, u32[]{:S(2)}, u32[]{:S(2)}) collective-permute-start(bf16[2496,128]{1,0:T(8,128)(2,1)S(1)} %spectral_backward_0_1_2.1.refs_1_), channel_id=1, source_target_pairs={{0,96},{32,0},{64,32},{96,64},{1,97},{33,1},{65,33},{97,65},{2,98}... | collective-permute-start | bytes 1916936 | tf_op jit(solution)/shard_map/ppermute | solution.py:952
  189.5 10.9 %copy-start.6 = (bf16[2496,128]{1,0:T(8,128)(2,1)}, bf16[2496,128]{1,0:T(8,128)(2,1)S(1)}, u32[]{:S(2)}) copy-start(bf16[2496,128]{1,0:T(8,128)(2,1)S(1)} %collective-permute-done.3.refs_3_.refs_0_) | copy-start | bytes 1916932
  197.7 3.9 %copy-start.4 = (bf16[6,384,512]{2,1,0:T(8,128)(2,1)S(1)}, bf16[6,384,512]{2,1,0:T(8,128)(2,1)}, u32[]{:S(2)}) copy-start(bf16[6,384,512]{2,1,0:T(8,128)(2,1)} %get-tuple-element.47.refs_1_) | copy-start | bytes 7077892
  200.5 14.7 %collective-permute-start.4 = (bf16[1152,256]{1,0:T(8,128)(2,1)S(1)}, bf16[1152,256]{1,0:T(8,128)(2,1)S(1)}, u32[]{:S(2)}, u32[]{:S(2)}) collective-permute-start(bf16[1152,256]{1,0:T(8,128)(2,1)S(1)} %get-tuple-element.51.refs_2_.refs_3_), channel_id=1, source_target_pairs={{0,96},{32,0},{64,32},{96,64},{1,97},{33,1},{65,33},{97,65},{2,98}... | collective-permute-start | bytes 1769480 | tf_op jit(solution)/shard_map/ppermute | solution.py:954
  202.7 12.5 %copy-start.7 = (bf16[2496,128]{1,0:T(8,128)(2,1)S(1)}, bf16[2496,128]{1,0:T(8,128)(2,1)}, u32[]{:S(2)}) copy-start(bf16[2496,128]{1,0:T(8,128)(2,1)} %copy-done.6) | copy-start | bytes 1916932
  202.7 12.5 %copy-start.9 = (f32[384,384]{1,0:T(8,128)S(1)}, f32[384,384]{1,0:T(8,128)}, u32[]{:S(2)}) copy-start(f32[384,384]{1,0:T(8,128)} %get-tuple-element.44.refs_7_.refs_2_) | copy-start | bytes 1769476
  202.7 12.5 %copy-start.12 = (bf16[384,384]{1,0:T(8,128)(2,1)S(1)}, bf16[384,384]{1,0:T(8,128)(2,1)}, u32[]{:S(2)}) copy-start(bf16[384,384]{1,0:T(8,128)(2,1)} %get-tuple-element.45.refs_8_.refs_3_) | copy-start | bytes 884740
  202.7 12.5 %copy-start.21 = (bf16[6,512,256]{2,1,0:T(8,128)(2,1)S(1)}, bf16[6,512,256]{2,1,0:T(8,128)(2,1)}, u32[]{:S(2)}) copy-start(bf16[6,512,256]{2,1,0:T(8,128)(2,1)} %get-tuple-element.52.refs_4_) | copy-start | bytes 4718596
  202.7 12.5 %copy-start.23 = (bf16[6,512,128]{2,1,0:T(8,128)(2,1)S(1)}, bf16[6,512,128]{2,1,0:T(8,128)(2,1)}, u32[]{:S(2)}) copy-start(bf16[6,512,128]{2,1,0:T(8,128)(2,1)} %get-tuple-element.53.refs_5_) | copy-start | bytes 2359300
  215.2 4.6 %copy-start.17 = (bf16[1152,256]{1,0:T(8,128)(2,1)}, bf16[1152,256]{1,0:T(8,128)(2,1)S(1)}, u32[]{:S(2)}) copy-start(bf16[1152,256]{1,0:T(8,128)(2,1)S(1)} %collective-permute-done.4.refs_1_) | copy-start | bytes 1769476
  219.8 42.2 %all-to-all-start.4 = ((bf16[32,112,384]{2,1,0:T(8,128)(2,1)}), bf16[32,112,384]{2,1,0:T(8,128)(2,1)S(1)}, u32[]{:S(2)}, u32[]{:S(2)}) async-start(bf16[32,112,384]{2,1,0:T(8,128)(2,1)} %bitcast.42), calls=%async_computation.4 | async-start | bytes 5505024 | tf_op jit(solution)/shard_map/all_to_all | solution.py:890
  225.6 18.8 %copy-start.8 = (bf16[2496,128]{1,0:T(8,128)(2,1)S(1)}, bf16[2496,128]{1,0:T(8,128)(2,1)}, u32[]{:S(2)}) copy-start(bf16[2496,128]{1,0:T(8,128)(2,1)} %copy-done.6) | copy-start | bytes 1916932
  225.6 18.8 %copy-start.10 = (f32[384,384]{1,0:T(8,128)S(1)}, f32[384,384]{1,0:T(8,128)}, u32[]{:S(2)}) copy-start(f32[384,384]{1,0:T(8,128)} %get-tuple-element.44.refs_7_.refs_2_) | copy-start | bytes 1769476
  225.6 18.8 %collective-permute-start.5 = (bf16[1344,256]{1,0:T(8,128)(2,1)S(1)}, bf16[1344,256]{1,0:T(8,128)(2,1)S(1)}, u32[]{:S(2)}, u32[]{:S(2)}) collective-permute-start(bf16[1344,256]{1,0:T(8,128)(2,1)S(1)} %hold.1), channel_id=1, source_target_pairs={{0,96},{32,0},{64,32},{96,64},{1,97},{33,1},{65,33},{97,65},{2,98}... | collective-permute-start | bytes 2064392 | tf_op jit(solution)/shard_map/ppermute | solution.py:969
  262.9 4.8 %copy-start.25 = (bf16[256,768]{1,0:T(8,128)(2,1)S(1)}, bf16[256,768]{1,0:T(8,128)(2,1)}, u32[]{:S(2)}) copy-start(bf16[256,768]{1,0:T(8,128)(2,1)} %constant.36.clone.refs_1_) | copy-start | bytes 1179652
  262.9 28.8 %all-to-all-start.5 = ((bf16[32,64,384]{2,1,0:T(8,128)(2,1)}), bf16[32,64,384]{2,1,0:T(8,128)(2,1)}, u32[]{:S(2)}, u32[]{:S(2)}) async-start(bf16[32,64,384]{2,1,0:T(8,128)(2,1)} %bitcast.43), calls=%async_computation.5 | async-start | bytes 3145728 | tf_op jit(solution)/shard_map/all_to_all | solution.py:890
  (18 other events, 30.7 us)

commit v10 on v9

--- a/solution.py
+++ b/solution.py
@@ -303,25 +303,19 @@
 
 
 def spectrum_kernel(field_ref, table_ref, out_ref, scratch):
-    step = pl.program_id(0)
     rows = table_ref.shape[0] // 2
     low = half_lanes((rows, LANES))
-    fields = field_ref[...].reshape(4 * C, NLON)
+    fields = field_ref[...].reshape(LAT_LOCAL * HALF, NLON)
     product = dot_nt(table_ref[...], fields)
-    for block in range(4 * GROUPS):
-        inner, index = block // GROUPS, block % GROUPS
-        lanes = slice(block // 2 * LANES, (block // 2 + 1) * LANES)
+    for lat in range(LAT_LOCAL):
+        lanes = slice(lat // 2 * LANES, (lat // 2 + 1) * LANES)
         real, imag = product[:rows, lanes], product[rows:, lanes]
-        if block % 2:
+        if lat % 2:
             tile = jnp.where(low, pltpu.roll(real, HALF, 1), imag)
         else:
             tile = jnp.where(low, real, pltpu.roll(imag, HALF, 1))
-        scratch[index, pl.ds(step * 4 + inner, rows, stride=LAT_LOCAL), :] = tile
-
-    @pl.when(step == LAT_LOCAL // 4 - 1)
-    def _():
-        for index in range(GROUPS):
-            out_ref[:, index * LANES : (index + 1) * LANES] = scratch[index].astype(BF16)
+        scratch[pl.ds(lat, rows, stride=LAT_LOCAL), :] = tile
+    out_ref[...] = scratch[...].astype(BF16)
 
 
 def spectrum_rows(field, table, after=()):
@@ -329,12 +323,12 @@
     return call(
         spectrum_kernel,
         (field, table),
-        [pl.BlockSpec((4, C, NLON), lambda b: (b, 0, 0)), whole(table.shape)],
-        whole((rows, 2 * C)),
+        [pl.BlockSpec((LAT_LOCAL, HALF, NLON), lambda q: (0, q, 0)), whole(table.shape)],
+        pl.BlockSpec((rows, LANES), lambda q: (0, q)),
         jax.ShapeDtypeStruct((rows, 2 * C), BF16),
-        (LAT_LOCAL // 4,),
+        (GROUPS,),
         after,
-        scratch_shapes=[pltpu.VMEM((GROUPS, rows, LANES), F32)],
+        scratch_shapes=[pltpu.VMEM((rows, LANES), F32)],
         name="spectrum_rows",
     )
 

time: 300 us -> 299 us (level)
  no operation moved by 1% of the time
where the time goes in v10:
time: 299 us; the launch traced here: 298 us
  waiting for transfers between devices  130 us (43%)
  Pallas kernels  108 us (36%)
  starting transfers between devices  37.2 us (12%)
  local copies, waits for them, and re-layouts  21.8 us (7%)
    pallas_call x18, Pallas kernels, call(): pl.pallas_call(body, grid=grid, in_specs=list(in_specs) + [pl.BlockSpec(m...  108 us
    all_to_all x6, waiting for transfers between devices, exchange(): moved = lax.all_to_all(flat, 'lat', split_axis=0, concat_axis=0, tiled=True)  59.8 us
    all_to_all x6, starting transfers between devices, exchange(): moved = lax.all_to_all(flat, 'lat', split_axis=0, concat_axis=0, tiled=True)  32.9 us
    ppermute x1, waiting for transfers between devices, shards(): lax.ppermute(mix_weight[0], 'section', shift)  27 us
    ppermute x1, waiting for transfers between devices, shards(): moved_0 = lax.ppermute(hold(mixed_0, (moved_rest,)), 'section', shift)  18.8 us
    ppermute x1, waiting for transfers between devices, shards(): moved_small = lax.ppermute(mixed_small, 'section', shift)  16.1 us
    unnamed x60, local copies, waits for them, and re-layouts  14.2 us
    ppermute x1, waiting for transfers between devices, shards(): moved_rest = lax.ppermute(mixed_rest, 'section', shift)  8.52 us
  transfers between devices with their start and end apart: 12, of which 10 were waited for; matrix products, arithmetic and copies ran while one was open for 3% of the time, Pallas kernels for 25%

profile of v10, /device:TPU:6, one launch (start us, length us, event | category | flops | bytes accessed | tf_op | source)
XLA Modules:
  0.0 297.8 jit_solution(12896885487955934196)
XLA Ops:
  0.6 7.3 %spectrum_rows.1.refs_5_.refs_3_ = bf16[4608,384]{1,0:T(8,128)(2,1)} custom-call(bf16[12,192,768]{2,1,0:T(8,128)(2,1)} %bitcast.46, bf16[768,768]{1,0:T(8,128)(2,1)} %constant.34.clone.refs_1_), custom_call_target="tpu_custom_call" | custom-call | flops 1 | bytes 1 | tf_op jit(solution)/shard_map/spectrum_rows/pallas_call | solution.py:81
  7.9 8.4 %all-to-all-start = ((bf16[32,144,384]{2,1,0:T(8,128)(2,1)}), bf16[32,144,384]{2,1,0:T(8,128)(2,1)}, u32[]{:S(2)}, u32[]{:S(2)}) async-start(bf16[32,144,384]{2,1,0:T(8,128)(2,1)} %bitcast.37), calls=%async_computation | async-start | bytes 7077888 | tf_op jit(solution)/shard_map/all_to_all | solution.py:884
  21.0 23.6 %legendre_tables.1 = (bf16[6,384,512]{2,1,0:T(8,128)(2,1)}, bf16[6,512,384]{2,1,0:T(8,128)(2,1)}, bf16[6,384,512]{2,1,0:T(8,128)(2,1)}, bf16[6,512,384]{2,1,0:T(...) custom-call(f32[16,128]{1,0:T(8,128)} %get-tuple-element.65.refs_0_,, ...), custom_call_target="tpu_custom_call" | custom-call | flops 1 | bytes 1 | tf_op jit(solution)/shard_map/legendre_tables/pallas_call | solution.py:81
  44.6 6.3 %copy.25.refs_9_.refs_2_ = bf16[12,768,192]{2,1,0:T(8,128)(2,1)} copy(bf16[12,768,192]{1,2,0:T(8,128)(2,1)} %bitcast.39) | data formatting | bytes 7077888 | tf_op jit(solution)/shard_map/transpose | solution.py:907
  50.9 11.7 %all-to-all-done = bf16[32,144,384]{2,1,0:T(8,128)(2,1)} async-done(((bf16[32,144,384]{2,1,0:T(8,128)(2,1)}), bf16[32,144,384]{2,1,0:T(8,128)(2,1)}, u32[]{:S(2)}, u32[]{:S(2)}) %all-to-all-start) | async-done | bytes 3538976 | tf_op jit(solution)/shard_map/all_to_all | solution.py:884
  62.6 11.0 %spectral_forward.1 = (bf16[2496,384]{1,0:T(8,128)(2,1)}, bf16[32,9,16,384]{3,2,1,0:T(8,128)(2,1)}) custom-call(bf16[32,9,16,384]{3,2,1,0:T(8,128)(2,1)} %bitcast.2.refs_0_, bf16[6,384,512]{2,1,0:T(8,128)(2,1)} %get-tuple-element.34.refs_1_, bf16[6,256,512]{2,1,0:T(8,128)(2,1)} %get-tuple-element.35.refs_2_, bf16[6,128,512]{2,1,0:T(8,128)(2,1)} %get-tuple-element.36.refs_3_, ...), custom_call_target="tpu_custom_call" | custom-call | flops 1 | bytes 1 | tf_op jit(solution)/shard_map/spectral_forward/pallas_call | solution.py:81
  73.6 5.0 %all-to-all-start.1 = ((bf16[32,144,384]{2,1,0:T(8,128)(2,1)}), bf16[32,144,384]{2,1,0:T(8,128)(2,1)}, u32[]{:S(2)}, u32[]{:S(2)}) async-start(bf16[32,144,384]{2,1,0:T(8,128)(2,1)} %bitcast.45), calls=%async_computation.1 | async-start | bytes 7077888 | tf_op jit(solution)/shard_map/all_to_all | solution.py:884
  80.1 27.0 %collective-permute-done.2.refs_1_ = bf16[2,192,192]{2,1,0:T(8,128)(2,1)S(1)} collective-permute-done((bf16[2,192,192]{2,1,0:T(8,128)(2,1)}, bf16[2,192,192]{2,1,0:T(8,128)(2,1)S(1)}, u32[]{:S(2)}, u32[]{:S(2)}) %collective-permute-start.2) | collective-permute-done | bytes 147488 | tf_op jit(solution)/shard_map/ppermute | solution.py:916
  110.9 13.9 %all-to-all-done.1 = bf16[32,144,384]{2,1,0:T(8,128)(2,1)} async-done(((bf16[32,144,384]{2,1,0:T(8,128)(2,1)}), bf16[32,144,384]{2,1,0:T(8,128)(2,1)}, u32[]{:S(2)}, u32[]{:S(2)}) %all-to-all-start.1) | async-done | bytes 3538976 | tf_op jit(solution)/shard_map/all_to_all | solution.py:884
  124.8 10.3 %grid_stage_1.1 = (bf16[4608,128]{1,0:T(8,128)(2,1)}, f32[192,128]{1,0:T(8,128)}) custom-call(bf16[4608,384]{1,0:T(8,128)(2,1)} %bitcast.12.refs_0_, bf16[12,192,768]{2,1,0:T(8,128)(2,1)} %bitcast.40, bf16[12,768,192]{2,1,0:T(8,128)(2,1)} %copy.25.refs_9_.refs_2_, bf16[192,384]{1,0:T(8,128)(2,1)} %get-tuple-element.42.refs_10_.refs_3_, ...), custom_call_target="tpu_custom_call" | custom-call | flops 1 | bytes 1 | tf_op jit(solution)/shard_map/grid_stage_1/pallas_call | solution.py:81
  135.1 4.0 %all-to-all-start.2 = ((bf16[32,144,128]{2,1,0:T(8,128)(2,1)}), bf16[32,144,128]{2,1,0:T(8,128)(2,1)S(1)}, u32[]{:S(2)}, u32[]{:S(2)}) async-start(bf16[32,144,128]{2,1,0:T(8,128)(2,1)} %bitcast.44), calls=%async_computation.2 | async-start | bytes 2359296 | tf_op jit(solution)/shard_map/all_to_all | solution.py:884
  139.1 17.6 %grid_stage_2.1 = (bf16[4608,256]{1,0:T(8,128)(2,1)}, f32[192,256]{1,0:T(8,128)}) custom-call(bf16[4608,384]{1,0:T(8,128)(2,1)} %bitcast.12.refs_0_, bf16[12,192,768]{2,1,0:T(8,128)(2,1)} %bitcast.41, bf16[12,768,192]{2,1,0:T(8,128)(2,1)} %copy.25.refs_9_.refs_2_, bf16[192,384]{1,0:T(8,128)(2,1)} %get-tuple-element.42.refs_10_.refs_3_, ...), custom_call_target="tpu_custom_call" | custom-call | flops 1 | bytes 1 | tf_op jit(solution)/shard_map/grid_stage_2/pallas_call | solution.py:81
  158.1 6.0 %all-to-all-start.3 = ((bf16[32,144,256]{2,1,0:T(8,128)(2,1)}), bf16[32,144,256]{2,1,0:T(8,128)(2,1)S(1)}, u32[]{:S(2)}, u32[]{:S(2)}) async-start(bf16[32,144,256]{2,1,0:T(8,128)(2,1)} %bitcast.47), calls=%async_computation.3 | async-start | bytes 4718592 | tf_op jit(solution)/shard_map/all_to_all | solution.py:884
  172.8 16.1 %collective-permute-done.3.refs_3_.refs_0_ = bf16[2496,128]{1,0:T(8,128)(2,1)S(1)} collective-permute-done((bf16[2496,128]{1,0:T(8,128)(2,1)S(1)}, bf16[2496,128]{1,0:T(8,128)(2,1)S(1)}, u32[]{:S(2)}, u32[]{:S(2)}) %collective-permute-start.3) | collective-permute-done | bytes 639008 | tf_op jit(solution)/shard_map/ppermute | solution.py:946
  188.9 8.3 %all-to-all-done.3 = bf16[32,144,256]{2,1,0:T(8,128)(2,1)S(1)} async-done(((bf16[32,144,256]{2,1,0:T(8,128)(2,1)}), bf16[32,144,256]{2,1,0:T(8,128)(2,1)S(1)}, u32[]{:S(2)}, u32[]{:S(2)}) %all-to-all-start.3) | async-done | bytes 2359328 | tf_op jit(solution)/shard_map/all_to_all | solution.py:884
  202.1 3.9 %weight_grads.1.refs_6_ = bf16[32,7,16,384]{3,2,1,0:T(8,128)(2,1)} custom-call(bf16[2496,384]{1,0:T(8,128)(2,1)S(1)} %copy-done.20, bf16[2496,128]{1,0:T(8,128)(2,1)S(1)} %copy-done.15, bf16[1344,256]{1,0:T(8,128)(2,1)S(1)} %spectral_backward_0.1.refs_2_.refs_0_, bf16[1152,256]{1,0:T(8,128)(2,1)S(1)} %get-tuple-element.51.refs_2_.refs_3_, ...), custom_call_target="tpu_custom_call" | custom-call | flops 1 | bytes 1 | tf_op jit(solution)/shard_map/weight_grads/pallas_call | solution.py:81
  206.0 8.5 %collective-permute-done.4.refs_1_ = bf16[1152,256]{1,0:T(8,128)(2,1)S(1)} collective-permute-done((bf16[1152,256]{1,0:T(8,128)(2,1)S(1)}, bf16[1152,256]{1,0:T(8,128)(2,1)S(1)}, u32[]{:S(2)}, u32[]{:S(2)}) %collective-permute-start.4) | collective-permute-done | bytes 589856 | tf_op jit(solution)/shard_map/ppermute | solution.py:948
  214.6 4.6 %analysis_back_1_2.1 = bf16[32,7,16,384]{3,2,1,0:T(8,128)(2,1)} custom-call(bf16[2496,128]{1,0:T(8,128)(2,1)S(1)} %copy-done.7, bf16[1152,256]{1,0:T(8,128)(2,1)S(1)} %collective-permute-done.4.refs_1_, f32[384,384]{1,0:T(8,128)S(1)} %copy-done.9, bf16[384,384]{1,0:T(8,128)(2,1)S(1)} %copy-done.12, ...), custom_call_target="tpu_custom_call", output_to_operand_aliasing={{}: (6, {})} | custom-call | flops 1 | bytes 1 | tf_op jit(solution)/shard_map/analysis_back_1_2/pallas_call | solution.py:81
  219.2 4.7 %all-to-all-start.4 = ((bf16[32,112,384]{2,1,0:T(8,128)(2,1)}), bf16[32,112,384]{2,1,0:T(8,128)(2,1)S(1)}, u32[]{:S(2)}, u32[]{:S(2)}) async-start(bf16[32,112,384]{2,1,0:T(8,128)(2,1)} %bitcast.42), calls=%async_computation.4 | async-start | bytes 5505024 | tf_op jit(solution)/shard_map/all_to_all | solution.py:884
  225.0 18.8 %collective-permute-done.5.refs_1_ = bf16[1344,256]{1,0:T(8,128)(2,1)S(1)} collective-permute-done((bf16[1344,256]{1,0:T(8,128)(2,1)S(1)}, bf16[1344,256]{1,0:T(8,128)(2,1)S(1)}, u32[]{:S(2)}, u32[]{:S(2)}) %collective-permute-start.5) | collective-permute-done | bytes 688160 | tf_op jit(solution)/shard_map/ppermute | solution.py:963
  250.0 11.4 %all-to-all-done.4 = bf16[32,112,384]{2,1,0:T(8,128)(2,1)S(1)} async-done(((bf16[32,112,384]{2,1,0:T(8,128)(2,1)}), bf16[32,112,384]{2,1,0:T(8,128)(2,1)S(1)}, u32[]{:S(2)}, u32[]{:S(2)}) %all-to-all-start.4) | async-done | bytes 2752544 | tf_op jit(solution)/shard_map/all_to_all | solution.py:884
  262.3 4.8 %all-to-all-start.5 = ((bf16[32,64,384]{2,1,0:T(8,128)(2,1)}), bf16[32,64,384]{2,1,0:T(8,128)(2,1)}, u32[]{:S(2)}, u32[]{:S(2)}) async-start(bf16[32,64,384]{2,1,0:T(8,128)(2,1)} %bitcast.43), calls=%async_computation.5 | async-start | bytes 3145728 | tf_op jit(solution)/shard_map/all_to_all | solution.py:884
  278.0 13.0 %all-to-all-done.5 = bf16[32,64,384]{2,1,0:T(8,128)(2,1)} async-done(((bf16[32,64,384]{2,1,0:T(8,128)(2,1)}), bf16[32,64,384]{2,1,0:T(8,128)(2,1)}, u32[]{:S(2)}, u32[]{:S(2)}) %all-to-all-start.5) | async-done | bytes 1572896 | tf_op jit(solution)/shard_map/all_to_all | solution.py:884
  291.1 6.7 %field_stage.5 = (bf16[12,192,768]{2,1,0:T(8,128)(2,1)}, f32[192,192]{1,0:T(8,128)}, f32[2,192,192]{2,1,0:T(8,128)}, f32[192,384]{1,0:T(8,128)}) custom-call(bf16[32,4,16,384]{3,2,1,0:T(8,128)(2,1)} %bitcast.21.refs_0_, bf16[256,768]{1,0:T(8,128)(2,1)} %constant.35.clone.refs_1_, bf16[12,192,768]{2,1,0:T(8,128)(2,1)} %field_stage.4.refs_2_), custom_call_target="tpu_custom_call" | custom-call | flops 1 | bytes 1 | tf_op jit(solution)/shard_map/field_stage/pallas_call | solution.py:81
  (80 shorter events, 43.9 us)
Async XLA Ops:
  7.9 54.7 %all-to-all-start = ((bf16[32,144,384]{2,1,0:T(8,128)(2,1)}), bf16[32,144,384]{2,1,0:T(8,128)(2,1)}, u32[]{:S(2)}, u32[]{:S(2)}) async-start(bf16[32,144,384]{2,1,0:T(8,128)(2,1)} %bitcast.37), calls=%async_computation | async-start | bytes 7077888 | tf_op jit(solution)/shard_map/all_to_all | solution.py:884
  16.4 94.5 %collective-permute-start = (bf16[12,192,768]{2,1,0:T(8,128)(2,1)}, bf16[12,192,768]{2,1,0:T(8,128)(2,1)S(1)}, u32[]{:S(2)}, u32[]{:S(2)}) collective-permute-start(bf16[12,192,768]{2,1,0:T(8,128)(2,1)} %bitcast.38), channel_id=1, source_target_pairs={{0,96},{32,0},{64,32},{96,64},{1,97},{33,1},{65,33},{97,65},{2,98}... | collective-permute-start | bytes 10616840 | tf_op jit(solution)/shard_map/ppermute | solution.py:906
  73.6 51.2 %all-to-all-start.1 = ((bf16[32,144,384]{2,1,0:T(8,128)(2,1)}), bf16[32,144,384]{2,1,0:T(8,128)(2,1)}, u32[]{:S(2)}, u32[]{:S(2)}) async-start(bf16[32,144,384]{2,1,0:T(8,128)(2,1)} %bitcast.45), calls=%async_computation.1 | async-start | bytes 7077888 | tf_op jit(solution)/shard_map/all_to_all | solution.py:884
  78.6 28.4 %collective-permute-start.1 = (f32[192,384]{1,0:T(8,128)}, f32[192,384]{1,0:T(8,128)S(1)}, u32[]{:S(2)}, u32[]{:S(2)}) collective-permute-start(f32[192,384]{1,0:T(8,128)} %bitcast.51), channel_id=1, source_target_pairs={{0,96},{32,0},{64,32},{96,64},{1,97},{33,1},{65,33},{97,65},{2,98}... | collective-permute-start | bytes 884744 | tf_op jit(solution)/shard_map/ppermute | solution.py:915
  79.5 27.5 %collective-permute-start.2 = (bf16[2,192,192]{2,1,0:T(8,128)(2,1)}, bf16[2,192,192]{2,1,0:T(8,128)(2,1)S(1)}, u32[]{:S(2)}, u32[]{:S(2)}) collective-permute-start(bf16[2,192,192]{2,1,0:T(8,128)(2,1)} %bitcast.53), channel_id=1, source_target_pairs={{0,96},{32,0},{64,32},{96,64},{1,97},{33,1},{65,33},{97,65},{2,98}... | collective-permute-start | bytes 442376 | tf_op jit(solution)/shard_map/ppermute | solution.py:916
  110.9 13.9 %copy-start.1 = (bf16[12,192,768]{2,1,0:T(8,128)(2,1)}, bf16[12,192,768]{2,1,0:T(8,128)(2,1)S(1)}, u32[]{:S(2)}) copy-start(bf16[12,192,768]{2,1,0:T(8,128)(2,1)S(1)} %collective-permute-done.refs_6_.refs_2_) | copy-start | bytes 10616836
  135.1 23.0 %all-to-all-start.2 = ((bf16[32,144,128]{2,1,0:T(8,128)(2,1)}), bf16[32,144,128]{2,1,0:T(8,128)(2,1)S(1)}, u32[]{:S(2)}, u32[]{:S(2)}) async-start(bf16[32,144,128]{2,1,0:T(8,128)(2,1)} %bitcast.44), calls=%async_computation.2 | async-start | bytes 2359296 | tf_op jit(solution)/shard_map/all_to_all | solution.py:884
  158.1 39.0 %all-to-all-start.3 = ((bf16[32,144,256]{2,1,0:T(8,128)(2,1)}), bf16[32,144,256]{2,1,0:T(8,128)(2,1)S(1)}, u32[]{:S(2)}, u32[]{:S(2)}) async-start(bf16[32,144,256]{2,1,0:T(8,128)(2,1)} %bitcast.47), calls=%async_computation.3 | async-start | bytes 4718592 | tf_op jit(solution)/shard_map/all_to_all | solution.py:884
  171.0 17.8 %collective-permute-start.3 = (bf16[2496,128]{1,0:T(8,128)(2,1)S(1)}, bf16[2496,128]{1,0:T(8,128)(2,1)S(1)}, u32[]{:S(2)}, u32[]{:S(2)}) collective-permute-start(bf16[2496,128]{1,0:T(8,128)(2,1)S(1)} %spectral_backward_0_1_2.1.refs_1_), channel_id=1, source_target_pairs={{0,96},{32,0},{64,32},{96,64},{1,97},{33,1},{65,33},{97,65},{2,98}... | collective-permute-start | bytes 1916936 | tf_op jit(solution)/shard_map/ppermute | solution.py:946
  188.9 10.9 %copy-start.6 = (bf16[2496,128]{1,0:T(8,128)(2,1)}, bf16[2496,128]{1,0:T(8,128)(2,1)S(1)}, u32[]{:S(2)}) copy-start(bf16[2496,128]{1,0:T(8,128)(2,1)S(1)} %collective-permute-done.3.refs_3_.refs_0_) | copy-start | bytes 1916932
  197.1 3.8 %copy-start.4 = (bf16[6,384,512]{2,1,0:T(8,128)(2,1)S(1)}, bf16[6,384,512]{2,1,0:T(8,128)(2,1)}, u32[]{:S(2)}) copy-start(bf16[6,384,512]{2,1,0:T(8,128)(2,1)} %get-tuple-element.47.refs_1_) | copy-start | bytes 7077892
  199.9 14.7 %collective-permute-start.4 = (bf16[1152,256]{1,0:T(8,128)(2,1)S(1)}, bf16[1152,256]{1,0:T(8,128)(2,1)S(1)}, u32[]{:S(2)}, u32[]{:S(2)}) collective-permute-start(bf16[1152,256]{1,0:T(8,128)(2,1)S(1)} %get-tuple-element.51.refs_2_.refs_3_), channel_id=1, source_target_pairs={{0,96},{32,0},{64,32},{96,64},{1,97},{33,1},{65,33},{97,65},{2,98}... | collective-permute-start | bytes 1769480 | tf_op jit(solution)/shard_map/ppermute | solution.py:948
  202.0 12.5 %copy-start.7 = (bf16[2496,128]{1,0:T(8,128)(2,1)S(1)}, bf16[2496,128]{1,0:T(8,128)(2,1)}, u32[]{:S(2)}) copy-start(bf16[2496,128]{1,0:T(8,128)(2,1)} %copy-done.6) | copy-start | bytes 1916932
  202.0 12.5 %copy-start.9 = (f32[384,384]{1,0:T(8,128)S(1)}, f32[384,384]{1,0:T(8,128)}, u32[]{:S(2)}) copy-start(f32[384,384]{1,0:T(8,128)} %get-tuple-element.44.refs_7_.refs_2_) | copy-start | bytes 1769476
  202.1 12.5 %copy-start.12 = (bf16[384,384]{1,0:T(8,128)(2,1)S(1)}, bf16[384,384]{1,0:T(8,128)(2,1)}, u32[]{:S(2)}) copy-start(bf16[384,384]{1,0:T(8,128)(2,1)} %get-tuple-element.45.refs_8_.refs_3_) | copy-start | bytes 884740
  202.1 12.5 %copy-start.21 = (bf16[6,512,256]{2,1,0:T(8,128)(2,1)S(1)}, bf16[6,512,256]{2,1,0:T(8,128)(2,1)}, u32[]{:S(2)}) copy-start(bf16[6,512,256]{2,1,0:T(8,128)(2,1)} %get-tuple-element.52.refs_4_) | copy-start | bytes 4718596
  202.1 12.5 %copy-start.23 = (bf16[6,512,128]{2,1,0:T(8,128)(2,1)S(1)}, bf16[6,512,128]{2,1,0:T(8,128)(2,1)}, u32[]{:S(2)}) copy-start(bf16[6,512,128]{2,1,0:T(8,128)(2,1)} %get-tuple-element.53.refs_5_) | copy-start | bytes 2359300
  214.5 4.7 %copy-start.17 = (bf16[1152,256]{1,0:T(8,128)(2,1)}, bf16[1152,256]{1,0:T(8,128)(2,1)S(1)}, u32[]{:S(2)}) copy-start(bf16[1152,256]{1,0:T(8,128)(2,1)S(1)} %collective-permute-done.4.refs_1_) | copy-start | bytes 1769476
  219.2 42.2 %all-to-all-start.4 = ((bf16[32,112,384]{2,1,0:T(8,128)(2,1)}), bf16[32,112,384]{2,1,0:T(8,128)(2,1)S(1)}, u32[]{:S(2)}, u32[]{:S(2)}) async-start(bf16[32,112,384]{2,1,0:T(8,128)(2,1)} %bitcast.42), calls=%async_computation.4 | async-start | bytes 5505024 | tf_op jit(solution)/shard_map/all_to_all | solution.py:884
  225.0 18.8 %copy-start.8 = (bf16[2496,128]{1,0:T(8,128)(2,1)S(1)}, bf16[2496,128]{1,0:T(8,128)(2,1)}, u32[]{:S(2)}) copy-start(bf16[2496,128]{1,0:T(8,128)(2,1)} %copy-done.6) | copy-start | bytes 1916932
  225.0 18.8 %copy-start.10 = (f32[384,384]{1,0:T(8,128)S(1)}, f32[384,384]{1,0:T(8,128)}, u32[]{:S(2)}) copy-start(f32[384,384]{1,0:T(8,128)} %get-tuple-element.44.refs_7_.refs_2_) | copy-start | bytes 1769476
  225.0 18.8 %collective-permute-start.5 = (bf16[1344,256]{1,0:T(8,128)(2,1)S(1)}, bf16[1344,256]{1,0:T(8,128)(2,1)S(1)}, u32[]{:S(2)}, u32[]{:S(2)}) collective-permute-start(bf16[1344,256]{1,0:T(8,128)(2,1)S(1)} %hold.1), channel_id=1, source_target_pairs={{0,96},{32,0},{64,32},{96,64},{1,97},{33,1},{65,33},{97,65},{2,98}... | collective-permute-start | bytes 2064392 | tf_op jit(solution)/shard_map/ppermute | solution.py:963
  262.3 4.8 %copy-start.25 = (bf16[256,768]{1,0:T(8,128)(2,1)S(1)}, bf16[256,768]{1,0:T(8,128)(2,1)}, u32[]{:S(2)}) copy-start(bf16[256,768]{1,0:T(8,128)(2,1)} %constant.36.clone.refs_1_) | copy-start | bytes 1179652
  262.3 28.8 %all-to-all-start.5 = ((bf16[32,64,384]{2,1,0:T(8,128)(2,1)}), bf16[32,64,384]{2,1,0:T(8,128)(2,1)}, u32[]{:S(2)}, u32[]{:S(2)}) async-start(bf16[32,64,384]{2,1,0:T(8,128)(2,1)} %bitcast.43), calls=%async_computation.5 | async-start | bytes 3145728 | tf_op jit(solution)/shard_map/all_to_all | solution.py:884
  (18 other events, 30.6 us)
